TPU v7x, 32 devices: a whole 2x2x4 slice. The times are simulated.
32 devices in a mesh: lat: 4 (over x, core), lon: 8 (over z, y).
Axes of the slice: x: 2, y: 2, z: 4, core: 2. Of those that a mesh axis runs over, the one named last changes fastest.
Arguments:
- air_temp: float32 [128, 2880, 128], P('lat', 'lon'), may hold values from -6 to 6
- sea_temp: float32 [128, 2880], P(('lat', 'lon')), may hold values from -6 to 6
- land_sea: int32 [128, 2880], P('lat', 'lon'), may hold values 0 or 1
- courant: float32 [128], replicated, may hold values from -0.4 to 0.4
- vertical_mix: float32 [128, 128], replicated, may hold values from -0.25 to 0.25
- cutoffs: int32 [32], replicated, may hold values from 1 to 127, as said below
Outputs:
- air_final: float32 [128, 2880, 128], P('lat', 'lon')
- sea_final: float32 [128, 2880], P(('lat', 'lon'))
Inputs may be any that keep to these rules, and one draw needn't show every extreme that they name: cutoffs holds the rows in the order of the filtered rows; some row keeps exactly 127.
All inputs are finite; a program needn't handle non-finite values. No bound on the sum of `land_sea` on one device may be relied on, other than what follows from the above.
Results may differ from a plain program's by a relative error of at most 0.0001.
Values sent between devices are 32-bit elements; how exact they have to be, the bound alone decides.
No kernel may reach another device: no remote copies, remote signals or barrier semaphores. Data moves between devices by JAX's collectives and lax.ppermute only.
A program may use at most 128 MiB of HBM per device.

v0:
```python
import math

import jax
import jax.numpy as jnp
from jax import lax
from jax.sharding import PartitionSpec as P

NLON = 2880
NPOLE = 16
KMAX = 127
STEPS = 6


diffusion_rate = 0.1
air_gain = 0.5
ocean_gain = 0.3
ocean_diffusion = 0.2
sea_coef = 0.5
land_coef = 0.15


def with_halo(array, sides, width, wrap):
    for axis, dim in sides:
        size, length = (lax.axis_size(axis), array.shape[dim])
        up = [(i, (i + 1) % size) for i in range(size if wrap else size - 1)]
        down = [(j, i) for i, j in up]
        last = lax.slice_in_dim(array, length - width, length, axis=dim)
        leading = lax.slice_in_dim(array, 0, width, axis=dim)
        before = lax.ppermute(last, axis, up)
        after = lax.ppermute(leading, axis, down)
        array = jnp.concatenate([before, array, after], axis=dim)
    return array


def horizontal(air_temp, courant):
    lat_padded = with_halo(air_temp, (("lat", 0),), 1, False)
    lon_padded = with_halo(air_temp, (("lon", 1),), 1, True)
    north_cell = lat_padded[:-2]
    south_cell = lat_padded[2:]
    west_cell = lon_padded[:, :-2]
    east_cell = lon_padded[:, 2:]
    laplace = north_cell + south_cell + east_cell + west_cell - 4.0 * air_temp
    return air_temp + diffusion_rate * laplace - 0.5 * courant * (east_cell - west_cell)


def tables(first_column, count):
    wavenum = jnp.arange(KMAX + 1, dtype=jnp.int32)
    columns = first_column + jnp.arange(count, dtype=jnp.int32)
    phase = (columns[:, None] * wavenum[None, :] % NLON).astype(jnp.float32) * (
        2.0 * math.pi / NLON
    )
    return (jnp.cos(phase), jnp.sin(phase))


def spectra(polar_rows, cosine, sine_table):
    real_part = jnp.einsum("pcl,ck->pkl", polar_rows, cosine, precision=lax.Precision.HIGHEST)
    imag_part = jnp.einsum("pcl,ck->pkl", polar_rows, sine_table, precision=lax.Precision.HIGHEST)
    return (real_part, imag_part)


def inverse(real_part, imag_part, cutoff, cosine, sine_table):
    wavenum = jnp.arange(KMAX + 1, dtype=jnp.int32)
    weights = (
        jnp.where(
            wavenum[None, :] <= cutoff[:, None], jnp.where(wavenum[None, :] == 0, 1.0, 2.0), 0.0
        )
        / NLON
    )
    weights = weights[:, :, None]
    return jnp.einsum(
        "pkl,ck->pcl", real_part * weights, cosine, precision=lax.Precision.HIGHEST
    ) + jnp.einsum("pkl,ck->pcl", imag_part * weights, sine_table, precision=lax.Precision.HIGHEST)


def ocean_step(sea_temp, flux_ocean):
    padded = with_halo(sea_temp, ((("lat", "lon"), 0),), 1, False)
    laplace = (
        padded[:-2]
        + padded[2:]
        + jnp.roll(sea_temp, 1, axis=1)
        + jnp.roll(sea_temp, -1, axis=1)
        - 4.0 * sea_temp
    )
    return sea_temp - ocean_gain * flux_ocean + ocean_diffusion * laplace


def local(air_temp, sea_temp, land_sea, courant, vertical_mix, cutoffs):
    row_count, col_count, levels = air_temp.shape
    band_index = lax.axis_index("lat")
    is_north = band_index == 0
    is_south = band_index == lax.axis_size("lat") - 1
    col_start = lax.axis_index("lon") * col_count
    cosine, sine_table = tables(col_start, col_count)
    exchange_coef = jnp.where(land_sea == 1, sea_coef, land_coef)
    for step_index in range(STEPS):
        sea_near = lax.all_to_all(sea_temp, "lon", split_axis=1, concat_axis=0, tiled=True)
        advanced = horizontal(air_temp, courant)
        polar_rows = jnp.where(is_north, advanced[:NPOLE], advanced[row_count - NPOLE :])
        cutoff = jnp.where(is_north, cutoffs[:NPOLE], cutoffs[NPOLE:])
        real_part, imag_part = spectra(polar_rows, cosine, sine_table)
        real_part, imag_part = lax.psum((real_part, imag_part), "lon")
        filtered = inverse(real_part, imag_part, cutoff, cosine, sine_table)
        north_block = jnp.concatenate([filtered, advanced[NPOLE:]], 0)
        south_block = jnp.concatenate([advanced[: row_count - NPOLE], filtered], 0)
        advanced = jnp.where(is_north, north_block, jnp.where(is_south, south_block, advanced))
        mixed = jnp.dot(advanced.reshape(-1, levels), vertical_mix, precision=lax.Precision.HIGHEST)
        air_next = advanced + mixed.reshape(advanced.shape)
        heat_flux = exchange_coef * (sea_near - air_next[:, :, 0])
        air_temp = air_next.at[:, :, 0].add(air_gain * heat_flux)
        flux_ocean = lax.all_to_all(heat_flux, "lon", split_axis=0, concat_axis=1, tiled=True)
        sea_temp = ocean_step(sea_temp, flux_ocean)
    return (air_temp, sea_temp)


def solution(mesh):
    placed = (P("lat", "lon", None), P(("lat", "lon"), None), P("lat", "lon"), P(), P(), P())
    return jax.shard_map(
        local,
        mesh=mesh,
        in_specs=placed,
        out_specs=(P("lat", "lon", None), P(("lat", "lon"), None)),
        check_vma=False,
    )
```

profile of v0, /device:TPU:0, one launch (start us, length us, event | category | flops | bytes accessed | tf_op | source)
XLA Modules:
  0.0 1181.3 jit_solution(2026962833797611923)
XLA Ops:
  12.9 5.4 collective-permute-start.2
  19.9 6.0 all-to-all-start
  26.6 14.0 %fusion.41 = f32[32,360,128]{2,1,0:T(8,128)S(1)} fusion(f32[32,360,128]{2,1,0:T(8,128)} %param.18, f32[1,360,128]{2,1,0:T(8,128)S(1)} %collective-permute-done.1, f32[1,360,128]{2,1,0:T(8,128)S(1)} %collective-permute-done, f32[32,1,128]{2,1,0:T(1,128)S(1)} %collective-permute-done.2, f32[32,1,128]{2,1,0:T(1,128)S(1)} %collective-permute-done.3, ...), kind=kLoop, calls=%fused_computation.64 | loop fusion | flops 20643840 | bytes 12198400 | tf_op jit(solution)/shard_map/sub | solution.py:43
  40.7 4.1 convolution_bitcast_fusion.10
  53.3 4.7 fusion.394
  58.0 97.0 %all-reduce.23.cloned.1.call-done = (f32[16,128,128]{2,1,0:T(8,128)}, f32[16,128,128]{2,1,0:T(8,128)}) async-done(((f32[16,128,128]{2,1,0:T(8,128)}, f32[16,128,128]{2,1,0:T(8,128)}), (f32[16,128,128]{2,1,0:T(8,128)}, f32[16,128,128]{2,1,0:T(8,128)})) %all-reduce.23.cloned.1.call-update) | async-done | bytes 2097168 | tf_op jit(solution)/shard_map/psum | solution.py:101
  155.0 4.6 fusion.70
  159.6 4.5 add_bitcast_fusion.5
  164.1 8.5 convolution_add_fusion.5
  180.4 7.5 slice_add_fusion.5
  187.9 12.0 %scatter-add.20 = f32[32,360,128]{2,1,0:T(8,128)} dynamic-update-slice(f32[32,360,128]{2,1,0:T(8,128)} %copy-done.5, f32[32,360,1]{2,1,0:T(8,128)} %slice_add_fusion.5, s32[]{:T(128)} %constant.163.clone.1, s32[]{:T(128)} %constant.163.clone.1, s32[]{:T(128)} %constant.163.clone.1) | dynamic-update-slice | bytes 92164 | tf_op jit(solution)/shard_map/scatter-add | solution.py:109
  201.6 4.4 all-to-all-start.1
  209.8 4.5 collective-permute-start.6
  220.8 14.5 %fusion.34 = f32[32,360,128]{2,1,0:T(8,128)S(1)} fusion(f32[32,360,128]{2,1,0:T(8,128)} %scatter-add.20, f32[1,360,128]{2,1,0:T(8,128)S(1)} %collective-permute-done.5, f32[1,360,128]{2,1,0:T(8,128)S(1)} %collective-permute-done.4, f32[32,1,128]{2,1,0:T(1,128)S(1)} %collective-permute-done.6, f32[32,1,128]{2,1,0:T(1,128)S(1)} %collective-permute-done.7, ...), kind=kLoop, calls=%fused_computation.53 | loop fusion | flops 20643840 | bytes 12198400 | tf_op jit(solution)/shard_map/sub | solution.py:43
  235.4 4.1 convolution_bitcast_fusion.8
  254.6 4.7 fusion.391
  259.3 89.4 %all-reduce.21.cloned.1.call-done = (f32[16,128,128]{2,1,0:T(8,128)}, f32[16,128,128]{2,1,0:T(8,128)}) async-done(((f32[16,128,128]{2,1,0:T(8,128)}, f32[16,128,128]{2,1,0:T(8,128)}), (f32[16,128,128]{2,1,0:T(8,128)}, f32[16,128,128]{2,1,0:T(8,128)})) %all-reduce.21.cloned.1.call-update) | async-done | bytes 2097168 | tf_op jit(solution)/shard_map/psum | solution.py:101
  348.7 4.6 fusion.67
  353.4 4.5 add_bitcast_fusion.4
  357.9 8.5 convolution_add_fusion.4
  371.3 4.4 all-to-all-start.3
  379.2 7.5 slice_add_fusion.4
  386.7 12.0 %scatter-add.21 = f32[32,360,128]{2,1,0:T(8,128)} dynamic-update-slice(f32[32,360,128]{2,1,0:T(8,128)} %copy-done.1, f32[32,360,1]{2,1,0:T(8,128)} %slice_add_fusion.4, s32[]{:T(128)} %constant.163.clone.1, s32[]{:T(128)} %constant.163.clone.1, s32[]{:T(128)} %constant.163.clone.1) | dynamic-update-slice | bytes 92164 | tf_op jit(solution)/shard_map/scatter-add | solution.py:109
  403.6 4.5 collective-permute-start.12
  414.5 14.5 %fusion.27 = f32[32,360,128]{2,1,0:T(8,128)S(1)} fusion(f32[32,360,128]{2,1,0:T(8,128)} %scatter-add.21, f32[1,360,128]{2,1,0:T(8,128)S(1)} %collective-permute-done.11, f32[1,360,128]{2,1,0:T(8,128)S(1)} %collective-permute-done.10, f32[32,1,128]{2,1,0:T(1,128)S(1)} %collective-permute-done.12, f32[32,1,128]{2,1,0:T(1,128)S(1)} %collective-permute-done.13, ...), kind=kLoop, calls=%fused_computation.42 | loop fusion | flops 20643840 | bytes 12198400 | tf_op jit(solution)/shard_map/sub | solution.py:43
  429.1 4.1 convolution_bitcast_fusion.6
  448.3 4.7 fusion.388
  453.0 89.4 %all-reduce.19.cloned.1.call-done = (f32[16,128,128]{2,1,0:T(8,128)}, f32[16,128,128]{2,1,0:T(8,128)}) async-done(((f32[16,128,128]{2,1,0:T(8,128)}, f32[16,128,128]{2,1,0:T(8,128)}), (f32[16,128,128]{2,1,0:T(8,128)}, f32[16,128,128]{2,1,0:T(8,128)})) %all-reduce.19.cloned.1.call-update) | async-done | bytes 2097168 | tf_op jit(solution)/shard_map/psum | solution.py:101
  542.4 4.6 fusion.64
  547.1 4.5 add_bitcast_fusion.3
  551.6 8.5 convolution_add_fusion.3
  565.0 4.4 all-to-all-start.5
  572.9 7.5 slice_add_fusion.3
  580.4 12.0 %scatter-add.24 = f32[32,360,128]{2,1,0:T(8,128)} dynamic-update-slice(f32[32,360,128]{2,1,0:T(8,128)} %copy-done.2, f32[32,360,1]{2,1,0:T(8,128)} %slice_add_fusion.3, s32[]{:T(128)} %constant.163.clone.1, s32[]{:T(128)} %constant.163.clone.1, s32[]{:T(128)} %constant.163.clone.1) | dynamic-update-slice | bytes 92164 | tf_op jit(solution)/shard_map/scatter-add | solution.py:109
  597.3 4.5 collective-permute-start.18
  608.2 14.5 %fusion.20 = f32[32,360,128]{2,1,0:T(8,128)S(1)} fusion(f32[32,360,128]{2,1,0:T(8,128)} %scatter-add.24, f32[1,360,128]{2,1,0:T(8,128)S(1)} %collective-permute-done.17, f32[1,360,128]{2,1,0:T(8,128)S(1)} %collective-permute-done.16, f32[32,1,128]{2,1,0:T(1,128)S(1)} %collective-permute-done.18, f32[32,1,128]{2,1,0:T(1,128)S(1)} %collective-permute-done.19, ...), kind=kLoop, calls=%fused_computation.31 | loop fusion | flops 20643840 | bytes 12198400 | tf_op jit(solution)/shard_map/sub | solution.py:43
  642.0 4.7 fusion.385
  646.7 89.4 %all-reduce.17.cloned.1.call-done = (f32[16,128,128]{2,1,0:T(8,128)}, f32[16,128,128]{2,1,0:T(8,128)}) async-done(((f32[16,128,128]{2,1,0:T(8,128)}, f32[16,128,128]{2,1,0:T(8,128)}), (f32[16,128,128]{2,1,0:T(8,128)}, f32[16,128,128]{2,1,0:T(8,128)})) %all-reduce.17.cloned.1.call-update) | async-done | bytes 2097168 | tf_op jit(solution)/shard_map/psum | solution.py:101
  736.2 4.6 fusion.61
  740.8 4.5 add_bitcast_fusion.2
  745.3 8.5 convolution_add_fusion.2
  758.8 4.4 all-to-all-start.7
  766.6 7.5 slice_add_fusion.2
  774.1 12.0 %scatter-add.25 = f32[32,360,128]{2,1,0:T(8,128)} dynamic-update-slice(f32[32,360,128]{2,1,0:T(8,128)} %copy-done.3, f32[32,360,1]{2,1,0:T(8,128)} %slice_add_fusion.2, s32[]{:T(128)} %constant.163.clone.1, s32[]{:T(128)} %constant.163.clone.1, s32[]{:T(128)} %constant.163.clone.1) | dynamic-update-slice | bytes 92164 | tf_op jit(solution)/shard_map/scatter-add | solution.py:109
  791.0 4.5 collective-permute-start.24
  801.9 14.5 %fusion.13 = f32[32,360,128]{2,1,0:T(8,128)S(1)} fusion(f32[32,360,128]{2,1,0:T(8,128)} %scatter-add.25, f32[1,360,128]{2,1,0:T(8,128)S(1)} %collective-permute-done.23, f32[1,360,128]{2,1,0:T(8,128)S(1)} %collective-permute-done.22, f32[32,1,128]{2,1,0:T(1,128)S(1)} %collective-permute-done.24, f32[32,1,128]{2,1,0:T(1,128)S(1)} %collective-permute-done.25, ...), kind=kLoop, calls=%fused_computation.20 | loop fusion | flops 20643840 | bytes 12198400 | tf_op jit(solution)/shard_map/sub | solution.py:43
  835.8 4.7 fusion.382
  840.5 89.4 %all-reduce.15.cloned.1.call-done = (f32[16,128,128]{2,1,0:T(8,128)}, f32[16,128,128]{2,1,0:T(8,128)}) async-done(((f32[16,128,128]{2,1,0:T(8,128)}, f32[16,128,128]{2,1,0:T(8,128)}), (f32[16,128,128]{2,1,0:T(8,128)}, f32[16,128,128]{2,1,0:T(8,128)})) %all-reduce.15.cloned.1.call-update) | async-done | bytes 2097168 | tf_op jit(solution)/shard_map/psum | solution.py:101
  929.9 4.6 fusion.58
  934.5 4.5 add_bitcast_fusion.1
  939.0 8.5 convolution_add_fusion.1
  952.5 4.4 all-to-all-start.9
  960.3 7.5 slice_add_fusion.1
  967.8 12.0 %scatter-add.26 = f32[32,360,128]{2,1,0:T(8,128)} dynamic-update-slice(f32[32,360,128]{2,1,0:T(8,128)} %copy-done.4, f32[32,360,1]{2,1,0:T(8,128)} %slice_add_fusion.1, s32[]{:T(128)} %constant.163.clone.1, s32[]{:T(128)} %constant.163.clone.1, s32[]{:T(128)} %constant.163.clone.1) | dynamic-update-slice | bytes 92164 | tf_op jit(solution)/shard_map/scatter-add | solution.py:109
  984.7 4.5 collective-permute-start.30
  995.7 14.5 %fusion.6 = f32[32,360,128]{2,1,0:T(8,128)S(1)} fusion(f32[32,360,128]{2,1,0:T(8,128)} %scatter-add.26, f32[1,360,128]{2,1,0:T(8,128)S(1)} %collective-permute-done.29, f32[1,360,128]{2,1,0:T(8,128)S(1)} %collective-permute-done.28, f32[32,1,128]{2,1,0:T(1,128)S(1)} %collective-permute-done.30, f32[32,1,128]{2,1,0:T(1,128)S(1)} %collective-permute-done.31, ...), kind=kLoop, calls=%fused_computation.9 | loop fusion | flops 20643840 | bytes 12198400 | tf_op jit(solution)/shard_map/sub | solution.py:43
  1029.5 4.7 fusion.379
  1034.2 89.4 %all-reduce.13.cloned.1.call-done = (f32[16,128,128]{2,1,0:T(8,128)}, f32[16,128,128]{2,1,0:T(8,128)}) async-done(((f32[16,128,128]{2,1,0:T(8,128)}, f32[16,128,128]{2,1,0:T(8,128)}), (f32[16,128,128]{2,1,0:T(8,128)}, f32[16,128,128]{2,1,0:T(8,128)})) %all-reduce.13.cloned.1.call-update) | async-done | bytes 2097168 | tf_op jit(solution)/shard_map/psum | solution.py:101
  1123.6 4.6 fusion.55
  1128.2 4.5 add_bitcast_fusion
  1132.7 8.3 convolution_add_fusion
  1146.0 4.4 all-to-all-start.11
  1153.8 7.5 slice_add_fusion
  1161.3 12.0 %scatter-add.29 = f32[32,360,128]{2,1,0:T(8,128)} dynamic-update-slice(f32[32,360,128]{2,1,0:T(8,128)} %copy-done.12, f32[32,360,1]{2,1,0:T(8,128)} %slice_add_fusion, s32[]{:T(128)} %constant.163.clone.1, s32[]{:T(128)} %constant.163.clone.1, s32[]{:T(128)} %constant.163.clone.1) | dynamic-update-slice | bytes 92164 | tf_op jit(solution)/shard_map/scatter-add | solution.py:109
  (249 shorter events, 211.6 us)
Async XLA Ops:
  7.2 156.9 %copy-start = (f32[128,128]{1,0:T(8,128)S(1)}, f32[128,128]{1,0:T(8,128)}, u32[]{:S(2)}) copy-start(f32[128,128]{1,0:T(8,128)} %param.22) | copy-start | bytes 196612
  8.3 18.4 %collective-permute-start = (f32[1,360,128]{2,1,0:T(8,128)S(1)}, f32[1,360,128]{2,1,0:T(8,128)S(1)}, u32[]{:S(2)}, u32[]{:S(2)}) collective-permute-start(f32[1,360,128]{2,1,0:T(8,128)S(1)} %get-tuple-element.133), channel_id=1, source_target_pairs={{0,8},{8,16},{16,24},{1,9},{9,17},{17,25},{2,10},{10,18},{18,26},{... | collective-permute-start | bytes 552968 | tf_op jit(solution)/shard_map/ppermute | solution.py:29
  10.6 16.0 %collective-permute-start.1 = (f32[1,360,128]{2,1,0:T(8,128)S(1)}, f32[1,360,128]{2,1,0:T(8,128)S(1)}, u32[]{:S(2)}, u32[]{:S(2)}) collective-permute-start(f32[1,360,128]{2,1,0:T(8,128)S(1)} %get-tuple-element.134), channel_id=1, source_target_pairs={{8,0},{16,8},{24,16},{9,1},{17,9},{25,17},{10,2},{18,10},{26,18},{... | collective-permute-start | bytes 552968 | tf_op jit(solution)/shard_map/ppermute | solution.py:30
  12.9 13.7 %collective-permute-start.2 = (f32[32,1,128]{2,1,0:T(1,128)S(1)}, f32[32,1,128]{2,1,0:T(1,128)S(1)}, u32[]{:S(2)}, u32[]{:S(2)}) collective-permute-start(f32[32,1,128]{2,1,0:T(1,128)S(1)} %get-tuple-element.132), channel_id=1, source_target_pairs={{1,0},{2,1},{3,2},{4,3},{5,4},{6,5},{7,6},{0,7},{9,8},{10,9},{11,1... | collective-permute-start | bytes 49160 | tf_op jit(solution)/shard_map/ppermute | solution.py:30
  18.4 8.2 collective-permute-start.3
  19.9 33.3 %all-to-all-start = ((f32[4,8,360]{2,0,1:T(4,128)}), f32[4,8,360]{2,0,1:T(4,128)S(1)}, u32[]{:S(2)}, u32[]{:S(2)}) async-start(f32[4,8,360]{2,0,1:T(4,128)} %copy.260), calls=%async_computation | async-start | bytes 98304 | tf_op jit(solution)/shard_map/all_to_all | solution.py:96
  25.9 129.1 %all-reduce.23.cloned.1.call-start = ((), (), s32[]{:S(2)}) async-start(), calls=%async_computation.17 | async-start | bytes 4194304 | tf_op jit(solution)/shard_map/psum | solution.py:101
  40.7 4.1 copy-start.11
  40.7 8.1 copy-start.19
  40.7 12.2 %copy-start.21 = (s32[32]{0:T(128)S(1)}, s32[32]{0:T(128)}, u32[]{:S(2)}) copy-start(s32[32]{0:T(128)} %param.23) | copy-start | bytes 388
  48.8 194.6 %collective-permute-start.8 = (f32[1,2880]{1,0:T(1,128)S(1)}, f32[1,2880]{1,0:T(1,128)S(1)}, u32[]{:S(2)}, u32[]{:S(2)}) collective-permute-start(f32[1,2880]{1,0:T(1,128)S(1)} %get-tuple-element.169), channel_id=1, source_target_pairs={{0,1},{1,2},{2,3},{3,4},{4,5},{5,6},{6,7},{7,8},{8,9},{9,10},{10,1... | collective-permute-start | bytes 34568 | tf_op jit(solution)/shard_map/ppermute | solution.py:29
  155.0 9.1 copy-start.14
  201.6 12.7 %all-to-all-start.1 = ((f32[8,4,360]{2,1,0:T(4,128)}), f32[8,4,360]{2,1,0:T(4,128)S(1)}, u32[]{:S(2)}, u32[]{:S(2)}) async-start(f32[8,4,360]{2,1,0:T(4,128)} %all_to_all.148), calls=%async_computation.1 | async-start | bytes 98304 | tf_op jit(solution)/shard_map/all_to_all | solution.py:110
  206.0 142.8 %all-reduce.21.cloned.1.call-start = ((), (), s32[]{:S(2)}) async-start(), calls=%async_computation.16 | async-start | bytes 4194304 | tf_op jit(solution)/shard_map/psum | solution.py:101
  207.0 13.8 %collective-permute-start.4 = (f32[1,360,128]{2,1,0:T(8,128)S(1)}, f32[1,360,128]{2,1,0:T(8,128)S(1)}, u32[]{:S(2)}, u32[]{:S(2)}) collective-permute-start(f32[1,360,128]{2,1,0:T(8,128)S(1)} %get-tuple-element.127), channel_id=1, source_target_pairs={{0,8},{8,16},{16,24},{1,9},{9,17},{17,25},{2,10},{10,18},{18,26},{... | collective-permute-start | bytes 552968 | tf_op jit(solution)/shard_map/ppermute | solution.py:29
  208.5 12.3 %collective-permute-start.5 = (f32[1,360,128]{2,1,0:T(8,128)S(1)}, f32[1,360,128]{2,1,0:T(8,128)S(1)}, u32[]{:S(2)}, u32[]{:S(2)}) collective-permute-start(f32[1,360,128]{2,1,0:T(8,128)S(1)} %get-tuple-element.128), channel_id=1, source_target_pairs={{8,0},{16,8},{24,16},{9,1},{17,9},{25,17},{10,2},{18,10},{26,18},{... | collective-permute-start | bytes 552968 | tf_op jit(solution)/shard_map/ppermute | solution.py:30
  209.8 6.0 collective-permute-start.6
  214.4 6.4 collective-permute-start.7
  215.8 27.6 %collective-permute-start.9 = (f32[1,2880]{1,0:T(1,128)S(1)}, f32[1,2880]{1,0:T(1,128)S(1)}, u32[]{:S(2)}, u32[]{:S(2)}) collective-permute-start(f32[1,2880]{1,0:T(1,128)S(1)} %get-tuple-element.170), channel_id=1, source_target_pairs={{1,0},{2,1},{3,2},{4,3},{5,4},{6,5},{7,6},{8,7},{9,8},{10,9},{11,1... | collective-permute-start | bytes 34568 | tf_op jit(solution)/shard_map/ppermute | solution.py:30
  244.3 10.3 all-to-all-start.2
  247.8 189.3 %collective-permute-start.14 = (f32[1,2880]{1,0:T(1,128)S(1)}, f32[1,2880]{1,0:T(1,128)S(1)}, u32[]{:S(2)}, u32[]{:S(2)}) collective-permute-start(f32[1,2880]{1,0:T(1,128)S(1)} %get-tuple-element.163), channel_id=1, source_target_pairs={{0,1},{1,2},{2,3},{3,4},{4,5},{5,6},{6,7},{7,8},{8,9},{9,10},{10,1... | collective-permute-start | bytes 34568 | tf_op jit(solution)/shard_map/ppermute | solution.py:29
  348.7 9.1 copy-start.15
  371.3 36.8 %all-to-all-start.3 = ((f32[8,4,360]{2,1,0:T(4,128)}), f32[8,4,360]{2,1,0:T(4,128)S(1)}, u32[]{:S(2)}, u32[]{:S(2)}) async-start(f32[8,4,360]{2,1,0:T(4,128)} %all_to_all.154), calls=%async_computation.3 | async-start | bytes 98304 | tf_op jit(solution)/shard_map/all_to_all | solution.py:110
  375.7 166.8 %all-reduce.19.cloned.1.call-start = ((), (), s32[]{:S(2)}) async-start(), calls=%async_computation.15 | async-start | bytes 4194304 | tf_op jit(solution)/shard_map/psum | solution.py:101
  400.7 13.8 %collective-permute-start.10 = (f32[1,360,128]{2,1,0:T(8,128)S(1)}, f32[1,360,128]{2,1,0:T(8,128)S(1)}, u32[]{:S(2)}, u32[]{:S(2)}) collective-permute-start(f32[1,360,128]{2,1,0:T(8,128)S(1)} %get-tuple-element.121), channel_id=1, source_target_pairs={{0,8},{8,16},{16,24},{1,9},{9,17},{17,25},{2,10},{10,18},{18,26},{... | collective-permute-start | bytes 552968 | tf_op jit(solution)/shard_map/ppermute | solution.py:29
  402.3 12.2 %collective-permute-start.11 = (f32[1,360,128]{2,1,0:T(8,128)S(1)}, f32[1,360,128]{2,1,0:T(8,128)S(1)}, u32[]{:S(2)}, u32[]{:S(2)}) collective-permute-start(f32[1,360,128]{2,1,0:T(8,128)S(1)} %get-tuple-element.122), channel_id=1, source_target_pairs={{8,0},{16,8},{24,16},{9,1},{17,9},{25,17},{10,2},{18,10},{26,18},{... | collective-permute-start | bytes 552968 | tf_op jit(solution)/shard_map/ppermute | solution.py:30
  403.6 5.9 collective-permute-start.12
  408.1 6.4 collective-permute-start.13
  409.5 27.7 %collective-permute-start.15 = (f32[1,2880]{1,0:T(1,128)S(1)}, f32[1,2880]{1,0:T(1,128)S(1)}, u32[]{:S(2)}, u32[]{:S(2)}) collective-permute-start(f32[1,2880]{1,0:T(1,128)S(1)} %get-tuple-element.164), channel_id=1, source_target_pairs={{1,0},{2,1},{3,2},{4,3},{5,4},{6,5},{7,6},{8,7},{9,8},{10,9},{11,1... | collective-permute-start | bytes 34568 | tf_op jit(solution)/shard_map/ppermute | solution.py:30
  438.0 10.3 all-to-all-start.4
  441.6 189.3 %collective-permute-start.20 = (f32[1,2880]{1,0:T(1,128)S(1)}, f32[1,2880]{1,0:T(1,128)S(1)}, u32[]{:S(2)}, u32[]{:S(2)}) collective-permute-start(f32[1,2880]{1,0:T(1,128)S(1)} %get-tuple-element.157), channel_id=1, source_target_pairs={{0,1},{1,2},{2,3},{3,4},{4,5},{5,6},{6,7},{7,8},{8,9},{9,10},{10,1... | collective-permute-start | bytes 34568 | tf_op jit(solution)/shard_map/ppermute | solution.py:29
  542.4 9.1 copy-start.16
  565.0 36.8 %all-to-all-start.5 = ((f32[8,4,360]{2,1,0:T(4,128)}), f32[8,4,360]{2,1,0:T(4,128)S(1)}, u32[]{:S(2)}, u32[]{:S(2)}) async-start(f32[8,4,360]{2,1,0:T(4,128)} %all_to_all.160), calls=%async_computation.5 | async-start | bytes 98304 | tf_op jit(solution)/shard_map/all_to_all | solution.py:110
  569.4 166.8 %all-reduce.17.cloned.1.call-start = ((), (), s32[]{:S(2)}) async-start(), calls=%async_computation.14 | async-start | bytes 4194304 | tf_op jit(solution)/shard_map/psum | solution.py:101
  594.5 13.8 %collective-permute-start.16 = (f32[1,360,128]{2,1,0:T(8,128)S(1)}, f32[1,360,128]{2,1,0:T(8,128)S(1)}, u32[]{:S(2)}, u32[]{:S(2)}) collective-permute-start(f32[1,360,128]{2,1,0:T(8,128)S(1)} %get-tuple-element.115), channel_id=1, source_target_pairs={{0,8},{8,16},{16,24},{1,9},{9,17},{17,25},{2,10},{10,18},{18,26},{... | collective-permute-start | bytes 552968 | tf_op jit(solution)/shard_map/ppermute | solution.py:29
  596.0 12.2 %collective-permute-start.17 = (f32[1,360,128]{2,1,0:T(8,128)S(1)}, f32[1,360,128]{2,1,0:T(8,128)S(1)}, u32[]{:S(2)}, u32[]{:S(2)}) collective-permute-start(f32[1,360,128]{2,1,0:T(8,128)S(1)} %get-tuple-element.116), channel_id=1, source_target_pairs={{8,0},{16,8},{24,16},{9,1},{17,9},{25,17},{10,2},{18,10},{26,18},{... | collective-permute-start | bytes 552968 | tf_op jit(solution)/shard_map/ppermute | solution.py:30
  597.3 5.9 collective-permute-start.18
  601.8 6.4 collective-permute-start.19
  603.2 27.6 %collective-permute-start.21 = (f32[1,2880]{1,0:T(1,128)S(1)}, f32[1,2880]{1,0:T(1,128)S(1)}, u32[]{:S(2)}, u32[]{:S(2)}) collective-permute-start(f32[1,2880]{1,0:T(1,128)S(1)} %get-tuple-element.158), channel_id=1, source_target_pairs={{1,0},{2,1},{3,2},{4,3},{5,4},{6,5},{7,6},{8,7},{9,8},{10,9},{11,1... | collective-permute-start | bytes 34568 | tf_op jit(solution)/shard_map/ppermute | solution.py:30
  631.7 10.3 all-to-all-start.6
  635.3 189.3 %collective-permute-start.26 = (f32[1,2880]{1,0:T(1,128)S(1)}, f32[1,2880]{1,0:T(1,128)S(1)}, u32[]{:S(2)}, u32[]{:S(2)}) collective-permute-start(f32[1,2880]{1,0:T(1,128)S(1)} %get-tuple-element.151), channel_id=1, source_target_pairs={{0,1},{1,2},{2,3},{3,4},{4,5},{5,6},{6,7},{7,8},{8,9},{9,10},{10,1... | collective-permute-start | bytes 34568 | tf_op jit(solution)/shard_map/ppermute | solution.py:29
  736.2 9.1 copy-start.17
  758.8 36.8 %all-to-all-start.7 = ((f32[8,4,360]{2,1,0:T(4,128)}), f32[8,4,360]{2,1,0:T(4,128)S(1)}, u32[]{:S(2)}, u32[]{:S(2)}) async-start(f32[8,4,360]{2,1,0:T(4,128)} %all_to_all.166), calls=%async_computation.7 | async-start | bytes 98304 | tf_op jit(solution)/shard_map/all_to_all | solution.py:110
  763.1 166.8 %all-reduce.15.cloned.1.call-start = ((), (), s32[]{:S(2)}) async-start(), calls=%async_computation.13 | async-start | bytes 4194304 | tf_op jit(solution)/shard_map/psum | solution.py:101
  788.2 13.8 %collective-permute-start.22 = (f32[1,360,128]{2,1,0:T(8,128)S(1)}, f32[1,360,128]{2,1,0:T(8,128)S(1)}, u32[]{:S(2)}, u32[]{:S(2)}) collective-permute-start(f32[1,360,128]{2,1,0:T(8,128)S(1)} %get-tuple-element.109), channel_id=1, source_target_pairs={{0,8},{8,16},{16,24},{1,9},{9,17},{17,25},{2,10},{10,18},{18,26},{... | collective-permute-start | bytes 552968 | tf_op jit(solution)/shard_map/ppermute | solution.py:29
  789.7 12.2 %collective-permute-start.23 = (f32[1,360,128]{2,1,0:T(8,128)S(1)}, f32[1,360,128]{2,1,0:T(8,128)S(1)}, u32[]{:S(2)}, u32[]{:S(2)}) collective-permute-start(f32[1,360,128]{2,1,0:T(8,128)S(1)} %get-tuple-element.110), channel_id=1, source_target_pairs={{8,0},{16,8},{24,16},{9,1},{17,9},{25,17},{10,2},{18,10},{26,18},{... | collective-permute-start | bytes 552968 | tf_op jit(solution)/shard_map/ppermute | solution.py:30
  791.0 5.9 collective-permute-start.24
  795.5 6.4 collective-permute-start.25
  797.0 27.6 %collective-permute-start.27 = (f32[1,2880]{1,0:T(1,128)S(1)}, f32[1,2880]{1,0:T(1,128)S(1)}, u32[]{:S(2)}, u32[]{:S(2)}) collective-permute-start(f32[1,2880]{1,0:T(1,128)S(1)} %get-tuple-element.152), channel_id=1, source_target_pairs={{1,0},{2,1},{3,2},{4,3},{5,4},{6,5},{7,6},{8,7},{9,8},{10,9},{11,1... | collective-permute-start | bytes 34568 | tf_op jit(solution)/shard_map/ppermute | solution.py:30
  825.4 10.3 all-to-all-start.8
  829.0 189.3 %collective-permute-start.32 = (f32[1,2880]{1,0:T(1,128)S(1)}, f32[1,2880]{1,0:T(1,128)S(1)}, u32[]{:S(2)}, u32[]{:S(2)}) collective-permute-start(f32[1,2880]{1,0:T(1,128)S(1)} %get-tuple-element.145), channel_id=1, source_target_pairs={{0,1},{1,2},{2,3},{3,4},{4,5},{5,6},{6,7},{7,8},{8,9},{9,10},{10,1... | collective-permute-start | bytes 34568 | tf_op jit(solution)/shard_map/ppermute | solution.py:29
  929.9 9.1 copy-start.18
  952.5 36.8 %all-to-all-start.9 = ((f32[8,4,360]{2,1,0:T(4,128)}), f32[8,4,360]{2,1,0:T(4,128)S(1)}, u32[]{:S(2)}, u32[]{:S(2)}) async-start(f32[8,4,360]{2,1,0:T(4,128)} %all_to_all.172), calls=%async_computation.9 | async-start | bytes 98304 | tf_op jit(solution)/shard_map/all_to_all | solution.py:110
  956.8 166.8 %all-reduce.13.cloned.1.call-start = ((), (), s32[]{:S(2)}) async-start(), calls=%async_computation.12 | async-start | bytes 4194304 | tf_op jit(solution)/shard_map/psum | solution.py:101
  981.9 13.8 %collective-permute-start.28 = (f32[1,360,128]{2,1,0:T(8,128)S(1)}, f32[1,360,128]{2,1,0:T(8,128)S(1)}, u32[]{:S(2)}, u32[]{:S(2)}) collective-permute-start(f32[1,360,128]{2,1,0:T(8,128)S(1)} %get-tuple-element.103), channel_id=1, source_target_pairs={{0,8},{8,16},{16,24},{1,9},{9,17},{17,25},{2,10},{10,18},{18,26},{... | collective-permute-start | bytes 552968 | tf_op jit(solution)/shard_map/ppermute | solution.py:29
  983.4 12.2 %collective-permute-start.29 = (f32[1,360,128]{2,1,0:T(8,128)S(1)}, f32[1,360,128]{2,1,0:T(8,128)S(1)}, u32[]{:S(2)}, u32[]{:S(2)}) collective-permute-start(f32[1,360,128]{2,1,0:T(8,128)S(1)} %get-tuple-element.104), channel_id=1, source_target_pairs={{8,0},{16,8},{24,16},{9,1},{17,9},{25,17},{10,2},{18,10},{26,18},{... | collective-permute-start | bytes 552968 | tf_op jit(solution)/shard_map/ppermute | solution.py:30
  984.7 5.9 collective-permute-start.30
  989.2 6.4 collective-permute-start.31
  990.7 27.6 %collective-permute-start.33 = (f32[1,2880]{1,0:T(1,128)S(1)}, f32[1,2880]{1,0:T(1,128)S(1)}, u32[]{:S(2)}, u32[]{:S(2)}) collective-permute-start(f32[1,2880]{1,0:T(1,128)S(1)} %get-tuple-element.146), channel_id=1, source_target_pairs={{1,0},{2,1},{3,2},{4,3},{5,4},{6,5},{7,6},{8,7},{9,8},{10,9},{11,1... | collective-permute-start | bytes 34568 | tf_op jit(solution)/shard_map/ppermute | solution.py:30
  1019.2 10.3 all-to-all-start.10
  1022.7 150.8 %collective-permute-start.34 = (f32[1,2880]{1,0:T(1,128)S(1)}, f32[1,2880]{1,0:T(1,128)S(1)}, u32[]{:S(2)}, u32[]{:S(2)}) collective-permute-start(f32[1,2880]{1,0:T(1,128)S(1)} %get-tuple-element.139), channel_id=1, source_target_pairs={{0,1},{1,2},{2,3},{3,4},{4,5},{5,6},{6,7},{7,8},{8,9},{9,10},{10,1... | collective-permute-start | bytes 34568 | tf_op jit(solution)/shard_map/ppermute | solution.py:29
  1026.5 147.0 %collective-permute-start.35 = (f32[1,2880]{1,0:T(1,128)S(1)}, f32[1,2880]{1,0:T(1,128)S(1)}, u32[]{:S(2)}, u32[]{:S(2)}) collective-permute-start(f32[1,2880]{1,0:T(1,128)S(1)} %get-tuple-element.140), channel_id=1, source_target_pairs={{1,0},{2,1},{3,2},{4,3},{5,4},{6,5},{7,6},{8,7},{9,8},{10,9},{11,1... | collective-permute-start | bytes 34568 | tf_op jit(solution)/shard_map/ppermute | solution.py:30
  1123.6 9.1 copy-start.13
  1146.0 27.3 %all-to-all-start.11 = ((f32[8,4,360]{2,1,0:T(4,128)}), f32[8,4,360]{2,1,0:T(4,128)S(1)}, u32[]{:S(2)}, u32[]{:S(2)}) async-start(f32[8,4,360]{2,1,0:T(4,128)} %all_to_all.178), calls=%async_computation.11 | async-start | bytes 98304 | tf_op jit(solution)/shard_map/all_to_all | solution.py:110
  (12 other events, 37.6 us)
Sparse Core Ops, SparseCore 0:
  48.9 106.0 all-reduce.22
  243.6 105.1 all-reduce.20
  437.3 105.1 all-reduce.18
  631.0 105.1 all-reduce.16
  824.7 105.1 all-reduce.14
  1018.4 105.1 all-reduce.12
where the time goes:
time: 1190 us; the launch traced here: 1180 us
  waiting for transfers between devices  582 us (49%)
  local copies, waits for them, and re-layouts  170 us (14%)
  matrix products  154 us (13%)
  other arithmetic  134 us (11%)
  starting transfers between devices  126 us (11%)
  between operations  15.5 us (1%)
    psum x6, waiting for transfers between devices, local(): real_part, imag_part = lax.psum((real_part, imag_part), 'lon')  544 us
    sub x6, other arithmetic, horizontal(): air_temp + diffusion_rate * laplace  86.7 us
    scatter-add x6, local copies, waits for them, and re-layouts, local(): air_temp = air_next.at[:, :, 0].add(air_gain * heat_flux)  72.3 us
    dot_general x6, matrix products, local(): jnp.dot(advanced.reshape(-1, levels), vertical_mix, precision=lax.Precisi...  51 us
    add x6, other arithmetic, local(): air_temp = air_next.at[:, :, 0].add(air_gain * heat_flux)  44.9 us
    ppermute x18, starting transfers between devices, with_halo(): after = lax.ppermute(leading, axis, down)  43.6 us
    ppermute x18, starting transfers between devices, with_halo(): before = lax.ppermute(last, axis, up)  33.8 us
    another operation x12, local copies, waits for them, and re-layouts  30.8 us
  transfers between devices with their start and end apart: 54, of which 21 were waited for; matrix products, arithmetic and copies ran while one was open for 37% of the time, Pallas kernels for 0%

commit v1 on v0

v1 whole, which is shorter than its diff:
```python
import functools
import math

import jax
import jax.numpy as jnp
import ml_dtypes
import numpy as np
from jax import lax
from jax.experimental import pallas as pl
from jax.experimental.pallas import tpu as pltpu
from jax.sharding import PartitionSpec as P

NPOLE = 16
KMAX = 127
STEPS = 6
NK = 2 * (KMAX + 1)
CAP = NPOLE + STEPS
HALO = 8
ROW0 = STEPS
WEDGE = STEPS - 1

diffusion_rate = 0.1
air_gain = 0.5
ocean_gain = 0.3
ocean_diffusion = 0.2
sea_coef = 0.5
land_coef = 0.15

F32 = jnp.float32
BF16 = jnp.bfloat16
VMEM_LIMIT = 56 * 1024 * 1024


def round_up(value, unit):
    return -(-value // unit) * unit


def two_parts(x):
    high = x.astype(BF16)
    return high, (x - high.astype(F32)).astype(BF16)


def dot(a, b):
    return jnp.dot(a, b, preferred_element_type=F32)


def dot_nt(a, b):
    return lax.dot_general(a, b, (((1,), (1,)), ((), ())), preferred_element_type=F32)


def table_dot(high, low, x):
    x_high, x_low = two_parts(x)
    both = dot(high, jnp.concatenate([x_high, x_low], axis=1))
    return both[:, :128] + both[:, 128:] + dot(low, x_high)


def numpy_parts(table):
    high = table.astype(ml_dtypes.bfloat16)
    low = (table - high.astype(np.float64)).astype(ml_dtypes.bfloat16)
    return high, low


@functools.lru_cache(maxsize=None)
def tables(blocks, count, width, depth):
    nlon = blocks * count
    wavenum = np.arange(KMAX + 1)
    weight = np.where(wavenum == 0, 1.0, 2.0) / nlon

    def table(columns):
        phase = (columns[:, None] * wavenum[None, :]) % nlon * (2.0 * math.pi / nlon)
        return np.concatenate([np.cos(phase), np.sin(phase)], 1)

    window = np.concatenate(
        [table((j * count - HALO + np.arange(width)) % nlon) for j in range(blocks)], 0
    )
    forward = np.zeros((blocks, NK, depth))
    for j in range(blocks):
        own = table(j * count + np.arange(count)) * np.tile(weight, 2)
        forward[j, :, :count] = own.T
    return numpy_parts(window), numpy_parts(forward), np.tile(weight, 2)


def lane_iota(shape):
    return lax.broadcasted_iota(jnp.int32, shape, len(shape) - 1)


def spectra_kernel(count, scal, air, high, low, out, padded):
    @pl.when(pl.program_id(0) == 0)
    def _():
        padded[...] = jnp.zeros_like(padded)

    @pl.when(scal[1] == 1)
    def _():
        padded[0:count, :] = air[0]
        out[0] = table_dot(high[...], low[...], padded[...])


def start_spectra(scal, air_temp, high, low):
    rows, count, levels = air_temp.shape
    depth = high.shape[1]

    def place(q, scal):
        return (jnp.where(scal[0] == 1, rows - 1 - q, q), 0, 0)

    return pl.pallas_call(
        functools.partial(spectra_kernel, count),
        out_shape=jax.ShapeDtypeStruct((CAP, NK, levels), F32),
        grid_spec=pltpu.PrefetchScalarGridSpec(
            num_scalar_prefetch=1,
            grid=(CAP,),
            in_specs=[
                pl.BlockSpec((1, count, levels), place),
                pl.BlockSpec((NK, depth), lambda q, scal: (0, 0)),
                pl.BlockSpec((NK, depth), lambda q, scal: (0, 0)),
            ],
            out_specs=pl.BlockSpec((1, NK, levels), lambda q, scal: (q, 0, 0)),
            scratch_shapes=[pltpu.VMEM((depth, levels), F32)],
        ),
        compiler_params=pltpu.CompilerParams(vmem_limit_bytes=VMEM_LIMIT),
        name="start_spectra",
    )(scal, air_temp, high, low)


def advance_row(width, buf, base, north_ref, north, south_ref, south, cour, vcat, adv, xcat, prev):
    c_east, c_west = cour[0:1, :], cour[1:2, :]
    for o in range(0, width, 128):
        here = buf[pl.ds(base + o, 128), :]
        east = buf[pl.ds(base + o + 1, 128), :]
        west = buf[pl.ds(base + o - 1, 128), :]
        around = north_ref[pl.ds(north + o, 128), :] + south_ref[pl.ds(south + o, 128), :]
        x = (
            (1.0 - 4.0 * diffusion_rate) * here
            + diffusion_rate * around
            + c_east * east
            + c_west * west
        )
        high, low = two_parts(x)
        prev[pl.ds(o, 128), :] = here
        adv[pl.ds(o, 128), :] = x
        xcat[pl.ds(o, 128), 0:128] = high
        xcat[pl.ds(o, 128), 128:256] = low
    mixed = dot(xcat[...], vcat[...])
    return adv[...] + mixed[:, :128] + mixed[:, 128:]


def exchange(y, lane, sea, coef):
    back = (128 - lane) % 128
    flux = pltpu.roll(coef, back, 1) * (pltpu.roll(sea, back, 1) - y)
    return jnp.where(lane_iota(y.shape) == 0, flux, 0.0)


def sea_next(width, polar, rows, sea, flux, pad):
    pad[pl.ds(8, width), :] = sea
    east = pad[pl.ds(9, width), :]
    west = pad[pl.ds(7, width), :]
    around = east + west + pltpu.roll(sea, 1, 1) + pltpu.roll(sea, 127, 1)
    new = sea - ocean_gain * flux + ocean_diffusion * (around - 4.0 * sea)
    lane = lane_iota(sea.shape)
    first = jnp.where(polar == 1, ROW0, 0)
    return jnp.where((lane >= first) & (lane < rows + 2 * ROW0), new, 0.0)


def outside_kernel(
    rows, count, width, fast,
    scal, air, west, east, north, south, sea_in, coef, cour, vcat,
    air_out, wedge, side, sea_hist, flux_hist,
    buf, prev, adv, xcat, sea, flux, pad, sems,
):
    flip, polar = scal[0], scal[1]
    total = rows + 2 * ROW0
    inner = count + 2 * HALO

    def base_of(q):
        return pl.multiple_of(8 + (q + ROW0) * width, 8)

    def q_of(r):
        return jnp.where(flip == 1, rows - 1 - r, r)

    buf[0:8, :] = jnp.zeros((8, 128), F32)
    buf[pl.ds(8 + total * width, 8), :] = jnp.zeros((8, 128), F32)
    pad[...] = jnp.zeros_like(pad)

    if fast:
        @pl.loop(0, rows)
        def _(r):
            base = base_of(q_of(r))
            pltpu.make_async_copy(west.at[r], buf.at[pl.ds(base, HALO)], sems.at[0]).start()
            pltpu.make_async_copy(air.at[r], buf.at[pl.ds(base + HALO, count)], sems.at[0]).start()
            pltpu.make_async_copy(
                east.at[r], buf.at[pl.ds(base + HALO + count, HALO)], sems.at[0]
            ).start()

        @pl.loop(0, ROW0)
        def _(r):
            pltpu.make_async_copy(
                north.at[r], buf.at[pl.ds(base_of(q_of(r - ROW0)), inner)], sems.at[0]
            ).start()
            pltpu.make_async_copy(
                south.at[r], buf.at[pl.ds(base_of(q_of(r + rows)), inner)], sems.at[0]
            ).start()

        if inner < width:
            @pl.loop(0, total)
            def _(e):
                buf[pl.ds(base_of(e - ROW0) + inner, width - inner), :] = jnp.zeros(
                    (width - inner, 128), F32
                )

        everything = buf.at[pl.ds(0, total * inner)]
    else:
        @pl.loop(0, total)
        def _(e):
            pltpu.make_async_copy(
                air.at[e], buf.at[pl.ds(base_of(q_of(e - ROW0)), width)], sems.at[0]
            ).start()

        everything = buf.at[pl.ds(0, total * width)]
    pltpu.make_async_copy(everything, everything, sems.at[0]).wait()

    sea[...] = sea_in[...]
    for step in range(1, STEPS + 1):
        lo = jnp.where(polar == 1, NPOLE + step - 1, step - STEPS)
        hi = rows - 1 + STEPS - step
        flux[...] = jnp.zeros_like(flux)
        prev[...] = buf[pl.ds(base_of(lo - 1), width), :]
        if step >= 2:
            side[step - 2] = buf[pl.ds(base_of(lo), width), :]

        @pl.loop(lo, hi + 1)
        def _(q):
            base = base_of(q)
            y = advance_row(
                width, buf, base, prev, 0, buf, base + width, cour, vcat, adv, xcat, prev
            )
            out = exchange(y, q + ROW0, sea[...], coef[...])
            buf[pl.ds(base, width), :] = y + air_gain * out
            flux[...] += pltpu.roll(out, q + ROW0, 1)

        new_sea = sea_next(width, polar, rows, sea[...], flux[...], pad)
        sea[...] = new_sea
        sea_hist[step - 1] = new_sea
        flux_hist[step - 1] = flux[...]

    for j in range(WEDGE):
        wedge[j] = buf[pl.ds(base_of(NPOLE + j), width), :]
    first = jnp.where(polar == 1, NPOLE + WEDGE, 0)
    start, extent = (HALO, count) if fast else (0, width)

    def back(q):
        return pltpu.make_async_copy(
            buf.at[pl.ds(base_of(q) + start, extent)], air_out.at[q_of(q)], sems.at[1]
        )

    @pl.loop(first, rows)
    def _(q):
        back(q).start()

    @pl.when(polar == 1)
    def _():
        whole = buf.at[pl.ds(0, (rows - NPOLE - WEDGE) * extent)]
        pltpu.make_async_copy(whole, whole, sems.at[1]).wait()

    @pl.when(polar == 0)
    def _():
        whole = buf.at[pl.ds(0, rows * extent)]
        pltpu.make_async_copy(whole, whole, sems.at[1]).wait()


def outside_steps(rows, count, width, fast, scal, air, halos, sea, coef, cour, vcat):
    levels = 128
    any_spec = pl.BlockSpec(memory_space=pl.ANY)
    vmem = pl.BlockSpec(memory_space=pltpu.VMEM)
    total = rows + 2 * ROW0
    shape = jax.ShapeDtypeStruct
    return pl.pallas_call(
        functools.partial(outside_kernel, rows, count, width, fast),
        out_shape=[
            shape((rows, count if fast else width, levels), F32),
            shape((WEDGE, width, levels), F32),
            shape((WEDGE, width, levels), F32),
            shape((STEPS, width, 128), F32),
            shape((STEPS, width, 128), F32),
        ],
        in_specs=[pl.BlockSpec(memory_space=pltpu.SMEM)] + [any_spec] * 5 + [vmem] * 4,
        out_specs=[any_spec] + [vmem] * 4,
        scratch_shapes=[
            pltpu.VMEM((total * width + 16, levels), F32),
            pltpu.VMEM((width, levels), F32),
            pltpu.VMEM((width, levels), F32),
            pltpu.VMEM((width, 2 * levels), BF16),
            pltpu.VMEM((width, 128), F32),
            pltpu.VMEM((width, 128), F32),
            pltpu.VMEM((width + 16, 128), F32),
            pltpu.SemaphoreType.DMA((2,)),
        ],
        compiler_params=pltpu.CompilerParams(vmem_limit_bytes=VMEM_LIMIT),
        cost_estimate=pl.CostEstimate(
            flops=STEPS * rows * width * levels * levels * 4,
            bytes_accessed=rows * width * levels * 10,
            transcendentals=0,
        ),
        name="outside_steps",
    )(scal, air, *halos, sea, coef, cour, vcat)


def cap_kernel(
    rows, count, width, blocks, fast, steps,
    scal, spec_in, t_high, t_low, stencil, weight, cour, vcat,
    wedge_in, side, sea_hist, flux_hist, coef, sea_in, flux_in,
    sea_ring_in, coef_ring, ring_flux_in, gathered, air_in,
    *outs_and_scratch,
):
    last = steps[-1] == STEPS
    if last:
        (air_out, sea_out, spec_a, spec_b, cur, prev, adv, xcat, kcat, point, sea, flux, pad, ring,
         sea_ring, shares, back, sems) = outs_and_scratch
    else:
        (spec_out, wedge_out, sea_out, flux_out, sea_ring_out, ring_out, gather_out,
         spec_a, spec_b, cur, prev, adv, xcat, kcat, point, sea, flux, pad, ring,
         sea_ring, shares) = outs_and_scratch
    flip, polar, block = scal[0], scal[1], scal[2]
    lanes = lane_iota((width, 128))
    own = pl.ds(pl.multiple_of(block * width, 128), width)

    def own_dot(x):
        return table_dot(t_high[own, :], t_low[own, :], x)

    def wedge_step(step):
        pending = flux_hist[step - 1]
        for j in range(step - 1):
            base = 8 + j * width
            if j == step - 2:
                south_ref, south = side.at[step - 2], 0
            else:
                south_ref, south = cur, base + width
            y = advance_row(
                width, cur, base, prev, 0, south_ref, south, cour, vcat, adv, xcat, prev
            )
            lane = NPOLE + j + ROW0
            out = exchange(y, lane, sea[...], coef[...])
            cur[pl.ds(base, width), :] = y + air_gain * out
            pending += pltpu.roll(out, lane, 1)
        return pending

    def cap_step(step, src, dst, slot):
        count_rows = CAP - step
        if step > 1:
            for j in range(blocks):
                ring[pl.ds(NPOLE, 8), pl.ds(j * width, width)] = gathered[
                    j, pl.ds(8 * slot, 8), :
                ]
            old, at = sea_ring[...], ring[...]
            place = lax.broadcasted_iota(jnp.int32, old.shape, 0)
            up = jnp.where(place == 0, 0.0, pltpu.roll(old, 1, 0))
            down = pltpu.roll(old, old.shape[0] - 1, 0)
            ring_width = blocks * width
            around = up + down + pltpu.roll(old, 1, 1) + pltpu.roll(old, ring_width - 1, 1)
            sea_ring[...] = old - ocean_gain * at + ocean_diffusion * (around - 4.0 * old)
            spot = lane_iota(at.shape) % width
            at = jnp.where((spot >= HALO) & (spot < HALO + count), at, 0.0)
            high, low = two_parts(at)
            both = dot(jnp.concatenate([high, low], axis=0), t_high[...])
            sums = both[:24] + both[24:] + dot(high, t_low[...])
            sums = sums * (air_gain * weight[0:1, :])
            sums = jnp.concatenate([sums, jnp.zeros((104, NK), F32)], axis=0)
            shares[...] = jnp.transpose(sums)

            @pl.loop(0, count_rows + 1)
            def _(q):
                moved = pltpu.roll(shares[...], lax.rem(128 - q, 128), 1)
                first = lane_iota((NK, 128)) == 0
                src[q + 1] += jnp.where(first, moved, 0.0)

        point[...] = jnp.zeros_like(point)

        @pl.loop(0, count_rows)
        def _(q):
            cut = scal[3 + q]
            for o, other in ((0, 128), (128, 0)):
                here = src[q + 1, pl.ds(o, 128), :]
                swapped = src[q + 1, pl.ds(other, 128), :]
                around = src[q, pl.ds(o, 128), :] + src[q + 2, pl.ds(o, 128), :]
                x = (
                    stencil[0, pl.ds(o, 128), :] * here
                    + diffusion_rate * around
                    + stencil[1, pl.ds(o, 128), :] * swapped
                )
                x = jnp.where(lax.broadcasted_iota(jnp.int32, x.shape, 0) <= cut, x, 0.0)
                high, low = two_parts(x)
                dst[q + 1, pl.ds(o, 128), :] = x
                kcat[pl.ds(o, 128), 0:128] = high
                kcat[pl.ds(o, 128), 128:256] = low
            mixed = dot(kcat[...], vcat[...])
            y = dst[q + 1] + mixed[:, :128] + mixed[:, 128:]
            dst[q + 1] = y
            first = lane_iota((NK, 128)) == 0
            point[...] += pltpu.roll(jnp.where(first, y, 0.0), q, 1)

        at_rows = jnp.transpose(point[...])[:NPOLE]
        high, low = two_parts(at_rows)
        both = dot_nt(jnp.concatenate([high, low], axis=0), t_high[...])
        surface = both[:NPOLE] + both[NPOLE:] + dot_nt(high, t_low[...])
        ring[0:NPOLE, :] = coef_ring[...] * (sea_ring[0:NPOLE, :] - surface)

        here = pltpu.roll(own_dot(point[...]), ROW0, 1)
        in_cap = (lanes >= ROW0) & (lanes < ROW0 + NPOLE)
        total = jnp.where(in_cap, coef[...] * (sea[...] - here), flux[...])
        flux[...] = total
        if step < STEPS:
            edge = pltpu.roll(total, 128 - (ROW0 + NPOLE - 1), 1)
            prev[...] = own_dot(dst[NPOLE]) + air_gain * jnp.where(lanes == 0, edge, 0.0)
        new = sea_next(width, polar, rows, sea[...], total, pad)
        sea[...] = jnp.where(lanes >= ROW0 + NPOLE + step - 1, sea_hist[step - 1], new)

    @pl.when(polar == 1)
    def _():
        spec_a[0] = jnp.zeros((NK, 128), F32)
        spec_b[0] = jnp.zeros((NK, 128), F32)
        spec_a[pl.ds(1, CAP)] = spec_in[...]
        cur[0:8, :] = jnp.zeros((8, 128), F32)
        for j in range(WEDGE):
            cur[pl.ds(8 + j * width, width), :] = wedge_in[j]
        cur[pl.ds(8 + WEDGE * width, 8), :] = jnp.zeros((8, 128), F32)
        pad[...] = jnp.zeros_like(pad)
        sea[...] = sea_in[...]
        flux[...] = flux_in[...]
        ring[0:NPOLE, :] = ring_flux_in[...]
        sea_ring[...] = sea_ring_in[...]
        src, dst = spec_a, spec_b
        for n, step in enumerate(steps):
            cap_step(step, src, dst, n)
            src, dst = dst, src
            if step < STEPS:
                pending = wedge_step(step + 1)
                flux[...] = pending
                if not last:
                    gather_out[pl.ds(8 * n, 8), :] = jnp.transpose(pending)[
                        NPOLE + ROW0 : NPOLE + ROW0 + 8
                    ]
        if last:
            start, extent = (HALO, count) if fast else (0, width)

            def send(ref, offset, q):
                r = jnp.where(flip == 1, rows - 1 - q, q)
                return pltpu.make_async_copy(
                    ref.at[pl.ds(offset + start, extent)], air_out.at[r], sems.at[q]
                )

            for j in range(WEDGE):
                send(cur, 8 + j * width, NPOLE + j).start()

            @pl.loop(0, NPOLE)
            def _(q):
                y = own_dot(src[q + 1])
                edge = pltpu.roll(flux[...], lax.rem(128 - ROW0 - q, 128), 1)
                back[q] = y + air_gain * jnp.where(lanes == 0, edge, 0.0)
                send(back.at[q], 0, q).start()

            @pl.loop(0, NPOLE)
            def _(q):
                send(back.at[q], 0, q).wait()

            for j in range(WEDGE):
                send(cur, 8 + j * width, NPOLE + j).wait()
            sea_out[...] = sea[...]
        else:
            spec_out[...] = src[pl.ds(1, CAP)]
            for j in range(WEDGE):
                wedge_out[j] = cur[pl.ds(8 + j * width, width), :]
            sea_out[...] = sea[...]
            flux_out[...] = flux[...]
            sea_ring_out[...] = sea_ring[...]
            ring_out[...] = ring[0:NPOLE, :]

    if last:
        @pl.when(polar == 0)
        def _():
            sea_out[...] = sea_hist[STEPS - 1]


def cap_steps(rows, count, width, blocks, fast, steps, operands):
    levels = 128
    ring_width = blocks * width
    last = steps[-1] == STEPS
    any_spec = pl.BlockSpec(memory_space=pl.ANY)
    vmem = pl.BlockSpec(memory_space=pltpu.VMEM)
    shape = jax.ShapeDtypeStruct
    if last:
        out_shape = [
            shape((rows, count if fast else width, levels), F32),
            shape((width, 128), F32),
        ]
        out_specs = [any_spec, vmem]
        extra = [pltpu.VMEM((NPOLE, width, levels), F32), pltpu.SemaphoreType.DMA((NPOLE + WEDGE,))]
        aliases = {len(operands) - 1: 0}
    else:
        out_shape = [
            shape((CAP, NK, levels), F32),
            shape((WEDGE, width, levels), F32),
            shape((width, 128), F32),
            shape((width, 128), F32),
            shape((24, ring_width), F32),
            shape((NPOLE, ring_width), F32),
            shape((16, width), F32),
        ]
        out_specs = [vmem] * 7
        extra = []
        aliases = {}
    return pl.pallas_call(
        functools.partial(cap_kernel, rows, count, width, blocks, fast, steps),
        out_shape=out_shape,
        in_specs=[pl.BlockSpec(memory_space=pltpu.SMEM)]
        + [vmem] * (len(operands) - 2)
        + [any_spec],
        out_specs=out_specs,
        scratch_shapes=[
            pltpu.VMEM((CAP + 2, NK, levels), F32),
            pltpu.VMEM((CAP + 2, NK, levels), F32),
            pltpu.VMEM((WEDGE * width + 16, levels), F32),
            pltpu.VMEM((width, levels), F32),
            pltpu.VMEM((width, levels), F32),
            pltpu.VMEM((width, 2 * levels), BF16),
            pltpu.VMEM((NK, 2 * levels), BF16),
            pltpu.VMEM((NK, 128), F32),
            pltpu.VMEM((width, 128), F32),
            pltpu.VMEM((width, 128), F32),
            pltpu.VMEM((width + 16, 128), F32),
            pltpu.VMEM((24, ring_width), F32),
            pltpu.VMEM((24, ring_width), F32),
            pltpu.VMEM((NK, 128), F32),
        ]
        + extra,
        input_output_aliases=aliases,
        compiler_params=pltpu.CompilerParams(vmem_limit_bytes=VMEM_LIMIT),
        cost_estimate=pl.CostEstimate(
            flops=len(steps) * CAP * NK * levels * levels * 4,
            bytes_accessed=20_000_000,
            transcendentals=0,
        ),
        name="cap_steps",
    )(*operands)


def shift(x, axis, by, wrap):
    size = lax.axis_size(axis)
    pairs = [(i, (i + by) % size) for i in range(size) if wrap or 0 <= i + by < size]
    return lax.ppermute(x, axis, pairs)


def to_all(x, blocks):
    copies = jnp.broadcast_to(x[None], (blocks,) + x.shape)
    return lax.all_to_all(copies, "lon", split_axis=0, concat_axis=0, tiled=True)


def local(air_temp, sea_temp, land_sea, courant, vertical_mix, cutoffs):
    rows, count, levels = air_temp.shape
    blocks, bands = lax.axis_size("lon"), lax.axis_size("lat")
    nlon = blocks * count
    width = round_up(count + 2 * HALO, 128)
    depth = round_up(count, 128)
    fast = count % 8 == 0
    band, block = lax.axis_index("lat"), lax.axis_index("lon")
    flip = band == bands - 1
    polar = (band == 0) | flip

    cut = jnp.where(flip, cutoffs[::-1][:NPOLE], cutoffs[:NPOLE])
    head = jnp.stack([flip, polar, block]).astype(jnp.int32)
    scal = jnp.concatenate([head, cut, jnp.full((STEPS + 1,), KMAX, jnp.int32)])
    window, forward, weight = tables(blocks, count, width, depth)
    t_high, t_low = (jnp.asarray(part) for part in window)
    own_high, own_low = (
        lax.dynamic_index_in_dim(jnp.asarray(part), block, 0, keepdims=False) for part in forward
    )
    theta = np.arange(KMAX + 1) * (2.0 * math.pi / nlon)
    cosine = np.tile(np.cos(theta), 2).astype(np.float32)
    sine = np.concatenate([-np.sin(theta), np.sin(theta)]).astype(np.float32)
    stay = 1.0 - 4.0 * diffusion_rate + 2.0 * diffusion_rate * jnp.asarray(cosine)
    stencil = jnp.stack(
        [
            jnp.broadcast_to(stay[:, None], (NK, levels)),
            (2.0 * 0.5) * jnp.asarray(sine)[:, None] * courant[None, :],
        ]
    )
    weights = jnp.broadcast_to(jnp.asarray(weight.astype(np.float32))[None], (8, NK))
    cour = jnp.stack([diffusion_rate - 0.5 * courant, diffusion_rate + 0.5 * courant])
    cour = jnp.concatenate([cour, jnp.zeros((6, levels), F32)], 0)
    v_round = lax.reduce_precision(vertical_mix, 8, 7)
    v_high, v_low = v_round.astype(BF16), (vertical_mix - v_round).astype(BF16)
    vcat = jnp.concatenate(
        [
            jnp.concatenate([v_high, v_low], 1),
            jnp.concatenate([v_high, jnp.zeros_like(v_low)], 1),
        ],
        0,
    )

    spec = start_spectra(scal, air_temp, own_high, own_low)
    spec = lax.psum(spec, "lon")

    west = shift(air_temp[:, count - HALO :], "lon", 1, True)
    east = shift(air_temp[:, :HALO], "lon", -1, True)

    def edge(part):
        return jnp.concatenate([west[part], air_temp[part], east[part]], 1)

    north = shift(edge(slice(rows - ROW0, rows)), "lat", 1, False)
    south = shift(edge(slice(0, ROW0)), "lat", -1, False)

    exchange_coef = jnp.where(land_sea == 1, sea_coef, land_coef).astype(F32)
    sea_band = lax.all_gather(sea_temp, "lon", axis=0, tiled=True)
    coef_band = lax.all_gather(exchange_coef, "lon", axis=1, tiled=True)
    pair = jnp.stack([sea_band, coef_band])
    above = shift(pair[:, rows - ROW0 :], "lat", 1, False)
    below = shift(pair[:, :ROW0], "lat", -1, False)
    pair = jnp.concatenate([above, pair, below], 1)
    pair = jnp.where(flip, pair[:, ::-1], pair)
    around = jnp.concatenate([pair[:, :, nlon - HALO :], pair, pair[:, :, : width]], 2)
    ring = jnp.concatenate(
        [around[:, ROW0 : ROW0 + 24, j * count : j * count + width] for j in range(blocks)], 2
    )
    mine = lax.dynamic_slice_in_dim(around, block * count, width, 2)
    mine = jnp.pad(mine.transpose(0, 2, 1), ((0, 0), (0, 0), (0, 128 - rows - 2 * ROW0)))
    sea, coef = mine[0], mine[1]
    sea_ring, coef_ring = ring[0], ring[1, :NPOLE]

    if fast:
        air = air_temp
    else:
        middle = jnp.concatenate([west, air_temp, east], 1)
        air = jnp.concatenate([north, middle, south], 0)
        air = jnp.pad(air, ((0, 0), (0, width - count - 2 * HALO), (0, 0)))
    halos = (west, east, north, south)
    air, wedge, side, sea_hist, flux_hist = outside_steps(
        rows, count, width, fast, scal, air, halos, sea, coef, cour, vcat
    )

    flux = flux_hist[0]
    first = NPOLE + ROW0
    gathered = jnp.zeros((16, width), F32).at[8:].set(flux[:, first : first + 8].T)
    gathered = lax.all_gather(gathered, "lon", axis=0, tiled=False)
    ring_flux = jnp.zeros((NPOLE, blocks * width), F32)
    for steps in ((1, 2), (3, 4), (5, 6)):
        operands = (
            scal, spec, t_high, t_low, stencil, weights, cour, vcat,
            wedge, side, sea_hist, flux_hist, coef, sea, flux,
            sea_ring, coef_ring, ring_flux, gathered, air,
        )
        outs = cap_steps(rows, count, width, blocks, fast, steps, operands)
        if steps[-1] < STEPS:
            spec, wedge, sea, flux, sea_ring, ring_flux, mine = outs
            gathered = to_all(mine, blocks).reshape(blocks, 16, width)
    air, sea = outs
    if not fast:
        air = air[:, HALO : HALO + count]
    sea = sea[HALO : HALO + count, ROW0 : ROW0 + rows].T
    sea = jnp.where(flip, sea[::-1], sea)
    sea = lax.all_to_all(sea, "lon", split_axis=0, concat_axis=1, tiled=True)
    return air, sea


def solution(mesh):
    placed = (P("lat", "lon", None), P(("lat", "lon"), None), P("lat", "lon"), P(), P(), P())
    return jax.shard_map(
        local,
        mesh=mesh,
        in_specs=placed,
        out_specs=(P("lat", "lon", None), P(("lat", "lon"), None)),
        check_vma=False,
    )
```

time: 1190 us -> 354 us (0.30)
  waiting for transfers between devices: 582 us -> 32.2 us
  matrix products: 154 us -> 0 us
  local copies, waits for them, and re-layouts: 170 us -> 19.9 us
  Pallas kernels: 0 us -> 138 us
  blocking collectives: 0 us -> 127 us
  other arithmetic: 134 us -> 7.44 us
  starting transfers between devices: 126 us -> 13.2 us
    psum x6 -> x1, waiting for transfers between devices: 544 us -> 32.1 us  [local(): spec = lax.psum(spec, 'lon')]
    dot_general x30 -> x0, matrix products: 154 us -> none  [the longest x6 51 us: local(): jnp.dot(advanced.reshape(-1, levels), vertical_mix, precision=lax.Precisi...]
    pallas_call x0 -> x5, Pallas kernels: none -> 138 us  [the longest x3 81.5 us: cap_steps(): pl.pallas_call(functools.partial(cap_kernel, rows, count, width, blocks,...]
    all_gather x0 -> x3, blocking collectives: none -> 95.5 us  [the longest x1 33 us: local(): gathered = lax.all_gather(gathered, 'lon', axis=0, tiled=False)]
    sub x6 -> x0, other arithmetic: 86.7 us -> none  [horizontal(): air_temp + diffusion_rate * laplace]
    scatter-add x6 -> x0, local copies, waits for them, and re-layouts: 72.3 us -> none  [local(): air_temp = air_next.at[:, :, 0].add(air_gain * heat_flux)]
    ppermute x36 -> x6, starting transfers between devices: 77.4 us -> 13.1 us  [shift(): return lax.ppermute(x, axis, pairs)]
    all_to_all x12 -> x0, starting transfers between devices: 48.8 us -> none  [the longest x6 26.1 us: local(): lax.all_to_all(heat_flux, 'lon', split_axis=0, concat_axis=1, tiled=True)]
  transfers between devices with their start and end apart: 54 -> 7, of which waited for: 21 -> 1; matrix products, arithmetic and copies ran while one was open for 37% -> 6% of each run, Pallas kernels for 0% -> 16%
where the time goes in v1:
time: 354 us; the launch traced here: 352 us
  Pallas kernels  138 us (39%)
  blocking collectives  127 us (36%)
  waiting for transfers between devices  32.2 us (9%)
  local copies, waits for them, and re-layouts  19.9 us (6%)
  between operations  14.4 us (4%)
  starting transfers between devices  13.2 us (4%)
  other arithmetic  7.44 us (2%)
    pallas_call x3, Pallas kernels, cap_steps(): pl.pallas_call(functools.partial(cap_kernel, rows, count, width, blocks,...  81.5 us
    pallas_call x1, Pallas kernels, outside_steps(): pl.pallas_call(functools.partial(outside_kernel, rows, count, width, fast...  40.9 us
    all_gather x1, blocking collectives, local(): gathered = lax.all_gather(gathered, 'lon', axis=0, tiled=False)  33 us
    psum x1, waiting for transfers between devices, local(): spec = lax.psum(spec, 'lon')  32.1 us
    all_gather x1, blocking collectives, local(): coef_band = lax.all_gather(exchange_coef, 'lon', axis=1, tiled=True)  31.6 us
    all_gather x1, blocking collectives, local(): sea_band = lax.all_gather(sea_temp, 'lon', axis=0, tiled=True)  30.9 us
    all_to_all x2, blocking collectives, to_all(): lax.all_to_all(copies, 'lon', split_axis=0, concat_axis=0, tiled=True)  22.2 us
    pallas_call x1, Pallas kernels, start_spectra(): pl.pallas_call(functools.partial(spectra_kernel, count), out_shape=jax.Sh...  16.1 us
  transfers between devices with their start and end apart: 7, of which 1 were waited for; matrix products, arithmetic and copies ran while one was open for 6% of the time, Pallas kernels for 16%

profile of v1, /device:TPU:0, one launch (start us, length us, event | category | flops | bytes accessed | tf_op | source)
XLA Modules:
  0.0 352.4 jit_solution(15022619376475034932)
XLA Ops:
  7.2 1.7 fusion.8
  8.9 6.0 %collective-permute-start.1 = (f32[32,8,128]{2,1,0:T(8,128)}, f32[32,8,128]{2,1,0:T(8,128)}, u32[]{:S(2)}, u32[]{:S(2)}) collective-permute-start(f32[32,8,128]{2,1,0:T(8,128)} %get-tuple-element.58), channel_id=1, source_target_pairs={{0,7},{1,0},{2,1},{3,2},{4,3},{5,4},{6,5},{7,6},{8,15},{9,8},{10,9... | collective-permute-start | bytes 393224 | tf_op jit(solution)/shard_map/ppermute | solution.py:547
  14.9 0.8 select_bitcast_fusion
  15.7 31.6 %all-gather.1 = f32[8,360,32]{1,2,0:T(8,128)S(1)} all-gather(f32[1,360,32]{1,2,0:T(8,128)S(1)} %select_bitcast_fusion), channel_id=1, replica_groups=mesh['lat'=4,'lon'=8] {'lon'}, dimensions={0}, use_global_device_ids=true | all-gather | bytes 414720 | tf_op jit(solution)/shard_map/all_gather | solution.py:611
  47.3 0.2 copy.47
  47.5 0.2 reshape.87
  47.7 30.9 %all-gather = f32[8,4,2880]{2,1,0:T(4,128)S(1)} all-gather(f32[1,4,2880]{2,1,0:T(4,128)S(1)} %bitcast.46), channel_id=1, replica_groups=mesh['lat'=4,'lon'=8] {'lon'}, dimensions={0}, use_global_device_ids=true | all-gather | bytes 414720 | tf_op jit(solution)/shard_map/all_gather | solution.py:610
  78.7 0.1 stack.42
  78.8 0.8 pad_maximum_fusion.5
  79.6 1.3 collective-permute-start.4
  80.9 1.3 collective-permute-start.5
  82.3 0.1 slice.109
  82.4 1.8 dynamic-slice_bitcast_fusion
  84.2 0.6 concatenate.38.scal
  84.8 16.1 %start_spectra.1 = f32[22,256,128]{2,1,0:T(8,128)} custom-call(s32[26]{0:T(128)} %concatenate.38.scal, f32[32,360,128]{2,1,0:T(8,128)} %air.3, bf16[256,384]{1,0:T(8,128)(2,1)} %get-tuple-element.73.high, bf16[256,384]{1,0:T(8,128)(2,1)} %get-tuple-element.72.low), custom_call_target="tpu_custom_call" | custom-call | tf_op jit(solution)/shard_map/start_spectra/pallas_call | solution.py:105
  101.0 1.8 fusion.7
  102.8 0.1 broadcast_multiply_fusion
  103.0 0.7 maximum_maximum_fusion.cour
  103.6 0.7 fusion.3.vcat
  104.3 0.1 stack_broadcast_in_dim.2
  104.4 0.7 pad_maximum_fusion.3.stencil
  105.1 0.8 fusion.10
  105.9 0.8 fusion.9
  106.7 1.1 pad_maximum_fusion
  107.7 3.3 collective-permute-start.2
  111.0 1.1 pad_maximum_fusion.1
  112.1 1.3 collective-permute-start.3
  113.4 0.1 pad_maximum_fusion.2
  113.6 0.8 rev.7
  114.4 0.2 broadcast_select_fusion
  114.7 0.1 fusion.5
  114.8 0.1 slice_dynamic-update-slice_fusion.5
  114.9 0.1 slice_dynamic-update-slice_fusion.4
  114.9 0.1 slice_dynamic-update-slice_fusion.3
  115.0 0.1 slice_dynamic-update-slice_fusion.2
  115.1 0.8 concatenate.46
  115.9 0.1 dynamic-slice_bitcast_fusion.2
  116.1 0.8 copy.49.coef
  116.9 0.8 copy.48.sea_in
  117.7 0.1 slice_dynamic-update-slice_fusion
  117.8 0.1 fusion.4
  117.9 0.7 slice_bitcast_fusion.2.coef_ring
  118.6 0.8 slice_bitcast_fusion.sea_ring_in
  119.4 40.9 %outside_steps.1 = (f32[32,360,128]{2,1,0:T(8,128)}, f32[5,384,128]{2,1,0:T(8,128)}, f32[5,384,128]{2,1,0:T(8,128)}, f32[6,384,128]{2,1,0:T(8,128)}, f32[6,384,128]{2,1,0:T(8,128)}) custom-call(s32[26]{0:T(128)} %concatenate.38.scal, f32[32,360,128]{2,1,0:T(8,128)} %air.3, f32[32,8,128]{2,1,0:T(8,128)} %collective-permute-done.west, ...), custom_call_target="tpu_custom_call" | custom-call | flops 4831838208 | bytes 15728640 | tf_op jit(solution)/shard_map/outside_steps/pallas_call | solution.py:275
  160.2 0.9 slice_bitcast_fusion.3.flux_in
  161.2 0.1 slice_bitcast_fusion.1
  161.3 0.1 copy.57
  161.4 33.0 %all_gather.15.gathered = f32[8,16,384]{2,1,0:T(8,128)} all-gather(f32[1,16,384]{2,1,0:T(8,128)S(1)} %scatter.4.clone), channel_id=1, replica_groups=mesh['lat'=4,'lon'=8] {'lon'}, dimensions={0}, use_global_device_ids=true | all-gather | bytes 221184 | tf_op jit(solution)/shard_map/all_gather | solution.py:640
  194.4 32.1 %all-reduce.5.cloned.1.call-done.spec_in = f32[22,256,128]{2,1,0:T(8,128)} async-done(((f32[22,256,128]{2,1,0:T(8,128)}), f32[22,256,128]{2,1,0:T(8,128)}) %all-reduce.5.cloned.1.call-update) | async-done | bytes 2883600 | tf_op jit(solution)/shard_map/psum | solution.py:598
  226.5 0.6 broadcast_in_dim.18.weight
  227.1 0.7 broadcast_in_dim.22.ring_flux_in
  227.8 25.0 %cap_steps.3 = (f32[22,256,128]{2,1,0:T(8,128)}, f32[5,384,128]{2,1,0:T(8,128)}, f32[384,128]{1,0:T(8,128)}, f32[384,128]{1,0:T(8,128)}, f32[24,3072]{1,0:T(8,12...) custom-call(s32[26]{0:T(128)} %concatenate.38.scal, f32[22,256,128]{2,1,0:T(8,128)} %all-reduce.5.cloned.1.call-done.spec_in, ...), custom_call_target="tpu_custom_call" | custom-call | flops 738197504 | bytes 20000000 | tf_op jit(solution)/shard_map/cap_steps/pallas_call | solution.py:509
  252.7 0.8 broadcast_in_dim.42
  253.5 11.3 %all_to_all.29.gathered = f32[8,16,384]{2,1,0:T(8,128)} all-to-all(f32[8,16,384]{2,1,0:T(8,128)S(1)} %broadcast_in_dim.42), channel_id=1, replica_groups=mesh['lat'=4,'lon'=8] {'lon'}, dimensions={0} | all-to-all | bytes 393216 | tf_op jit(solution)/shard_map/all_to_all | solution.py:552
  264.8 27.6 %cap_steps.4 = (f32[22,256,128]{2,1,0:T(8,128)}, f32[5,384,128]{2,1,0:T(8,128)}, f32[384,128]{1,0:T(8,128)}, f32[384,128]{1,0:T(8,128)}, f32[24,3072]{1,0:T(8,12...) custom-call(s32[26]{0:T(128)} %concatenate.38.scal, f32[22,256,128]{2,1,0:T(8,128)} %get-tuple-element.40.spec_in, ...), custom_call_target="tpu_custom_call" | custom-call | flops 738197504 | bytes 20000000 | tf_op jit(solution)/shard_map/cap_steps/pallas_call | solution.py:509
  292.4 0.8 broadcast_in_dim.43
  293.1 10.8 %all_to_all.30.gathered = f32[8,16,384]{2,1,0:T(8,128)} all-to-all(f32[8,16,384]{2,1,0:T(8,128)S(1)} %broadcast_in_dim.43), channel_id=1, replica_groups=mesh['lat'=4,'lon'=8] {'lon'}, dimensions={0} | all-to-all | bytes 393216 | tf_op jit(solution)/shard_map/all_to_all | solution.py:552
  304.0 29.0 %cap_steps.5 = (f32[32,360,128]{2,1,0:T(8,128)}, f32[384,128]{1,0:T(8,128)}) custom-call(s32[26]{0:T(128)} %concatenate.38.scal, f32[22,256,128]{2,1,0:T(8,128)} %get-tuple-element.47.spec_in, bf16[3072,256]{1,0:T(8,128)(2,1)} %constant.86.clone.t_high, bf16[3072,256]{1,0:T(8,128)(2,1)} %constant.87.clone.t_low, ...), custom_call_target="tpu_custom_call", output_to_operand_aliasing={{0}: (19, {})} | custom-call | flops 738197504 | bytes 20000000 | tf_op jit(solution)/shard_map/cap_steps/pallas_call | solution.py:509
  332.9 1.0 slice_bitcast_fusion.4
  334.0 0.5 rev.8
  334.5 1.0 broadcast_select_fusion.1
  335.5 0.1 copy.55
  335.7 9.2 %all_to_all.31 = f32[8,4,360]{2,1,0:T(4,128)S(1)} all-to-all(f32[8,4,360]{2,1,0:T(4,128)S(1)} %all_to_all.22), channel_id=1, replica_groups=mesh['lat'=4,'lon'=8] {'lon'}, dimensions={0} | all-to-all | bytes 92160 | tf_op jit(solution)/shard_map/all_to_all | solution.py:657
  344.9 0.7 all_to_all.25
  (39 shorter events, 0.5 us)
Async XLA Ops:
  7.2 219.3 %all-reduce.5.cloned.1.call-start = ((), (), s32[]{:S(2)}) async-start(), calls=%async_computation.3 | async-start | bytes 5767168 | tf_op jit(solution)/shard_map/psum | solution.py:598
  8.9 38.8 %copy-start.2 = (f32[4,2880]{1,0:T(4,128)S(1)}, f32[4,2880]{1,0:T(4,128)}, u32[]{:S(2)}) copy-start(f32[4,2880]{1,0:T(4,128)} %param.16) | copy-start | bytes 138244
  8.9 96.2 %collective-permute-start.1 = (f32[32,8,128]{2,1,0:T(8,128)}, f32[32,8,128]{2,1,0:T(8,128)}, u32[]{:S(2)}, u32[]{:S(2)}) collective-permute-start(f32[32,8,128]{2,1,0:T(8,128)} %get-tuple-element.58), channel_id=1, source_target_pairs={{0,7},{1,0},{2,1},{3,2},{4,3},{5,4},{6,5},{7,6},{8,15},{9,8},{10,9... | collective-permute-start | bytes 393224 | tf_op jit(solution)/shard_map/ppermute | solution.py:547
  14.9 91.0 %collective-permute-start = (f32[32,8,128]{2,1,0:T(8,128)}, f32[32,8,128]{2,1,0:T(8,128)}, u32[]{:S(2)}, u32[]{:S(2)}) collective-permute-start(f32[32,8,128]{2,1,0:T(8,128)} %get-tuple-element.59), channel_id=1, source_target_pairs={{0,1},{1,2},{2,3},{3,4},{4,5},{5,6},{6,7},{7,0},{8,9},{9,10},{10,1... | collective-permute-start | bytes 393224 | tf_op jit(solution)/shard_map/ppermute | solution.py:547
  47.7 34.5 %copy-start.7 = (s32[32]{0:T(128)S(1)}, s32[32]{0:T(128)}, u32[]{:S(2)}) copy-start(s32[32]{0:T(128)} %param.20) | copy-start | bytes 388
  79.6 33.8 %collective-permute-start.4 = (f32[2,6,2880]{2,1,0:T(8,128)}, f32[2,6,2880]{2,1,0:T(8,128)S(1)}, u32[]{:S(2)}, u32[]{:S(2)}) collective-permute-start(f32[2,6,2880]{2,1,0:T(8,128)} %get-tuple-element.60), channel_id=1, source_target_pairs={{0,8},{8,16},{16,24},{1,9},{9,17},{17,25},{2,10},{10,18},{18,26},{... | collective-permute-start | bytes 414728 | tf_op jit(solution)/shard_map/ppermute | solution.py:547
  80.9 32.6 %collective-permute-start.5 = (f32[2,6,2880]{2,1,0:T(8,128)}, f32[2,6,2880]{2,1,0:T(8,128)S(1)}, u32[]{:S(2)}, u32[]{:S(2)}) collective-permute-start(f32[2,6,2880]{2,1,0:T(8,128)} %get-tuple-element.61), channel_id=1, source_target_pairs={{8,0},{16,8},{24,16},{9,1},{17,9},{25,17},{10,2},{18,10},{26,18},{... | collective-permute-start | bytes 414728 | tf_op jit(solution)/shard_map/ppermute | solution.py:547
  100.9 1.8 copy-start.6
  100.9 1.8 copy-start.1
  101.0 1.8 copy-start.4
  101.0 3.3 copy-start.3
  107.7 11.6 %collective-permute-start.2 = (f32[6,376,128]{2,1,0:T(8,128)}, f32[6,376,128]{2,1,0:T(8,128)}, u32[]{:S(2)}, u32[]{:S(2)}) collective-permute-start(f32[6,376,128]{2,1,0:T(8,128)} %pad_maximum_fusion), channel_id=1, source_target_pairs={{0,8},{8,16},{16,24},{1,9},{9,17},{17,25},{2,10},{10,18},{18,26},{... | collective-permute-start | bytes 3465224 | tf_op jit(solution)/shard_map/ppermute | solution.py:547
  112.1 7.2 %collective-permute-start.3 = (f32[6,376,128]{2,1,0:T(8,128)}, f32[6,376,128]{2,1,0:T(8,128)}, u32[]{:S(2)}, u32[]{:S(2)}) collective-permute-start(f32[6,376,128]{2,1,0:T(8,128)} %pad_maximum_fusion.1), channel_id=1, source_target_pairs={{8,0},{16,8},{24,16},{9,1},{17,9},{25,17},{10,2},{18,10},{26,18},{... | collective-permute-start | bytes 3465224 | tf_op jit(solution)/shard_map/ppermute | solution.py:547
  160.2 66.3 %copy-start.5 = (f32[256]{0:T(256)S(1)}, f32[256]{0:T(256)}, u32[]{:S(2)}) copy-start(f32[256]{0:T(256)} %constant.92.clone) | copy-start | bytes 3076
  161.2 66.6 %copy-start = (f32[384,128]{1,0:T(8,128)}, f32[384,128]{1,0:T(8,128)S(1)}, u32[]{:S(2)}) copy-start(f32[384,128]{1,0:T(8,128)S(1)} %slice_bitcast_fusion.3.flux_in) | copy-start | bytes 589828
Sparse Core Ops, SparseCore 0:
  101.1 125.4 all-reduce.4

commit v2 on v1

v2 whole, which is shorter than its diff:
```python
import functools
import math

import jax
import jax.numpy as jnp
import ml_dtypes
import numpy as np
from jax import lax
from jax.experimental import pallas as pl
from jax.experimental.pallas import tpu as pltpu
from jax.sharding import PartitionSpec as P

NPOLE = 16
KMAX = 127
STEPS = 6
NK = 2 * (KMAX + 1)
CAP = NPOLE + STEPS
HALO = 8
ROW0 = STEPS
WEDGE = STEPS - 1

diffusion_rate = 0.1
air_gain = 0.5
ocean_gain = 0.3
ocean_diffusion = 0.2
sea_coef = 0.5
land_coef = 0.15

F32 = jnp.float32
BF16 = jnp.bfloat16
VMEM_LIMIT = 56 * 1024 * 1024


def round_up(value, unit):
    return -(-value // unit) * unit


def two_parts(x):
    high = x.astype(BF16)
    return high, (x - high.astype(F32)).astype(BF16)


def dot(a, b):
    return jnp.dot(a, b, preferred_element_type=F32)


def dot_nt(a, b):
    return lax.dot_general(a, b, (((1,), (1,)), ((), ())), preferred_element_type=F32)


def table_dot(high, low, x):
    x_high, x_low = two_parts(x)
    both = dot(high, jnp.concatenate([x_high, x_low], axis=1))
    return both[:, :128] + both[:, 128:] + dot(low, x_high)


def numpy_parts(table):
    high = table.astype(ml_dtypes.bfloat16)
    low = (table - high.astype(np.float64)).astype(ml_dtypes.bfloat16)
    return high, low


@functools.lru_cache(maxsize=None)
def tables(blocks, count, width, depth):
    nlon = blocks * count
    wavenum = np.arange(KMAX + 1)
    weight = np.where(wavenum == 0, 1.0, 2.0) / nlon

    def table(columns):
        phase = (columns[:, None] * wavenum[None, :]) % nlon * (2.0 * math.pi / nlon)
        return np.concatenate([np.cos(phase), np.sin(phase)], 1)

    window = np.concatenate(
        [table((j * count - HALO + np.arange(width)) % nlon) for j in range(blocks)], 0
    )
    forward = np.zeros((blocks, NK, depth))
    for j in range(blocks):
        own = table(j * count + np.arange(count)) * np.tile(weight, 2)
        forward[j, :, :count] = own.T
    high, low = numpy_parts(forward)
    return numpy_parts(window), np.concatenate([high, high, low], 2), np.tile(weight, 2)


def lane_iota(shape):
    return lax.broadcasted_iota(jnp.int32, shape, len(shape) - 1)


def spectra_kernel(count, blocks, scal, air, table, keep, send, stacked, sums):
    depth = stacked.shape[0] // 3
    half, part = blocks // 2, NK // blocks
    flip, block = scal[0], scal[2]
    side, place = lax.rem(block, 2), block // 2

    @pl.when(pl.program_id(0) == 0)
    def _():
        stacked[...] = jnp.zeros_like(stacked)

    @pl.when(scal[1] == 1)
    def _():
        for n in range(2):
            high, low = two_parts(air[n])
            lanes = slice(128 * n, 128 * n + 128)
            stacked[0:count, lanes] = high
            stacked[depth : depth + count, lanes] = low
            stacked[2 * depth : 2 * depth + count, lanes] = high
        sums[...] = dot(table[...], stacked[...])
        for n in range(2):
            to = jnp.where(flip == 1, 1 - n, n)
            lanes = slice(128 * n, 128 * n + 128)
            for z in range(half):
                at = jnp.bitwise_xor(place, z)
                mine = pl.multiple_of((side * half + z) * part, part)
                other = pl.multiple_of(((1 - side) * half + z) * part, part)
                keep[at, to] = sums[pl.ds(mine, part), lanes]
                send[at, to] = sums[pl.ds(other, part), lanes]


def start_spectra(blocks, scal, air_temp, table):
    rows, count, levels = air_temp.shape
    half, part = blocks // 2, NK // blocks
    depth = table.shape[1] // 3

    def place(p, scal):
        return (jnp.where(scal[0] == 1, rows // 2 - 1 - p, p), 0, 0)

    out = jax.ShapeDtypeStruct((half, CAP, part, levels), F32)
    out_spec = pl.BlockSpec((half, 2, part, levels), lambda p, scal: (0, p, 0, 0))
    return pl.pallas_call(
        functools.partial(spectra_kernel, count, blocks),
        out_shape=[out, out],
        grid_spec=pltpu.PrefetchScalarGridSpec(
            num_scalar_prefetch=1,
            grid=(CAP // 2,),
            in_specs=[
                pl.BlockSpec((2, count, levels), place),
                pl.BlockSpec((NK, 3 * depth), lambda p, scal: (0, 0)),
            ],
            out_specs=[out_spec, out_spec],
            scratch_shapes=[
                pltpu.VMEM((3 * depth, 2 * levels), BF16),
                pltpu.VMEM((NK, 2 * levels), F32),
            ],
        ),
        compiler_params=pltpu.CompilerParams(vmem_limit_bytes=VMEM_LIMIT // 2),
        name="start_spectra",
    )(scal, air_temp, table)


def advance(
    width, here_ref, base, north_ref, north, south_ref, south, cour, adv, xcat, more=None
):
    c_east, c_west = cour[0:1, :], cour[1:2, :]
    for o in range(0, width, 128):
        around = north_ref[pl.ds(north + o, 128), :] + south_ref[pl.ds(south + o, 128), :]
        x = (
            (1.0 - 4.0 * diffusion_rate) * here_ref[pl.ds(base + o, 128), :]
            + diffusion_rate * around
            + c_east * here_ref[pl.ds(base + o + 1, 128), :]
            + c_west * here_ref[pl.ds(base + o - 1, 128), :]
        )
        if more is not None:
            moved = pltpu.roll(more[0][pl.ds(o, 128), :], more[1], 1)
            x += jnp.where(lane_iota(x.shape) == 0, moved, 0.0)
        high, low = two_parts(x)
        adv[pl.ds(o, 128), :] = x
        xcat[pl.ds(o, 128), 0:128] = high
        xcat[pl.ds(o, 128), 128:256] = low


def two_at_a_time(first, pairs, load, finish):
    load(first, 0)

    @pl.loop(0, pairs)
    def _(n):
        q = first + 2 * n
        finish(q, 0, lambda: load(q + 1, 1))
        finish(q + 1, 1, lambda: load(q + 2, 0))


def exchange(y, lane, sea, coef):
    back = (128 - lane) % 128
    flux = pltpu.roll(coef, back, 1) * (pltpu.roll(sea, back, 1) - y)
    return jnp.where(lane_iota(y.shape) == 0, flux, 0.0)


def sea_next(width, polar, rows, sea, flux, pad):
    pad[pl.ds(8, width), :] = sea
    east = pad[pl.ds(9, width), :]
    west = pad[pl.ds(7, width), :]
    around = east + west + pltpu.roll(sea, 1, 1) + pltpu.roll(sea, 127, 1)
    new = sea - ocean_gain * flux + ocean_diffusion * (around - 4.0 * sea)
    lane = lane_iota(sea.shape)
    first = jnp.where(polar == 1, ROW0, 0)
    return jnp.where((lane >= first) & (lane < rows + 2 * ROW0), new, 0.0)


def windows_kernel(rows, count, width, blocks, scal, got, own, ring_sea, ring_coef, wide):
    per = rows // blocks
    for j in range(blocks):
        columns = slice(j * width + HALO, j * width + HALO + count)
        for i in range(blocks):
            wide[0, per * i : per * (i + 1), columns] = got[i, per * j : per * (j + 1), :]
        wide[1, :, columns] = got[j, rows:, :]
    rest = width - HALO - count
    for j in range(blocks):
        before = ((j - 1) % blocks) * width + count
        after = ((j + 1) % blocks) * width + HALO
        end = j * width + HALO + count
        wide[:, :, j * width : j * width + HALO] = wide[:, :, before : before + HALO]
        wide[:, :, end : end + rest] = wide[:, :, after : after + rest]
    own[...] = wide[:, :, pl.ds(pl.multiple_of(scal[2] * width, 128), width)]

    @pl.when(scal[1] == 1)
    def _():
        @pl.loop(0, 24)
        def _(q):
            r = jnp.where(scal[0] == 1, rows - 1 - q, q)
            ring_sea[pl.ds(q, 1), :] = wide[0, pl.ds(r, 1), :]

        @pl.loop(0, NPOLE)
        def _(q):
            r = jnp.where(scal[0] == 1, rows - 1 - q, q)
            ring_coef[pl.ds(q, 1), :] = wide[1, pl.ds(r, 1), :]


def windows(rows, count, width, blocks, scal, got):
    vmem = pl.BlockSpec(memory_space=pltpu.VMEM)
    shape = jax.ShapeDtypeStruct
    return pl.pallas_call(
        functools.partial(windows_kernel, rows, count, width, blocks),
        out_shape=[
            shape((2, rows, width), F32),
            shape((24, blocks * width), F32),
            shape((NPOLE, blocks * width), F32),
        ],
        in_specs=[pl.BlockSpec(memory_space=pltpu.SMEM), vmem],
        out_specs=[vmem] * 3,
        scratch_shapes=[pltpu.VMEM((2, rows, blocks * width), F32)],
        compiler_params=pltpu.CompilerParams(vmem_limit_bytes=VMEM_LIMIT // 2),
        name="windows",
    )(scal, got)


def outside_kernel(rows, count, width, fast, steps, scal, *refs):
    first, last = steps[0] == 1, steps[-1] == STEPS
    if first:
        (air, west, east, north, south, own, above, below, cour, vcat), refs = refs[:10], refs[10:]
        (state, wedge, side, sea_hist, flux_hist, sea_start, coef, gather_out), refs = (
            refs[:8], refs[8:])
    else:
        (state, sea_hist_in, flux_hist_in, coef, cour, vcat), refs = refs[:6], refs[6:]
        (air_out, wedge, side, sea_hist, flux_hist), refs = refs[:5], refs[5:]
    (buf_a, buf_b, adv_a, adv_b, xcat_a, xcat_b, sea, flux, point, more, turn, pad, sems) = refs
    flip, polar = scal[0], scal[1]
    total = rows + 2 * ROW0
    inner = count + 2 * HALO
    lanes = lane_iota((width, 128))

    def base_of(q):
        return pl.multiple_of(8 + (q + ROW0) * width, 8)

    def q_of(r):
        return jnp.where(flip == 1, rows - 1 - r, r)

    def low_row(step):
        return jnp.where(polar == 1, NPOLE + step - 1, step - STEPS)

    def row_range(body, step, *sizes):
        hi = rows - 1 + STEPS - step
        ref, extent, sem = sizes

        @pl.loop(low_row(step), hi + 1)
        def _(q):
            body(q).start()

        for kind, count_rows in ((1, hi + 1 - NPOLE - step + 1), (0, hi + 1 + STEPS - step)):
            @pl.when(polar == kind)
            def _(count_rows=count_rows):
                whole = ref.at[pl.ds(0, count_rows * extent)]
                pltpu.make_async_copy(whole, whole, sem).wait()

    def begin():
        beyond = 8 + total * width
        for ref in (buf_a, buf_b):
            ref[0:8, :] = jnp.zeros((8, 128), F32)
            ref[pl.ds(beyond, 3 * width + 8), :] = jnp.zeros((3 * width + 8, 128), F32)
        pad[...] = jnp.zeros_like(pad)

    if first:
        if fast:
            @pl.loop(0, rows)
            def _(r):
                base = base_of(q_of(r))
                for ref, offset, size in (
                    (west, 0, HALO), (air, HALO, count), (east, HALO + count, HALO)
                ):
                    pltpu.make_async_copy(
                        ref.at[r], buf_a.at[pl.ds(base + offset, size)], sems.at[0]
                    ).start()

            @pl.loop(0, ROW0)
            def _(r):
                for ref, at in ((north, r - ROW0), (south, r + rows)):
                    pltpu.make_async_copy(
                        ref.at[r], buf_a.at[pl.ds(base_of(q_of(at)), inner)], sems.at[0]
                    ).start()

            if inner < width:
                @pl.loop(0, total)
                def _(e):
                    buf_a[pl.ds(base_of(e - ROW0) + inner, width - inner), :] = jnp.zeros(
                        (width - inner, 128), F32
                    )

            everything = buf_a.at[pl.ds(0, total * inner)]
        else:
            @pl.loop(0, total)
            def _(e):
                pltpu.make_async_copy(
                    air.at[e], buf_a.at[pl.ds(base_of(q_of(e - ROW0)), width)], sems.at[0]
                ).start()

            everything = buf_a.at[pl.ds(0, total * width)]
        begin()
        for n, ref in ((0, sea), (1, coef)):
            turn[...] = jnp.zeros_like(turn)
            for source, size, at in ((above, ROW0, -ROW0), (own, rows, 0), (below, ROW0, rows)):
                @pl.loop(0, size)
                def _(r, source=source, at=at):
                    turn[pl.ds(q_of(r + at) + ROW0, 1), :] = source[n, pl.ds(r, 1), :]

            ref[...] = jnp.transpose(turn[...])
        sea_start[...] = sea[...]
        pltpu.make_async_copy(everything, everything, sems.at[0]).wait()
    else:
        begin()
        sea[...] = sea_hist_in[steps[0] - 2]
        flux[...] = flux_hist_in[steps[0] - 2]
        row_range(
            lambda q: pltpu.make_async_copy(
                state.at[q + ROW0], buf_a.at[pl.ds(base_of(q), width)], sems.at[0]
            ),
            steps[0] - 1, buf_a, width, sems.at[0],
        )

    def with_flux(y, q):
        gain = air_gain * pltpu.roll(flux[...], 128 - (q + ROW0), 1)
        return y + jnp.where(lanes == 0, gain, 0.0)

    advs, xcats = (adv_a, adv_b), (xcat_a, xcat_b)
    src, dst = buf_a, buf_b
    for n, step in enumerate(steps):
        lo = low_row(step)
        hi = rows - 1 + STEPS - step
        pairs = jnp.where(polar == 1, (hi - NPOLE - step + 3) // 2, (hi + 1 + STEPS - step) // 2)
        if step > 1:
            gain = air_gain * flux[...]
            pad[pl.ds(8, width), :] = gain
            more[...] = (
                (1.0 - 4.0 * diffusion_rate) * gain
                + diffusion_rate * (pltpu.roll(gain, 1, 1) + pltpu.roll(gain, 127, 1))
                + cour[2:3, :] * pad[pl.ds(9, width), :]
                + cour[3:4, :] * pad[pl.ds(7, width), :]
            )
        point[...] = jnp.zeros_like(point)

        def load(q, slot, src=src, step=step):
            base = base_of(q)
            advance(width, src, base, src, base - width, src, base + width, cour,
                    advs[slot], xcats[slot], (more, 128 - (q + ROW0)) if step > 1 else None)

        def finish(q, slot, between, dst=dst):
            mixed = dot(xcats[slot][...], vcat[...])
            between()
            y = advs[slot][...] + mixed[:, :128] + mixed[:, 128:]
            dst[pl.ds(base_of(q), width), :] = y
            point[...] += pltpu.roll(jnp.where(lanes == 0, y, 0.0), q + ROW0, 1)

        two_at_a_time(lo, pairs, load, finish)

        total_flux = jnp.where(lanes >= lo + ROW0, coef[...] * (sea[...] - point[...]), 0.0)
        flux[...] = total_flux
        new_sea = sea_next(width, polar, rows, sea[...], total_flux, pad)
        sea[...] = new_sea
        sea_hist[n] = new_sea
        flux_hist[n] = total_flux
        if step <= WEDGE:
            @pl.when(polar == 1)
            def _(dst=dst, step=step, n=n):
                for ref, q in ((wedge, NPOLE + step - 1), (side, NPOLE + step)):
                    ref[n] = with_flux(dst[pl.ds(base_of(q), width), :], q)
        src, dst = dst, src

    if first:
        state_rows = row_range(
            lambda q: pltpu.make_async_copy(
                src.at[pl.ds(base_of(q), width)], state.at[q + ROW0], sems.at[1]
            ),
            steps[-1], src, width, sems.at[1],
        )
        turned = jnp.transpose(flux_hist[0])[NPOLE + ROW0 : NPOLE + ROW0 + 8]
        gather_out[...] = jnp.concatenate([jnp.zeros_like(turned), turned], axis=0)
    else:
        start, extent = (HALO, count) if fast else (0, width)
        first_row = jnp.where(polar == 1, NPOLE + WEDGE, 0)

        @pl.loop(first_row, rows)
        def _(q):
            row = pl.ds(base_of(q), width)
            src[row, :] = with_flux(src[row, :], q)
            pltpu.make_async_copy(
                src.at[pl.ds(base_of(q) + start, extent)], air_out.at[q_of(q)], sems.at[1]
            ).start()

        for kind, count_rows in ((1, rows - NPOLE - WEDGE), (0, rows)):
            @pl.when(polar == kind)
            def _(count_rows=count_rows):
                whole = src.at[pl.ds(0, count_rows * extent)]
                pltpu.make_async_copy(whole, whole, sems.at[1]).wait()


def outside_steps(rows, count, width, fast, steps, scal, big, small):
    levels = 128
    any_spec = pl.BlockSpec(memory_space=pl.ANY)
    vmem = pl.BlockSpec(memory_space=pltpu.VMEM)
    total = rows + 2 * ROW0
    shape = jax.ShapeDtypeStruct
    square = shape((width, 128), F32)
    hist = [shape((len(steps), width, 128), F32)] * 4
    if steps[0] == 1:
        out_shape = [shape((total, width, levels), F32)] + hist + [square, square]
        out_shape.append(shape((16, width), F32))
    else:
        out_shape = [shape((rows, count if fast else width, levels), F32)] + hist
    return pl.pallas_call(
        functools.partial(outside_kernel, rows, count, width, fast, steps),
        out_shape=out_shape,
        in_specs=[pl.BlockSpec(memory_space=pltpu.SMEM)]
        + [any_spec] * len(big)
        + [vmem] * len(small),
        out_specs=[any_spec] + [vmem] * (len(out_shape) - 1),
        scratch_shapes=[
            pltpu.VMEM(((total + 3) * width + 16, levels), F32),
            pltpu.VMEM(((total + 3) * width + 16, levels), F32),
            pltpu.VMEM((width, levels), F32),
            pltpu.VMEM((width, levels), F32),
            pltpu.VMEM((width, 2 * levels), BF16),
            pltpu.VMEM((width, 2 * levels), BF16),
            pltpu.VMEM((width, 128), F32),
            pltpu.VMEM((width, 128), F32),
            pltpu.VMEM((width, 128), F32),
            pltpu.VMEM((width, 128), F32),
            pltpu.VMEM((128, width), F32),
            pltpu.VMEM((width + 16, 128), F32),
            pltpu.SemaphoreType.DMA((2,)),
        ],
        compiler_params=pltpu.CompilerParams(vmem_limit_bytes=VMEM_LIMIT),
        cost_estimate=pl.CostEstimate(
            flops=len(steps) * rows * width * levels * levels * 4,
            bytes_accessed=rows * width * levels * 10,
            transcendentals=0,
        ),
        name="outside_steps",
    )(scal, *big, *small)


def cap_kernel(rows, count, width, blocks, fast, steps, parts, scal, *refs):
    last = steps[-1] == STEPS
    wedge_steps = [step + 1 for step in steps if step < STEPS]
    spec_in, refs = refs[:parts], refs[parts:]
    hists, refs = refs[: 4 * len(cap_hists(steps))], refs[4 * len(cap_hists(steps)) :]
    names = ["t_high", "t_low", "stencil", "coef", "sea", "sea_ring", "coef_ring", "gathered"]
    if steps[0] > 1:
        names += ["flux", "ring_flux", "wedge"]
    loads = dict(zip(names, refs[: len(names)]))
    refs = refs[len(names) :]
    weight, cour, vcat = refs[:3]
    refs = refs[3:]
    if last:
        refs = refs[1:]
        (air_out, sea_out), refs = refs[:2], refs[2:]
    else:
        (spec_out, wedge_out, sea_out, flux_out, sea_ring_out, ring_out, gather_out), refs = (
            refs[:7], refs[7:])
    (spec_a, spec_b, cur, prev, adv, xcat, kcat_a, kcat_b, kadv_a, kadv_b, point, sea, flux, pad,
     ring, sea_ring, shares, t_high, t_low, stencil, coef, coef_ring, gathered, sea_hist,
     flux_hist, side, turn, load_sems) = refs[:28]
    if last:
        back, sems = refs[28:]
    flip, polar, block = scal[0], scal[1], scal[2]
    lanes = lane_iota((width, 128))
    own = pl.ds(pl.multiple_of(block * width, 128), width)

    def hist(kind, step):
        at = cap_hists(steps).index(0 if step <= 3 else 1)
        return hists[4 * at + kind].at[(step - 1) % 3]

    def own_dot(x):
        return table_dot(t_high[own, :], t_low[own, :], x)

    def wedge_step(step):
        at = wedge_steps.index(step)
        pending = flux_hist[at]
        for j in range(step - 1):
            base = 8 + j * width
            if j == step - 2:
                south_ref, south = side.at[at], 0
            else:
                south_ref, south = cur, base + width
            advance(width, cur, base, prev, 0, south_ref, south, cour, adv, xcat)
            prev[...] = cur[pl.ds(base, width), :]
            mixed = dot(xcat[...], vcat[...])
            y = adv[...] + mixed[:, :128] + mixed[:, 128:]
            lane = NPOLE + j + ROW0
            out = exchange(y, lane, sea[...], coef[...])
            cur[pl.ds(base, width), :] = y + air_gain * out
            pending += pltpu.roll(out, lane, 1)
        return pending

    def cap_step(step, src, dst, slot):
        count_rows = CAP - step
        if step > 1:
            ready("gathered", "t_high", "t_low", "stencil", "sea_ring", "ring_flux")
        if step > 1:
            for j in range(blocks):
                ring[pl.ds(NPOLE, 8), pl.ds(j * width, width)] = gathered[
                    j, pl.ds(8 * slot, 8), :
                ]
            old, at = sea_ring[...], ring[...]
            place = lax.broadcasted_iota(jnp.int32, old.shape, 0)
            up = jnp.where(place == 0, 0.0, pltpu.roll(old, 1, 0))
            down = pltpu.roll(old, old.shape[0] - 1, 0)
            ring_width = blocks * width
            around = up + down + pltpu.roll(old, 1, 1) + pltpu.roll(old, ring_width - 1, 1)
            sea_ring[...] = old - ocean_gain * at + ocean_diffusion * (around - 4.0 * old)
            spot = lane_iota(at.shape) % width
            at = jnp.where((spot >= HALO) & (spot < HALO + count), at, 0.0)
            high, low = two_parts(at)
            both = dot(jnp.concatenate([high, low], axis=0), t_high[...])
            sums = both[:24] + both[24:] + dot(high, t_low[...])
            sums = sums * (air_gain * weight[0:1, :])
            sums = jnp.concatenate([sums, jnp.zeros((104, NK), F32)], axis=0)
            moved = jnp.transpose(sums)
            swapped = jnp.concatenate([moved[128:], moved[:128]], axis=0)
            beside = pltpu.roll(moved, 1, 1) + pltpu.roll(moved, 127, 1)
            shares[...] = stencil[0] * moved + diffusion_rate * beside + stencil[2] * swapped

        ready("spec", "stencil")
        point[...] = jnp.zeros_like(point)
        kcats, kadvs = (kcat_a, kcat_b), (kadv_a, kadv_b)
        first = lane_iota((128, 128)) == 0

        def load(q, slot):
            cut = scal[3 + q]
            for o, other in ((0, 128), (128, 0)):
                here = src[q + 1, pl.ds(o, 128), :]
                swapped = src[q + 1, pl.ds(other, 128), :]
                around = src[q, pl.ds(o, 128), :] + src[q + 2, pl.ds(o, 128), :]
                x = (
                    stencil[0, pl.ds(o, 128), :] * here
                    + diffusion_rate * around
                    + stencil[1, pl.ds(o, 128), :] * swapped
                )
                if step > 1:
                    more = pltpu.roll(shares[pl.ds(o, 128), :], lax.rem(128 - q, 128), 1)
                    x += jnp.where(first, more, 0.0)
                x = jnp.where(lax.broadcasted_iota(jnp.int32, x.shape, 0) <= cut, x, 0.0)
                high, low = two_parts(x)
                kadvs[slot][pl.ds(o, 128), :] = x
                kcats[slot][pl.ds(o, 128), 0:128] = high
                kcats[slot][pl.ds(o, 128), 128:256] = low

        def finish(q, slot, between):
            mixed = dot(kcats[slot][...], vcat[...])
            between()
            y = kadvs[slot][...] + mixed[:, :128] + mixed[:, 128:]
            dst[q + 1] = y
            point[...] += pltpu.roll(jnp.where(lane_iota(y.shape) == 0, y, 0.0), q, 1)

        two_at_a_time(0, (count_rows + 1) // 2, load, finish)

        ready("t_high", "t_low", "sea_ring", "coef_ring", "coef", "sea", "flux", "hist")
        at_rows = jnp.transpose(point[...])[:NPOLE]
        high, low = two_parts(at_rows)
        both = dot_nt(jnp.concatenate([high, low], axis=0), t_high[...])
        surface = both[:NPOLE] + both[NPOLE:] + dot_nt(high, t_low[...])
        ring[0:NPOLE, :] = coef_ring[...] * (sea_ring[0:NPOLE, :] - surface)

        here = pltpu.roll(own_dot(point[...]), ROW0, 1)
        in_cap = (lanes >= ROW0) & (lanes < ROW0 + NPOLE)
        total = jnp.where(in_cap, coef[...] * (sea[...] - here), flux[...])
        flux[...] = total
        if step < STEPS:
            edge = pltpu.roll(total, 128 - (ROW0 + NPOLE - 1), 1)
            prev[...] = own_dot(dst[NPOLE]) + air_gain * jnp.where(lanes == 0, edge, 0.0)
        new = sea_next(width, polar, rows, sea[...], total, pad)
        sea[...] = jnp.where(lanes >= ROW0 + NPOLE + step - 1, sea_hist[slot], new)

    copies = {}
    order = []

    def fetch(name, source, target):
        copy = pltpu.make_async_copy(source, target, load_sems.at[len(order)])
        order.append(copy)
        copies.setdefault(name, []).append(copy)
        copy.start()

    def ready(*wanted):
        for name in wanted:
            for copy in copies.pop(name, ()):
                copy.wait()

    @pl.when(polar == 1)
    def _():
        if steps[0] == 1:
            half, part = blocks // 2, NK // blocks
            y, z = lax.rem(block, 2), block // 2
            for n, ref in enumerate(spec_in):
                at = jnp.bitwise_xor(z, n % half) + half * (y if n < half else 1 - y)
                at = pl.ds(pl.multiple_of(at * part, part), part)
                fetch("spec", ref, spec_a.at[pl.ds(1, CAP), at])
        else:
            fetch("spec", spec_in[0], spec_a.at[pl.ds(1, CAP)])
        fetch("stencil", loads["stencil"], stencil)
        if steps[0] > 1:
            fetch("gathered", loads["gathered"], gathered)
            fetch("sea_ring", loads["sea_ring"], sea_ring)
            fetch("ring_flux", loads["ring_flux"], ring.at[pl.ds(0, NPOLE)])
        fetch("t_high", loads["t_high"], t_high)
        fetch("t_low", loads["t_low"], t_low)
        if steps[0] == 1:
            fetch("sea_ring", loads["sea_ring"], sea_ring)
            fetch("gathered", loads["gathered"], gathered)
        fetch("coef_ring", loads["coef_ring"], coef_ring)
        fetch("coef", loads["coef"], coef)
        fetch("sea", loads["sea"], sea)
        fetch("flux", loads["flux"] if steps[0] > 1 else hist(3, 1), flux)
        for n, step in enumerate(steps):
            fetch("hist", hist(2, step), sea_hist.at[n])
        for n, step in enumerate(wedge_steps):
            fetch("hist", hist(3, step), flux_hist.at[n])
            fetch("hist", hist(1, step - 1), side.at[n])
            row = pl.ds(8 + (step - 2) * width, width)
            fetch("hist", hist(0, step - 1), cur.at[row])
        kept = steps[0] - 1
        for j in range(kept):
            fetch("hist", loads["wedge"].at[j], cur.at[pl.ds(8 + j * width, width)])
        for ref in (spec_a, spec_b):
            ref[0] = jnp.zeros((NK, 128), F32)
            for beyond in range(CAP + 1, CAP + 4):
                ref[beyond] = jnp.zeros((NK, 128), F32)
        cur[0:8, :] = jnp.zeros((8, 128), F32)
        pad[...] = jnp.zeros_like(pad)

        src, dst = spec_a, spec_b
        for n, step in enumerate(steps):
            cap_step(step, src, dst, n)
            src, dst = dst, src
            if step < STEPS:
                pending = wedge_step(step + 1)
                flux[...] = pending
                if not last:
                    gather_out[pl.ds(8 * n, 8), :] = jnp.transpose(pending)[
                        NPOLE + ROW0 : NPOLE + ROW0 + 8
                    ]
        ready(*list(copies))
        if last:
            start, extent = (HALO, count) if fast else (0, width)

            def send(ref, offset, q):
                r = jnp.where(flip == 1, rows - 1 - q, q)
                return pltpu.make_async_copy(
                    ref.at[pl.ds(offset + start, extent)], air_out.at[r], sems.at[q]
                )

            for j in range(WEDGE):
                send(cur, 8 + j * width, NPOLE + j).start()

            @pl.loop(0, NPOLE)
            def _(q):
                y = own_dot(src[q + 1])
                edge = pltpu.roll(flux[...], lax.rem(128 - ROW0 - q, 128), 1)
                back[q] = y + air_gain * jnp.where(lanes == 0, edge, 0.0)
                send(back.at[q], 0, q).start()

            @pl.loop(0, NPOLE)
            def _(q):
                send(back.at[q], 0, q).wait()

            for j in range(WEDGE):
                send(cur, 8 + j * width, NPOLE + j).wait()
        else:
            stores = [pltpu.make_async_copy(src.at[pl.ds(1, CAP)], spec_out, load_sems.at[0])]
            for j in range(len(wedge_steps) + kept):
                stores.append(
                    pltpu.make_async_copy(
                        cur.at[pl.ds(8 + j * width, width)], wedge_out.at[j], load_sems.at[1 + j]
                    )
                )
            for copy in stores:
                copy.start()
            sea_out[...] = sea[...]
            flux_out[...] = flux[...]
            sea_ring_out[...] = sea_ring[...]
            ring_out[...] = ring[0:NPOLE, :]
            for copy in stores:
                copy.wait()

    if last:
        @pl.when(polar == 0)
        def _():
            copy = pltpu.make_async_copy(hist(2, STEPS), sea, load_sems.at[0])
            copy.start()
            copy.wait()

        turn[...] = jnp.transpose(sea[...])

        @pl.loop(0, rows)
        def _(q):
            r = jnp.where(flip == 1, rows - 1 - q, q)
            sea_out[pl.ds(r, 1), :] = turn[pl.ds(q + ROW0, 1), :]


def cap_hists(steps):
    return [0] if steps[-1] < 3 else [0, 1] if steps[0] < 5 else [1]


def cap_steps(rows, count, width, blocks, fast, steps, scal, spec, big, small, air):
    levels = 128
    ring_width = blocks * width
    last = steps[-1] == STEPS
    any_spec = pl.BlockSpec(memory_space=pl.ANY)
    vmem = pl.BlockSpec(memory_space=pltpu.VMEM)
    shape = jax.ShapeDtypeStruct
    square = pltpu.VMEM((width, 128), F32)
    aliases = {}
    extra = []
    if last:
        out_shape = [
            shape((rows, count if fast else width, levels), F32),
            shape((rows, width), F32),
        ]
        out_specs = [any_spec, vmem]
        extra = [pltpu.VMEM((NPOLE, width, levels), F32), pltpu.SemaphoreType.DMA((NPOLE + WEDGE,))]
        aliases = {1 + len(spec) + len(big) + len(small): 0}
    else:
        out_shape = [
            shape((CAP, NK, levels), F32),
            shape((steps[-1], width, levels), F32),
            shape((width, 128), F32),
            shape((width, 128), F32),
            shape((24, ring_width), F32),
            shape((NPOLE, ring_width), F32),
            shape((16, width), F32),
        ]
        out_specs = [any_spec] * 2 + [vmem] * 5
    return pl.pallas_call(
        functools.partial(cap_kernel, rows, count, width, blocks, fast, steps, len(spec)),
        out_shape=out_shape,
        in_specs=[pl.BlockSpec(memory_space=pltpu.SMEM)]
        + [any_spec] * (len(spec) + len(big))
        + [vmem] * len(small)
        + [any_spec] * len(air),
        out_specs=out_specs,
        scratch_shapes=[
            pltpu.VMEM((CAP + 4, NK, levels), F32),
            pltpu.VMEM((CAP + 4, NK, levels), F32),
            pltpu.VMEM((WEDGE * width + 16, levels), F32),
            square,
            square,
            pltpu.VMEM((width, 2 * levels), BF16),
            pltpu.VMEM((NK, 2 * levels), BF16),
            pltpu.VMEM((NK, 2 * levels), BF16),
            pltpu.VMEM((NK, 128), F32),
            pltpu.VMEM((NK, 128), F32),
            pltpu.VMEM((NK, 128), F32),
            square,
            square,
            pltpu.VMEM((width + 16, 128), F32),
            pltpu.VMEM((24, ring_width), F32),
            pltpu.VMEM((24, ring_width), F32),
            pltpu.VMEM((NK, 128), F32),
            pltpu.VMEM((ring_width, NK), BF16),
            pltpu.VMEM((ring_width, NK), BF16),
            pltpu.VMEM((3, NK, levels), F32),
            square,
            pltpu.VMEM((NPOLE, ring_width), F32),
            pltpu.VMEM((blocks, 16, width), F32),
            pltpu.VMEM((2, width, 128), F32),
            pltpu.VMEM((2, width, 128), F32),
            pltpu.VMEM((2, width, 128), F32),
            pltpu.VMEM((128, width), F32),
            pltpu.SemaphoreType.DMA((blocks + 32,)),
        ]
        + extra,
        input_output_aliases=aliases,
        compiler_params=pltpu.CompilerParams(vmem_limit_bytes=VMEM_LIMIT),
        cost_estimate=pl.CostEstimate(
            flops=len(steps) * CAP * NK * levels * levels * 4,
            bytes_accessed=20_000_000,
            transcendentals=0,
        ),
        name="cap_steps",
    )(scal, *spec, *big, *small, *air)


def shift(x, axis, by, wrap):
    size = lax.axis_size(axis)
    pairs = [(i, (i + by) % size) for i in range(size) if wrap or 0 <= i + by < size]
    return lax.ppermute(x, axis, pairs)


def between_caps(x, by):
    size, bands = lax.axis_size("lon"), lax.axis_size("lat")
    pairs = [(b * size + i, b * size + (i ^ by)) for b in (0, bands - 1) for i in range(size)]
    return lax.ppermute(x, ("lat", "lon"), pairs)


def to_all(x, blocks):
    copies = jnp.broadcast_to(x[None], (blocks,) + x.shape)
    return lax.all_to_all(copies, "lon", split_axis=0, concat_axis=0, tiled=True)


def local(air_temp, sea_temp, land_sea, courant, vertical_mix, cutoffs):
    rows, count, levels = air_temp.shape
    blocks, bands = lax.axis_size("lon"), lax.axis_size("lat")
    nlon = blocks * count
    width = round_up(count + 2 * HALO, 128)
    depth = round_up(count, 128)
    fast = count % 8 == 0
    band, block = lax.axis_index("lat"), lax.axis_index("lon")
    flip = band == bands - 1
    polar = (band == 0) | flip

    cut = jnp.where(flip, cutoffs[::-1][:NPOLE], cutoffs[:NPOLE])
    head = jnp.stack([flip, polar, block]).astype(jnp.int32)
    scal = jnp.concatenate([head, cut, jnp.full((STEPS + 4,), KMAX, jnp.int32)])
    window, forward, weight = tables(blocks, count, width, depth)
    t_high, t_low = (jnp.asarray(part) for part in window)
    own_table = lax.dynamic_index_in_dim(jnp.asarray(forward), block, 0, keepdims=False)
    theta = np.arange(KMAX + 1) * (2.0 * math.pi / nlon)
    cosine = np.tile(np.cos(theta), 2).astype(np.float32)
    sine = np.concatenate([-np.sin(theta), np.sin(theta)]).astype(np.float32)
    stay = 1.0 - 4.0 * diffusion_rate + 2.0 * diffusion_rate * jnp.asarray(cosine)
    stencil = jnp.stack(
        [
            jnp.broadcast_to(stay[:, None], (NK, levels)),
            jnp.asarray(sine)[:, None] * courant[None, :],
            jnp.asarray(sine)[:, None] * jnp.broadcast_to(courant[:1], (levels,))[None, :],
        ]
    )
    weights = jnp.broadcast_to(jnp.asarray(weight.astype(np.float32))[None], (8, NK))
    cour = jnp.stack([diffusion_rate - 0.5 * courant, diffusion_rate + 0.5 * courant])
    surface = jnp.broadcast_to(cour[:, :1], cour.shape)
    cour = jnp.concatenate([cour, surface, jnp.zeros((4, levels), F32)], 0)
    v_round = lax.reduce_precision(vertical_mix, 8, 7)
    v_high, v_low = v_round.astype(BF16), (vertical_mix - v_round).astype(BF16)
    vcat = jnp.concatenate(
        [
            jnp.concatenate([v_high, v_low], 1),
            jnp.concatenate([v_high, jnp.zeros_like(v_low)], 1),
        ],
        0,
    )

    west = shift(air_temp[:, count - HALO :], "lon", 1, True)
    east = shift(air_temp[:, :HALO], "lon", -1, True)

    half = blocks // 2
    keep, send = start_spectra(blocks, scal, air_temp, own_table)
    send, sea_temp, land_sea, west, east = lax.optimization_barrier(
        (send, sea_temp, land_sea, west, east)
    )
    half_sum = keep + between_caps(send, 1)

    exchange_coef = jnp.where(land_sea == 1, sea_coef, land_coef).astype(F32)
    sea_blocks = sea_temp.reshape(-1, blocks, count).transpose(1, 0, 2).reshape(rows, count)
    got = to_all(jnp.concatenate([sea_blocks, exchange_coef], 0), blocks)
    own_window, sea_ring, coef_ring = windows(
        rows, count, width, blocks, scal, got.reshape(blocks, 2 * rows, count)
    )
    above = shift(own_window[:, rows - ROW0 :], "lat", 1, False)
    below = shift(own_window[:, :ROW0], "lat", -1, False)

    def edge(part):
        return jnp.concatenate([west[part], air_temp[part], east[part]], 1)

    north = shift(edge(slice(rows - ROW0, rows)), "lat", 1, False)
    south = shift(edge(slice(0, ROW0)), "lat", -1, False)

    if fast:
        air = air_temp
    else:
        middle = jnp.concatenate([west, air_temp, east], 1)
        air = jnp.concatenate([north, middle, south], 0)
        air = jnp.pad(air, ((0, 0), (0, width - count - 2 * HALO), (0, 0)))
    half_sum, own_window = lax.optimization_barrier((half_sum, own_window))
    parts = [between_caps(half_sum[j], 2 * j) for j in range(1, half)]
    outs = outside_steps(
        rows, count, width, fast, (1, 2, 3), scal, (air, west, east, north, south),
        (own_window, above, below, cour, vcat),
    )
    state, early, sea, coef, gathered = outs[0], tuple(outs[1:5]), outs[5], outs[6], outs[7]
    own = functools.reduce(jnp.add, parts, half_sum[0])
    own, state = lax.optimization_barrier((own, state))
    near = [own] + [between_caps(own, 2 * j) for j in range(1, half)]
    gathered = to_all(gathered, blocks).reshape(blocks, 16, width)
    near, gathered = lax.optimization_barrier((near, gathered))
    outs = outside_steps(
        rows, count, width, fast, (4, 5, 6), scal, (state,),
        (early[2], early[3], coef, cour, vcat),
    )
    air, late = outs[0], tuple(outs[1:5])
    far = between_caps(jnp.stack(near), 1)
    spec = tuple(near) + tuple(far[j] for j in range(half))
    spec, air, late = lax.optimization_barrier((spec, air, late))

    more = ()
    for steps in ((1, 2), (3, 4), (5, 6)):
        hists = sum(((early, late)[h] for h in cap_hists(steps)), ())
        big = hists + (t_high, t_low, stencil, coef, sea, sea_ring, coef_ring, gathered) + more
        outs = cap_steps(
            rows, count, width, blocks, fast, steps, scal, spec, big,
            (weights, cour, vcat), (air,) if steps[-1] == STEPS else (),
        )
        if steps[-1] < STEPS:
            spec, wedge, sea, flux, sea_ring, ring_flux, mine = outs
            spec, more = (spec,), (flux, ring_flux, wedge)
            gathered = to_all(mine, blocks).reshape(blocks, 16, width)
    air, sea = outs
    if not fast:
        air = air[:, HALO : HALO + count]
    sea = sea[:, HALO : HALO + count]
    sea = lax.all_to_all(sea, "lon", split_axis=0, concat_axis=1, tiled=True)
    return air, sea


def solution(mesh):
    placed = (P("lat", "lon", None), P(("lat", "lon"), None), P("lat", "lon"), P(), P(), P())
    return jax.shard_map(
        local,
        mesh=mesh,
        in_specs=placed,
        out_specs=(P("lat", "lon", None), P(("lat", "lon"), None)),
        check_vma=False,
    )
```

time: 354 us -> 238 us (0.67)
  blocking collectives: 127 us -> 49.4 us
  Pallas kernels: 138 us -> 105 us
  starting transfers between devices: 13.2 us -> 44 us
  waiting for transfers between devices: 32.2 us -> 12.4 us
  between operations: 14.4 us -> 1.19 us
    all_gather x3 -> x0, blocking collectives: 95.5 us -> none  [the longest x1 33 us: local(): gathered = lax.all_gather(gathered, 'lon', axis=0, tiled=False)]
    psum x1 -> x0, waiting for transfers between devices: 32.1 us -> none  [local(): spec = lax.psum(spec, 'lon')]
    ppermute x0 -> x8, starting transfers between devices: none -> 25.2 us  [between_caps(): return lax.ppermute(x, ('lat', 'lon'), pairs)]
    pallas_call x3, Pallas kernels: 81.5 us -> 58.3 us  [cap_steps(): pl.pallas_call(functools.partial(cap_kernel, rows, count, width, blocks,...]
    all_to_all x2 -> x3, blocking collectives: 22.2 us -> 40.2 us  [to_all(): lax.all_to_all(copies, 'lon', split_axis=0, concat_axis=0, tiled=True)]
    all_to_all x0 -> x1, waiting for transfers between devices: none -> 11.3 us  [to_all(): lax.all_to_all(copies, 'lon', split_axis=0, concat_axis=0, tiled=True)]
    pallas_call x1 -> x2, Pallas kernels: 16.1 us -> 9.07 us  [the longest x1 7.2 us: start_spectra(): pl.pallas_call(functools.partial(spectra_kernel, count, blocks), out_shap...]
    all_to_all x0 -> x1, starting transfers between devices: none -> 4.64 us  [to_all(): lax.all_to_all(copies, 'lon', split_axis=0, concat_axis=0, tiled=True)]
  transfers between devices with their start and end apart: 7 -> 15, of which waited for: 1 -> 2; matrix products, arithmetic and copies ran while one was open for 6% -> 6% of each run, Pallas kernels for 16% -> 20%
where the time goes in v2:
time: 238 us; the launch traced here: 237 us
  Pallas kernels  105 us (44%)
  blocking collectives  49.4 us (21%)
  starting transfers between devices  44 us (18%)
  local copies, waits for them, and re-layouts  16.6 us (7%)
  waiting for transfers between devices  12.4 us (5%)
  other arithmetic  7.91 us (3%)
    pallas_call x3, Pallas kernels, cap_steps(): pl.pallas_call(functools.partial(cap_kernel, rows, count, width, blocks,...  58.3 us
    all_to_all x3, blocking collectives, to_all(): lax.all_to_all(copies, 'lon', split_axis=0, concat_axis=0, tiled=True)  40.2 us
    pallas_call x2, Pallas kernels, outside_steps(): pl.pallas_call(functools.partial(outside_kernel, rows, count, width, fast...  37.9 us
    ppermute x8, starting transfers between devices, between_caps(): return lax.ppermute(x, ('lat', 'lon'), pairs)  25.2 us
    ppermute x6, starting transfers between devices, shift(): return lax.ppermute(x, axis, pairs)  14.2 us
    all_to_all x1, waiting for transfers between devices, to_all(): lax.all_to_all(copies, 'lon', split_axis=0, concat_axis=0, tiled=True)  11.3 us
    all_to_all x1, blocking collectives, local(): sea = lax.all_to_all(sea, 'lon', split_axis=0, concat_axis=1, tiled=True)  9.2 us
    pallas_call x1, Pallas kernels, start_spectra(): pl.pallas_call(functools.partial(spectra_kernel, count, blocks), out_shap...  7.2 us
  transfers between devices with their start and end apart: 15, of which 2 were waited for; matrix products, arithmetic and copies ran while one was open for 6% of the time, Pallas kernels for 20%

profile of v2, /device:TPU:0, one launch (start us, length us, event | category | flops | bytes accessed | tf_op | source)
XLA Modules:
  0.0 236.8 jit_solution(9745444956602663749)
XLA Ops:
  0.6 1.0 fusion.6
  1.6 3.0 %collective-permute-start = (f32[32,8,128]{2,1,0:T(8,128)S(1)}, f32[32,8,128]{2,1,0:T(8,128)S(1)}, u32[]{:S(2)}, u32[]{:S(2)}) collective-permute-start(f32[32,8,128]{2,1,0:T(8,128)S(1)} %get-tuple-element.127), channel_id=1, source_target_pairs={{0,1},{1,2},{2,3},{3,4},{4,5},{5,6},{6,7},{7,0},{8,9},{9,10},{10,1... | collective-permute-start | bytes 393224 | tf_op jit(solution)/shard_map/ppermute | solution.py:810
  4.6 3.1 %collective-permute-start.1 = (f32[32,8,128]{2,1,0:T(8,128)S(1)}, f32[32,8,128]{2,1,0:T(8,128)S(1)}, u32[]{:S(2)}, u32[]{:S(2)}) collective-permute-start(f32[32,8,128]{2,1,0:T(8,128)S(1)} %get-tuple-element.126), channel_id=1, source_target_pairs={{0,7},{1,0},{2,1},{3,2},{4,3},{5,4},{6,5},{7,6},{8,15},{9,8},{10,9... | collective-permute-start | bytes 393224 | tf_op jit(solution)/shard_map/ppermute | solution.py:810
  7.7 2.7 %fusion.5 = (f32[6,360,128]{2,1,0:T(8,128)}, f32[6,360,128]{2,1,0:T(8,128)S(1)}) fusion(f32[32,360,128]{2,1,0:T(8,128)} %refs_0_.1), kind=kLoop, calls=%fused_computation.32 | loop fusion | bytes 4423680 | tf_op jit(solution)/shard_map/slice | solution.py:886
  10.5 0.1 slice.74
  10.5 0.1 slice.75
  10.7 0.1 concatenate.25.scal
  10.7 1.1 dynamic-slice_bitcast_fusion.table
  11.9 2.7 %copy-done = f32[32,360,128]{2,1,0:T(8,128)S(1)} copy-done((f32[32,360,128]{2,1,0:T(8,128)S(1)}, f32[32,360,128]{2,1,0:T(8,128)}, u32[]{:S(2)}) %copy-start) | copy-done | bytes 5898264
  14.5 7.2 %start_spectra.1 = (f32[4,22,32,128]{3,2,1,0:T(8,128)S(1)}, f32[4,22,32,128]{3,2,1,0:T(8,128)}) custom-call(s32[29]{0:T(128)S(1)} %concatenate.25.scal, f32[32,360,128]{2,1,0:T(8,128)S(1)} %copy-done, bf16[256,1152]{1,0:T(8,128)(2,1)S(1)} %dynamic-slice_bitcast_fusion.table), custom_call_target="tpu_custom_call" | custom-call | tf_op jit(solution)/shard_map/start_spectra/pallas_call | solution.py:128
  21.8 0.1 reshape.62
  22.0 1.9 collective-permute-start.2
  23.9 1.0 broadcast_in_dim.26
  24.9 4.6 %all-to-all-start = ((f32[8,64,360]{2,1,0:T(8,128)}), f32[8,64,360]{2,1,0:T(8,128)S(1)}, u32[]{:S(2)}, u32[]{:S(2)}) async-start(f32[8,64,360]{2,1,0:T(8,128)} %broadcast_in_dim.26), calls=%async_computation | async-start | bytes 1572864 | tf_op jit(solution)/shard_map/all_to_all | solution.py:821
  29.5 0.8 fusion.7
  30.3 2.3 pad_maximum_fusion.2
  32.6 1.4 collective-permute-start.7
  34.0 1.2 pad_maximum_fusion.1
  35.2 4.0 %collective-permute-start.6 = (f32[6,376,128]{2,1,0:T(8,128)}, f32[6,376,128]{2,1,0:T(8,128)}, u32[]{:S(2)}, u32[]{:S(2)}) collective-permute-start(f32[6,376,128]{2,1,0:T(8,128)} %pad_maximum_fusion.1), channel_id=1, source_target_pairs={{0,8},{8,16},{16,24},{1,9},{9,17},{17,25},{2,10},{10,18},{18,26},{... | collective-permute-start | bytes 3465224 | tf_op jit(solution)/shard_map/ppermute | solution.py:810
  39.3 0.1 slice_reduce_fusion
  39.4 0.1 pad.13.clone
  39.5 0.1 pad.14.clone
  39.6 0.7 maximum_maximum_fusion.refs_8_.refs_4_.refs_21_.refs_17_
  40.2 11.3 %all-to-all-done.got = f32[8,64,360]{2,1,0:T(8,128)S(1)} async-done(((f32[8,64,360]{2,1,0:T(8,128)}), f32[8,64,360]{2,1,0:T(8,128)S(1)}, u32[]{:S(2)}, u32[]{:S(2)}) %all-to-all-start) | async-done | bytes 737312 | tf_op jit(solution)/shard_map/all_to_all | solution.py:821
  51.5 1.9 windows.1
  53.4 1.9 add.28
  55.3 0.1 slice_bitcast_fusion.6
  55.4 1.9 collective-permute-start.3
  57.3 4.4 %collective-permute-start.4 = (f32[22,32,128]{2,1,0:T(8,128)S(1)}, f32[22,32,128]{2,1,0:T(8,128)S(1)}, u32[]{:S(2)}, u32[]{:S(2)}) collective-permute-start(f32[22,32,128]{2,1,0:T(8,128)S(1)} %get-tuple-element.134), channel_id=1, source_target_pairs={{0,4},{1,5},{2,6},{3,7},{4,0},{5,1},{6,2},{7,3},{24,28},{25,29},{2... | collective-permute-start | bytes 1081352 | tf_op jit(solution)/shard_map/ppermute | solution.py:816
  61.7 3.8 %collective-permute-start.5 = (f32[22,32,128]{2,1,0:T(8,128)S(1)}, f32[22,32,128]{2,1,0:T(8,128)S(1)}, u32[]{:S(2)}, u32[]{:S(2)}) collective-permute-start(f32[22,32,128]{2,1,0:T(8,128)S(1)} %get-tuple-element.133), channel_id=1, source_target_pairs={{0,6},{1,7},{2,4},{3,5},{4,2},{5,3},{6,0},{7,1},{24,30},{25,31},{2... | collective-permute-start | bytes 1081352 | tf_op jit(solution)/shard_map/ppermute | solution.py:816
  65.6 1.3 collective-permute-start.8
  66.9 1.3 collective-permute-start.9
  68.2 0.7 fusion.3.refs_9_.refs_5_.refs_22_.refs_18_
  68.8 1.1 collective-permute-done.9.refs_7_
  70.0 0.6 copy-done.21
  70.6 21.2 %outside_steps.2 = (f32[44,384,128]{2,1,0:T(8,128)}, f32[3,384,128]{2,1,0:T(8,128)}, f32[3,384,128]{2,1,0:T(8,128)}, f32[3,384,128]{2,1,0:T(8,128)}, f32[3,384,1...) custom-call(s32[29]{0:T(128)} %copy-done.3, f32[32,360,128]{2,1,0:T(8,128)} %refs_0_.1, ...), custom_call_target="tpu_custom_call" | custom-call | flops 2415919104 | bytes 15728640 | tf_op jit(solution)/shard_map/outside_steps/pallas_call | solution.py:435
  91.8 0.1 fusion.1.refs_0_
  91.9 1.9 collective-permute-start.10
  93.9 4.4 %collective-permute-start.11 = (f32[22,32,128]{2,1,0:T(8,128)S(1)}, f32[22,32,128]{2,1,0:T(8,128)S(1)}, u32[]{:S(2)}, u32[]{:S(2)}) collective-permute-start(f32[22,32,128]{2,1,0:T(8,128)S(1)} %fusion.1.refs_0_), channel_id=1, source_target_pairs={{0,4},{1,5},{2,6},{3,7},{4,0},{5,1},{6,2},{7,3},{24,28},{25,29},{2... | collective-permute-start | bytes 1081352 | tf_op jit(solution)/shard_map/ppermute | solution.py:816
  98.3 3.8 %collective-permute-start.12 = (f32[22,32,128]{2,1,0:T(8,128)S(1)}, f32[22,32,128]{2,1,0:T(8,128)S(1)}, u32[]{:S(2)}, u32[]{:S(2)}) collective-permute-start(f32[22,32,128]{2,1,0:T(8,128)S(1)} %fusion.1.refs_0_), channel_id=1, source_target_pairs={{0,6},{1,7},{2,4},{3,5},{4,2},{5,3},{6,0},{7,1},{24,30},{25,31},{2... | collective-permute-start | bytes 1081352 | tf_op jit(solution)/shard_map/ppermute | solution.py:816
  102.1 18.0 %all_to_all.39.refs_19_ = f32[8,16,384]{2,1,0:T(8,128)} all-to-all(f32[8,16,384]{2,1,0:T(8,128)S(1)} %broadcast_in_dim.30), channel_id=1, replica_groups=mesh['lat'=4,'lon'=8] {'lon'}, dimensions={0} | all-to-all | bytes 393216 | tf_op jit(solution)/shard_map/all_to_all | solution.py:821
  120.1 0.0 copy-start.15
  120.2 0.1 pad_maximum_fusion
  120.3 0.5 copy-done.6
  120.8 0.1 copy-done.7
  120.9 0.2 copy-done.8
  121.1 3.1 %collective-permute-start.13 = (f32[4,22,32,128]{3,2,1,0:T(8,128)S(1)}, f32[4,22,32,128]{3,2,1,0:T(8,128)S(1)}, u32[]{:S(2)}, u32[]{:S(2)}) collective-permute-start(f32[4,22,32,128]{3,2,1,0:T(8,128)S(1)} %pad_maximum_fusion), channel_id=1, source_target_pairs={{0,1},{1,0},{2,3},{3,2},{4,5},{5,4},{6,7},{7,6},{24,25},{25,24},{2... | collective-permute-start | bytes 4325384 | tf_op jit(solution)/shard_map/ppermute | solution.py:816
  124.3 0.1 broadcast_multiply_fusion
  124.4 0.1 stack.59
  124.5 0.1 stack_broadcast_in_dim.2
  124.6 0.8 pad_maximum_fusion.3.refs_14_.refs_11_.refs_7_
  125.4 16.7 %outside_steps.3 = (f32[32,360,128]{2,1,0:T(8,128)}, f32[3,384,128]{2,1,0:T(8,128)}, f32[3,384,128]{2,1,0:T(8,128)}, f32[3,384,128]{2,1,0:T(8,128)}, f32[3,384,128]{2,1,0:T(8,128)}) custom-call(s32[29]{0:T(128)} %copy-done.3, f32[44,384,128]{2,1,0:T(8,128)} %get-tuple-element.80.refs_0_, f32[3,384,128]{2,1,0:T(8,128)} %get-tuple-element.81.refs_1_.refs_10_.refs_3_, ...), custom_call_target="tpu_custom_call" | custom-call | flops 2415919104 | bytes 15728640 | tf_op jit(solution)/shard_map/outside_steps/pallas_call | solution.py:435
  142.1 1.2 slice_bitcast_fusion
  143.3 0.6 broadcast_in_dim.31.refs_20_.refs_16_
  143.9 17.1 %cap_steps.3 = (f32[22,256,128]{2,1,0:T(8,128)}, f32[2,384,128]{2,1,0:T(8,128)}, f32[384,128]{1,0:T(8,128)}, f32[384,128]{1,0:T(8,128)}, f32[24,3072]{1,0:T(8,12...) custom-call(s32[29]{0:T(128)} %copy-done.3, f32[22,32,128]{2,1,0:T(8,128)} %copy-done.5, f32[22,32,128]{2,1,0:T(8,128)} %copy-done.6, ...), custom_call_target="tpu_custom_call" | custom-call | flops 738197504 | bytes 20000000 | tf_op jit(solution)/shard_map/cap_steps/pallas_call | solution.py:757
  161.0 0.8 broadcast_in_dim.32
  161.7 11.4 %all_to_all.40.refs_16_ = f32[8,16,384]{2,1,0:T(8,128)} all-to-all(f32[8,16,384]{2,1,0:T(8,128)S(1)} %broadcast_in_dim.32), channel_id=1, replica_groups=mesh['lat'=4,'lon'=8] {'lon'}, dimensions={0} | all-to-all | bytes 393216 | tf_op jit(solution)/shard_map/all_to_all | solution.py:821
  173.1 18.8 %cap_steps.4 = (f32[22,256,128]{2,1,0:T(8,128)}, f32[4,384,128]{2,1,0:T(8,128)}, f32[384,128]{1,0:T(8,128)}, f32[384,128]{1,0:T(8,128)}, f32[24,3072]{1,0:T(8,12...) custom-call(s32[29]{0:T(128)} %copy-done.3, f32[22,256,128]{2,1,0:T(8,128)} %get-tuple-element.103.refs_0_, ...), custom_call_target="tpu_custom_call" | custom-call | flops 738197504 | bytes 20000000 | tf_op jit(solution)/shard_map/cap_steps/pallas_call | solution.py:757
  192.0 0.8 broadcast_in_dim.62
  192.7 10.9 %all_to_all.41.refs_12_ = f32[8,16,384]{2,1,0:T(8,128)} all-to-all(f32[8,16,384]{2,1,0:T(8,128)S(1)} %broadcast_in_dim.62), channel_id=1, replica_groups=mesh['lat'=4,'lon'=8] {'lon'}, dimensions={0} | all-to-all | bytes 393216 | tf_op jit(solution)/shard_map/all_to_all | solution.py:821
  203.6 22.3 %cap_steps.5 = (f32[32,360,128]{2,1,0:T(8,128)}, f32[32,384]{1,0:T(8,128)}) custom-call(s32[29]{0:T(128)} %copy-done.3, f32[22,256,128]{2,1,0:T(8,128)} %get-tuple-element.114.refs_0_, f32[3,384,128]{2,1,0:T(8,128)} %get-tuple-element.104.refs_5_.refs_1_, f32[3,384,128]{2,1,0:T(8,128)} %get-tuple-element.105.refs_6_.refs_2_, ...), custom_call_target="tpu_custom_call", output_to_operand_aliasing={{0}: (20, {})} | custom-call | flops 738197504 | bytes 20000000 | tf_op jit(solution)/shard_map/cap_steps/pallas_call | solution.py:757
  225.9 0.9 slice.98
  226.8 9.2 %all_to_all.42 = f32[8,4,360]{2,1,0:T(4,128)S(1)} all-to-all(f32[8,4,360]{2,1,0:T(4,128)S(1)} %all_to_all.30), channel_id=1, replica_groups=mesh['lat'=4,'lon'=8] {'lon'}, dimensions={0} | all-to-all | bytes 92160 | tf_op jit(solution)/shard_map/all_to_all | solution.py:934
  236.0 0.7 all_to_all.33
  (66 shorter events, 0.3 us)
Async XLA Ops:
  1.6 20.1 %collective-permute-start = (f32[32,8,128]{2,1,0:T(8,128)S(1)}, f32[32,8,128]{2,1,0:T(8,128)S(1)}, u32[]{:S(2)}, u32[]{:S(2)}) collective-permute-start(f32[32,8,128]{2,1,0:T(8,128)S(1)} %get-tuple-element.127), channel_id=1, source_target_pairs={{0,1},{1,2},{2,3},{3,4},{4,5},{5,6},{6,7},{7,0},{8,9},{9,10},{10,1... | collective-permute-start | bytes 393224 | tf_op jit(solution)/shard_map/ppermute | solution.py:810
  4.6 17.1 %collective-permute-start.1 = (f32[32,8,128]{2,1,0:T(8,128)S(1)}, f32[32,8,128]{2,1,0:T(8,128)S(1)}, u32[]{:S(2)}, u32[]{:S(2)}) collective-permute-start(f32[32,8,128]{2,1,0:T(8,128)S(1)} %get-tuple-element.126), channel_id=1, source_target_pairs={{0,7},{1,0},{2,1},{3,2},{4,3},{5,4},{6,5},{7,6},{8,15},{9,8},{10,9... | collective-permute-start | bytes 393224 | tf_op jit(solution)/shard_map/ppermute | solution.py:810
  7.7 2.7 %copy-start.19 = (s32[32]{0:T(128)S(1)}, s32[32]{0:T(128)}, u32[]{:S(2)}) copy-start(s32[32]{0:T(128)} %param.17) | copy-start | bytes 388
  10.7 40.8 %copy-start.3 = (s32[29]{0:T(128)}, s32[29]{0:T(128)S(1)}, u32[]{:S(2)}) copy-start(s32[29]{0:T(128)S(1)} %concatenate.25.scal) | copy-start | bytes 352
  11.9 2.7 %copy-start = (f32[32,360,128]{2,1,0:T(8,128)S(1)}, f32[32,360,128]{2,1,0:T(8,128)}, u32[]{:S(2)}) copy-start(f32[32,360,128]{2,1,0:T(8,128)} %refs_0_.1) | copy-start | bytes 17694724
  14.5 7.2 %copy-start.11 = (f32[4,2880]{1,0:T(4,128)S(1)}, f32[4,2880]{1,0:T(4,128)}, u32[]{:S(2)}) copy-start(f32[4,2880]{1,0:T(4,128)} %param.13) | copy-start | bytes 138244
  14.5 7.4 %copy-start.10 = (s32[32,360]{1,0:T(8,128)S(1)}, s32[32,360]{1,0:T(8,128)}, u32[]{:S(2)}) copy-start(s32[32,360]{1,0:T(8,128)} %param.14) | copy-start | bytes 138244
  21.7 7.8 %copy-start.13 = (f32[32,8,128]{2,1,0:T(8,128)}, f32[32,8,128]{2,1,0:T(8,128)S(1)}, u32[]{:S(2)}) copy-start(f32[32,8,128]{2,1,0:T(8,128)S(1)} %collective-permute-done.refs_1_) | copy-start | bytes 393220
  21.8 3.1 %copy-start.14 = (f32[32,8,128]{2,1,0:T(8,128)}, f32[32,8,128]{2,1,0:T(8,128)S(1)}, u32[]{:S(2)}) copy-start(f32[32,8,128]{2,1,0:T(8,128)S(1)} %collective-permute-done.1.refs_2_) | copy-start | bytes 393220
  21.9 7.6 %copy-start.16 = (f32[128]{0:T(128)S(1)}, f32[128]{0:T(128)}, u32[]{:S(2)}) copy-start(f32[128]{0:T(128)} %param.15) | copy-start | bytes 1540
  22.0 31.5 %collective-permute-start.2 = (f32[4,22,32,128]{3,2,1,0:T(8,128)}, f32[4,22,32,128]{3,2,1,0:T(8,128)}, u32[]{:S(2)}, u32[]{:S(2)}) collective-permute-start(f32[4,22,32,128]{3,2,1,0:T(8,128)} %get-tuple-element.65), channel_id=1, source_target_pairs={{0,1},{1,0},{2,3},{3,2},{4,5},{5,4},{6,7},{7,6},{24,25},{25,24},{2... | collective-permute-start | bytes 4325384 | tf_op jit(solution)/shard_map/ppermute | solution.py:816
  24.9 26.6 %all-to-all-start = ((f32[8,64,360]{2,1,0:T(8,128)}), f32[8,64,360]{2,1,0:T(8,128)S(1)}, u32[]{:S(2)}, u32[]{:S(2)}) async-start(f32[8,64,360]{2,1,0:T(8,128)} %broadcast_in_dim.26), calls=%async_computation | async-start | bytes 1572864 | tf_op jit(solution)/shard_map/all_to_all | solution.py:821
  32.6 7.6 %copy-start.9 = (f32[128,128]{1,0:T(8,128)S(1)}, f32[128,128]{1,0:T(8,128)}, u32[]{:S(2)}) copy-start(f32[128,128]{1,0:T(8,128)} %param.16) | copy-start | bytes 196612
  32.6 32.9 %collective-permute-start.7 = (f32[6,376,128]{2,1,0:T(8,128)}, f32[6,376,128]{2,1,0:T(8,128)}, u32[]{:S(2)}, u32[]{:S(2)}) collective-permute-start(f32[6,376,128]{2,1,0:T(8,128)} %pad_maximum_fusion.2), channel_id=1, source_target_pairs={{8,0},{16,8},{24,16},{9,1},{17,9},{25,17},{10,2},{18,10},{26,18},{... | collective-permute-start | bytes 3465224 | tf_op jit(solution)/shard_map/ppermute | solution.py:810
  35.2 31.6 %collective-permute-start.6 = (f32[6,376,128]{2,1,0:T(8,128)}, f32[6,376,128]{2,1,0:T(8,128)}, u32[]{:S(2)}, u32[]{:S(2)}) collective-permute-start(f32[6,376,128]{2,1,0:T(8,128)} %pad_maximum_fusion.1), channel_id=1, source_target_pairs={{0,8},{8,16},{16,24},{1,9},{9,17},{17,25},{2,10},{10,18},{18,26},{... | collective-permute-start | bytes 3465224 | tf_op jit(solution)/shard_map/ppermute | solution.py:810
  53.4 1.9 copy-start.1
  53.4 1.9 copy-start.2
  53.4 12.1 %copy-start.4 = (f32[2,32,384]{2,1,0:T(8,128)}, f32[2,32,384]{2,1,0:T(8,128)S(1)}, u32[]{:S(2)}) copy-start(f32[2,32,384]{2,1,0:T(8,128)S(1)} %get-tuple-element.72.refs_5_) | copy-start | bytes 294916
  55.4 36.4 %collective-permute-start.3 = (f32[22,32,128]{2,1,0:T(8,128)S(1)}, f32[22,32,128]{2,1,0:T(8,128)S(1)}, u32[]{:S(2)}, u32[]{:S(2)}) collective-permute-start(f32[22,32,128]{2,1,0:T(8,128)S(1)} %get-tuple-element.132), channel_id=1, source_target_pairs={{0,2},{1,3},{2,0},{3,1},{4,6},{5,7},{6,4},{7,5},{24,26},{25,27},{2... | collective-permute-start | bytes 1081352 | tf_op jit(solution)/shard_map/ppermute | solution.py:816
  57.3 34.5 %collective-permute-start.4 = (f32[22,32,128]{2,1,0:T(8,128)S(1)}, f32[22,32,128]{2,1,0:T(8,128)S(1)}, u32[]{:S(2)}, u32[]{:S(2)}) collective-permute-start(f32[22,32,128]{2,1,0:T(8,128)S(1)} %get-tuple-element.134), channel_id=1, source_target_pairs={{0,4},{1,5},{2,6},{3,7},{4,0},{5,1},{6,2},{7,3},{24,28},{25,29},{2... | collective-permute-start | bytes 1081352 | tf_op jit(solution)/shard_map/ppermute | solution.py:816
  61.7 30.1 %collective-permute-start.5 = (f32[22,32,128]{2,1,0:T(8,128)S(1)}, f32[22,32,128]{2,1,0:T(8,128)S(1)}, u32[]{:S(2)}, u32[]{:S(2)}) collective-permute-start(f32[22,32,128]{2,1,0:T(8,128)S(1)} %get-tuple-element.133), channel_id=1, source_target_pairs={{0,6},{1,7},{2,4},{3,5},{4,2},{5,3},{6,0},{7,1},{24,30},{25,31},{2... | collective-permute-start | bytes 1081352 | tf_op jit(solution)/shard_map/ppermute | solution.py:816
  65.6 3.3 %collective-permute-start.8 = (f32[2,6,384]{2,1,0:T(8,128)S(1)}, f32[2,6,384]{2,1,0:T(8,128)S(1)}, u32[]{:S(2)}, u32[]{:S(2)}) collective-permute-start(f32[2,6,384]{2,1,0:T(8,128)S(1)} %get-tuple-element.140), channel_id=1, source_target_pairs={{0,8},{8,16},{16,24},{1,9},{9,17},{17,25},{2,10},{10,18},{18,26},{... | collective-permute-start | bytes 55304 | tf_op jit(solution)/shard_map/ppermute | solution.py:810
  66.9 3.1 %collective-permute-start.9 = (f32[2,6,384]{2,1,0:T(8,128)S(1)}, f32[2,6,384]{2,1,0:T(8,128)S(1)}, u32[]{:S(2)}, u32[]{:S(2)}) collective-permute-start(f32[2,6,384]{2,1,0:T(8,128)S(1)} %get-tuple-element.139), channel_id=1, source_target_pairs={{8,0},{16,8},{24,16},{9,1},{17,9},{25,17},{10,2},{18,10},{26,18},{... | collective-permute-start | bytes 55304 | tf_op jit(solution)/shard_map/ppermute | solution.py:810
  68.8 1.1 copy-start.20
  70.0 0.6 copy-start.21
  91.8 10.3 %copy-start.12 = (f32[16,384]{1,0:T(8,128)S(1)}, f32[16,384]{1,0:T(8,128)}, u32[]{:S(2)}) copy-start(f32[16,384]{1,0:T(8,128)} %get-tuple-element.75) | copy-start | bytes 73732
  91.9 28.3 %copy-start.5 = (f32[22,32,128]{2,1,0:T(8,128)}, f32[22,32,128]{2,1,0:T(8,128)S(1)}, u32[]{:S(2)}) copy-start(f32[22,32,128]{2,1,0:T(8,128)S(1)} %fusion.1.refs_0_) | copy-start | bytes 1081348
  91.9 28.1 %collective-permute-start.10 = (f32[22,32,128]{2,1,0:T(8,128)S(1)}, f32[22,32,128]{2,1,0:T(8,128)S(1)}, u32[]{:S(2)}, u32[]{:S(2)}) collective-permute-start(f32[22,32,128]{2,1,0:T(8,128)S(1)} %fusion.1.refs_0_), channel_id=1, source_target_pairs={{0,2},{1,3},{2,0},{3,1},{4,6},{5,7},{6,4},{7,5},{24,26},{25,27},{2... | collective-permute-start | bytes 1081352 | tf_op jit(solution)/shard_map/ppermute | solution.py:816
  93.9 26.2 %collective-permute-start.11 = (f32[22,32,128]{2,1,0:T(8,128)S(1)}, f32[22,32,128]{2,1,0:T(8,128)S(1)}, u32[]{:S(2)}, u32[]{:S(2)}) collective-permute-start(f32[22,32,128]{2,1,0:T(8,128)S(1)} %fusion.1.refs_0_), channel_id=1, source_target_pairs={{0,4},{1,5},{2,6},{3,7},{4,0},{5,1},{6,2},{7,3},{24,28},{25,29},{2... | collective-permute-start | bytes 1081352 | tf_op jit(solution)/shard_map/ppermute | solution.py:816
  98.3 21.9 %collective-permute-start.12 = (f32[22,32,128]{2,1,0:T(8,128)S(1)}, f32[22,32,128]{2,1,0:T(8,128)S(1)}, u32[]{:S(2)}, u32[]{:S(2)}) collective-permute-start(f32[22,32,128]{2,1,0:T(8,128)S(1)} %fusion.1.refs_0_), channel_id=1, source_target_pairs={{0,6},{1,7},{2,4},{3,5},{4,2},{5,3},{6,0},{7,1},{24,30},{25,31},{2... | collective-permute-start | bytes 1081352 | tf_op jit(solution)/shard_map/ppermute | solution.py:816
  120.1 0.7 copy-start.6
  120.1 0.8 copy-start.7
  120.1 1.0 copy-start.8
  120.1 4.1 %copy-start.15 = (f32[256]{0:T(256)S(1)}, f32[256]{0:T(256)}, u32[]{:S(2)}) copy-start(f32[256]{0:T(256)} %constant.52.clone) | copy-start | bytes 3076
  120.1 4.3 %copy-start.17 = (f32[256]{0:T(256)S(1)}, f32[256]{0:T(256)}, u32[]{:S(2)}) copy-start(f32[256]{0:T(256)} %constant.58) | copy-start | bytes 3076
  121.1 21.0 %collective-permute-start.13 = (f32[4,22,32,128]{3,2,1,0:T(8,128)S(1)}, f32[4,22,32,128]{3,2,1,0:T(8,128)S(1)}, u32[]{:S(2)}, u32[]{:S(2)}) collective-permute-start(f32[4,22,32,128]{3,2,1,0:T(8,128)S(1)} %pad_maximum_fusion), channel_id=1, source_target_pairs={{0,1},{1,0},{2,3},{3,2},{4,5},{5,4},{6,7},{7,6},{24,25},{25,24},{2... | collective-permute-start | bytes 4325384 | tf_op jit(solution)/shard_map/ppermute | solution.py:816
  142.1 1.2 copy-start.18

commit v3 on v2

--- a/solution.py
+++ b/solution.py
@@ -60,6 +60,11 @@
     return high, low
 
 
+def owner_order(blocks):
+    k = np.arange(KMAX + 1).reshape(blocks, -1)
+    return np.concatenate([k, k + KMAX + 1], 1).reshape(-1)
+
+
 @functools.lru_cache(maxsize=None)
 def tables(blocks, count, width, depth):
     nlon = blocks * count
@@ -76,9 +81,32 @@
     forward = np.zeros((blocks, NK, depth))
     for j in range(blocks):
         own = table(j * count + np.arange(count)) * np.tile(weight, 2)
-        forward[j, :, :count] = own.T
+        forward[j, :, :count] = own.T[owner_order(blocks)]
     high, low = numpy_parts(forward)
     return numpy_parts(window), np.concatenate([high, high, low], 2), np.tile(weight, 2)
+
+
+@functools.lru_cache(maxsize=None)
+def rotations(nlon):
+    theta = np.arange(KMAX + 1) * (2.0 * math.pi / nlon)
+    stay = 1.0 - 4.0 * diffusion_rate + 2.0 * diffusion_rate * np.tile(np.cos(theta), 2)
+    turn = np.concatenate([-np.sin(theta), np.sin(theta)])
+    both = np.stack([stay, turn]).astype(np.float32)
+    return np.ascontiguousarray(np.broadcast_to(both[:, :, None], (2, NK, 128)))
+
+
+def mixing(mix, vcat):
+    high, low = two_parts(mix[...])
+    vcat[0:128, 0:128] = high
+    vcat[128:256, 0:128] = high
+    vcat[0:128, 128:256] = low
+    vcat[128:256, 128:256] = jnp.zeros_like(low)
+
+
+def winds(courant):
+    c = courant[0:1, :]
+    top = jnp.broadcast_to(c[:, 0:1], c.shape)
+    return [diffusion_rate + sign * 0.5 * x for x in (c, top) for sign in (-1.0, 1.0)]
 
 
 def lane_iota(shape):
@@ -103,7 +131,7 @@
             stacked[0:count, lanes] = high
             stacked[depth : depth + count, lanes] = low
             stacked[2 * depth : 2 * depth + count, lanes] = high
-        sums[...] = dot(table[...], stacked[...])
+        sums[...] = dot(table[0], stacked[...])
         for n in range(2):
             to = jnp.where(flip == 1, 1 - n, n)
             lanes = slice(128 * n, 128 * n + 128)
@@ -118,7 +146,7 @@
 def start_spectra(blocks, scal, air_temp, table):
     rows, count, levels = air_temp.shape
     half, part = blocks // 2, NK // blocks
-    depth = table.shape[1] // 3
+    depth = table.shape[2] // 3
 
     def place(p, scal):
         return (jnp.where(scal[0] == 1, rows // 2 - 1 - p, p), 0, 0)
@@ -133,7 +161,7 @@
             grid=(CAP // 2,),
             in_specs=[
                 pl.BlockSpec((2, count, levels), place),
-                pl.BlockSpec((NK, 3 * depth), lambda p, scal: (0, 0)),
+                pl.BlockSpec((1, NK, 3 * depth), lambda p, scal: (scal[2], 0, 0)),
             ],
             out_specs=[out_spec, out_spec],
             scratch_shapes=[
@@ -141,15 +169,85 @@
                 pltpu.VMEM((NK, 2 * levels), F32),
             ],
         ),
-        compiler_params=pltpu.CompilerParams(vmem_limit_bytes=VMEM_LIMIT // 2),
+        compiler_params=pltpu.CompilerParams(vmem_limit_bytes=VMEM_LIMIT),
         name="start_spectra",
     )(scal, air_temp, table)
+
+
+def free_kernel(blocks, parts, scal, *refs):
+    sums, refs = refs[:parts], refs[parts:]
+    rotate, courant, mix, edge, early, late, state, mask, adv, xcat, vcat = refs
+    part = NK // blocks
+    some = part // 2
+    owner = lax.rem(scal[2], 2) * (blocks // 2) + scal[2] // 2
+
+    @pl.when(scal[1] == 1)
+    def _():
+        mixing(mix, vcat)
+        state[0] = jnp.zeros((part, 128), F32)
+        state[1 : CAP + 1] = functools.reduce(jnp.add, [ref[...] for ref in sums])
+        at = pl.ds(pl.multiple_of(owner * part, part), part)
+        stay, turn = rotate[0, at, :], rotate[1, at, :] * courant[0:1, :]
+        wavenum = lax.broadcasted_iota(jnp.int32, (part, 128), 0) % some + owner * some
+        for q in range(CAP):
+            mask[q] = jnp.where(wavenum <= scal[3 + q], 1.0, 0.0)
+        first = lane_iota((part, 128)) == 0
+        top = jnp.zeros((part, 128), F32)
+        for step in range(1, STEPS + 1):
+            size = CAP - step
+            here = state[1 : size + 1]
+            swapped = jnp.concatenate([here[:, some:], here[:, :some]], axis=1)
+            x = stay * here + diffusion_rate * (state[0:size] + state[2 : size + 2])
+            x = (x + turn * swapped) * mask[0:size]
+            x = x.reshape(size * part, 128)
+            high, low = two_parts(x)
+            adv[0 : size * part, :] = x
+            xcat[0 : size * part, 0:128] = high
+            xcat[0 : size * part, 128:256] = low
+            mixed = dot(xcat[0 : size * part, :], vcat[...])
+            y = adv[0 : size * part, :] + mixed[:, :128] + mixed[:, 128:]
+            state[1 : size + 1] = y.reshape(size, part, 128)
+            for q in range(NPOLE):
+                lane = NPOLE * (step - 1) + q
+                top += pltpu.roll(jnp.where(first, state[q + 1], 0.0), lane, 1)
+            if step < STEPS:
+                for to in range(blocks):
+                    early[to, part * step : part * (step + 1), :] = state[NPOLE]
+            else:
+                late[...] = state[1 : NPOLE + 1]
+        for to in range(blocks):
+            early[to, 0:part, :] = top
+            early[to, STEPS * part :, :] = edge[...]
+
+
+def free_steps(blocks, scal, sums, rotate, courant, mix, edge):
+    part = NK // blocks
+    vmem = pl.BlockSpec(memory_space=pltpu.VMEM)
+    shape = jax.ShapeDtypeStruct
+    return pl.pallas_call(
+        functools.partial(free_kernel, blocks, len(sums)),
+        out_shape=[
+            shape((blocks, STEPS * part + edge.shape[0], 128), F32),
+            shape((NPOLE, part, 128), F32),
+        ],
+        in_specs=[pl.BlockSpec(memory_space=pltpu.SMEM)] + [vmem] * (len(sums) + 4),
+        out_specs=[vmem] * 2,
+        scratch_shapes=[
+            pltpu.VMEM((CAP + 2, part, 128), F32),
+            pltpu.VMEM((CAP, part, 128), F32),
+            pltpu.VMEM((CAP * part, 128), F32),
+            pltpu.VMEM((CAP * part, 256), BF16),
+            pltpu.VMEM((256, 256), BF16),
+        ],
+        compiler_params=pltpu.CompilerParams(vmem_limit_bytes=VMEM_LIMIT),
+        name="free_steps",
+    )(scal, *sums, rotate, courant, mix, edge)
 
 
 def advance(
     width, here_ref, base, north_ref, north, south_ref, south, cour, adv, xcat, more=None
 ):
-    c_east, c_west = cour[0:1, :], cour[1:2, :]
+    c_east, c_west = cour
     for o in range(0, width, 128):
         around = north_ref[pl.ds(north + o, 128), :] + south_ref[pl.ds(south + o, 128), :]
         x = (
@@ -167,11 +265,13 @@
         xcat[pl.ds(o, 128), 128:256] = low
 
 
-def two_at_a_time(first, pairs, load, finish):
+def two_at_a_time(first, pairs, load, finish, arrive=None):
     load(first, 0)
 
     @pl.loop(0, pairs)
     def _(n):
+        if arrive is not None:
+            arrive(n)
         q = first + 2 * n
         finish(q, 0, lambda: load(q + 1, 1))
         finish(q + 1, 1, lambda: load(q + 2, 0))
@@ -244,13 +344,13 @@
 def outside_kernel(rows, count, width, fast, steps, scal, *refs):
     first, last = steps[0] == 1, steps[-1] == STEPS
     if first:
-        (air, west, east, north, south, own, above, below, cour, vcat), refs = refs[:10], refs[10:]
+        (air, west, east, north, south, own, above, below, courant, mix), refs = refs[:10], refs[10:]
         (state, wedge, side, sea_hist, flux_hist, sea_start, coef, gather_out), refs = (
             refs[:8], refs[8:])
     else:
-        (state, sea_hist_in, flux_hist_in, coef, cour, vcat), refs = refs[:6], refs[6:]
+        (state, sea_hist_in, flux_hist_in, coef, courant, mix), refs = refs[:6], refs[6:]
         (air_out, wedge, side, sea_hist, flux_hist), refs = refs[:5], refs[5:]
-    (buf_a, buf_b, adv_a, adv_b, xcat_a, xcat_b, sea, flux, point, more, turn, pad, sems) = refs
+    (buf_a, buf_b, adv_a, adv_b, xcat_a, xcat_b, sea, flux, point, more, turn, pad, vcat, sems) = refs
     flip, polar = scal[0], scal[1]
     total = rows + 2 * ROW0
     inner = count + 2 * HALO
@@ -280,6 +380,7 @@
                 pltpu.make_async_copy(whole, whole, sem).wait()
 
     def begin():
+        mixing(mix, vcat)
         beyond = 8 + total * width
         for ref in (buf_a, buf_b):
             ref[0:8, :] = jnp.zeros((8, 128), F32)
@@ -348,6 +449,7 @@
         return y + jnp.where(lanes == 0, gain, 0.0)
 
     advs, xcats = (adv_a, adv_b), (xcat_a, xcat_b)
+    cour = winds(courant)
     src, dst = buf_a, buf_b
     for n, step in enumerate(steps):
         lo = low_row(step)
@@ -359,14 +461,14 @@
             more[...] = (
                 (1.0 - 4.0 * diffusion_rate) * gain
                 + diffusion_rate * (pltpu.roll(gain, 1, 1) + pltpu.roll(gain, 127, 1))
-                + cour[2:3, :] * pad[pl.ds(9, width), :]
-                + cour[3:4, :] * pad[pl.ds(7, width), :]
+                + cour[2] * pad[pl.ds(9, width), :]
+                + cour[3] * pad[pl.ds(7, width), :]
             )
         point[...] = jnp.zeros_like(point)
 
         def load(q, slot, src=src, step=step):
             base = base_of(q)
-            advance(width, src, base, src, base - width, src, base + width, cour,
+            advance(width, src, base, src, base - width, src, base + width, cour[:2],
                     advs[slot], xcats[slot], (more, 128 - (q + ROW0)) if step > 1 else None)
 
         def finish(q, slot, between, dst=dst):
@@ -399,7 +501,8 @@
             steps[-1], src, width, sems.at[1],
         )
         turned = jnp.transpose(flux_hist[0])[NPOLE + ROW0 : NPOLE + ROW0 + 8]
-        gather_out[...] = jnp.concatenate([jnp.zeros_like(turned), turned], axis=0)
+        for o in range(width // 128):
+            gather_out[8 * o : 8 * o + 8, :] = turned[:, 128 * o : 128 * o + 128]
     else:
         start, extent = (HALO, count) if fast else (0, width)
         first_row = jnp.where(polar == 1, NPOLE + WEDGE, 0)
@@ -429,7 +532,7 @@
     hist = [shape((len(steps), width, 128), F32)] * 4
     if steps[0] == 1:
         out_shape = [shape((total, width, levels), F32)] + hist + [square, square]
-        out_shape.append(shape((16, width), F32))
+        out_shape.append(shape((width // 16, 128), F32))
     else:
         out_shape = [shape((rows, count if fast else width, levels), F32)] + hist
     return pl.pallas_call(
@@ -452,6 +555,7 @@
             pltpu.VMEM((width, 128), F32),
             pltpu.VMEM((128, width), F32),
             pltpu.VMEM((width + 16, 128), F32),
+            pltpu.VMEM((256, 256), BF16),
             pltpu.SemaphoreType.DMA((2,)),
         ],
         compiler_params=pltpu.CompilerParams(vmem_limit_bytes=VMEM_LIMIT),
@@ -469,12 +573,14 @@
     wedge_steps = [step + 1 for step in steps if step < STEPS]
     spec_in, refs = refs[:parts], refs[parts:]
     hists, refs = refs[: 4 * len(cap_hists(steps))], refs[4 * len(cap_hists(steps)) :]
-    names = ["t_high", "t_low", "stencil", "coef", "sea", "sea_ring", "coef_ring", "gathered"]
+    names = ["free", "t_high", "t_low", "rotate", "coef", "sea", "sea_ring", "coef_ring"]
     if steps[0] > 1:
-        names += ["flux", "ring_flux", "wedge"]
+        names += ["gathered", "flux", "ring_flux", "wedge"]
+    if last:
+        names += list(range(blocks // 2))
     loads = dict(zip(names, refs[: len(names)]))
     refs = refs[len(names) :]
-    weight, cour, vcat = refs[:3]
+    weight, courant, mix = refs[:3]
     refs = refs[3:]
     if last:
         refs = refs[1:]
@@ -484,9 +590,9 @@
             refs[:7], refs[7:])
     (spec_a, spec_b, cur, prev, adv, xcat, kcat_a, kcat_b, kadv_a, kadv_b, point, sea, flux, pad,
      ring, sea_ring, shares, t_high, t_low, stencil, coef, coef_ring, gathered, sea_hist,
-     flux_hist, side, turn, load_sems) = refs[:28]
+     flux_hist, side, turn, free_top, free_row, vcat, load_sems, row_sems) = refs[:32]
     if last:
-        back, sems = refs[28:]
+        back, free_late, sems = refs[32:]
     flip, polar, block = scal[0], scal[1], scal[2]
     lanes = lane_iota((width, 128))
     own = pl.ds(pl.multiple_of(block * width, 128), width)
@@ -507,7 +613,7 @@
                 south_ref, south = side.at[at], 0
             else:
                 south_ref, south = cur, base + width
-            advance(width, cur, base, prev, 0, south_ref, south, cour, adv, xcat)
+            advance(width, cur, base, prev, 0, south_ref, south, winds(courant)[:2], adv, xcat)
             prev[...] = cur[pl.ds(base, width), :]
             mixed = dot(xcat[...], vcat[...])
             y = adv[...] + mixed[:, :128] + mixed[:, 128:]
@@ -520,7 +626,7 @@
     def cap_step(step, src, dst, slot):
         count_rows = CAP - step
         if step > 1:
-            ready("gathered", "t_high", "t_low", "stencil", "sea_ring", "ring_flux")
+            ready("gathered", "sea_ring", "ring_flux")
         if step > 1:
             for j in range(blocks):
                 ring[pl.ds(NPOLE, 8), pl.ds(j * width, width)] = gathered[
@@ -536,6 +642,7 @@
             spot = lane_iota(at.shape) % width
             at = jnp.where((spot >= HALO) & (spot < HALO + count), at, 0.0)
             high, low = two_parts(at)
+            ready("t_high", "t_low", "rotate")
             both = dot(jnp.concatenate([high, low], axis=0), t_high[...])
             sums = both[:24] + both[24:] + dot(high, t_low[...])
             sums = sums * (air_gain * weight[0:1, :])
@@ -543,9 +650,12 @@
             moved = jnp.transpose(sums)
             swapped = jnp.concatenate([moved[128:], moved[:128]], axis=0)
             beside = pltpu.roll(moved, 1, 1) + pltpu.roll(moved, 127, 1)
-            shares[...] = stencil[0] * moved + diffusion_rate * beside + stencil[2] * swapped
-
-        ready("spec", "stencil")
+            top = jnp.broadcast_to(courant[0:1, 0:1], (1, 128))
+            shares[...] = (
+                stencil[0] * moved + diffusion_rate * beside + (stencil[2] * top) * swapped
+            )
+            stencil[1] = stencil[2] * courant[0:1, :]
+
         point[...] = jnp.zeros_like(point)
         kcats, kadvs = (kcat_a, kcat_b), (kadv_a, kadv_b)
         first = lane_iota((128, 128)) == 0
@@ -553,22 +663,24 @@
         def load(q, slot):
             cut = scal[3 + q]
             for o, other in ((0, 128), (128, 0)):
-                here = src[q + 1, pl.ds(o, 128), :]
-                swapped = src[q + 1, pl.ds(other, 128), :]
-                around = src[q, pl.ds(o, 128), :] + src[q + 2, pl.ds(o, 128), :]
-                x = (
-                    stencil[0, pl.ds(o, 128), :] * here
-                    + diffusion_rate * around
-                    + stencil[1, pl.ds(o, 128), :] * swapped
-                )
-                if step > 1:
-                    more = pltpu.roll(shares[pl.ds(o, 128), :], lax.rem(128 - q, 128), 1)
-                    x += jnp.where(first, more, 0.0)
+                more = pltpu.roll(shares[pl.ds(o, 128), :], lax.rem(128 - q, 128), 1)
+                x = jnp.where(first, more, 0.0)
+                if step > 2:
+                    here = src[q + 1, pl.ds(o, 128), :]
+                    swapped = src[q + 1, pl.ds(other, 128), :]
+                    around = src[q, pl.ds(o, 128), :] + src[q + 2, pl.ds(o, 128), :]
+                    x += (
+                        stencil[0, pl.ds(o, 128), :] * here
+                        + diffusion_rate * around
+                        + stencil[1, pl.ds(o, 128), :] * swapped
+                    )
                 x = jnp.where(lax.broadcasted_iota(jnp.int32, x.shape, 0) <= cut, x, 0.0)
                 high, low = two_parts(x)
                 kadvs[slot][pl.ds(o, 128), :] = x
                 kcats[slot][pl.ds(o, 128), 0:128] = high
                 kcats[slot][pl.ds(o, 128), 128:256] = low
+
+        streamed = step == steps[0] and step > 1
 
         def finish(q, slot, between):
             mixed = dot(kcats[slot][...], vcat[...])
@@ -577,7 +689,23 @@
             dst[q + 1] = y
             point[...] += pltpu.roll(jnp.where(lane_iota(y.shape) == 0, y, 0.0), q, 1)
 
-        two_at_a_time(0, (count_rows + 1) // 2, load, finish)
+        pairs = (count_rows + 1) // 2
+        if streamed:
+            spec_row(0).wait()
+            spec_row(1).wait()
+
+        def arrive(n):
+            spec_row(2 * n + 2).wait()
+            spec_row(2 * n + 3).wait()
+
+        if step > 1:
+            two_at_a_time(0, pairs, load, finish, arrive if streamed else None)
+        if streamed:
+            for q in range(2 * pairs + 2, CAP):
+                spec_row(q).wait()
+        ready("free")
+        top = pltpu.roll(free_top[...], (128 - NPOLE * (step - 1)) % 128, 1)
+        point[...] += jnp.where(lane_iota((NK, 128)) < NPOLE, top, 0.0)
 
         ready("t_high", "t_low", "sea_ring", "coef_ring", "coef", "sea", "flux", "hist")
         at_rows = jnp.transpose(point[...])[:NPOLE]
@@ -592,7 +720,8 @@
         flux[...] = total
         if step < STEPS:
             edge = pltpu.roll(total, 128 - (ROW0 + NPOLE - 1), 1)
-            prev[...] = own_dot(dst[NPOLE]) + air_gain * jnp.where(lanes == 0, edge, 0.0)
+            row = free_row[slot] if step == 1 else dst[NPOLE] + free_row[slot]
+            prev[...] = own_dot(row) + air_gain * jnp.where(lanes == 0, edge, 0.0)
         new = sea_next(width, polar, rows, sea[...], total, pad)
         sea[...] = jnp.where(lanes >= ROW0 + NPOLE + step - 1, sea_hist[slot], new)
 
@@ -610,27 +739,58 @@
             for copy in copies.pop(name, ()):
                 copy.wait()
 
+    def spec_row(q):
+        return pltpu.make_async_copy(spec_in[0].at[q], spec_a.at[q + 1], row_sems.at[q])
+
     @pl.when(polar == 1)
     def _():
-        if steps[0] == 1:
-            half, part = blocks // 2, NK // blocks
-            y, z = lax.rem(block, 2), block // 2
-            for n, ref in enumerate(spec_in):
-                at = jnp.bitwise_xor(z, n % half) + half * (y if n < half else 1 - y)
-                at = pl.ds(pl.multiple_of(at * part, part), part)
-                fetch("spec", ref, spec_a.at[pl.ds(1, CAP), at])
-        else:
-            fetch("spec", spec_in[0], spec_a.at[pl.ds(1, CAP)])
-        fetch("stencil", loads["stencil"], stencil)
         if steps[0] > 1:
             fetch("gathered", loads["gathered"], gathered)
             fetch("sea_ring", loads["sea_ring"], sea_ring)
             fetch("ring_flux", loads["ring_flux"], ring.at[pl.ds(0, NPOLE)])
         fetch("t_high", loads["t_high"], t_high)
         fetch("t_low", loads["t_low"], t_low)
+        fetch("rotate", loads["rotate"].at[0], stencil.at[0])
+        fetch("rotate", loads["rotate"].at[1], stencil.at[2])
+        if steps[0] > 1:
+            @pl.loop(0, CAP)
+            def _(q):
+                spec_row(q).start()
+
+        mixing(mix, vcat)
+        part = NK // blocks
+        some = part // 2
+        rows_15 = [step for step in steps if step < STEPS]
+        for i in range(blocks):
+            owner = (i % 2) * (blocks // 2) + i // 2
+            for n in range(2):
+                at = pl.ds(KMAX * n + n + some * owner, some)
+                take = pl.ds(some * n, some)
+                fetch("free", loads["free"].at[i, take], free_top.at[at])
+                for slot, step in enumerate(rows_15):
+                    take = pl.ds(part * step + some * n, some)
+                    fetch("free", loads["free"].at[i, take], free_row.at[slot, at])
+        if last:
+            side_y, place_z = lax.rem(block, 2), block // 2
+            for z in range(blocks // 2):
+                for y in range(2):
+                    owner = (blocks // 2) * jnp.bitwise_xor(side_y, y) + jnp.bitwise_xor(place_z, z)
+                    for n in range(2):
+                        at = pl.multiple_of((KMAX + 1) * n + some * owner, some)
+                        fetch(
+                            "late",
+                            loads[z].at[y, :, pl.ds(some * n, some)],
+                            free_late.at[:, pl.ds(at, some)],
+                        )
         if steps[0] == 1:
             fetch("sea_ring", loads["sea_ring"], sea_ring)
-            fetch("gathered", loads["gathered"], gathered)
+            for i in range(blocks):
+                for o in range(width // 128):
+                    fetch(
+                        "gathered",
+                        loads["free"].at[i, pl.ds(STEPS * part + 8 * o, 8)],
+                        gathered.at[i, pl.ds(8, 8), pl.ds(128 * o, 128)],
+                    )
         fetch("coef_ring", loads["coef_ring"], coef_ring)
         fetch("coef", loads["coef"], coef)
         fetch("sea", loads["sea"], sea)
@@ -660,9 +820,9 @@
                 pending = wedge_step(step + 1)
                 flux[...] = pending
                 if not last:
-                    gather_out[pl.ds(8 * n, 8), :] = jnp.transpose(pending)[
-                        NPOLE + ROW0 : NPOLE + ROW0 + 8
-                    ]
+                    turned = jnp.transpose(pending)[NPOLE + ROW0 : NPOLE + ROW0 + 8]
+                    for to in range(blocks):
+                        gather_out[to, pl.ds(8 * n, 8), :] = turned
         ready(*list(copies))
         if last:
             start, extent = (HALO, count) if fast else (0, width)
@@ -678,7 +838,7 @@
 
             @pl.loop(0, NPOLE)
             def _(q):
-                y = own_dot(src[q + 1])
+                y = own_dot(src[q + 1] + free_late[q])
                 edge = pltpu.roll(flux[...], lax.rem(128 - ROW0 - q, 128), 1)
                 back[q] = y + air_gain * jnp.where(lanes == 0, edge, 0.0)
                 send(back.at[q], 0, q).start()
@@ -741,7 +901,11 @@
             shape((rows, width), F32),
         ]
         out_specs = [any_spec, vmem]
-        extra = [pltpu.VMEM((NPOLE, width, levels), F32), pltpu.SemaphoreType.DMA((NPOLE + WEDGE,))]
+        extra = [
+            pltpu.VMEM((NPOLE, width, levels), F32),
+            pltpu.VMEM((NPOLE, NK, levels), F32),
+            pltpu.SemaphoreType.DMA((NPOLE + WEDGE,)),
+        ]
         aliases = {1 + len(spec) + len(big) + len(small): 0}
     else:
         out_shape = [
@@ -751,7 +915,7 @@
             shape((width, 128), F32),
             shape((24, ring_width), F32),
             shape((NPOLE, ring_width), F32),
-            shape((16, width), F32),
+            shape((blocks, 16, width), F32),
         ]
         out_specs = [any_spec] * 2 + [vmem] * 5
     return pl.pallas_call(
@@ -790,7 +954,11 @@
             pltpu.VMEM((2, width, 128), F32),
             pltpu.VMEM((2, width, 128), F32),
             pltpu.VMEM((128, width), F32),
-            pltpu.SemaphoreType.DMA((blocks + 32,)),
+            pltpu.VMEM((NK, 128), F32),
+            pltpu.VMEM((2, NK, 128), F32),
+            pltpu.VMEM((256, 256), BF16),
+            pltpu.SemaphoreType.DMA((9 * blocks + 32,)),
+            pltpu.SemaphoreType.DMA((CAP,)),
         ]
         + extra,
         input_output_aliases=aliases,
@@ -816,8 +984,7 @@
     return lax.ppermute(x, ("lat", "lon"), pairs)
 
 
-def to_all(x, blocks):
-    copies = jnp.broadcast_to(x[None], (blocks,) + x.shape)
+def spread(copies):
     return lax.all_to_all(copies, "lon", split_axis=0, concat_axis=0, tiled=True)
 
 
@@ -837,56 +1004,32 @@
     scal = jnp.concatenate([head, cut, jnp.full((STEPS + 4,), KMAX, jnp.int32)])
     window, forward, weight = tables(blocks, count, width, depth)
     t_high, t_low = (jnp.asarray(part) for part in window)
-    own_table = lax.dynamic_index_in_dim(jnp.asarray(forward), block, 0, keepdims=False)
-    theta = np.arange(KMAX + 1) * (2.0 * math.pi / nlon)
-    cosine = np.tile(np.cos(theta), 2).astype(np.float32)
-    sine = np.concatenate([-np.sin(theta), np.sin(theta)]).astype(np.float32)
-    stay = 1.0 - 4.0 * diffusion_rate + 2.0 * diffusion_rate * jnp.asarray(cosine)
-    stencil = jnp.stack(
-        [
-            jnp.broadcast_to(stay[:, None], (NK, levels)),
-            jnp.asarray(sine)[:, None] * courant[None, :],
-            jnp.asarray(sine)[:, None] * jnp.broadcast_to(courant[:1], (levels,))[None, :],
-        ]
-    )
-    weights = jnp.broadcast_to(jnp.asarray(weight.astype(np.float32))[None], (8, NK))
-    cour = jnp.stack([diffusion_rate - 0.5 * courant, diffusion_rate + 0.5 * courant])
-    surface = jnp.broadcast_to(cour[:, :1], cour.shape)
-    cour = jnp.concatenate([cour, surface, jnp.zeros((4, levels), F32)], 0)
-    v_round = lax.reduce_precision(vertical_mix, 8, 7)
-    v_high, v_low = v_round.astype(BF16), (vertical_mix - v_round).astype(BF16)
-    vcat = jnp.concatenate(
-        [
-            jnp.concatenate([v_high, v_low], 1),
-            jnp.concatenate([v_high, jnp.zeros_like(v_low)], 1),
-        ],
-        0,
-    )
+    rotate = rotations(nlon)
+    rotate_owned = jnp.asarray(rotate[:, owner_order(blocks)])
+    rotate = jnp.asarray(rotate)
+    weights = jnp.asarray(np.tile(weight.astype(np.float32), (8, 1)))
+    courant = courant.reshape(1, levels)
 
     west = shift(air_temp[:, count - HALO :], "lon", 1, True)
     east = shift(air_temp[:, :HALO], "lon", -1, True)
-
-    half = blocks // 2
-    keep, send = start_spectra(blocks, scal, air_temp, own_table)
-    send, sea_temp, land_sea, west, east = lax.optimization_barrier(
-        (send, sea_temp, land_sea, west, east)
-    )
-    half_sum = keep + between_caps(send, 1)
-
     exchange_coef = jnp.where(land_sea == 1, sea_coef, land_coef).astype(F32)
     sea_blocks = sea_temp.reshape(-1, blocks, count).transpose(1, 0, 2).reshape(rows, count)
-    got = to_all(jnp.concatenate([sea_blocks, exchange_coef], 0), blocks)
-    own_window, sea_ring, coef_ring = windows(
-        rows, count, width, blocks, scal, got.reshape(blocks, 2 * rows, count)
-    )
+    mine = jnp.concatenate([sea_blocks, exchange_coef], 0)
+    got = spread(jnp.broadcast_to(mine[None], (blocks,) + mine.shape))
+    half = blocks // 2
+    keep, send = start_spectra(blocks, scal, air_temp, jnp.asarray(forward))
+    send, west, east, got = lax.optimization_barrier((send, west, east, got))
+
+    half_sum = keep + between_caps(send, 1)
+
+    def edge(part):
+        return jnp.concatenate([west[part], air_temp[part], east[part]], 1)
+
+    north = shift(edge(slice(rows - ROW0, rows)), "lat", 1, False)
+    south = shift(edge(slice(0, ROW0)), "lat", -1, False)
+    own_window, sea_ring, coef_ring = windows(rows, count, width, blocks, scal, got)
     above = shift(own_window[:, rows - ROW0 :], "lat", 1, False)
     below = shift(own_window[:, :ROW0], "lat", -1, False)
-
-    def edge(part):
-        return jnp.concatenate([west[part], air_temp[part], east[part]], 1)
-
-    north = shift(edge(slice(rows - ROW0, rows)), "lat", 1, False)
-    south = shift(edge(slice(0, ROW0)), "lat", -1, False)
 
     if fast:
         air = air_temp
@@ -898,35 +1041,42 @@
     parts = [between_caps(half_sum[j], 2 * j) for j in range(1, half)]
     outs = outside_steps(
         rows, count, width, fast, (1, 2, 3), scal, (air, west, east, north, south),
-        (own_window, above, below, cour, vcat),
+        (own_window, above, below, courant, vertical_mix),
     )
     state, early, sea, coef, gathered = outs[0], tuple(outs[1:5]), outs[5], outs[6], outs[7]
-    own = functools.reduce(jnp.add, parts, half_sum[0])
-    own, state = lax.optimization_barrier((own, state))
-    near = [own] + [between_caps(own, 2 * j) for j in range(1, half)]
-    gathered = to_all(gathered, blocks).reshape(blocks, 16, width)
-    near, gathered = lax.optimization_barrier((near, gathered))
+    parts, state = lax.optimization_barrier((parts, state))
+    gathered, late_free = free_steps(
+        blocks, scal, (half_sum[0], *parts), rotate_owned, courant, vertical_mix, gathered
+    )
+    gathered, state = lax.optimization_barrier((gathered, state))
+    late_pair = jnp.stack([late_free, between_caps(late_free, 1)])
+    free = spread(gathered)
     outs = outside_steps(
         rows, count, width, fast, (4, 5, 6), scal, (state,),
-        (early[2], early[3], coef, cour, vcat),
+        (early[2], early[3], coef, courant, vertical_mix),
     )
     air, late = outs[0], tuple(outs[1:5])
-    far = between_caps(jnp.stack(near), 1)
-    spec = tuple(near) + tuple(far[j] for j in range(half))
-    spec, air, late = lax.optimization_barrier((spec, air, late))
-
-    more = ()
+    free, air, late = lax.optimization_barrier((free, air, late))
+
+    more, spec = (), ()
     for steps in ((1, 2), (3, 4), (5, 6)):
         hists = sum(((early, late)[h] for h in cap_hists(steps)), ())
-        big = hists + (t_high, t_low, stencil, coef, sea, sea_ring, coef_ring, gathered) + more
+        big = hists + (free, t_high, t_low, rotate, coef, sea, sea_ring, coef_ring) + more
+        if steps[-1] == STEPS:
+            big += tuple(late_free)
         outs = cap_steps(
             rows, count, width, blocks, fast, steps, scal, spec, big,
-            (weights, cour, vcat), (air,) if steps[-1] == STEPS else (),
+            (weights, courant, vertical_mix), (air,) if steps[-1] == STEPS else (),
         )
         if steps[-1] < STEPS:
             spec, wedge, sea, flux, sea_ring, ring_flux, mine = outs
-            spec, more = (spec,), (flux, ring_flux, wedge)
-            gathered = to_all(mine, blocks).reshape(blocks, 16, width)
+            if steps[0] == 1:
+                late_pair, mine = lax.optimization_barrier((late_pair, mine))
+                late_free = [late_pair] + [
+                    between_caps(late_pair, 2 * j) for j in range(1, half)
+                ]
+            gathered = spread(mine)
+            spec, more = (spec,), (gathered, flux, ring_flux, wedge)
     air, sea = outs
     if not fast:
         air = air[:, HALO : HALO + count]

time: 238 us -> 219 us (0.920)
  blocking collectives: 49.4 us -> 9.22 us
  starting transfers between devices: 44 us -> 62.9 us
  Pallas kernels: 105 us -> 112 us
  other arithmetic: 7.91 us -> 1.32 us
  waiting for transfers between devices: 12.4 us -> 18.7 us
  local copies, waits for them, and re-layouts: 16.6 us -> 12.6 us
    all_to_all x3 -> x0, blocking collectives: 40.2 us -> none  [to_all(): lax.all_to_all(copies, 'lon', split_axis=0, concat_axis=0, tiled=True)]
    all_to_all x1 -> x4, starting transfers between devices: 4.64 us -> 22 us  [spread(): lax.all_to_all(copies, 'lon', split_axis=0, concat_axis=0, tiled=True)]
    ppermute x8, waiting for transfers between devices: 0.02 us -> 6.04 us  [between_caps(): return lax.ppermute(x, ('lat', 'lon'), pairs)]
    pallas_call x0 -> x1, Pallas kernels: none -> 3.78 us  [free_steps(): pl.pallas_call(functools.partial(free_kernel, blocks, len(sums)), out_sha...]
    pallas_call x1, Pallas kernels: 7.2 us -> 10.8 us  [start_spectra(): pl.pallas_call(functools.partial(spectra_kernel, count, blocks), out_shap...]
    ppermute x8, starting transfers between devices: 25.2 us -> 28.8 us  [between_caps(): return lax.ppermute(x, ('lat', 'lon'), pairs)]
    concatenate x2, other arithmetic: 3.5 us -> 0.15 us  [edge(): return jnp.concatenate([west[part], air_temp[part], east[part]], 1)]
    all_to_all x1 -> x4, waiting for transfers between devices: 11.3 us -> 9.54 us  [spread(): lax.all_to_all(copies, 'lon', split_axis=0, concat_axis=0, tiled=True)]
  transfers between devices with their start and end apart: 15 -> 18, of which waited for: 2 -> 5; matrix products, arithmetic and copies ran while one was open for 6% -> 2% of each run, Pallas kernels for 20% -> 32%
where the time goes in v3:
time: 219 us; the launch traced here: 218 us
  Pallas kernels  112 us (51%)
  starting transfers between devices  62.9 us (29%)
  waiting for transfers between devices  18.7 us (9%)
  local copies, waits for them, and re-layouts  12.6 us (6%)
  blocking collectives  9.22 us (4%)
    pallas_call x3, Pallas kernels, cap_steps(): pl.pallas_call(functools.partial(cap_kernel, rows, count, width, blocks,...  57.4 us
    pallas_call x2, Pallas kernels, outside_steps(): pl.pallas_call(functools.partial(outside_kernel, rows, count, width, fast...  38.1 us
    ppermute x8, starting transfers between devices, between_caps(): return lax.ppermute(x, ('lat', 'lon'), pairs)  28.8 us
    all_to_all x4, starting transfers between devices, spread(): lax.all_to_all(copies, 'lon', split_axis=0, concat_axis=0, tiled=True)  22 us
    ppermute x6, starting transfers between devices, shift(): return lax.ppermute(x, axis, pairs)  12 us
    pallas_call x1, Pallas kernels, start_spectra(): pl.pallas_call(functools.partial(spectra_kernel, count, blocks), out_shap...  10.8 us
    all_to_all x4, waiting for transfers between devices, spread(): lax.all_to_all(copies, 'lon', split_axis=0, concat_axis=0, tiled=True)  9.54 us
    all_to_all x1, blocking collectives, local(): sea = lax.all_to_all(sea, 'lon', split_axis=0, concat_axis=1, tiled=True)  9.22 us
  transfers between devices with their start and end apart: 18, of which 5 were waited for; matrix products, arithmetic and copies ran while one was open for 2% of the time, Pallas kernels for 32%

profile of v3, /device:TPU:0, one launch (start us, length us, event | category | flops | bytes accessed | tf_op | source)
XLA Modules:
  0.0 217.8 jit_solution(10949944926516340296)
XLA Ops:
  0.6 0.9 reshape.17
  1.6 0.8 compare_select_fusion
  2.4 0.9 broadcast_in_dim.16
  3.3 7.4 %all-to-all-start = ((f32[8,64,360]{2,1,0:T(8,128)}), f32[8,64,360]{2,1,0:T(8,128)S(1)}, u32[]{:S(2)}, u32[]{:S(2)}) async-start(f32[8,64,360]{2,1,0:T(8,128)} %broadcast_in_dim.16), calls=%async_computation | async-start | bytes 1572864 | tf_op jit(solution)/shard_map/all_to_all | solution.py:988
  10.8 1.0 fusion.1
  11.7 4.8 %collective-permute-start.1 = (f32[32,8,128]{2,1,0:T(8,128)S(1)}, f32[32,8,128]{2,1,0:T(8,128)S(1)}, u32[]{:S(2)}, u32[]{:S(2)}) collective-permute-start(f32[32,8,128]{2,1,0:T(8,128)S(1)} %get-tuple-element.116), channel_id=1, source_target_pairs={{0,7},{1,0},{2,1},{3,2},{4,3},{5,4},{6,5},{7,6},{8,15},{9,8},{10,9... | collective-permute-start | bytes 393224 | tf_op jit(solution)/shard_map/ppermute | solution.py:978
  16.5 0.1 slice.54
  16.6 0.1 slice.55
  16.7 0.7 concatenate.12.scal
  17.4 10.8 %start_spectra.1 = (f32[4,22,32,128]{3,2,1,0:T(8,128)}, f32[4,22,32,128]{3,2,1,0:T(8,128)}) custom-call(s32[29]{0:T(128)} %concatenate.12.scal, f32[32,360,128]{2,1,0:T(8,128)} %refs_0_.1, bf16[8,256,1152]{2,1,0:T(8,128)(2,1)} %constant.37.clone.table), custom_call_target="tpu_custom_call" | custom-call | tf_op jit(solution)/shard_map/start_spectra/pallas_call | solution.py:156
  28.2 0.0 collective-permute-done.1.refs_2_
  28.2 3.1 %collective-permute-done.refs_1_ = f32[32,8,128]{2,1,0:T(8,128)S(1)} collective-permute-done((f32[32,8,128]{2,1,0:T(8,128)S(1)}, f32[32,8,128]{2,1,0:T(8,128)S(1)}, u32[]{:S(2)}, u32[]{:S(2)}) %collective-permute-start) | collective-permute-done | bytes 131104 | tf_op jit(solution)/shard_map/ppermute | solution.py:978
  31.3 1.0 all-to-all-done.got
  32.3 4.7 %collective-permute-start.4 = (f32[4,22,32,128]{3,2,1,0:T(8,128)}, f32[4,22,32,128]{3,2,1,0:T(8,128)S(1)}, u32[]{:S(2)}, u32[]{:S(2)}) collective-permute-start(f32[4,22,32,128]{3,2,1,0:T(8,128)} %get-tuple-element.62), channel_id=1, source_target_pairs={{0,1},{1,0},{2,3},{3,2},{4,5},{5,4},{6,7},{7,6},{24,25},{25,24},{2... | collective-permute-start | bytes 4325384 | tf_op jit(solution)/shard_map/ppermute | solution.py:984
  37.0 1.7 fusion
  38.8 0.1 pad_maximum_fusion
  38.9 1.4 collective-permute-start.2
  40.3 0.0 copy-start.6
  40.3 0.1 pad_maximum_fusion.1
  40.4 1.4 collective-permute-start.3
  41.8 1.9 windows.1
  43.7 1.3 collective-permute-start.6
  45.0 3.2 %collective-permute-start.5 = (f32[2,6,384]{2,1,0:T(8,128)S(1)}, f32[2,6,384]{2,1,0:T(8,128)S(1)}, u32[]{:S(2)}, u32[]{:S(2)}) collective-permute-start(f32[2,6,384]{2,1,0:T(8,128)S(1)} %get-tuple-element.127), channel_id=1, source_target_pairs={{0,8},{8,16},{16,24},{1,9},{9,17},{17,25},{2,10},{10,18},{18,26},{... | collective-permute-start | bytes 55304 | tf_op jit(solution)/shard_map/ppermute | solution.py:978
  48.2 6.0 %collective-permute-done.4 = f32[4,22,32,128]{3,2,1,0:T(8,128)S(1)} collective-permute-done((f32[4,22,32,128]{3,2,1,0:T(8,128)}, f32[4,22,32,128]{3,2,1,0:T(8,128)S(1)}, u32[]{:S(2)}, u32[]{:S(2)}) %collective-permute-start.4) | collective-permute-done | bytes 1441824 | tf_op jit(solution)/shard_map/ppermute | solution.py:984
  54.2 0.3 add.3
  54.6 0.9 slice_bitcast_fusion
  55.5 3.6 %collective-permute-start.9 = (f32[22,32,128]{2,1,0:T(8,128)S(1)}, f32[22,32,128]{2,1,0:T(8,128)S(1)}, u32[]{:S(2)}, u32[]{:S(2)}) collective-permute-start(f32[22,32,128]{2,1,0:T(8,128)S(1)} %get-tuple-element.118), channel_id=1, source_target_pairs={{0,6},{1,7},{2,4},{3,5},{4,2},{5,3},{6,0},{7,1},{24,30},{25,31},{2... | collective-permute-start | bytes 1081352 | tf_op jit(solution)/shard_map/ppermute | solution.py:984
  59.1 0.0 collective-permute-done.6.refs_7_
  59.1 2.6 %collective-permute-start.8 = (f32[22,32,128]{2,1,0:T(8,128)S(1)}, f32[22,32,128]{2,1,0:T(8,128)S(1)}, u32[]{:S(2)}, u32[]{:S(2)}) collective-permute-start(f32[22,32,128]{2,1,0:T(8,128)S(1)} %get-tuple-element.119), channel_id=1, source_target_pairs={{0,4},{1,5},{2,6},{3,7},{4,0},{5,1},{6,2},{7,3},{24,28},{25,29},{2... | collective-permute-start | bytes 1081352 | tf_op jit(solution)/shard_map/ppermute | solution.py:984
  61.7 0.0 copy-start.22
  61.7 3.9 %collective-permute-start.7 = (f32[22,32,128]{2,1,0:T(8,128)S(1)}, f32[22,32,128]{2,1,0:T(8,128)S(1)}, u32[]{:S(2)}, u32[]{:S(2)}) collective-permute-start(f32[22,32,128]{2,1,0:T(8,128)S(1)} %get-tuple-element.120), channel_id=1, source_target_pairs={{0,2},{1,3},{2,0},{3,1},{4,6},{5,7},{6,4},{7,5},{24,26},{25,27},{2... | collective-permute-start | bytes 1081352 | tf_op jit(solution)/shard_map/ppermute | solution.py:984
  65.6 0.0 collective-permute-done.2.refs_3_
  65.6 0.0 copy-start.19
  65.7 1.0 copy-done.19
  66.6 0.4 copy-done.20
  67.0 21.3 %outside_steps.2 = (f32[44,384,128]{2,1,0:T(8,128)}, f32[3,384,128]{2,1,0:T(8,128)}, f32[3,384,128]{2,1,0:T(8,128)}, f32[3,384,128]{2,1,0:T(8,128)}, f32[3,384,1...) custom-call(s32[29]{0:T(128)} %concatenate.12.scal, f32[32,360,128]{2,1,0:T(8,128)} %refs_0_.1, ...), custom_call_target="tpu_custom_call" | custom-call | flops 2415919104 | bytes 15728640 | tf_op jit(solution)/shard_map/outside_steps/pallas_call | solution.py:538
  88.4 0.0 collective-permute-done.8.refs_2_
  88.4 0.0 collective-permute-done.7.refs_1_
  88.4 0.0 copy-start.14
  88.4 0.7 copy-done.12
  89.1 0.1 copy-done.13
  89.2 0.1 copy-done.14
  89.3 3.8 %free_steps.1 = (f32[8,216,128]{2,1,0:T(8,128)}, f32[16,32,128]{2,1,0:T(8,128)}) custom-call(s32[29]{0:T(128)} %concatenate.12.scal, f32[22,32,128]{2,1,0:T(8,128)} %get-tuple-element.121.refs_0_, f32[22,32,128]{2,1,0:T(8,128)} %copy-done.14, f32[22,32,128]{2,1,0:T(8,128)} %copy-done.13, f32[22,32,128]{2,1,0:T(8,128)} %copy-done.12, ...), custom_call_target="tpu_custom_call" | custom-call | tf_op jit(solution)/shard_map/free_steps/pallas_call | solution.py:227
  93.1 3.7 %all-to-all-start.1 = ((f32[8,216,128]{2,1,0:T(8,128)}), f32[8,216,128]{2,1,0:T(8,128)S(1)}, u32[]{:S(2)}, u32[]{:S(2)}) async-start(f32[8,216,128]{2,1,0:T(8,128)} %get-tuple-element.78), calls=%async_computation.1 | async-start | bytes 1769472 | tf_op jit(solution)/shard_map/all_to_all | solution.py:988
  96.8 3.9 %collective-permute-start.10 = (f32[16,32,128]{2,1,0:T(8,128)S(1)}, f32[16,32,128]{2,1,0:T(8,128)S(1)}, u32[]{:S(2)}, u32[]{:S(2)}) collective-permute-start(f32[16,32,128]{2,1,0:T(8,128)S(1)} %copy-done.15), channel_id=1, source_target_pairs={{0,1},{1,0},{2,3},{3,2},{4,5},{5,4},{6,7},{7,6},{24,25},{25,24},{2... | collective-permute-start | bytes 786440 | tf_op jit(solution)/shard_map/ppermute | solution.py:984
  100.7 16.8 %outside_steps.3 = (f32[32,360,128]{2,1,0:T(8,128)}, f32[3,384,128]{2,1,0:T(8,128)}, f32[3,384,128]{2,1,0:T(8,128)}, f32[3,384,128]{2,1,0:T(8,128)}, f32[3,384,128]{2,1,0:T(8,128)}) custom-call(s32[29]{0:T(128)} %concatenate.12.scal, f32[44,384,128]{2,1,0:T(8,128)} %get-tuple-element.79.refs_0_, f32[3,384,128]{2,1,0:T(8,128)} %get-tuple-element.68.refs_1_.refs_2_.refs_3_, ...), custom_call_target="tpu_custom_call" | custom-call | flops 2415919104 | bytes 15728640 | tf_op jit(solution)/shard_map/outside_steps/pallas_call | solution.py:538
  117.5 0.0 collective-permute-done.10
  117.6 0.8 all-to-all-done.1.refs_4_.refs_9_.refs_5_
  118.4 0.9 copy-done.4
  119.3 15.8 %cap_steps.3 = (f32[22,256,128]{2,1,0:T(8,128)}, f32[2,384,128]{2,1,0:T(8,128)}, f32[384,128]{1,0:T(8,128)}, f32[384,128]{1,0:T(8,128)}, f32[24,3072]{1,0:T(8,12...) custom-call(s32[29]{0:T(128)} %concatenate.12.scal, f32[3,384,128]{2,1,0:T(8,128)} %get-tuple-element.66.refs_0_.refs_1_, ...), custom_call_target="tpu_custom_call" | custom-call | flops 738197504 | bytes 20000000 | tf_op jit(solution)/shard_map/cap_steps/pallas_call | solution.py:921
  135.1 5.0 %all-to-all-start.2 = ((f32[8,16,384]{2,1,0:T(8,128)}), f32[8,16,384]{2,1,0:T(8,128)S(1)}, u32[]{:S(2)}, u32[]{:S(2)}) async-start(f32[8,16,384]{2,1,0:T(8,128)} %get-tuple-element.99), calls=%async_computation.2 | async-start | bytes 393216 | tf_op jit(solution)/shard_map/all_to_all | solution.py:988
  140.0 5.7 %collective-permute-start.13 = (f32[2,16,32,128]{3,2,1,0:T(8,128)S(1)}, f32[2,16,32,128]{3,2,1,0:T(8,128)S(1)}, u32[]{:S(2)}, u32[]{:S(2)}) collective-permute-start(f32[2,16,32,128]{3,2,1,0:T(8,128)S(1)} %pad_maximum_fusion.2.refs_17_), channel_id=1, source_target_pairs={{0,6},{1,7},{2,4},{3,5},{4,2},{5,3},{6,0},{7,1},{24,30},{25,31},{2... | collective-permute-start | bytes 1572872 | tf_op jit(solution)/shard_map/ppermute | solution.py:984
  145.8 1.9 collective-permute-start.12
  147.7 2.5 %collective-permute-start.11 = (f32[2,16,32,128]{3,2,1,0:T(8,128)S(1)}, f32[2,16,32,128]{3,2,1,0:T(8,128)S(1)}, u32[]{:S(2)}, u32[]{:S(2)}) collective-permute-start(f32[2,16,32,128]{3,2,1,0:T(8,128)S(1)} %pad_maximum_fusion.2.refs_17_), channel_id=1, source_target_pairs={{0,2},{1,3},{2,0},{3,1},{4,6},{5,7},{6,4},{7,5},{24,26},{25,27},{2... | collective-permute-start | bytes 1572872 | tf_op jit(solution)/shard_map/ppermute | solution.py:984
  150.2 0.0 all-to-all-done.2.refs_17_
  150.2 0.7 copy-done.8
  150.9 19.0 %cap_steps.4 = (f32[22,256,128]{2,1,0:T(8,128)}, f32[4,384,128]{2,1,0:T(8,128)}, f32[384,128]{1,0:T(8,128)}, f32[384,128]{1,0:T(8,128)}, f32[24,3072]{1,0:T(8,12...) custom-call(s32[29]{0:T(128)} %concatenate.12.scal, f32[22,256,128]{2,1,0:T(8,128)} %get-tuple-element.90.refs_0_, ...), custom_call_target="tpu_custom_call" | custom-call | flops 738197504 | bytes 20000000 | tf_op jit(solution)/shard_map/cap_steps/pallas_call | solution.py:921
  169.9 6.0 %all-to-all-start.3 = ((f32[8,16,384]{2,1,0:T(8,128)}), f32[8,16,384]{2,1,0:T(8,128)S(1)}, u32[]{:S(2)}, u32[]{:S(2)}) async-start(f32[8,16,384]{2,1,0:T(8,128)} %get-tuple-element.106), calls=%async_computation.3 | async-start | bytes 393216 | tf_op jit(solution)/shard_map/all_to_all | solution.py:988
  176.0 7.7 %all-to-all-done.3.refs_13_ = f32[8,16,384]{2,1,0:T(8,128)S(1)} async-done(((f32[8,16,384]{2,1,0:T(8,128)}), f32[8,16,384]{2,1,0:T(8,128)S(1)}, u32[]{:S(2)}, u32[]{:S(2)}) %all-to-all-start.3) | async-done | bytes 196640 | tf_op jit(solution)/shard_map/all_to_all | solution.py:988
  183.7 0.7 copy-done.7
  184.4 22.5 %cap_steps.5 = (f32[32,360,128]{2,1,0:T(8,128)}, f32[32,384]{1,0:T(8,128)}) custom-call(s32[29]{0:T(128)} %concatenate.12.scal, f32[22,256,128]{2,1,0:T(8,128)} %get-tuple-element.103.refs_0_, f32[3,384,128]{2,1,0:T(8,128)} %get-tuple-element.91.refs_5_.refs_1_, f32[3,384,128]{2,1,0:T(8,128)} %get-tuple-element.92.refs_6_.refs_2_, ...), custom_call_target="tpu_custom_call", output_to_operand_aliasing={{0}: (25, {})} | custom-call | flops 738197504 | bytes 20000000 | tf_op jit(solution)/shard_map/cap_steps/pallas_call | solution.py:921
  206.9 0.9 slice.71
  207.8 9.2 %all_to_all.39 = f32[8,4,360]{2,1,0:T(4,128)S(1)} all-to-all(f32[8,4,360]{2,1,0:T(4,128)S(1)} %all_to_all.30), channel_id=1, replica_groups=mesh['lat'=4,'lon'=8] {'lon'}, dimensions={0} | all-to-all | bytes 92160 | tf_op jit(solution)/shard_map/all_to_all | solution.py:1084
  217.1 0.7 all_to_all.33
  (51 shorter events, 0.2 us)
Async XLA Ops:
  3.3 13.2 %copy-start.18 = (s32[32]{0:T(128)S(1)}, s32[32]{0:T(128)}, u32[]{:S(2)}) copy-start(s32[32]{0:T(128)} %param.17) | copy-start | bytes 388
  3.3 29.0 %all-to-all-start = ((f32[8,64,360]{2,1,0:T(8,128)}), f32[8,64,360]{2,1,0:T(8,128)S(1)}, u32[]{:S(2)}, u32[]{:S(2)}) async-start(f32[8,64,360]{2,1,0:T(8,128)} %broadcast_in_dim.16), calls=%async_computation | async-start | bytes 1572864 | tf_op jit(solution)/shard_map/all_to_all | solution.py:988
  11.7 16.5 %collective-permute-start.1 = (f32[32,8,128]{2,1,0:T(8,128)S(1)}, f32[32,8,128]{2,1,0:T(8,128)S(1)}, u32[]{:S(2)}, u32[]{:S(2)}) collective-permute-start(f32[32,8,128]{2,1,0:T(8,128)S(1)} %get-tuple-element.116), channel_id=1, source_target_pairs={{0,7},{1,0},{2,1},{3,2},{4,3},{5,4},{6,5},{7,6},{8,15},{9,8},{10,9... | collective-permute-start | bytes 393224 | tf_op jit(solution)/shard_map/ppermute | solution.py:978
  16.5 14.8 %collective-permute-start = (f32[32,8,128]{2,1,0:T(8,128)S(1)}, f32[32,8,128]{2,1,0:T(8,128)S(1)}, u32[]{:S(2)}, u32[]{:S(2)}) collective-permute-start(f32[32,8,128]{2,1,0:T(8,128)S(1)} %get-tuple-element.117), channel_id=1, source_target_pairs={{0,1},{1,2},{2,3},{3,4},{4,5},{5,6},{6,7},{7,0},{8,9},{9,10},{10,1... | collective-permute-start | bytes 393224 | tf_op jit(solution)/shard_map/ppermute | solution.py:978
  28.2 10.5 %copy-start.16 = (f32[32,8,128]{2,1,0:T(8,128)}, f32[32,8,128]{2,1,0:T(8,128)S(1)}, u32[]{:S(2)}) copy-start(f32[32,8,128]{2,1,0:T(8,128)S(1)} %collective-permute-done.1.refs_2_) | copy-start | bytes 393220
  31.3 7.5 %copy-start.17 = (f32[32,8,128]{2,1,0:T(8,128)}, f32[32,8,128]{2,1,0:T(8,128)S(1)}, u32[]{:S(2)}) copy-start(f32[32,8,128]{2,1,0:T(8,128)S(1)} %collective-permute-done.refs_1_) | copy-start | bytes 393220
  32.3 21.9 %collective-permute-start.4 = (f32[4,22,32,128]{3,2,1,0:T(8,128)}, f32[4,22,32,128]{3,2,1,0:T(8,128)S(1)}, u32[]{:S(2)}, u32[]{:S(2)}) collective-permute-start(f32[4,22,32,128]{3,2,1,0:T(8,128)} %get-tuple-element.62), channel_id=1, source_target_pairs={{0,1},{1,0},{2,3},{3,2},{4,5},{5,4},{6,7},{7,6},{24,25},{25,24},{2... | collective-permute-start | bytes 4325384 | tf_op jit(solution)/shard_map/ppermute | solution.py:984
  38.9 26.7 %collective-permute-start.2 = (f32[6,376,128]{2,1,0:T(8,128)S(1)}, f32[6,376,128]{2,1,0:T(8,128)S(1)}, u32[]{:S(2)}, u32[]{:S(2)}) collective-permute-start(f32[6,376,128]{2,1,0:T(8,128)S(1)} %pad_maximum_fusion), channel_id=1, source_target_pairs={{0,8},{8,16},{16,24},{1,9},{9,17},{17,25},{2,10},{10,18},{18,26},{... | collective-permute-start | bytes 3465224 | tf_op jit(solution)/shard_map/ppermute | solution.py:978
  40.3 1.5 copy-start.2
  40.3 14.0 %copy-start.6 = (f32[4,22,32,128]{3,2,1,0:T(8,128)S(1)}, f32[4,22,32,128]{3,2,1,0:T(8,128)}, u32[]{:S(2)}) copy-start(f32[4,22,32,128]{3,2,1,0:T(8,128)} %get-tuple-element.61) | copy-start | bytes 4325380
  40.4 25.3 %collective-permute-start.3 = (f32[6,376,128]{2,1,0:T(8,128)S(1)}, f32[6,376,128]{2,1,0:T(8,128)S(1)}, u32[]{:S(2)}, u32[]{:S(2)}) collective-permute-start(f32[6,376,128]{2,1,0:T(8,128)S(1)} %pad_maximum_fusion.1), channel_id=1, source_target_pairs={{8,0},{16,8},{24,16},{9,1},{17,9},{25,17},{10,2},{18,10},{26,18},{... | collective-permute-start | bytes 3465224 | tf_op jit(solution)/shard_map/ppermute | solution.py:978
  43.7 10.9 %copy-start = (f32[16,3072]{1,0:T(8,128)}, f32[16,3072]{1,0:T(8,128)S(1)}, u32[]{:S(2)}) copy-start(f32[16,3072]{1,0:T(8,128)S(1)} %get-tuple-element.89.refs_11_.refs_16_.refs_12_) | copy-start | bytes 589828
  43.7 10.9 %copy-start.1 = (f32[24,3072]{1,0:T(8,128)}, f32[24,3072]{1,0:T(8,128)S(1)}, u32[]{:S(2)}) copy-start(f32[24,3072]{1,0:T(8,128)S(1)} %get-tuple-element.88.refs_10_) | copy-start | bytes 884740
  43.7 10.9 %copy-start.3 = (f32[2,32,384]{2,1,0:T(8,128)}, f32[2,32,384]{2,1,0:T(8,128)S(1)}, u32[]{:S(2)}) copy-start(f32[2,32,384]{2,1,0:T(8,128)S(1)} %get-tuple-element.65.refs_5_) | copy-start | bytes 294916
  43.7 15.4 %collective-permute-start.6 = (f32[2,6,384]{2,1,0:T(8,128)S(1)}, f32[2,6,384]{2,1,0:T(8,128)S(1)}, u32[]{:S(2)}, u32[]{:S(2)}) collective-permute-start(f32[2,6,384]{2,1,0:T(8,128)S(1)} %get-tuple-element.126), channel_id=1, source_target_pairs={{8,0},{16,8},{24,16},{9,1},{17,9},{25,17},{10,2},{18,10},{26,18},{... | collective-permute-start | bytes 55304 | tf_op jit(solution)/shard_map/ppermute | solution.py:978
  45.0 16.7 %collective-permute-start.5 = (f32[2,6,384]{2,1,0:T(8,128)S(1)}, f32[2,6,384]{2,1,0:T(8,128)S(1)}, u32[]{:S(2)}, u32[]{:S(2)}) collective-permute-start(f32[2,6,384]{2,1,0:T(8,128)S(1)} %get-tuple-element.127), channel_id=1, source_target_pairs={{0,8},{8,16},{16,24},{1,9},{9,17},{17,25},{2,10},{10,18},{18,26},{... | collective-permute-start | bytes 55304 | tf_op jit(solution)/shard_map/ppermute | solution.py:978
  55.5 32.9 %collective-permute-start.9 = (f32[22,32,128]{2,1,0:T(8,128)S(1)}, f32[22,32,128]{2,1,0:T(8,128)S(1)}, u32[]{:S(2)}, u32[]{:S(2)}) collective-permute-start(f32[22,32,128]{2,1,0:T(8,128)S(1)} %get-tuple-element.118), channel_id=1, source_target_pairs={{0,6},{1,7},{2,4},{3,5},{4,2},{5,3},{6,0},{7,1},{24,30},{25,31},{2... | collective-permute-start | bytes 1081352 | tf_op jit(solution)/shard_map/ppermute | solution.py:984
  59.1 6.6 %copy-start.21 = (f32[2,6,384]{2,1,0:T(8,128)}, f32[2,6,384]{2,1,0:T(8,128)S(1)}, u32[]{:S(2)}) copy-start(f32[2,6,384]{2,1,0:T(8,128)S(1)} %collective-permute-done.6.refs_7_) | copy-start | bytes 55300
  59.1 29.2 %collective-permute-start.8 = (f32[22,32,128]{2,1,0:T(8,128)S(1)}, f32[22,32,128]{2,1,0:T(8,128)S(1)}, u32[]{:S(2)}, u32[]{:S(2)}) collective-permute-start(f32[22,32,128]{2,1,0:T(8,128)S(1)} %get-tuple-element.119), channel_id=1, source_target_pairs={{0,4},{1,5},{2,6},{3,7},{4,0},{5,1},{6,2},{7,3},{24,28},{25,29},{2... | collective-permute-start | bytes 1081352 | tf_op jit(solution)/shard_map/ppermute | solution.py:984
  61.7 3.9 %copy-start.22 = (f32[2,6,384]{2,1,0:T(8,128)}, f32[2,6,384]{2,1,0:T(8,128)S(1)}, u32[]{:S(2)}) copy-start(f32[2,6,384]{2,1,0:T(8,128)S(1)} %collective-permute-done.5.refs_6_) | copy-start | bytes 55300
  61.7 26.6 %collective-permute-start.7 = (f32[22,32,128]{2,1,0:T(8,128)S(1)}, f32[22,32,128]{2,1,0:T(8,128)S(1)}, u32[]{:S(2)}, u32[]{:S(2)}) collective-permute-start(f32[22,32,128]{2,1,0:T(8,128)S(1)} %get-tuple-element.120), channel_id=1, source_target_pairs={{0,2},{1,3},{2,0},{3,1},{4,6},{5,7},{6,4},{7,5},{24,26},{25,27},{2... | collective-permute-start | bytes 1081352 | tf_op jit(solution)/shard_map/ppermute | solution.py:984
  65.6 1.0 copy-start.19
  65.7 1.4 copy-start.20
  88.3 0.7 copy-start.12
  88.4 0.9 copy-start.13
  88.4 0.9 copy-start.14
  93.1 3.7 %copy-start.15 = (f32[16,32,128]{2,1,0:T(8,128)S(1)}, f32[16,32,128]{2,1,0:T(8,128)}, u32[]{:S(2)}) copy-start(f32[16,32,128]{2,1,0:T(8,128)} %get-tuple-element.97) | copy-start | bytes 786436
  93.1 25.2 %all-to-all-start.1 = ((f32[8,216,128]{2,1,0:T(8,128)}), f32[8,216,128]{2,1,0:T(8,128)S(1)}, u32[]{:S(2)}, u32[]{:S(2)}) async-start(f32[8,216,128]{2,1,0:T(8,128)} %get-tuple-element.78), calls=%async_computation.1 | async-start | bytes 1769472 | tf_op jit(solution)/shard_map/all_to_all | solution.py:988
  96.8 20.7 %collective-permute-start.10 = (f32[16,32,128]{2,1,0:T(8,128)S(1)}, f32[16,32,128]{2,1,0:T(8,128)S(1)}, u32[]{:S(2)}, u32[]{:S(2)}) collective-permute-start(f32[16,32,128]{2,1,0:T(8,128)S(1)} %copy-done.15), channel_id=1, source_target_pairs={{0,1},{1,0},{2,3},{3,2},{4,5},{5,4},{6,7},{7,6},{24,25},{25,24},{2... | collective-permute-start | bytes 786440 | tf_op jit(solution)/shard_map/ppermute | solution.py:984
  117.5 30.2 %copy-start.5 = (f32[2,16,32,128]{3,2,1,0:T(8,128)}, f32[2,16,32,128]{3,2,1,0:T(8,128)S(1)}, u32[]{:S(2)}) copy-start(f32[2,16,32,128]{3,2,1,0:T(8,128)S(1)} %pad_maximum_fusion.2.refs_17_) | copy-start | bytes 1572868
  118.4 0.9 copy-start.4
  135.1 15.1 %all-to-all-start.2 = ((f32[8,16,384]{2,1,0:T(8,128)}), f32[8,16,384]{2,1,0:T(8,128)S(1)}, u32[]{:S(2)}, u32[]{:S(2)}) async-start(f32[8,16,384]{2,1,0:T(8,128)} %get-tuple-element.99), calls=%async_computation.2 | async-start | bytes 393216 | tf_op jit(solution)/shard_map/all_to_all | solution.py:988
  140.0 35.9 %collective-permute-start.13 = (f32[2,16,32,128]{3,2,1,0:T(8,128)S(1)}, f32[2,16,32,128]{3,2,1,0:T(8,128)S(1)}, u32[]{:S(2)}, u32[]{:S(2)}) collective-permute-start(f32[2,16,32,128]{3,2,1,0:T(8,128)S(1)} %pad_maximum_fusion.2.refs_17_), channel_id=1, source_target_pairs={{0,6},{1,7},{2,4},{3,5},{4,2},{5,3},{6,0},{7,1},{24,30},{25,31},{2... | collective-permute-start | bytes 1572872 | tf_op jit(solution)/shard_map/ppermute | solution.py:984
  145.8 30.2 %collective-permute-start.12 = (f32[2,16,32,128]{3,2,1,0:T(8,128)S(1)}, f32[2,16,32,128]{3,2,1,0:T(8,128)S(1)}, u32[]{:S(2)}, u32[]{:S(2)}) collective-permute-start(f32[2,16,32,128]{3,2,1,0:T(8,128)S(1)} %pad_maximum_fusion.2.refs_17_), channel_id=1, source_target_pairs={{0,4},{1,5},{2,6},{3,7},{4,0},{5,1},{6,2},{7,3},{24,28},{25,29},{2... | collective-permute-start | bytes 1572872 | tf_op jit(solution)/shard_map/ppermute | solution.py:984
  147.7 28.3 %collective-permute-start.11 = (f32[2,16,32,128]{3,2,1,0:T(8,128)S(1)}, f32[2,16,32,128]{3,2,1,0:T(8,128)S(1)}, u32[]{:S(2)}, u32[]{:S(2)}) collective-permute-start(f32[2,16,32,128]{3,2,1,0:T(8,128)S(1)} %pad_maximum_fusion.2.refs_17_), channel_id=1, source_target_pairs={{0,2},{1,3},{2,0},{3,1},{4,6},{5,7},{6,4},{7,5},{24,26},{25,27},{2... | collective-permute-start | bytes 1572872 | tf_op jit(solution)/shard_map/ppermute | solution.py:984
  150.2 0.7 copy-start.8
  169.9 13.8 %all-to-all-start.3 = ((f32[8,16,384]{2,1,0:T(8,128)}), f32[8,16,384]{2,1,0:T(8,128)S(1)}, u32[]{:S(2)}, u32[]{:S(2)}) async-start(f32[8,16,384]{2,1,0:T(8,128)} %get-tuple-element.106), calls=%async_computation.3 | async-start | bytes 393216 | tf_op jit(solution)/shard_map/all_to_all | solution.py:988
  175.9 7.8 %copy-start.9 = (f32[2,16,32,128]{3,2,1,0:T(8,128)}, f32[2,16,32,128]{3,2,1,0:T(8,128)S(1)}, u32[]{:S(2)}) copy-start(f32[2,16,32,128]{3,2,1,0:T(8,128)S(1)} %collective-permute-done.13.refs_20_) | copy-start | bytes 1572868
  176.0 7.8 %copy-start.10 = (f32[2,16,32,128]{3,2,1,0:T(8,128)}, f32[2,16,32,128]{3,2,1,0:T(8,128)S(1)}, u32[]{:S(2)}) copy-start(f32[2,16,32,128]{3,2,1,0:T(8,128)S(1)} %collective-permute-done.12.refs_19_) | copy-start | bytes 1572868
  176.0 7.7 %copy-start.11 = (f32[2,16,32,128]{3,2,1,0:T(8,128)}, f32[2,16,32,128]{3,2,1,0:T(8,128)S(1)}, u32[]{:S(2)}) copy-start(f32[2,16,32,128]{3,2,1,0:T(8,128)S(1)} %collective-permute-done.11.refs_18_) | copy-start | bytes 1572868
  183.7 0.7 copy-start.7

commit v4 on v3

--- a/solution.py
+++ b/solution.py
@@ -18,6 +18,8 @@
 HALO = 8
 ROW0 = STEPS
 WEDGE = STEPS - 1
+BEYOND = 5
+SPLIT = 2
 
 diffusion_rate = 0.1
 air_gain = 0.5
@@ -96,7 +98,8 @@
 
 
 def mixing(mix, vcat):
-    high, low = two_parts(mix[...])
+    row = lax.broadcasted_iota(jnp.int32, (128, 128), 0)
+    high, low = two_parts(jnp.where(row == lane_iota((128, 128)), mix[...] + 1.0, mix[...]))
     vcat[0:128, 0:128] = high
     vcat[128:256, 0:128] = high
     vcat[0:128, 128:256] = low
@@ -113,62 +116,96 @@
     return lax.broadcasted_iota(jnp.int32, shape, len(shape) - 1)
 
 
-def spectra_kernel(count, blocks, scal, air, table, keep, send, stacked, sums):
-    depth = stacked.shape[0] // 3
+def spectra_kernel(
+    rows, count, blocks,
+    scal, air, table, keep_out, send_out,
+    held, own_table, stacked_a, stacked_b, sums, keep, send, sems,
+):
+    depth = stacked_a.shape[0] // 3
     half, part = blocks // 2, NK // blocks
     flip, block = scal[0], scal[2]
     side, place = lax.rem(block, 2), block // 2
-
-    @pl.when(pl.program_id(0) == 0)
-    def _():
-        stacked[...] = jnp.zeros_like(stacked)
+    pairs = CAP // 2
+
+    def row(q):
+        r = jnp.where(flip == 1, rows - 1 - q, q)
+        return pltpu.make_async_copy(air.at[r], held.at[q], sems.at[q])
 
     @pl.when(scal[1] == 1)
     def _():
-        for n in range(2):
-            high, low = two_parts(air[n])
-            lanes = slice(128 * n, 128 * n + 128)
-            stacked[0:count, lanes] = high
-            stacked[depth : depth + count, lanes] = low
-            stacked[2 * depth : 2 * depth + count, lanes] = high
-        sums[...] = dot(table[0], stacked[...])
-        for n in range(2):
-            to = jnp.where(flip == 1, 1 - n, n)
-            lanes = slice(128 * n, 128 * n + 128)
-            for z in range(half):
-                at = jnp.bitwise_xor(place, z)
-                mine = pl.multiple_of((side * half + z) * part, part)
-                other = pl.multiple_of(((1 - side) * half + z) * part, part)
-                keep[at, to] = sums[pl.ds(mine, part), lanes]
-                send[at, to] = sums[pl.ds(other, part), lanes]
+        fetch = pltpu.make_async_copy(table.at[block], own_table, sems.at[CAP])
+        row(0).start()
+        row(1).start()
+        fetch.start()
+
+        @pl.loop(2, CAP)
+        def _(q):
+            row(q).start()
+
+        for ref in (stacked_a, stacked_b):
+            ref[...] = jnp.zeros_like(ref)
+
+        def load(p, slot):
+            ref = (stacked_a, stacked_b)[slot]
+            for n in range(2):
+                high, low = two_parts(held[2 * p + n])
+                lanes = slice(128 * n, 128 * n + 128)
+                ref[0:count, lanes] = high
+                ref[depth : depth + count, lanes] = low
+                ref[2 * depth : 2 * depth + count, lanes] = high
+
+        def finish(p, slot, between):
+            sums[slot] = dot(own_table[...], (stacked_a, stacked_b)[slot][...])
+            between()
+            for n in range(2):
+                lanes = slice(128 * n, 128 * n + 128)
+                for z in range(half):
+                    at = jnp.bitwise_xor(place, z)
+                    mine = pl.multiple_of((side * half + z) * part, part)
+                    other = pl.multiple_of(((1 - side) * half + z) * part, part)
+                    keep[at, 2 * p + n] = sums[slot, pl.ds(mine, part), lanes]
+                    send[at, 2 * p + n] = sums[slot, pl.ds(other, part), lanes]
+
+        def arrive(n):
+            for q in range(2, 6):
+                row(4 * n + q).wait()
+
+        row(0).wait()
+        row(1).wait()
+        fetch.wait()
+        two_at_a_time(0, pairs // 2, load, finish, arrive)
+        finish(pairs - 1, 0, lambda: None)
+        out = [
+            pltpu.make_async_copy(send.at[:, pl.ds(0, CAP)], send_out, sems.at[0]),
+            pltpu.make_async_copy(keep.at[:, pl.ds(0, CAP)], keep_out, sems.at[1]),
+        ]
+        for copy in out:
+            copy.start()
+        for copy in out:
+            copy.wait()
 
 
 def start_spectra(blocks, scal, air_temp, table):
     rows, count, levels = air_temp.shape
     half, part = blocks // 2, NK // blocks
     depth = table.shape[2] // 3
-
-    def place(p, scal):
-        return (jnp.where(scal[0] == 1, rows // 2 - 1 - p, p), 0, 0)
-
+    any_spec = pl.BlockSpec(memory_space=pl.ANY)
     out = jax.ShapeDtypeStruct((half, CAP, part, levels), F32)
-    out_spec = pl.BlockSpec((half, 2, part, levels), lambda p, scal: (0, p, 0, 0))
     return pl.pallas_call(
-        functools.partial(spectra_kernel, count, blocks),
+        functools.partial(spectra_kernel, rows, count, blocks),
         out_shape=[out, out],
-        grid_spec=pltpu.PrefetchScalarGridSpec(
-            num_scalar_prefetch=1,
-            grid=(CAP // 2,),
-            in_specs=[
-                pl.BlockSpec((2, count, levels), place),
-                pl.BlockSpec((1, NK, 3 * depth), lambda p, scal: (scal[2], 0, 0)),
-            ],
-            out_specs=[out_spec, out_spec],
-            scratch_shapes=[
-                pltpu.VMEM((3 * depth, 2 * levels), BF16),
-                pltpu.VMEM((NK, 2 * levels), F32),
-            ],
-        ),
+        in_specs=[pl.BlockSpec(memory_space=pltpu.SMEM), any_spec, any_spec],
+        out_specs=[any_spec, any_spec],
+        scratch_shapes=[
+            pltpu.VMEM((CAP, count, levels), F32),
+            pltpu.VMEM((NK, 3 * depth), BF16),
+            pltpu.VMEM((3 * depth, 2 * levels), BF16),
+            pltpu.VMEM((3 * depth, 2 * levels), BF16),
+            pltpu.VMEM((2, NK, 2 * levels), F32),
+            pltpu.VMEM((half, CAP, part, levels), F32),
+            pltpu.VMEM((half, CAP, part, levels), F32),
+            pltpu.SemaphoreType.DMA((CAP + 2,)),
+        ],
         compiler_params=pltpu.CompilerParams(vmem_limit_bytes=VMEM_LIMIT),
         name="start_spectra",
     )(scal, air_temp, table)
@@ -176,7 +213,7 @@
 
 def free_kernel(blocks, parts, scal, *refs):
     sums, refs = refs[:parts], refs[parts:]
-    rotate, courant, mix, edge, early, late, state, mask, adv, xcat, vcat = refs
+    rotate, courant, mix, edge, early, late, state, mask, xcat, vcat = refs
     part = NK // blocks
     some = part // 2
     owner = lax.rem(scal[2], 2) * (blocks // 2) + scal[2] // 2
@@ -201,11 +238,10 @@
             x = (x + turn * swapped) * mask[0:size]
             x = x.reshape(size * part, 128)
             high, low = two_parts(x)
-            adv[0 : size * part, :] = x
             xcat[0 : size * part, 0:128] = high
             xcat[0 : size * part, 128:256] = low
             mixed = dot(xcat[0 : size * part, :], vcat[...])
-            y = adv[0 : size * part, :] + mixed[:, :128] + mixed[:, 128:]
+            y = mixed[:, :128] + mixed[:, 128:]
             state[1 : size + 1] = y.reshape(size, part, 128)
             for q in range(NPOLE):
                 lane = NPOLE * (step - 1) + q
@@ -235,17 +271,16 @@
         scratch_shapes=[
             pltpu.VMEM((CAP + 2, part, 128), F32),
             pltpu.VMEM((CAP, part, 128), F32),
-            pltpu.VMEM((CAP * part, 128), F32),
             pltpu.VMEM((CAP * part, 256), BF16),
             pltpu.VMEM((256, 256), BF16),
         ],
-        compiler_params=pltpu.CompilerParams(vmem_limit_bytes=VMEM_LIMIT),
+        compiler_params=pltpu.CompilerParams(vmem_limit_bytes=VMEM_LIMIT // 4),
         name="free_steps",
     )(scal, *sums, rotate, courant, mix, edge)
 
 
 def advance(
-    width, here_ref, base, north_ref, north, south_ref, south, cour, adv, xcat, more=None
+    width, here_ref, base, north_ref, north, south_ref, south, cour, xcat, more=None, to=0
 ):
     c_east, c_west = cour
     for o in range(0, width, 128):
@@ -260,21 +295,20 @@
             moved = pltpu.roll(more[0][pl.ds(o, 128), :], more[1], 1)
             x += jnp.where(lane_iota(x.shape) == 0, moved, 0.0)
         high, low = two_parts(x)
-        adv[pl.ds(o, 128), :] = x
-        xcat[pl.ds(o, 128), 0:128] = high
-        xcat[pl.ds(o, 128), 128:256] = low
-
-
-def two_at_a_time(first, pairs, load, finish, arrive=None):
+        xcat[pl.ds(to + o, 128), 0:128] = high
+        xcat[pl.ds(to + o, 128), 128:256] = low
+
+
+def two_at_a_time(first, pairs, load, finish, arrive=None, size=1):
     load(first, 0)
 
     @pl.loop(0, pairs)
     def _(n):
         if arrive is not None:
             arrive(n)
-        q = first + 2 * n
-        finish(q, 0, lambda: load(q + 1, 1))
-        finish(q + 1, 1, lambda: load(q + 2, 0))
+        q = first + 2 * size * n
+        finish(q, 0, lambda: load(q + size, 1))
+        finish(q + size, 1, lambda: load(q + 2 * size, 0))
 
 
 def exchange(y, lane, sea, coef):
@@ -294,7 +328,23 @@
     return jnp.where((lane >= first) & (lane < rows + 2 * ROW0), new, 0.0)
 
 
-def windows_kernel(rows, count, width, blocks, scal, got, own, ring_sea, ring_coef, wide):
+def windows_kernel(rows, count, width, blocks, scal, got, air, west, east, *refs):
+    own, ring_sea, ring_coef = refs[:3]
+    wide, sems = refs[-2:]
+    edges = list(zip(refs[3:-2], (rows - ROW0, 0)))
+    copies = []
+    for n, (ref, first) in enumerate(edges):
+        some = pl.ds(first, ROW0)
+        for m, (source, offset, size) in enumerate(
+            ((west, 0, HALO), (air, HALO, count), (east, HALO + count, HALO))
+        ):
+            copies.append(
+                pltpu.make_async_copy(
+                    source.at[some], ref.at[:, pl.ds(offset, size)], sems.at[3 * n + m]
+                )
+            )
+    for copy in copies:
+        copy.start()
     per = rows // blocks
     for j in range(blocks):
         columns = slice(j * width + HALO, j * width + HALO + count)
@@ -309,6 +359,13 @@
         wide[:, :, j * width : j * width + HALO] = wide[:, :, before : before + HALO]
         wide[:, :, end : end + rest] = wide[:, :, after : after + rest]
     own[...] = wide[:, :, pl.ds(pl.multiple_of(scal[2] * width, 128), width)]
+    for ref, first in edges:
+        base = count + 2 * HALO
+        for n in range(2):
+            for r in range(ROW0):
+                for o in range(width // 128):
+                    at = base + n * (width // 128) + o
+                    ref[r, at : at + 1, :] = own[n, first + r : first + r + 1, pl.ds(128 * o, 128)]
 
     @pl.when(scal[1] == 1)
     def _():
@@ -322,8 +379,18 @@
             r = jnp.where(scal[0] == 1, rows - 1 - q, q)
             ring_coef[pl.ds(q, 1), :] = wide[1, pl.ds(r, 1), :]
 
-
-def windows(rows, count, width, blocks, scal, got):
+    for copy in copies:
+        copy.wait()
+
+
+def edge_extent(count, width):
+    inner = count + 2 * HALO
+    return round_up(inner, 8), round_up(inner, 8) + 8
+
+
+def windows(rows, count, width, blocks, fast, scal, got, air, west, east):
+    any_spec = pl.BlockSpec(memory_space=pl.ANY)
+    edges = [jax.ShapeDtypeStruct((ROW0, edge_extent(count, width)[1], 128), F32)] * 2
     vmem = pl.BlockSpec(memory_space=pltpu.VMEM)
     shape = jax.ShapeDtypeStruct
     return pl.pallas_call(
@@ -332,29 +399,40 @@
             shape((2, rows, width), F32),
             shape((24, blocks * width), F32),
             shape((NPOLE, blocks * width), F32),
+        ]
+        + (edges if fast else []),
+        in_specs=[pl.BlockSpec(memory_space=pltpu.SMEM), vmem] + [any_spec] * 3,
+        out_specs=[vmem] * (5 if fast else 3),
+        scratch_shapes=[
+            pltpu.VMEM((2, rows, blocks * width), F32),
+            pltpu.SemaphoreType.DMA((6,)),
         ],
-        in_specs=[pl.BlockSpec(memory_space=pltpu.SMEM), vmem],
-        out_specs=[vmem] * 3,
-        scratch_shapes=[pltpu.VMEM((2, rows, blocks * width), F32)],
-        compiler_params=pltpu.CompilerParams(vmem_limit_bytes=VMEM_LIMIT // 2),
+        compiler_params=pltpu.CompilerParams(vmem_limit_bytes=VMEM_LIMIT),
         name="windows",
-    )(scal, got)
+    )(scal, got, air, west, east)
 
 
 def outside_kernel(rows, count, width, fast, steps, scal, *refs):
     first, last = steps[0] == 1, steps[-1] == STEPS
     if first:
-        (air, west, east, north, south, own, above, below, courant, mix), refs = refs[:10], refs[10:]
-        (state, wedge, side, sea_hist, flux_hist, sea_start, coef, gather_out), refs = (
-            refs[:8], refs[8:])
+        (air, west, east, north, south, own, courant, mix), refs = refs[:8], refs[8:]
+        (state, *hist_outs, sea_start, coef_out, gather_out), refs = refs[:8], refs[8:]
     else:
-        (state, sea_hist_in, flux_hist_in, coef, courant, mix), refs = refs[:6], refs[6:]
-        (air_out, wedge, side, sea_hist, flux_hist), refs = refs[:5], refs[5:]
-    (buf_a, buf_b, adv_a, adv_b, xcat_a, xcat_b, sea, flux, point, more, turn, pad, vcat, sems) = refs
+        (state, sea_hist_in, flux_hist_in, coef_in, courant, mix), refs = refs[:6], refs[6:]
+        (air_out, *hist_outs), refs = refs[:5], refs[5:]
+    (buf_a, buf_b, xcat_a, xcat_b, sea, flux, point, more, turn, pad, vcat, edge_seas,
+     coef, wedge, side, sea_hist, flux_hist, hist_sems, sems) = refs
     flip, polar = scal[0], scal[1]
     total = rows + 2 * ROW0
     inner = count + 2 * HALO
     lanes = lane_iota((width, 128))
+    hist = tuple(zip((wedge, side, sea_hist, flux_hist), hist_outs))
+
+    def hist_copies(n, kinds):
+        return [
+            pltpu.make_async_copy(hist[k][0].at[n], hist[k][1].at[n], hist_sems.at[4 * n + k])
+            for k in kinds
+        ]
 
     def base_of(q):
         return pl.multiple_of(8 + (q + ROW0) * width, 8)
@@ -384,27 +462,39 @@
         beyond = 8 + total * width
         for ref in (buf_a, buf_b):
             ref[0:8, :] = jnp.zeros((8, 128), F32)
-            ref[pl.ds(beyond, 3 * width + 8), :] = jnp.zeros((3 * width + 8, 128), F32)
+            ref[pl.ds(beyond, BEYOND * width + 8), :] = jnp.zeros((BEYOND * width + 8, 128), F32)
         pad[...] = jnp.zeros_like(pad)
 
     if first:
+        needed = jnp.where(polar == 1, NPOLE - 1, -ROW0)
+        at, after = edge_extent(count, width)
+        for n, ref in enumerate((north, south)):
+            pltpu.make_async_copy(
+                ref.at[:, pl.ds(at, 8)], edge_seas.at[n], sems.at[2 + n]
+            ).start()
         if fast:
             @pl.loop(0, rows)
             def _(r):
-                base = base_of(q_of(r))
-                for ref, offset, size in (
-                    (west, 0, HALO), (air, HALO, count), (east, HALO + count, HALO)
-                ):
-                    pltpu.make_async_copy(
-                        ref.at[r], buf_a.at[pl.ds(base + offset, size)], sems.at[0]
-                    ).start()
+                @pl.when(q_of(r) >= needed)
+                def _():
+                    base = base_of(q_of(r))
+                    for ref, offset, size in (
+                        (west, 0, HALO), (air, HALO, count), (east, HALO + count, HALO)
+                    ):
+                        pltpu.make_async_copy(
+                            ref.at[r], buf_a.at[pl.ds(base + offset, size)], sems.at[0]
+                        ).start()
 
             @pl.loop(0, ROW0)
             def _(r):
-                for ref, at in ((north, r - ROW0), (south, r + rows)):
-                    pltpu.make_async_copy(
-                        ref.at[r], buf_a.at[pl.ds(base_of(q_of(at)), inner)], sems.at[0]
-                    ).start()
+                for ref, place in ((north, r - ROW0), (south, r + rows)):
+                    @pl.when(q_of(place) >= needed)
+                    def _(ref=ref, place=place):
+                        pltpu.make_async_copy(
+                            ref.at[r, pl.ds(0, inner)],
+                            buf_a.at[pl.ds(base_of(q_of(place)), inner)],
+                            sems.at[0],
+                        ).start()
 
             if inner < width:
                 @pl.loop(0, total)
@@ -413,7 +503,7 @@
                         (width - inner, 128), F32
                     )
 
-            everything = buf_a.at[pl.ds(0, total * inner)]
+            extents = ((1, (rows + ROW0 - NPOLE + 1) * inner), (0, total * inner))
         else:
             @pl.loop(0, total)
             def _(e):
@@ -421,22 +511,49 @@
                     air.at[e], buf_a.at[pl.ds(base_of(q_of(e - ROW0)), width)], sems.at[0]
                 ).start()
 
-            everything = buf_a.at[pl.ds(0, total * width)]
+            extents = ((1, total * width), (0, total * width))
         begin()
+        for n, ref in enumerate((north, south)):
+            pltpu.make_async_copy(
+                ref.at[:, pl.ds(at, 8)], edge_seas.at[n], sems.at[2 + n]
+            ).wait()
+        chunks = width // 128
         for n, ref in ((0, sea), (1, coef)):
             turn[...] = jnp.zeros_like(turn)
-            for source, size, at in ((above, ROW0, -ROW0), (own, rows, 0), (below, ROW0, rows)):
-                @pl.loop(0, size)
-                def _(r, source=source, at=at):
-                    turn[pl.ds(q_of(r + at) + ROW0, 1), :] = source[n, pl.ds(r, 1), :]
+
+            @pl.loop(0, rows)
+            def _(r):
+                turn[pl.ds(q_of(r) + ROW0, 1), :] = own[n, pl.ds(r, 1), :]
+
+            for m, place in ((0, -ROW0), (1, rows)):
+                @pl.loop(0, ROW0)
+                def _(r, m=m, place=place):
+                    pieces = [
+                        edge_seas[m, r, pl.ds(n * chunks + o, 1), :] for o in range(chunks)
+                    ]
+                    turn[pl.ds(q_of(r + place) + ROW0, 1), :] = jnp.concatenate(pieces, axis=1)
 
             ref[...] = jnp.transpose(turn[...])
         sea_start[...] = sea[...]
-        pltpu.make_async_copy(everything, everything, sems.at[0]).wait()
+        coef_out[...] = coef[...]
+        for kind, extent in extents:
+            @pl.when(polar == kind)
+            def _(extent=extent):
+                whole = buf_a.at[pl.ds(0, extent)]
+                pltpu.make_async_copy(whole, whole, sems.at[0]).wait()
     else:
+        small = [
+            pltpu.make_async_copy(source, target, sems.at[1 + n])
+            for n, (source, target) in enumerate(
+                ((sea_hist_in.at[SPLIT - 1], sea), (flux_hist_in.at[SPLIT - 1], flux),
+                 (coef_in, coef))
+            )
+        ]
+        for copy in small:
+            copy.start()
         begin()
-        sea[...] = sea_hist_in[steps[0] - 2]
-        flux[...] = flux_hist_in[steps[0] - 2]
+        for copy in small:
+            copy.wait()
         row_range(
             lambda q: pltpu.make_async_copy(
                 state.at[q + ROW0], buf_a.at[pl.ds(base_of(q), width)], sems.at[0]
@@ -448,7 +565,7 @@
         gain = air_gain * pltpu.roll(flux[...], 128 - (q + ROW0), 1)
         return y + jnp.where(lanes == 0, gain, 0.0)
 
-    advs, xcats = (adv_a, adv_b), (xcat_a, xcat_b)
+    xcats = (xcat_a, xcat_b)
     cour = winds(courant)
     src, dst = buf_a, buf_b
     for n, step in enumerate(steps):
@@ -467,18 +584,28 @@
         point[...] = jnp.zeros_like(point)
 
         def load(q, slot, src=src, step=step):
-            base = base_of(q)
-            advance(width, src, base, src, base - width, src, base + width, cour[:2],
-                    advs[slot], xcats[slot], (more, 128 - (q + ROW0)) if step > 1 else None)
+            for n in range(2):
+                base = base_of(q + n)
+                shared = (more, lax.rem(128 - (q + n + ROW0), 128)) if step > 1 else None
+                advance(width, src, base, src, base - width, src, base + width, cour[:2],
+                        xcats[slot], shared, n * width)
 
         def finish(q, slot, between, dst=dst):
             mixed = dot(xcats[slot][...], vcat[...])
             between()
-            y = advs[slot][...] + mixed[:, :128] + mixed[:, 128:]
-            dst[pl.ds(base_of(q), width), :] = y
-            point[...] += pltpu.roll(jnp.where(lanes == 0, y, 0.0), q + ROW0, 1)
-
-        two_at_a_time(lo, pairs, load, finish)
+            tops = []
+            for n in range(2):
+                row = slice(n * width, (n + 1) * width)
+                y = mixed[row, :128] + mixed[row, 128:]
+                dst[pl.ds(base_of(q + n), width), :] = y
+                tops.append(pltpu.roll(jnp.where(lanes == 0, y, 0.0), q + n + ROW0, 1))
+            point[...] += tops[0] + tops[1]
+
+        two_at_a_time(lo, pairs // 2, load, finish, None, 2)
+
+        @pl.when(lax.rem(pairs, 2) == 1)
+        def _(finish=finish, lo=lo, pairs=pairs):
+            finish(lo + 2 * (pairs - 1), 0, lambda: None)
 
         total_flux = jnp.where(lanes >= lo + ROW0, coef[...] * (sea[...] - point[...]), 0.0)
         flux[...] = total_flux
@@ -486,11 +613,15 @@
         sea[...] = new_sea
         sea_hist[n] = new_sea
         flux_hist[n] = total_flux
+        for copy in hist_copies(n, (2, 3)):
+            copy.start()
         if step <= WEDGE:
             @pl.when(polar == 1)
             def _(dst=dst, step=step, n=n):
                 for ref, q in ((wedge, NPOLE + step - 1), (side, NPOLE + step)):
                     ref[n] = with_flux(dst[pl.ds(base_of(q), width), :], q)
+                for copy in hist_copies(n, (0, 1)):
+                    copy.start()
         src, dst = dst, src
 
     if first:
@@ -500,10 +631,16 @@
             ),
             steps[-1], src, width, sems.at[1],
         )
+        for n in range(len(steps)):
+            for copy in hist_copies(n, (2, 3)):
+                copy.wait()
         turned = jnp.transpose(flux_hist[0])[NPOLE + ROW0 : NPOLE + ROW0 + 8]
         for o in range(width // 128):
             gather_out[8 * o : 8 * o + 8, :] = turned[:, 128 * o : 128 * o + 128]
     else:
+        for n in range(len(steps)):
+            for copy in hist_copies(n, (2, 3)):
+                copy.wait()
         start, extent = (HALO, count) if fast else (0, width)
         first_row = jnp.where(polar == 1, NPOLE + WEDGE, 0)
 
@@ -520,6 +657,13 @@
             def _(count_rows=count_rows):
                 whole = src.at[pl.ds(0, count_rows * extent)]
                 pltpu.make_async_copy(whole, whole, sems.at[1]).wait()
+
+    @pl.when(polar == 1)
+    def _():
+        for n, step in enumerate(steps):
+            if step <= WEDGE:
+                for copy in hist_copies(n, (0, 1)):
+                    copy.wait()
 
 
 def outside_steps(rows, count, width, fast, steps, scal, big, small):
@@ -541,14 +685,12 @@
         in_specs=[pl.BlockSpec(memory_space=pltpu.SMEM)]
         + [any_spec] * len(big)
         + [vmem] * len(small),
-        out_specs=[any_spec] + [vmem] * (len(out_shape) - 1),
+        out_specs=[any_spec] * 5 + [vmem] * (len(out_shape) - 5),
         scratch_shapes=[
-            pltpu.VMEM(((total + 3) * width + 16, levels), F32),
-            pltpu.VMEM(((total + 3) * width + 16, levels), F32),
-            pltpu.VMEM((width, levels), F32),
-            pltpu.VMEM((width, levels), F32),
-            pltpu.VMEM((width, 2 * levels), BF16),
-            pltpu.VMEM((width, 2 * levels), BF16),
+            pltpu.VMEM(((total + BEYOND) * width + 16, levels), F32),
+            pltpu.VMEM(((total + BEYOND) * width + 16, levels), F32),
+            pltpu.VMEM((2 * width, 2 * levels), BF16),
+            pltpu.VMEM((2 * width, 2 * levels), BF16),
             pltpu.VMEM((width, 128), F32),
             pltpu.VMEM((width, 128), F32),
             pltpu.VMEM((width, 128), F32),
@@ -556,7 +698,13 @@
             pltpu.VMEM((128, width), F32),
             pltpu.VMEM((width + 16, 128), F32),
             pltpu.VMEM((256, 256), BF16),
-            pltpu.SemaphoreType.DMA((2,)),
+            pltpu.VMEM((2, ROW0, 8, 128), F32),
+            pltpu.VMEM((width, 128), F32),
+        ]
+        + [pltpu.VMEM((len(steps), width, 128), F32)] * 4
+        + [
+            pltpu.SemaphoreType.DMA((4 * len(steps),)),
+            pltpu.SemaphoreType.DMA((4,)),
         ],
         compiler_params=pltpu.CompilerParams(vmem_limit_bytes=VMEM_LIMIT),
         cost_estimate=pl.CostEstimate(
@@ -580,26 +728,27 @@
         names += list(range(blocks // 2))
     loads = dict(zip(names, refs[: len(names)]))
     refs = refs[len(names) :]
-    weight, courant, mix = refs[:3]
-    refs = refs[3:]
+    small_in, refs = refs[:3], refs[3:]
     if last:
         refs = refs[1:]
         (air_out, sea_out), refs = refs[:2], refs[2:]
     else:
-        (spec_out, wedge_out, sea_out, flux_out, sea_ring_out, ring_out, gather_out), refs = (
+        (spec_out, wedge_out, sea_out, flux_out, sea_ring_out, ring_out, gather_to), refs = (
             refs[:7], refs[7:])
-    (spec_a, spec_b, cur, prev, adv, xcat, kcat_a, kcat_b, kadv_a, kadv_b, point, sea, flux, pad,
+    (spec_a, spec_b, cur, prev, xcat, kcat_a, kcat_b, point, sea, flux, pad,
      ring, sea_ring, shares, t_high, t_low, stencil, coef, coef_ring, gathered, sea_hist,
-     flux_hist, side, turn, free_top, free_row, vcat, load_sems, row_sems) = refs[:32]
+     flux_hist, side, turn, free_top, free_row, vcat, weight, courant, mix, load_sems, row_sems) = refs[:32]
     if last:
         back, free_late, sems = refs[32:]
+    else:
+        gather_out, store_sems = refs[32:]
     flip, polar, block = scal[0], scal[1], scal[2]
     lanes = lane_iota((width, 128))
     own = pl.ds(pl.multiple_of(block * width, 128), width)
 
     def hist(kind, step):
-        at = cap_hists(steps).index(0 if step <= 3 else 1)
-        return hists[4 * at + kind].at[(step - 1) % 3]
+        half = 0 if step <= SPLIT else 1
+        return hists[4 * cap_hists(steps).index(half) + kind].at[step - 1 - SPLIT * half]
 
     def own_dot(x):
         return table_dot(t_high[own, :], t_low[own, :], x)
@@ -613,10 +762,10 @@
                 south_ref, south = side.at[at], 0
             else:
                 south_ref, south = cur, base + width
-            advance(width, cur, base, prev, 0, south_ref, south, winds(courant)[:2], adv, xcat)
+            advance(width, cur, base, prev, 0, south_ref, south, winds(courant)[:2], xcat)
             prev[...] = cur[pl.ds(base, width), :]
             mixed = dot(xcat[...], vcat[...])
-            y = adv[...] + mixed[:, :128] + mixed[:, 128:]
+            y = mixed[:, :128] + mixed[:, 128:]
             lane = NPOLE + j + ROW0
             out = exchange(y, lane, sea[...], coef[...])
             cur[pl.ds(base, width), :] = y + air_gain * out
@@ -642,7 +791,7 @@
             spot = lane_iota(at.shape) % width
             at = jnp.where((spot >= HALO) & (spot < HALO + count), at, 0.0)
             high, low = two_parts(at)
-            ready("t_high", "t_low", "rotate")
+            ready("t_high", "t_low", "rotate", "weight")
             both = dot(jnp.concatenate([high, low], axis=0), t_high[...])
             sums = both[:24] + both[24:] + dot(high, t_low[...])
             sums = sums * (air_gain * weight[0:1, :])
@@ -657,7 +806,7 @@
             stencil[1] = stencil[2] * courant[0:1, :]
 
         point[...] = jnp.zeros_like(point)
-        kcats, kadvs = (kcat_a, kcat_b), (kadv_a, kadv_b)
+        kcats = (kcat_a, kcat_b)
         first = lane_iota((128, 128)) == 0
 
         def load(q, slot):
@@ -676,7 +825,6 @@
                     )
                 x = jnp.where(lax.broadcasted_iota(jnp.int32, x.shape, 0) <= cut, x, 0.0)
                 high, low = two_parts(x)
-                kadvs[slot][pl.ds(o, 128), :] = x
                 kcats[slot][pl.ds(o, 128), 0:128] = high
                 kcats[slot][pl.ds(o, 128), 128:256] = low
 
@@ -685,7 +833,7 @@
         def finish(q, slot, between):
             mixed = dot(kcats[slot][...], vcat[...])
             between()
-            y = kadvs[slot][...] + mixed[:, :128] + mixed[:, 128:]
+            y = mixed[:, :128] + mixed[:, 128:]
             dst[q + 1] = y
             point[...] += pltpu.roll(jnp.where(lane_iota(y.shape) == 0, y, 0.0), q, 1)
 
@@ -703,6 +851,8 @@
         if streamed:
             for q in range(2 * pairs + 2, CAP):
                 spec_row(q).wait()
+        if step == steps[-1] and not last:
+            store(dst.at[pl.ds(1, CAP)], spec_out)
         ready("free")
         top = pltpu.roll(free_top[...], (128 - NPOLE * (step - 1)) % 128, 1)
         point[...] += jnp.where(lane_iota((NK, 128)) < NPOLE, top, 0.0)
@@ -727,6 +877,12 @@
 
     copies = {}
     order = []
+    stores = []
+
+    def store(source, target):
+        copy = pltpu.make_async_copy(source, target, store_sems.at[len(stores)])
+        stores.append(copy)
+        copy.start()
 
     def fetch(name, source, target):
         copy = pltpu.make_async_copy(source, target, load_sems.at[len(order)])
@@ -744,6 +900,8 @@
 
     @pl.when(polar == 1)
     def _():
+        for n, (source, target) in enumerate(zip(small_in, (weight, courant, mix))):
+            fetch(("weight", "courant", "mix")[n], source, target)
         if steps[0] > 1:
             fetch("gathered", loads["gathered"], gathered)
             fetch("sea_ring", loads["sea_ring"], sea_ring)
@@ -757,7 +915,6 @@
             def _(q):
                 spec_row(q).start()
 
-        mixing(mix, vcat)
         part = NK // blocks
         some = part // 2
         rows_15 = [step for step in steps if step < STEPS]
@@ -805,6 +962,8 @@
         kept = steps[0] - 1
         for j in range(kept):
             fetch("hist", loads["wedge"].at[j], cur.at[pl.ds(8 + j * width, width)])
+        ready("mix", "courant")
+        mixing(mix, vcat)
         for ref in (spec_a, spec_b):
             ref[0] = jnp.zeros((NK, 128), F32)
             for beyond in range(CAP + 1, CAP + 4):
@@ -836,12 +995,19 @@
             for j in range(WEDGE):
                 send(cur, 8 + j * width, NPOLE + j).start()
 
-            @pl.loop(0, NPOLE)
-            def _(q):
-                y = own_dot(src[q + 1] + free_late[q])
-                edge = pltpu.roll(flux[...], lax.rem(128 - ROW0 - q, 128), 1)
-                back[q] = y + air_gain * jnp.where(lanes == 0, edge, 0.0)
-                send(back.at[q], 0, q).start()
+            @pl.loop(0, NPOLE // 2)
+            def _(pair):
+                parts_of = [two_parts(src[2 * pair + n + 1] + free_late[2 * pair + n])
+                            for n in range(2)]
+                highs = jnp.concatenate([high for high, _ in parts_of], axis=1)
+                crossed = dot(t_low[own, :], highs)
+                for n, (high, low) in enumerate(parts_of):
+                    q = 2 * pair + n
+                    both = dot(t_high[own, :], jnp.concatenate([high, low], axis=1))
+                    y = both[:, :128] + both[:, 128:] + crossed[:, 128 * n : 128 * n + 128]
+                    edge = pltpu.roll(flux[...], lax.rem(128 - ROW0 - q, 128), 1)
+                    back[q] = y + air_gain * jnp.where(lanes == 0, edge, 0.0)
+                    send(back.at[q], 0, q).start()
 
             @pl.loop(0, NPOLE)
             def _(q):
@@ -850,19 +1016,13 @@
             for j in range(WEDGE):
                 send(cur, 8 + j * width, NPOLE + j).wait()
         else:
-            stores = [pltpu.make_async_copy(src.at[pl.ds(1, CAP)], spec_out, load_sems.at[0])]
             for j in range(len(wedge_steps) + kept):
-                stores.append(
-                    pltpu.make_async_copy(
-                        cur.at[pl.ds(8 + j * width, width)], wedge_out.at[j], load_sems.at[1 + j]
-                    )
-                )
-            for copy in stores:
-                copy.start()
-            sea_out[...] = sea[...]
-            flux_out[...] = flux[...]
-            sea_ring_out[...] = sea_ring[...]
-            ring_out[...] = ring[0:NPOLE, :]
+                store(cur.at[pl.ds(8 + j * width, width)], wedge_out.at[j])
+            for source, target in (
+                (sea, sea_out), (flux, flux_out), (sea_ring, sea_ring_out),
+                (ring.at[pl.ds(0, NPOLE)], ring_out), (gather_out, gather_to),
+            ):
+                store(source, target)
             for copy in stores:
                 copy.wait()
 
@@ -873,16 +1033,16 @@
             copy.start()
             copy.wait()
 
-        turn[...] = jnp.transpose(sea[...])
+        turn[...] = jnp.transpose(pltpu.roll(sea[...], width - HALO, 0))
 
         @pl.loop(0, rows)
         def _(q):
             r = jnp.where(flip == 1, rows - 1 - q, q)
-            sea_out[pl.ds(r, 1), :] = turn[pl.ds(q + ROW0, 1), :]
+            sea_out[pl.ds(r, 1), :] = turn[pl.ds(q + ROW0, 1), pl.ds(0, count)]
 
 
 def cap_hists(steps):
-    return [0] if steps[-1] < 3 else [0, 1] if steps[0] < 5 else [1]
+    return ([0] if steps[0] <= SPLIT + 1 else []) + ([1] if steps[-1] + 1 > SPLIT else [])
 
 
 def cap_steps(rows, count, width, blocks, fast, steps, scal, spec, big, small, air):
@@ -898,7 +1058,7 @@
     if last:
         out_shape = [
             shape((rows, count if fast else width, levels), F32),
-            shape((rows, width), F32),
+            shape((rows, count), F32),
         ]
         out_specs = [any_spec, vmem]
         extra = [
@@ -917,26 +1077,23 @@
             shape((NPOLE, ring_width), F32),
             shape((blocks, 16, width), F32),
         ]
-        out_specs = [any_spec] * 2 + [vmem] * 5
+        out_specs = [any_spec] * 7
+        extra = [pltpu.VMEM((blocks, 16, width), F32), pltpu.SemaphoreType.DMA((16,))]
     return pl.pallas_call(
         functools.partial(cap_kernel, rows, count, width, blocks, fast, steps, len(spec)),
         out_shape=out_shape,
         in_specs=[pl.BlockSpec(memory_space=pltpu.SMEM)]
         + [any_spec] * (len(spec) + len(big))
-        + [vmem] * len(small)
-        + [any_spec] * len(air),
+        + [any_spec] * (len(small) + len(air)),
         out_specs=out_specs,
         scratch_shapes=[
             pltpu.VMEM((CAP + 4, NK, levels), F32),
             pltpu.VMEM((CAP + 4, NK, levels), F32),
             pltpu.VMEM((WEDGE * width + 16, levels), F32),
             square,
-            square,
             pltpu.VMEM((width, 2 * levels), BF16),
             pltpu.VMEM((NK, 2 * levels), BF16),
             pltpu.VMEM((NK, 2 * levels), BF16),
-            pltpu.VMEM((NK, 128), F32),
-            pltpu.VMEM((NK, 128), F32),
             pltpu.VMEM((NK, 128), F32),
             square,
             square,
@@ -957,6 +1114,9 @@
             pltpu.VMEM((NK, 128), F32),
             pltpu.VMEM((2, NK, 128), F32),
             pltpu.VMEM((256, 256), BF16),
+            pltpu.VMEM((8, NK), F32),
+            pltpu.VMEM((1, 128), F32),
+            pltpu.VMEM((128, 128), F32),
             pltpu.SemaphoreType.DMA((9 * blocks + 32,)),
             pltpu.SemaphoreType.DMA((CAP,)),
         ]
@@ -1015,33 +1175,42 @@
     exchange_coef = jnp.where(land_sea == 1, sea_coef, land_coef).astype(F32)
     sea_blocks = sea_temp.reshape(-1, blocks, count).transpose(1, 0, 2).reshape(rows, count)
     mine = jnp.concatenate([sea_blocks, exchange_coef], 0)
-    got = spread(jnp.broadcast_to(mine[None], (blocks,) + mine.shape))
     half = blocks // 2
     keep, send = start_spectra(blocks, scal, air_temp, jnp.asarray(forward))
-    send, west, east, got = lax.optimization_barrier((send, west, east, got))
+    mine, west, east, send = lax.optimization_barrier((mine, west, east, send))
+    got = spread(jnp.broadcast_to(mine[None], (blocks,) + mine.shape))
 
     half_sum = keep + between_caps(send, 1)
 
-    def edge(part):
-        return jnp.concatenate([west[part], air_temp[part], east[part]], 1)
-
-    north = shift(edge(slice(rows - ROW0, rows)), "lat", 1, False)
-    south = shift(edge(slice(0, ROW0)), "lat", -1, False)
-    own_window, sea_ring, coef_ring = windows(rows, count, width, blocks, scal, got)
-    above = shift(own_window[:, rows - ROW0 :], "lat", 1, False)
-    below = shift(own_window[:, :ROW0], "lat", -1, False)
+    outs = windows(rows, count, width, blocks, fast, scal, got, air_temp, west, east)
+    own_window, sea_ring, coef_ring = outs[:3]
+    if fast:
+        last_rows, first_rows = outs[3:]
+    else:
+        def edge(part):
+            extra = own_window[:, part].transpose(1, 0, 2).reshape(ROW0, -1, levels)
+            at, after = edge_extent(count, width)
+            row = jnp.concatenate([west[part], air_temp[part], east[part]], 1)
+            row = jnp.pad(row, ((0, 0), (0, at - row.shape[1]), (0, 0)))
+            extra = jnp.pad(extra, ((0, 0), (0, after - at - extra.shape[1]), (0, 0)))
+            return jnp.concatenate([row, extra], 1)
+
+        last_rows, first_rows = edge(slice(rows - ROW0, rows)), edge(slice(0, ROW0))
+    north = shift(last_rows, "lat", 1, False)
+    south = shift(first_rows, "lat", -1, False)
 
     if fast:
         air = air_temp
     else:
         middle = jnp.concatenate([west, air_temp, east], 1)
-        air = jnp.concatenate([north, middle, south], 0)
+        inner = count + 2 * HALO
+        air = jnp.concatenate([north[:, :inner], middle, south[:, :inner]], 0)
         air = jnp.pad(air, ((0, 0), (0, width - count - 2 * HALO), (0, 0)))
     half_sum, own_window = lax.optimization_barrier((half_sum, own_window))
     parts = [between_caps(half_sum[j], 2 * j) for j in range(1, half)]
     outs = outside_steps(
-        rows, count, width, fast, (1, 2, 3), scal, (air, west, east, north, south),
-        (own_window, above, below, courant, vertical_mix),
+        rows, count, width, fast, tuple(range(1, SPLIT + 1)), scal, (air, west, east, north, south),
+        (own_window, courant, vertical_mix),
     )
     state, early, sea, coef, gathered = outs[0], tuple(outs[1:5]), outs[5], outs[6], outs[7]
     parts, state = lax.optimization_barrier((parts, state))
@@ -1052,8 +1221,8 @@
     late_pair = jnp.stack([late_free, between_caps(late_free, 1)])
     free = spread(gathered)
     outs = outside_steps(
-        rows, count, width, fast, (4, 5, 6), scal, (state,),
-        (early[2], early[3], coef, courant, vertical_mix),
+        rows, count, width, fast, tuple(range(SPLIT + 1, STEPS + 1)), scal,
+        (state, early[2], early[3], coef), (courant, vertical_mix),
     )
     air, late = outs[0], tuple(outs[1:5])
     free, air, late = lax.optimization_barrier((free, air, late))
@@ -1080,7 +1249,6 @@
     air, sea = outs
     if not fast:
         air = air[:, HALO : HALO + count]
-    sea = sea[:, HALO : HALO + count]
     sea = lax.all_to_all(sea, "lon", split_axis=0, concat_axis=1, tiled=True)
     return air, sea
 

time: 219 us -> 209 us (0.954)
  Pallas kernels: 112 us -> 105 us
  starting transfers between devices: 62.9 us -> 58.3 us
    all_to_all x4, waiting for transfers between devices: 9.54 us -> 16.9 us  [spread(): lax.all_to_all(copies, 'lon', split_axis=0, concat_axis=0, tiled=True)]
    ppermute x8, waiting for transfers between devices: 6.04 us -> 2.58 us  [between_caps(): return lax.ppermute(x, ('lat', 'lon'), pairs)]
    pallas_call x1, Pallas kernels: 10.8 us -> 7.52 us  [start_spectra(): pl.pallas_call(functools.partial(spectra_kernel, rows, count, blocks), ou...]
    pallas_call x3, Pallas kernels: 57.4 us -> 54.1 us  [cap_steps(): pl.pallas_call(functools.partial(cap_kernel, rows, count, width, blocks,...]
    ppermute x6 -> x4, starting transfers between devices: 12 us -> 8.72 us  [shift(): return lax.ppermute(x, axis, pairs)]
    ppermute x6 -> x4, waiting for transfers between devices: 3.07 us -> 0.01 us  [shift(): return lax.ppermute(x, axis, pairs)]
    pallas_call x1, Pallas kernels: 1.87 us -> 4.91 us  [windows(): pl.pallas_call(functools.partial(windows_kernel, rows, count, width, bloc...]
    slice x4 -> x0, local copies, waits for them, and re-layouts: 2.61 us -> none  [the longest x2 1.73 us: edge(): return jnp.concatenate([west[part], air_temp[part], east[part]], 1)]
  transfers between devices with their start and end apart: 18 -> 16, of which waited for: 5 -> 3; matrix products, arithmetic and copies ran while one was open for 2% -> 3% of each run, Pallas kernels for 32% -> 32%
where the time goes in v4:
time: 209 us; the launch traced here: 208 us
  Pallas kernels  105 us (50%)
  starting transfers between devices  58.3 us (28%)
  waiting for transfers between devices  19.5 us (9%)
  local copies, waits for them, and re-layouts  11.4 us (5%)
  blocking collectives  9.22 us (4%)
  other arithmetic  3.18 us (2%)
    pallas_call x3, Pallas kernels, cap_steps(): pl.pallas_call(functools.partial(cap_kernel, rows, count, width, blocks,...  54.1 us
    pallas_call x2, Pallas kernels, outside_steps(): pl.pallas_call(functools.partial(outside_kernel, rows, count, width, fast...  35.6 us
    ppermute x8, starting transfers between devices, between_caps(): return lax.ppermute(x, ('lat', 'lon'), pairs)  28.2 us
    all_to_all x4, starting transfers between devices, spread(): lax.all_to_all(copies, 'lon', split_axis=0, concat_axis=0, tiled=True)  21.4 us
    all_to_all x4, waiting for transfers between devices, spread(): lax.all_to_all(copies, 'lon', split_axis=0, concat_axis=0, tiled=True)  16.9 us
    all_to_all x1, blocking collectives, local(): sea = lax.all_to_all(sea, 'lon', split_axis=0, concat_axis=1, tiled=True)  9.22 us
    ppermute x4, starting transfers between devices, shift(): return lax.ppermute(x, axis, pairs)  8.72 us
    pallas_call x1, Pallas kernels, start_spectra(): pl.pallas_call(functools.partial(spectra_kernel, rows, count, blocks), ou...  7.52 us
  transfers between devices with their start and end apart: 16, of which 3 were waited for; matrix products, arithmetic and copies ran while one was open for 3% of the time, Pallas kernels for 32%

profile of v4, /device:TPU:0, one launch (start us, length us, event | category | flops | bytes accessed | tf_op | source)
XLA Modules:
  0.0 207.6 jit_solution(13387744562115666165)
XLA Ops:
  0.6 1.0 fusion
  1.6 6.1 %collective-permute-start.1 = (f32[32,8,128]{2,1,0:T(8,128)S(1)}, f32[32,8,128]{2,1,0:T(8,128)S(1)}, u32[]{:S(2)}, u32[]{:S(2)}) collective-permute-start(f32[32,8,128]{2,1,0:T(8,128)S(1)} %get-tuple-element.118), channel_id=1, source_target_pairs={{0,7},{1,0},{2,1},{3,2},{4,3},{5,4},{6,5},{7,6},{8,15},{9,8},{10,9... | collective-permute-start | bytes 393224 | tf_op jit(solution)/shard_map/ppermute | solution.py:1138
  7.7 0.0 collective-permute-start
  7.7 0.7 slice.27
  8.4 0.1 slice.28
  8.5 0.8 compare_select_fusion
  9.3 0.7 broadcast_select_fusion
  10.0 0.9 reshape.17
  10.9 0.7 concatenate.6.scal
  11.6 7.5 %start_spectra.1 = (f32[4,22,32,128]{3,2,1,0:T(8,128)}, f32[4,22,32,128]{3,2,1,0:T(8,128)}) custom-call(s32[29]{0:T(128)} %concatenate.6.scal, f32[32,360,128]{2,1,0:T(8,128)} %refs_0_.1, bf16[8,256,1152]{2,1,0:T(8,128)(2,1)} %constant.37.clone.table), custom_call_target="tpu_custom_call" | custom-call | tf_op jit(solution)/shard_map/start_spectra/pallas_call | solution.py:194
  19.1 0.0 collective-permute-done.1.east.refs_2_
  19.2 0.0 collective-permute-done.west.refs_1_
  19.2 0.0 copy-start.14
  19.2 1.0 broadcast_in_dim.16
  20.1 6.0 %all-to-all-start = ((f32[8,64,360]{2,1,0:T(8,128)}), f32[8,64,360]{2,1,0:T(8,128)S(1)}, u32[]{:S(2)}, u32[]{:S(2)}) async-start(f32[8,64,360]{2,1,0:T(8,128)} %broadcast_in_dim.16), calls=%async_computation | async-start | bytes 1572864 | tf_op jit(solution)/shard_map/all_to_all | solution.py:1148
  26.2 4.0 %collective-permute-start.4 = (f32[4,22,32,128]{3,2,1,0:T(8,128)}, f32[4,22,32,128]{3,2,1,0:T(8,128)}, u32[]{:S(2)}, u32[]{:S(2)}) collective-permute-start(f32[4,22,32,128]{3,2,1,0:T(8,128)} %get-tuple-element.67), channel_id=1, source_target_pairs={{0,1},{1,0},{2,3},{3,2},{4,5},{5,4},{6,7},{7,6},{24,25},{25,24},{2... | collective-permute-start | bytes 4325384 | tf_op jit(solution)/shard_map/ppermute | solution.py:1144
  30.2 9.2 %all-to-all-done.got = f32[8,64,360]{2,1,0:T(8,128)S(1)} async-done(((f32[8,64,360]{2,1,0:T(8,128)}), f32[8,64,360]{2,1,0:T(8,128)S(1)}, u32[]{:S(2)}, u32[]{:S(2)}) %all-to-all-start) | async-done | bytes 737312 | tf_op jit(solution)/shard_map/all_to_all | solution.py:1148
  39.4 0.0 copy-done.14
  39.4 0.9 copy-done.6
  40.3 4.9 %windows.1 = (f32[2,32,384]{2,1,0:T(8,128)}, f32[24,3072]{1,0:T(8,128)}, f32[16,3072]{1,0:T(8,128)}, f32[6,384,128]{2,1,0:T(8,128)}, f32[6,384,128]{2,1,0:T(8,128)}) custom-call(s32[29]{0:T(128)} %concatenate.6.scal, f32[8,64,360]{2,1,0:T(8,128)} %copy-done.6, f32[32,360,128]{2,1,0:T(8,128)} %refs_0_.1, f32[32,8,128]{2,1,0:T(8,128)} %copy-done.14, ...), custom_call_target="tpu_custom_call" | custom-call | tf_op jit(solution)/shard_map/windows/pallas_call | solution.py:396
  45.2 1.4 collective-permute-start.2
  46.6 1.3 collective-permute-start.3
  47.9 2.6 %collective-permute-done.4 = f32[4,22,32,128]{3,2,1,0:T(8,128)} collective-permute-done((f32[4,22,32,128]{3,2,1,0:T(8,128)}, f32[4,22,32,128]{3,2,1,0:T(8,128)}, u32[]{:S(2)}, u32[]{:S(2)}) %collective-permute-start.4) | collective-permute-done | bytes 1441824 | tf_op jit(solution)/shard_map/ppermute | solution.py:1144
  50.5 1.7 add.3
  52.1 0.1 slice_bitcast_fusion
  52.2 5.5 %collective-permute-start.7 = (f32[22,32,128]{2,1,0:T(8,128)S(1)}, f32[22,32,128]{2,1,0:T(8,128)S(1)}, u32[]{:S(2)}, u32[]{:S(2)}) collective-permute-start(f32[22,32,128]{2,1,0:T(8,128)S(1)} %get-tuple-element.120), channel_id=1, source_target_pairs={{0,6},{1,7},{2,4},{3,5},{4,2},{5,3},{6,0},{7,1},{24,30},{25,31},{2... | collective-permute-start | bytes 1081352 | tf_op jit(solution)/shard_map/ppermute | solution.py:1144
  57.7 1.9 collective-permute-start.6
  59.6 2.7 %collective-permute-start.5 = (f32[22,32,128]{2,1,0:T(8,128)S(1)}, f32[22,32,128]{2,1,0:T(8,128)S(1)}, u32[]{:S(2)}, u32[]{:S(2)}) collective-permute-start(f32[22,32,128]{2,1,0:T(8,128)S(1)} %get-tuple-element.122), channel_id=1, source_target_pairs={{0,2},{1,3},{2,0},{3,1},{4,6},{5,7},{6,4},{7,5},{24,26},{25,27},{2... | collective-permute-start | bytes 1081352 | tf_op jit(solution)/shard_map/ppermute | solution.py:1144
  62.4 0.0 collective-permute-done.2.refs_3_
  62.4 0.0 copy-start.9
  62.4 0.0 collective-permute-done.3.refs_4_
  62.4 1.0 copy-done.9
  63.4 0.4 copy-done.10
  63.8 15.2 %outside_steps.2 = (f32[44,384,128]{2,1,0:T(8,128)}, f32[2,384,128]{2,1,0:T(8,128)}, f32[2,384,128]{2,1,0:T(8,128)}, f32[2,384,128]{2,1,0:T(8,128)}, f32[2,384,1...) custom-call(s32[29]{0:T(128)} %concatenate.6.scal, f32[32,360,128]{2,1,0:T(8,128)} %refs_0_.1, ...), custom_call_target="tpu_custom_call" | custom-call | flops 1610612736 | bytes 15728640 | tf_op jit(solution)/shard_map/outside_steps/pallas_call | solution.py:682
  79.0 0.0 collective-permute-done.7.refs_3_
  79.1 0.0 collective-permute-done.6.refs_2_
  79.1 0.0 collective-permute-done.5.refs_1_
  79.1 0.0 copy-start.4
  79.1 0.7 copy-done.4
  79.8 2.8 %free_steps.1 = (f32[8,216,128]{2,1,0:T(8,128)}, f32[16,32,128]{2,1,0:T(8,128)S(1)}) custom-call(s32[29]{0:T(128)S(1)} %copy-done.2, f32[22,32,128]{2,1,0:T(8,128)S(1)} %get-tuple-element.123.refs_0_, f32[22,32,128]{2,1,0:T(8,128)S(1)} %collective-permute-done.5.refs_1_, f32[22,32,128]{2,1,0:T(8,128)S(1)} %collective-permute-done.6.refs_2_, ...), custom_call_target="tpu_custom_call" | custom-call | tf_op jit(solution)/shard_map/free_steps/pallas_call | solution.py:263
  82.7 4.8 %all-to-all-start.1 = ((f32[8,216,128]{2,1,0:T(8,128)}), f32[8,216,128]{2,1,0:T(8,128)S(1)}, u32[]{:S(2)}, u32[]{:S(2)}) async-start(f32[8,216,128]{2,1,0:T(8,128)} %get-tuple-element.82), calls=%async_computation.1 | async-start | bytes 1769472 | tf_op jit(solution)/shard_map/all_to_all | solution.py:1148
  87.5 3.9 %collective-permute-start.8 = (f32[16,32,128]{2,1,0:T(8,128)S(1)}, f32[16,32,128]{2,1,0:T(8,128)S(1)}, u32[]{:S(2)}, u32[]{:S(2)}) collective-permute-start(f32[16,32,128]{2,1,0:T(8,128)S(1)} %get-tuple-element.101), channel_id=1, source_target_pairs={{0,1},{1,0},{2,3},{3,2},{4,5},{5,4},{6,7},{7,6},{24,25},{25,24},{2... | collective-permute-start | bytes 786440 | tf_op jit(solution)/shard_map/ppermute | solution.py:1144
  91.4 20.4 %outside_steps.3 = (f32[32,360,128]{2,1,0:T(8,128)}, f32[4,384,128]{2,1,0:T(8,128)}, f32[4,384,128]{2,1,0:T(8,128)}, f32[4,384,128]{2,1,0:T(8,128)}, f32[4,384,128]{2,1,0:T(8,128)}) custom-call(s32[29]{0:T(128)} %concatenate.6.scal, f32[44,384,128]{2,1,0:T(8,128)} %get-tuple-element.83.refs_0_, f32[2,384,128]{2,1,0:T(8,128)} %get-tuple-element.72.refs_1_.refs_2_.refs_3_, ...), custom_call_target="tpu_custom_call" | custom-call | flops 3221225472 | bytes 15728640 | tf_op jit(solution)/shard_map/outside_steps/pallas_call | solution.py:682
  111.8 0.0 collective-permute-done.8
  111.9 0.0 all-to-all-done.1.refs_8_.refs_9_.refs_5_
  111.9 1.0 copy-done.5
  112.9 14.9 %cap_steps.3 = (f32[22,256,128]{2,1,0:T(8,128)}, f32[2,384,128]{2,1,0:T(8,128)}, f32[384,128]{1,0:T(8,128)}, f32[384,128]{1,0:T(8,128)}, f32[24,3072]{1,0:T(8,12...) custom-call(s32[29]{0:T(128)} %concatenate.6.scal, f32[2,384,128]{2,1,0:T(8,128)} %get-tuple-element.70.refs_0_.refs_1_, ...), custom_call_target="tpu_custom_call" | custom-call | flops 738197504 | bytes 20000000 | tf_op jit(solution)/shard_map/cap_steps/pallas_call | solution.py:1082
  127.8 4.6 %all-to-all-start.2 = ((f32[8,16,384]{2,1,0:T(8,128)}), f32[8,16,384]{2,1,0:T(8,128)S(1)}, u32[]{:S(2)}, u32[]{:S(2)}) async-start(f32[8,16,384]{2,1,0:T(8,128)} %get-tuple-element.103), calls=%async_computation.2 | async-start | bytes 393216 | tf_op jit(solution)/shard_map/all_to_all | solution.py:1148
  132.3 5.7 %collective-permute-start.11 = (f32[2,16,32,128]{3,2,1,0:T(8,128)S(1)}, f32[2,16,32,128]{3,2,1,0:T(8,128)S(1)}, u32[]{:S(2)}, u32[]{:S(2)}) collective-permute-start(f32[2,16,32,128]{3,2,1,0:T(8,128)S(1)} %pad_maximum_fusion.refs_17_), channel_id=1, source_target_pairs={{0,6},{1,7},{2,4},{3,5},{4,2},{5,3},{6,0},{7,1},{24,30},{25,31},{2... | collective-permute-start | bytes 1572872 | tf_op jit(solution)/shard_map/ppermute | solution.py:1144
  138.1 1.9 collective-permute-start.10
  140.0 2.5 %collective-permute-start.9 = (f32[2,16,32,128]{3,2,1,0:T(8,128)S(1)}, f32[2,16,32,128]{3,2,1,0:T(8,128)S(1)}, u32[]{:S(2)}, u32[]{:S(2)}) collective-permute-start(f32[2,16,32,128]{3,2,1,0:T(8,128)S(1)} %pad_maximum_fusion.refs_17_), channel_id=1, source_target_pairs={{0,2},{1,3},{2,0},{3,1},{4,6},{5,7},{6,4},{7,5},{24,26},{25,27},{2... | collective-permute-start | bytes 1572872 | tf_op jit(solution)/shard_map/ppermute | solution.py:1144
  142.5 0.0 all-to-all-done.2.refs_17_
  142.5 0.7 copy-done.12
  143.2 18.7 %cap_steps.4 = (f32[22,256,128]{2,1,0:T(8,128)}, f32[4,384,128]{2,1,0:T(8,128)}, f32[384,128]{1,0:T(8,128)}, f32[384,128]{1,0:T(8,128)}, f32[24,3072]{1,0:T(8,12...) custom-call(s32[29]{0:T(128)} %concatenate.6.scal, f32[22,256,128]{2,1,0:T(8,128)} %get-tuple-element.98.refs_0_, ...), custom_call_target="tpu_custom_call" | custom-call | flops 738197504 | bytes 20000000 | tf_op jit(solution)/shard_map/cap_steps/pallas_call | solution.py:1082
  161.9 6.0 %all-to-all-start.3 = ((f32[8,16,384]{2,1,0:T(8,128)}), f32[8,16,384]{2,1,0:T(8,128)S(1)}, u32[]{:S(2)}, u32[]{:S(2)}) async-start(f32[8,16,384]{2,1,0:T(8,128)} %get-tuple-element.110), calls=%async_computation.3 | async-start | bytes 393216 | tf_op jit(solution)/shard_map/all_to_all | solution.py:1148
  167.9 0.0 collective-permute-done.11.refs_20_
  167.9 0.0 collective-permute-done.10.refs_19_
  167.9 0.0 collective-permute-done.9.refs_18_
  167.9 7.7 %all-to-all-done.3.refs_13_ = f32[8,16,384]{2,1,0:T(8,128)S(1)} async-done(((f32[8,16,384]{2,1,0:T(8,128)}), f32[8,16,384]{2,1,0:T(8,128)S(1)}, u32[]{:S(2)}, u32[]{:S(2)}) %all-to-all-start.3) | async-done | bytes 196640 | tf_op jit(solution)/shard_map/all_to_all | solution.py:1148
  175.7 0.7 copy-done.11
  176.3 20.5 %cap_steps.5 = (f32[32,360,128]{2,1,0:T(8,128)}, f32[32,360]{1,0:T(8,128)}) custom-call(s32[29]{0:T(128)} %concatenate.6.scal, f32[22,256,128]{2,1,0:T(8,128)} %get-tuple-element.107.refs_0_, f32[4,384,128]{2,1,0:T(8,128)} %get-tuple-element.90.refs_4_.refs_5_.refs_1_, ...), custom_call_target="tpu_custom_call", output_to_operand_aliasing={{0}: (25, {})} | custom-call | flops 738197504 | bytes 20000000 | tf_op jit(solution)/shard_map/cap_steps/pallas_call | solution.py:1082
  196.8 0.8 all_to_all.30
  197.6 9.2 %all_to_all.39 = f32[8,4,360]{2,1,0:T(4,128)S(1)} all-to-all(f32[8,4,360]{2,1,0:T(4,128)S(1)} %all_to_all.30), channel_id=1, replica_groups=mesh['lat'=4,'lon'=8] {'lon'}, dimensions={0} | all-to-all | bytes 92160 | tf_op jit(solution)/shard_map/all_to_all | solution.py:1252
  206.9 0.7 all_to_all.33
  (31 shorter events, 0.1 us)
Async XLA Ops:
  1.6 17.5 %collective-permute-start.1 = (f32[32,8,128]{2,1,0:T(8,128)S(1)}, f32[32,8,128]{2,1,0:T(8,128)S(1)}, u32[]{:S(2)}, u32[]{:S(2)}) collective-permute-start(f32[32,8,128]{2,1,0:T(8,128)S(1)} %get-tuple-element.118), channel_id=1, source_target_pairs={{0,7},{1,0},{2,1},{3,2},{4,3},{5,4},{6,5},{7,6},{8,15},{9,8},{10,9... | collective-permute-start | bytes 393224 | tf_op jit(solution)/shard_map/ppermute | solution.py:1138
  7.7 11.5 %collective-permute-start = (f32[32,8,128]{2,1,0:T(8,128)S(1)}, f32[32,8,128]{2,1,0:T(8,128)S(1)}, u32[]{:S(2)}, u32[]{:S(2)}) collective-permute-start(f32[32,8,128]{2,1,0:T(8,128)S(1)} %get-tuple-element.119), channel_id=1, source_target_pairs={{0,1},{1,2},{2,3},{3,4},{4,5},{5,6},{6,7},{7,0},{8,9},{9,10},{10,1... | collective-permute-start | bytes 393224 | tf_op jit(solution)/shard_map/ppermute | solution.py:1138
  19.2 20.2 %copy-start.13 = (f32[32,8,128]{2,1,0:T(8,128)}, f32[32,8,128]{2,1,0:T(8,128)S(1)}, u32[]{:S(2)}) copy-start(f32[32,8,128]{2,1,0:T(8,128)S(1)} %collective-permute-done.1.east.refs_2_) | copy-start | bytes 393220
  19.2 20.2 %copy-start.14 = (f32[32,8,128]{2,1,0:T(8,128)}, f32[32,8,128]{2,1,0:T(8,128)S(1)}, u32[]{:S(2)}) copy-start(f32[32,8,128]{2,1,0:T(8,128)S(1)} %collective-permute-done.west.refs_1_) | copy-start | bytes 393220
  20.1 19.2 %all-to-all-start = ((f32[8,64,360]{2,1,0:T(8,128)}), f32[8,64,360]{2,1,0:T(8,128)S(1)}, u32[]{:S(2)}, u32[]{:S(2)}) async-start(f32[8,64,360]{2,1,0:T(8,128)} %broadcast_in_dim.16), calls=%async_computation | async-start | bytes 1572864 | tf_op jit(solution)/shard_map/all_to_all | solution.py:1148
  26.1 24.3 %copy-start.8 = (f32[4,22,32,128]{3,2,1,0:T(8,128)S(1)}, f32[4,22,32,128]{3,2,1,0:T(8,128)}, u32[]{:S(2)}) copy-start(f32[4,22,32,128]{3,2,1,0:T(8,128)} %get-tuple-element.66) | copy-start | bytes 4325380
  26.2 24.3 %collective-permute-start.4 = (f32[4,22,32,128]{3,2,1,0:T(8,128)}, f32[4,22,32,128]{3,2,1,0:T(8,128)}, u32[]{:S(2)}, u32[]{:S(2)}) collective-permute-start(f32[4,22,32,128]{3,2,1,0:T(8,128)} %get-tuple-element.67), channel_id=1, source_target_pairs={{0,1},{1,0},{2,3},{3,2},{4,5},{5,4},{6,7},{7,6},{24,25},{25,24},{2... | collective-permute-start | bytes 4325384 | tf_op jit(solution)/shard_map/ppermute | solution.py:1144
  39.4 0.9 copy-start.6
  45.2 17.2 %collective-permute-start.2 = (f32[6,384,128]{2,1,0:T(8,128)}, f32[6,384,128]{2,1,0:T(8,128)S(1)}, u32[]{:S(2)}, u32[]{:S(2)}) collective-permute-start(f32[6,384,128]{2,1,0:T(8,128)} %get-tuple-element.64), channel_id=1, source_target_pairs={{0,8},{8,16},{16,24},{1,9},{9,17},{17,25},{2,10},{10,18},{18,26},{... | collective-permute-start | bytes 3538952 | tf_op jit(solution)/shard_map/ppermute | solution.py:1138
  46.6 15.8 %collective-permute-start.3 = (f32[6,384,128]{2,1,0:T(8,128)}, f32[6,384,128]{2,1,0:T(8,128)S(1)}, u32[]{:S(2)}, u32[]{:S(2)}) collective-permute-start(f32[6,384,128]{2,1,0:T(8,128)} %get-tuple-element.65), channel_id=1, source_target_pairs={{8,0},{16,8},{24,16},{9,1},{17,9},{25,17},{10,2},{18,10},{26,18},{... | collective-permute-start | bytes 3538952 | tf_op jit(solution)/shard_map/ppermute | solution.py:1138
  52.2 26.8 %collective-permute-start.7 = (f32[22,32,128]{2,1,0:T(8,128)S(1)}, f32[22,32,128]{2,1,0:T(8,128)S(1)}, u32[]{:S(2)}, u32[]{:S(2)}) collective-permute-start(f32[22,32,128]{2,1,0:T(8,128)S(1)} %get-tuple-element.120), channel_id=1, source_target_pairs={{0,6},{1,7},{2,4},{3,5},{4,2},{5,3},{6,0},{7,1},{24,30},{25,31},{2... | collective-permute-start | bytes 1081352 | tf_op jit(solution)/shard_map/ppermute | solution.py:1144
  57.7 21.3 %collective-permute-start.6 = (f32[22,32,128]{2,1,0:T(8,128)S(1)}, f32[22,32,128]{2,1,0:T(8,128)S(1)}, u32[]{:S(2)}, u32[]{:S(2)}) collective-permute-start(f32[22,32,128]{2,1,0:T(8,128)S(1)} %get-tuple-element.121), channel_id=1, source_target_pairs={{0,4},{1,5},{2,6},{3,7},{4,0},{5,1},{6,2},{7,3},{24,28},{25,29},{2... | collective-permute-start | bytes 1081352 | tf_op jit(solution)/shard_map/ppermute | solution.py:1144
  59.6 19.4 %collective-permute-start.5 = (f32[22,32,128]{2,1,0:T(8,128)S(1)}, f32[22,32,128]{2,1,0:T(8,128)S(1)}, u32[]{:S(2)}, u32[]{:S(2)}) collective-permute-start(f32[22,32,128]{2,1,0:T(8,128)S(1)} %get-tuple-element.122), channel_id=1, source_target_pairs={{0,2},{1,3},{2,0},{3,1},{4,6},{5,7},{6,4},{7,5},{24,26},{25,27},{2... | collective-permute-start | bytes 1081352 | tf_op jit(solution)/shard_map/ppermute | solution.py:1144
  62.4 1.0 copy-start.9
  62.4 1.4 copy-start.10
  63.8 15.3 %copy-start = (f32[128,128]{1,0:T(8,128)S(1)}, f32[128,128]{1,0:T(8,128)}, u32[]{:S(2)}) copy-start(f32[128,128]{1,0:T(8,128)} %refs_23_.3) | copy-start | bytes 196612
  63.8 15.3 %copy-start.1 = (f32[2,256,128]{2,1,0:T(8,128)S(1)}, f32[2,256,128]{2,1,0:T(8,128)}, u32[]{:S(2)}) copy-start(f32[2,256,128]{2,1,0:T(8,128)} %constant.34.clone.refs_4_) | copy-start | bytes 786436
  63.8 15.3 %copy-start.2 = (s32[29]{0:T(128)S(1)}, s32[29]{0:T(128)}, u32[]{:S(2)}) copy-start(s32[29]{0:T(128)} %concatenate.6.scal) | copy-start | bytes 352
  63.8 15.3 %copy-start.3 = (f32[128]{0:T(128)S(1)}, f32[128]{0:T(128)}, u32[]{:S(2)}) copy-start(f32[128]{0:T(128)} %param.15) | copy-start | bytes 1540
  79.1 0.7 copy-start.4
  82.7 29.2 %all-to-all-start.1 = ((f32[8,216,128]{2,1,0:T(8,128)}), f32[8,216,128]{2,1,0:T(8,128)S(1)}, u32[]{:S(2)}, u32[]{:S(2)}) async-start(f32[8,216,128]{2,1,0:T(8,128)} %get-tuple-element.82), calls=%async_computation.1 | async-start | bytes 1769472 | tf_op jit(solution)/shard_map/all_to_all | solution.py:1148
  87.5 24.3 %collective-permute-start.8 = (f32[16,32,128]{2,1,0:T(8,128)S(1)}, f32[16,32,128]{2,1,0:T(8,128)S(1)}, u32[]{:S(2)}, u32[]{:S(2)}) collective-permute-start(f32[16,32,128]{2,1,0:T(8,128)S(1)} %get-tuple-element.101), channel_id=1, source_target_pairs={{0,1},{1,0},{2,3},{3,2},{4,5},{5,4},{6,7},{7,6},{24,25},{25,24},{2... | collective-permute-start | bytes 786440 | tf_op jit(solution)/shard_map/ppermute | solution.py:1144
  111.8 28.1 %copy-start.7 = (f32[2,16,32,128]{3,2,1,0:T(8,128)}, f32[2,16,32,128]{3,2,1,0:T(8,128)S(1)}, u32[]{:S(2)}) copy-start(f32[2,16,32,128]{3,2,1,0:T(8,128)S(1)} %pad_maximum_fusion.refs_17_) | copy-start | bytes 1572868
  111.9 1.0 copy-start.5
  127.8 14.7 %all-to-all-start.2 = ((f32[8,16,384]{2,1,0:T(8,128)}), f32[8,16,384]{2,1,0:T(8,128)S(1)}, u32[]{:S(2)}, u32[]{:S(2)}) async-start(f32[8,16,384]{2,1,0:T(8,128)} %get-tuple-element.103), calls=%async_computation.2 | async-start | bytes 393216 | tf_op jit(solution)/shard_map/all_to_all | solution.py:1148
  132.3 35.5 %collective-permute-start.11 = (f32[2,16,32,128]{3,2,1,0:T(8,128)S(1)}, f32[2,16,32,128]{3,2,1,0:T(8,128)S(1)}, u32[]{:S(2)}, u32[]{:S(2)}) collective-permute-start(f32[2,16,32,128]{3,2,1,0:T(8,128)S(1)} %pad_maximum_fusion.refs_17_), channel_id=1, source_target_pairs={{0,6},{1,7},{2,4},{3,5},{4,2},{5,3},{6,0},{7,1},{24,30},{25,31},{2... | collective-permute-start | bytes 1572872 | tf_op jit(solution)/shard_map/ppermute | solution.py:1144
  138.1 29.8 %collective-permute-start.10 = (f32[2,16,32,128]{3,2,1,0:T(8,128)S(1)}, f32[2,16,32,128]{3,2,1,0:T(8,128)S(1)}, u32[]{:S(2)}, u32[]{:S(2)}) collective-permute-start(f32[2,16,32,128]{3,2,1,0:T(8,128)S(1)} %pad_maximum_fusion.refs_17_), channel_id=1, source_target_pairs={{0,4},{1,5},{2,6},{3,7},{4,0},{5,1},{6,2},{7,3},{24,28},{25,29},{2... | collective-permute-start | bytes 1572872 | tf_op jit(solution)/shard_map/ppermute | solution.py:1144
  140.0 27.9 %collective-permute-start.9 = (f32[2,16,32,128]{3,2,1,0:T(8,128)S(1)}, f32[2,16,32,128]{3,2,1,0:T(8,128)S(1)}, u32[]{:S(2)}, u32[]{:S(2)}) collective-permute-start(f32[2,16,32,128]{3,2,1,0:T(8,128)S(1)} %pad_maximum_fusion.refs_17_), channel_id=1, source_target_pairs={{0,2},{1,3},{2,0},{3,1},{4,6},{5,7},{6,4},{7,5},{24,26},{25,27},{2... | collective-permute-start | bytes 1572872 | tf_op jit(solution)/shard_map/ppermute | solution.py:1144
  142.5 0.7 copy-start.12
  161.9 13.8 %all-to-all-start.3 = ((f32[8,16,384]{2,1,0:T(8,128)}), f32[8,16,384]{2,1,0:T(8,128)S(1)}, u32[]{:S(2)}, u32[]{:S(2)}) async-start(f32[8,16,384]{2,1,0:T(8,128)} %get-tuple-element.110), calls=%async_computation.3 | async-start | bytes 393216 | tf_op jit(solution)/shard_map/all_to_all | solution.py:1148
  167.9 7.8 %copy-start.15 = (f32[2,16,32,128]{3,2,1,0:T(8,128)}, f32[2,16,32,128]{3,2,1,0:T(8,128)S(1)}, u32[]{:S(2)}) copy-start(f32[2,16,32,128]{3,2,1,0:T(8,128)S(1)} %collective-permute-done.11.refs_20_) | copy-start | bytes 1572868
  167.9 7.8 %copy-start.16 = (f32[2,16,32,128]{3,2,1,0:T(8,128)}, f32[2,16,32,128]{3,2,1,0:T(8,128)S(1)}, u32[]{:S(2)}) copy-start(f32[2,16,32,128]{3,2,1,0:T(8,128)S(1)} %collective-permute-done.10.refs_19_) | copy-start | bytes 1572868
  167.9 7.7 %copy-start.17 = (f32[2,16,32,128]{3,2,1,0:T(8,128)}, f32[2,16,32,128]{3,2,1,0:T(8,128)S(1)}, u32[]{:S(2)}) copy-start(f32[2,16,32,128]{3,2,1,0:T(8,128)S(1)} %collective-permute-done.9.refs_18_) | copy-start | bytes 1572868
  175.7 0.7 copy-start.11

commit v5 on v4

--- a/solution.py
+++ b/solution.py
@@ -112,6 +112,23 @@
     return [diffusion_rate + sign * 0.5 * x for x in (c, top) for sign in (-1.0, 1.0)]
 
 
+class Place:
+    def __init__(self, cutoffs):
+        band, bands = lax.axis_index("lat"), lax.axis_size("lat")
+        flip = (band == bands - 1).astype(jnp.int32)
+        polar = jnp.maximum(flip, (band == 0).astype(jnp.int32))
+        self.cutoffs = cutoffs
+        self.head = (flip, polar, lax.axis_index("lon"))
+
+    def __getitem__(self, at):
+        if isinstance(at, int) and at < 3:
+            return self.head[at]
+        q = at - 3
+        inside = jnp.minimum(q, NPOLE - 1)
+        r = jnp.where(self.head[0] == 1, 2 * NPOLE - 1 - inside, inside)
+        return jnp.where(q < NPOLE, self.cutoffs[r], KMAX)
+
+
 def lane_iota(shape):
     return lax.broadcasted_iota(jnp.int32, shape, len(shape) - 1)
 
@@ -121,6 +138,7 @@
     scal, air, table, keep_out, send_out,
     held, own_table, stacked_a, stacked_b, sums, keep, send, sems,
 ):
+    scal = Place(scal)
     depth = stacked_a.shape[0] // 3
     half, part = blocks // 2, NK // blocks
     flip, block = scal[0], scal[2]
@@ -212,6 +230,7 @@
 
 
 def free_kernel(blocks, parts, scal, *refs):
+    scal = Place(scal)
     sums, refs = refs[:parts], refs[parts:]
     rotate, courant, mix, edge, early, late, state, mask, xcat, vcat = refs
     part = NK // blocks
@@ -328,7 +347,31 @@
     return jnp.where((lane >= first) & (lane < rows + 2 * ROW0), new, 0.0)
 
 
+def share_kernel(rows, count, blocks, sea, land, out):
+    per = rows // blocks
+    for i in range(blocks):
+        piece = sea[:, i * count : (i + 1) * count]
+        for to in range(blocks):
+            out[to, i * per : (i + 1) * per, :] = piece
+    coef = jnp.where(land[...] == 1, sea_coef, land_coef).astype(F32)
+    for to in range(blocks):
+        out[to, rows:, :] = coef
+
+
+def shares_of_sea(rows, count, blocks, sea, land):
+    vmem = pl.BlockSpec(memory_space=pltpu.VMEM)
+    return pl.pallas_call(
+        functools.partial(share_kernel, rows, count, blocks),
+        out_shape=jax.ShapeDtypeStruct((blocks, 2 * rows, count), F32),
+        in_specs=[vmem, vmem],
+        out_specs=vmem,
+        compiler_params=pltpu.CompilerParams(vmem_limit_bytes=VMEM_LIMIT // 4),
+        name="shares_of_sea",
+    )(sea, land)
+
+
 def windows_kernel(rows, count, width, blocks, scal, got, air, west, east, *refs):
+    scal = Place(scal)
     own, ring_sea, ring_coef = refs[:3]
     wide, sems = refs[-2:]
     edges = list(zip(refs[3:-2], (rows - ROW0, 0)))
@@ -413,6 +456,7 @@
 
 
 def outside_kernel(rows, count, width, fast, steps, scal, *refs):
+    scal = Place(scal)
     first, last = steps[0] == 1, steps[-1] == STEPS
     if first:
         (air, west, east, north, south, own, courant, mix), refs = refs[:8], refs[8:]
@@ -717,6 +761,7 @@
 
 
 def cap_kernel(rows, count, width, blocks, fast, steps, parts, scal, *refs):
+    scal = Place(scal)
     last = steps[-1] == STEPS
     wedge_steps = [step + 1 for step in steps if step < STEPS]
     spec_in, refs = refs[:parts], refs[parts:]
@@ -1150,18 +1195,13 @@
 
 def local(air_temp, sea_temp, land_sea, courant, vertical_mix, cutoffs):
     rows, count, levels = air_temp.shape
-    blocks, bands = lax.axis_size("lon"), lax.axis_size("lat")
+    blocks = lax.axis_size("lon")
     nlon = blocks * count
     width = round_up(count + 2 * HALO, 128)
     depth = round_up(count, 128)
     fast = count % 8 == 0
-    band, block = lax.axis_index("lat"), lax.axis_index("lon")
-    flip = band == bands - 1
-    polar = (band == 0) | flip
-
-    cut = jnp.where(flip, cutoffs[::-1][:NPOLE], cutoffs[:NPOLE])
-    head = jnp.stack([flip, polar, block]).astype(jnp.int32)
-    scal = jnp.concatenate([head, cut, jnp.full((STEPS + 4,), KMAX, jnp.int32)])
+    scal = cutoffs
+
     window, forward, weight = tables(blocks, count, width, depth)
     t_high, t_low = (jnp.asarray(part) for part in window)
     rotate = rotations(nlon)
@@ -1172,15 +1212,14 @@
 
     west = shift(air_temp[:, count - HALO :], "lon", 1, True)
     east = shift(air_temp[:, :HALO], "lon", -1, True)
-    exchange_coef = jnp.where(land_sea == 1, sea_coef, land_coef).astype(F32)
-    sea_blocks = sea_temp.reshape(-1, blocks, count).transpose(1, 0, 2).reshape(rows, count)
-    mine = jnp.concatenate([sea_blocks, exchange_coef], 0)
+    mine = shares_of_sea(rows, count, blocks, sea_temp, land_sea)
     half = blocks // 2
     keep, send = start_spectra(blocks, scal, air_temp, jnp.asarray(forward))
     mine, west, east, send = lax.optimization_barrier((mine, west, east, send))
-    got = spread(jnp.broadcast_to(mine[None], (blocks,) + mine.shape))
-
-    half_sum = keep + between_caps(send, 1)
+    got = spread(mine)
+
+    taken = between_caps(send, 1)
+    half_sum = [keep[j] + taken[j] for j in range(half)]
 
     outs = windows(rows, count, width, blocks, fast, scal, got, air_temp, west, east)
     own_window, sea_ring, coef_ring = outs[:3]

time: 209 us -> 207 us (level)
    unnamed x36 -> x40, local copies, waits for them, and re-layouts: 5.36 us -> 6.95 us
  transfers between devices with their start and end apart: 16 -> 16, of which waited for: 3 -> 3; matrix products, arithmetic and copies ran while one was open for 3% -> 1% of each run, Pallas kernels for 32% -> 33%
where the time goes in v5:
time: 207 us; the launch traced here: 205 us
  Pallas kernels  106 us (51%)
  starting transfers between devices  58.4 us (28%)
  waiting for transfers between devices  19.7 us (10%)
  local copies, waits for them, and re-layouts  9.49 us (5%)
  blocking collectives  9.22 us (4%)
    pallas_call x3, Pallas kernels, cap_steps(): pl.pallas_call(functools.partial(cap_kernel, rows, count, width, blocks,...  54 us
    pallas_call x2, Pallas kernels, outside_steps(): pl.pallas_call(functools.partial(outside_kernel, rows, count, width, fast...  35.6 us
    ppermute x8, starting transfers between devices, between_caps(): return lax.ppermute(x, ('lat', 'lon'), pairs)  28.2 us
    all_to_all x4, starting transfers between devices, spread(): lax.all_to_all(copies, 'lon', split_axis=0, concat_axis=0, tiled=True)  21.5 us
    all_to_all x4, waiting for transfers between devices, spread(): lax.all_to_all(copies, 'lon', split_axis=0, concat_axis=0, tiled=True)  17.7 us
    all_to_all x1, blocking collectives, local(): sea = lax.all_to_all(sea, 'lon', split_axis=0, concat_axis=1, tiled=True)  9.22 us
    ppermute x4, starting transfers between devices, shift(): return lax.ppermute(x, axis, pairs)  8.72 us
    pallas_call x1, Pallas kernels, start_spectra(): pl.pallas_call(functools.partial(spectra_kernel, rows, count, blocks), ou...  7.53 us
  transfers between devices with their start and end apart: 16, of which 3 were waited for; matrix products, arithmetic and copies ran while one was open for 1% of the time, Pallas kernels for 33%

profile of v5, /device:TPU:0, one launch (start us, length us, event | category | flops | bytes accessed | tf_op | source)
XLA Modules:
  0.0 205.4 jit_solution(1847860437265849734)
XLA Ops:
  0.6 1.0 fusion.4
  1.6 6.1 %collective-permute-start.1 = (f32[32,8,128]{2,1,0:T(8,128)S(1)}, f32[32,8,128]{2,1,0:T(8,128)S(1)}, u32[]{:S(2)}, u32[]{:S(2)}) collective-permute-start(f32[32,8,128]{2,1,0:T(8,128)S(1)} %get-tuple-element.124), channel_id=1, source_target_pairs={{0,7},{1,0},{2,1},{3,2},{4,3},{5,4},{6,5},{7,6},{8,15},{9,8},{10,9... | collective-permute-start | bytes 393224 | tf_op jit(solution)/shard_map/ppermute | solution.py:1183
  7.7 0.0 collective-permute-start
  7.7 0.8 copy-done.2
  8.5 0.8 copy-done.3
  9.3 1.0 shares_of_sea.1
  10.3 7.5 %start_spectra.1 = (f32[4,22,32,128]{3,2,1,0:T(8,128)}, f32[4,22,32,128]{3,2,1,0:T(8,128)}) custom-call(s32[32]{0:T(128)} %scal.15, f32[32,360,128]{2,1,0:T(8,128)} %refs_0_.1, bf16[8,256,1152]{2,1,0:T(8,128)(2,1)} %constant.17.clone.table), custom_call_target="tpu_custom_call" | custom-call | tf_op jit(solution)/shard_map/start_spectra/pallas_call | solution.py:212
  17.8 0.0 collective-permute-done.1.east.refs_2_
  17.8 0.0 copy-start.15
  17.8 0.0 collective-permute-done.west.refs_1_
  17.9 0.0 copy-start.16
  17.9 6.0 %all-to-all-start = ((f32[8,64,360]{2,1,0:T(8,128)}), f32[8,64,360]{2,1,0:T(8,128)S(1)}, u32[]{:S(2)}, u32[]{:S(2)}) async-start(f32[8,64,360]{2,1,0:T(8,128)} %shares_of_sea.1), calls=%async_computation | async-start | bytes 1572864 | tf_op jit(solution)/shard_map/all_to_all | solution.py:1193
  23.9 4.0 %collective-permute-start.4 = (f32[4,22,32,128]{3,2,1,0:T(8,128)}, f32[4,22,32,128]{3,2,1,0:T(8,128)}, u32[]{:S(2)}, u32[]{:S(2)}) collective-permute-start(f32[4,22,32,128]{3,2,1,0:T(8,128)} %get-tuple-element.70), channel_id=1, source_target_pairs={{0,1},{1,0},{2,3},{3,2},{4,5},{5,4},{6,7},{7,6},{24,25},{25,24},{2... | collective-permute-start | bytes 4325384 | tf_op jit(solution)/shard_map/ppermute | solution.py:1189
  27.9 10.0 %all-to-all-done.got = f32[8,64,360]{2,1,0:T(8,128)S(1)} async-done(((f32[8,64,360]{2,1,0:T(8,128)}), f32[8,64,360]{2,1,0:T(8,128)S(1)}, u32[]{:S(2)}, u32[]{:S(2)}) %all-to-all-start) | async-done | bytes 737312 | tf_op jit(solution)/shard_map/all_to_all | solution.py:1193
  37.9 0.0 copy-done.15
  37.9 0.0 copy-done.16
  37.9 0.9 copy-done.8
  38.8 4.9 %windows.1 = (f32[2,32,384]{2,1,0:T(8,128)}, f32[24,3072]{1,0:T(8,128)}, f32[16,3072]{1,0:T(8,128)}, f32[6,384,128]{2,1,0:T(8,128)}, f32[6,384,128]{2,1,0:T(8,128)}) custom-call(s32[32]{0:T(128)} %scal.15, f32[8,64,360]{2,1,0:T(8,128)} %copy-done.8, f32[32,360,128]{2,1,0:T(8,128)} %refs_0_.1, f32[32,8,128]{2,1,0:T(8,128)} %copy-done.16, f32[32,8,128]{2,1,0:T(8,128)} %copy-done.15), custom_call_target="tpu_custom_call" | custom-call | tf_op jit(solution)/shard_map/windows/pallas_call | solution.py:439
  43.8 1.4 collective-permute-start.2
  45.1 1.3 collective-permute-start.3
  46.4 1.9 collective-permute-done.4
  48.4 1.6 fusion
  50.0 3.3 %collective-permute-start.5 = (f32[22,32,128]{2,1,0:T(8,128)S(1)}, f32[22,32,128]{2,1,0:T(8,128)S(1)}, u32[]{:S(2)}, u32[]{:S(2)}) collective-permute-start(f32[22,32,128]{2,1,0:T(8,128)S(1)} %get-tuple-element.78), channel_id=1, source_target_pairs={{0,2},{1,3},{2,0},{3,1},{4,6},{5,7},{6,4},{7,5},{24,26},{25,27},{2... | collective-permute-start | bytes 1081352 | tf_op jit(solution)/shard_map/ppermute | solution.py:1189
  53.3 4.7 %collective-permute-start.6 = (f32[22,32,128]{2,1,0:T(8,128)S(1)}, f32[22,32,128]{2,1,0:T(8,128)S(1)}, u32[]{:S(2)}, u32[]{:S(2)}) collective-permute-start(f32[22,32,128]{2,1,0:T(8,128)S(1)} %get-tuple-element.79), channel_id=1, source_target_pairs={{0,4},{1,5},{2,6},{3,7},{4,0},{5,1},{6,2},{7,3},{24,28},{25,29},{2... | collective-permute-start | bytes 1081352 | tf_op jit(solution)/shard_map/ppermute | solution.py:1189
  58.0 2.1 %collective-permute-start.7 = (f32[22,32,128]{2,1,0:T(8,128)S(1)}, f32[22,32,128]{2,1,0:T(8,128)S(1)}, u32[]{:S(2)}, u32[]{:S(2)}) collective-permute-start(f32[22,32,128]{2,1,0:T(8,128)S(1)} %get-tuple-element.80), channel_id=1, source_target_pairs={{0,6},{1,7},{2,4},{3,5},{4,2},{5,3},{6,0},{7,1},{24,30},{25,31},{2... | collective-permute-start | bytes 1081352 | tf_op jit(solution)/shard_map/ppermute | solution.py:1189
  60.1 0.0 collective-permute-done.2.refs_3_
  60.1 0.0 copy-start.11
  60.2 0.0 collective-permute-done.3.refs_4_
  60.2 0.0 copy-start.12
  60.2 1.0 copy-done.11
  61.2 0.4 copy-done.12
  61.6 15.2 %outside_steps.2 = (f32[44,384,128]{2,1,0:T(8,128)}, f32[2,384,128]{2,1,0:T(8,128)}, f32[2,384,128]{2,1,0:T(8,128)}, f32[2,384,128]{2,1,0:T(8,128)}, f32[2,384,1...) custom-call(s32[32]{0:T(128)} %scal.15, f32[32,360,128]{2,1,0:T(8,128)} %refs_0_.1, ...), custom_call_target="tpu_custom_call" | custom-call | flops 1610612736 | bytes 15728640 | tf_op jit(solution)/shard_map/outside_steps/pallas_call | solution.py:726
  76.8 0.0 collective-permute-done.5.refs_1_
  76.8 0.0 collective-permute-done.6.refs_2_
  76.8 0.0 collective-permute-done.7.refs_3_
  76.9 0.0 copy-start.6
  76.9 0.7 copy-done.6
  77.6 2.9 %free_steps.1 = (f32[8,216,128]{2,1,0:T(8,128)}, f32[16,32,128]{2,1,0:T(8,128)S(1)}) custom-call(s32[32]{0:T(128)S(1)} %copy-done.4, f32[22,32,128]{2,1,0:T(8,128)S(1)} %get-tuple-element.77.refs_0_, f32[22,32,128]{2,1,0:T(8,128)S(1)} %collective-permute-done.5.refs_1_, f32[22,32,128]{2,1,0:T(8,128)S(1)} %collective-permute-done.6.refs_2_, ...), custom_call_target="tpu_custom_call" | custom-call | tf_op jit(solution)/shard_map/free_steps/pallas_call | solution.py:282
  80.4 4.9 %all-to-all-start.1 = ((f32[8,216,128]{2,1,0:T(8,128)}), f32[8,216,128]{2,1,0:T(8,128)S(1)}, u32[]{:S(2)}, u32[]{:S(2)}) async-start(f32[8,216,128]{2,1,0:T(8,128)} %get-tuple-element.88), calls=%async_computation.1 | async-start | bytes 1769472 | tf_op jit(solution)/shard_map/all_to_all | solution.py:1193
  85.3 3.9 %collective-permute-start.8 = (f32[16,32,128]{2,1,0:T(8,128)S(1)}, f32[16,32,128]{2,1,0:T(8,128)S(1)}, u32[]{:S(2)}, u32[]{:S(2)}) collective-permute-start(f32[16,32,128]{2,1,0:T(8,128)S(1)} %get-tuple-element.107), channel_id=1, source_target_pairs={{0,1},{1,0},{2,3},{3,2},{4,5},{5,4},{6,7},{7,6},{24,25},{25,24},{2... | collective-permute-start | bytes 786440 | tf_op jit(solution)/shard_map/ppermute | solution.py:1189
  89.3 20.4 %outside_steps.3 = (f32[32,360,128]{2,1,0:T(8,128)}, f32[4,384,128]{2,1,0:T(8,128)}, f32[4,384,128]{2,1,0:T(8,128)}, f32[4,384,128]{2,1,0:T(8,128)}, f32[4,384,128]{2,1,0:T(8,128)}) custom-call(s32[32]{0:T(128)} %scal.15, f32[44,384,128]{2,1,0:T(8,128)} %get-tuple-element.89.refs_0_, f32[2,384,128]{2,1,0:T(8,128)} %get-tuple-element.75.refs_1_.refs_2_.refs_3_, ...), custom_call_target="tpu_custom_call" | custom-call | flops 3221225472 | bytes 15728640 | tf_op jit(solution)/shard_map/outside_steps/pallas_call | solution.py:726
  109.6 0.0 collective-permute-done.8
  109.7 0.0 all-to-all-done.1.refs_8_.refs_9_.refs_5_
  109.7 1.0 copy-done.7
  110.7 14.8 %cap_steps.3 = (f32[22,256,128]{2,1,0:T(8,128)}, f32[2,384,128]{2,1,0:T(8,128)}, f32[384,128]{1,0:T(8,128)}, f32[384,128]{1,0:T(8,128)}, f32[24,3072]{1,0:T(8,12...) custom-call(s32[32]{0:T(128)} %scal.15, f32[2,384,128]{2,1,0:T(8,128)} %get-tuple-element.73.refs_0_.refs_1_, ...), custom_call_target="tpu_custom_call" | custom-call | flops 738197504 | bytes 20000000 | tf_op jit(solution)/shard_map/cap_steps/pallas_call | solution.py:1127
  125.6 4.6 %all-to-all-start.2 = ((f32[8,16,384]{2,1,0:T(8,128)}), f32[8,16,384]{2,1,0:T(8,128)S(1)}, u32[]{:S(2)}, u32[]{:S(2)}) async-start(f32[8,16,384]{2,1,0:T(8,128)} %get-tuple-element.109), calls=%async_computation.2 | async-start | bytes 393216 | tf_op jit(solution)/shard_map/all_to_all | solution.py:1193
  130.1 5.7 %collective-permute-start.11 = (f32[2,16,32,128]{3,2,1,0:T(8,128)S(1)}, f32[2,16,32,128]{3,2,1,0:T(8,128)S(1)}, u32[]{:S(2)}, u32[]{:S(2)}) collective-permute-start(f32[2,16,32,128]{3,2,1,0:T(8,128)S(1)} %pad_maximum_fusion.refs_17_), channel_id=1, source_target_pairs={{0,6},{1,7},{2,4},{3,5},{4,2},{5,3},{6,0},{7,1},{24,30},{25,31},{2... | collective-permute-start | bytes 1572872 | tf_op jit(solution)/shard_map/ppermute | solution.py:1189
  135.9 1.9 collective-permute-start.10
  137.8 2.5 %collective-permute-start.9 = (f32[2,16,32,128]{3,2,1,0:T(8,128)S(1)}, f32[2,16,32,128]{3,2,1,0:T(8,128)S(1)}, u32[]{:S(2)}, u32[]{:S(2)}) collective-permute-start(f32[2,16,32,128]{3,2,1,0:T(8,128)S(1)} %pad_maximum_fusion.refs_17_), channel_id=1, source_target_pairs={{0,2},{1,3},{2,0},{3,1},{4,6},{5,7},{6,4},{7,5},{24,26},{25,27},{2... | collective-permute-start | bytes 1572872 | tf_op jit(solution)/shard_map/ppermute | solution.py:1189
  140.3 0.0 all-to-all-done.2.refs_17_
  140.3 0.0 copy-start.14
  140.3 0.7 copy-done.14
  141.0 18.7 %cap_steps.4 = (f32[22,256,128]{2,1,0:T(8,128)}, f32[4,384,128]{2,1,0:T(8,128)}, f32[384,128]{1,0:T(8,128)}, f32[384,128]{1,0:T(8,128)}, f32[24,3072]{1,0:T(8,12...) custom-call(s32[32]{0:T(128)} %scal.15, f32[22,256,128]{2,1,0:T(8,128)} %get-tuple-element.104.refs_0_, ...), custom_call_target="tpu_custom_call" | custom-call | flops 738197504 | bytes 20000000 | tf_op jit(solution)/shard_map/cap_steps/pallas_call | solution.py:1127
  159.7 6.0 %all-to-all-start.3 = ((f32[8,16,384]{2,1,0:T(8,128)}), f32[8,16,384]{2,1,0:T(8,128)S(1)}, u32[]{:S(2)}, u32[]{:S(2)}) async-start(f32[8,16,384]{2,1,0:T(8,128)} %get-tuple-element.116), calls=%async_computation.3 | async-start | bytes 393216 | tf_op jit(solution)/shard_map/all_to_all | solution.py:1193
  165.7 0.0 collective-permute-done.11.refs_20_
  165.7 0.0 collective-permute-done.10.refs_19_
  165.7 0.0 collective-permute-done.9.refs_18_
  165.7 7.7 %all-to-all-done.3.refs_13_ = f32[8,16,384]{2,1,0:T(8,128)S(1)} async-done(((f32[8,16,384]{2,1,0:T(8,128)}), f32[8,16,384]{2,1,0:T(8,128)S(1)}, u32[]{:S(2)}, u32[]{:S(2)}) %all-to-all-start.3) | async-done | bytes 196640 | tf_op jit(solution)/shard_map/all_to_all | solution.py:1193
  173.5 0.0 copy-done.19
  173.5 0.7 copy-done.13
  174.1 20.5 %cap_steps.5 = (f32[32,360,128]{2,1,0:T(8,128)}, f32[32,360]{1,0:T(8,128)}) custom-call(s32[32]{0:T(128)} %scal.15, f32[22,256,128]{2,1,0:T(8,128)} %get-tuple-element.113.refs_0_, f32[4,384,128]{2,1,0:T(8,128)} %get-tuple-element.96.refs_4_.refs_5_.refs_1_, ...), custom_call_target="tpu_custom_call", output_to_operand_aliasing={{0}: (25, {})} | custom-call | flops 738197504 | bytes 20000000 | tf_op jit(solution)/shard_map/cap_steps/pallas_call | solution.py:1127
  194.6 0.8 all_to_all.30
  195.4 9.2 %all_to_all.39 = f32[8,4,360]{2,1,0:T(4,128)S(1)} all-to-all(f32[8,4,360]{2,1,0:T(4,128)S(1)} %all_to_all.30), channel_id=1, replica_groups=mesh['lat'=4,'lon'=8] {'lon'}, dimensions={0} | all-to-all | bytes 92160 | tf_op jit(solution)/shard_map/all_to_all | solution.py:1291
  204.7 0.7 all_to_all.33
  (24 shorter events, 0.1 us)
Async XLA Ops:
  1.6 16.2 %collective-permute-start.1 = (f32[32,8,128]{2,1,0:T(8,128)S(1)}, f32[32,8,128]{2,1,0:T(8,128)S(1)}, u32[]{:S(2)}, u32[]{:S(2)}) collective-permute-start(f32[32,8,128]{2,1,0:T(8,128)S(1)} %get-tuple-element.124), channel_id=1, source_target_pairs={{0,7},{1,0},{2,1},{3,2},{4,3},{5,4},{6,5},{7,6},{8,15},{9,8},{10,9... | collective-permute-start | bytes 393224 | tf_op jit(solution)/shard_map/ppermute | solution.py:1183
  7.7 10.2 %collective-permute-start = (f32[32,8,128]{2,1,0:T(8,128)S(1)}, f32[32,8,128]{2,1,0:T(8,128)S(1)}, u32[]{:S(2)}, u32[]{:S(2)}) collective-permute-start(f32[32,8,128]{2,1,0:T(8,128)S(1)} %get-tuple-element.125), channel_id=1, source_target_pairs={{0,1},{1,2},{2,3},{3,4},{4,5},{5,6},{6,7},{7,0},{8,9},{9,10},{10,1... | collective-permute-start | bytes 393224 | tf_op jit(solution)/shard_map/ppermute | solution.py:1183
  7.7 0.8 copy-start.2
  8.5 0.8 copy-start.3
  17.8 20.1 %copy-start.15 = (f32[32,8,128]{2,1,0:T(8,128)}, f32[32,8,128]{2,1,0:T(8,128)S(1)}, u32[]{:S(2)}) copy-start(f32[32,8,128]{2,1,0:T(8,128)S(1)} %collective-permute-done.1.east.refs_2_) | copy-start | bytes 393220
  17.9 20.1 %copy-start.16 = (f32[32,8,128]{2,1,0:T(8,128)}, f32[32,8,128]{2,1,0:T(8,128)S(1)}, u32[]{:S(2)}) copy-start(f32[32,8,128]{2,1,0:T(8,128)S(1)} %collective-permute-done.west.refs_1_) | copy-start | bytes 393220
  17.9 20.0 %all-to-all-start = ((f32[8,64,360]{2,1,0:T(8,128)}), f32[8,64,360]{2,1,0:T(8,128)S(1)}, u32[]{:S(2)}, u32[]{:S(2)}) async-start(f32[8,64,360]{2,1,0:T(8,128)} %shares_of_sea.1), calls=%async_computation | async-start | bytes 1572864 | tf_op jit(solution)/shard_map/all_to_all | solution.py:1193
  23.9 24.5 %copy-start.10 = (f32[4,22,32,128]{3,2,1,0:T(8,128)S(1)}, f32[4,22,32,128]{3,2,1,0:T(8,128)}, u32[]{:S(2)}) copy-start(f32[4,22,32,128]{3,2,1,0:T(8,128)} %get-tuple-element.69) | copy-start | bytes 4325380
  23.9 24.5 %collective-permute-start.4 = (f32[4,22,32,128]{3,2,1,0:T(8,128)}, f32[4,22,32,128]{3,2,1,0:T(8,128)}, u32[]{:S(2)}, u32[]{:S(2)}) collective-permute-start(f32[4,22,32,128]{3,2,1,0:T(8,128)} %get-tuple-element.70), channel_id=1, source_target_pairs={{0,1},{1,0},{2,3},{3,2},{4,5},{5,4},{6,7},{7,6},{24,25},{25,24},{2... | collective-permute-start | bytes 4325384 | tf_op jit(solution)/shard_map/ppermute | solution.py:1189
  37.9 0.9 copy-start.8
  43.8 16.4 %collective-permute-start.2 = (f32[6,384,128]{2,1,0:T(8,128)}, f32[6,384,128]{2,1,0:T(8,128)S(1)}, u32[]{:S(2)}, u32[]{:S(2)}) collective-permute-start(f32[6,384,128]{2,1,0:T(8,128)} %get-tuple-element.67), channel_id=1, source_target_pairs={{0,8},{8,16},{16,24},{1,9},{9,17},{17,25},{2,10},{10,18},{18,26},{... | collective-permute-start | bytes 3538952 | tf_op jit(solution)/shard_map/ppermute | solution.py:1183
  45.1 15.0 %collective-permute-start.3 = (f32[6,384,128]{2,1,0:T(8,128)}, f32[6,384,128]{2,1,0:T(8,128)S(1)}, u32[]{:S(2)}, u32[]{:S(2)}) collective-permute-start(f32[6,384,128]{2,1,0:T(8,128)} %get-tuple-element.68), channel_id=1, source_target_pairs={{8,0},{16,8},{24,16},{9,1},{17,9},{25,17},{10,2},{18,10},{26,18},{... | collective-permute-start | bytes 3538952 | tf_op jit(solution)/shard_map/ppermute | solution.py:1183
  50.0 26.8 %collective-permute-start.5 = (f32[22,32,128]{2,1,0:T(8,128)S(1)}, f32[22,32,128]{2,1,0:T(8,128)S(1)}, u32[]{:S(2)}, u32[]{:S(2)}) collective-permute-start(f32[22,32,128]{2,1,0:T(8,128)S(1)} %get-tuple-element.78), channel_id=1, source_target_pairs={{0,2},{1,3},{2,0},{3,1},{4,6},{5,7},{6,4},{7,5},{24,26},{25,27},{2... | collective-permute-start | bytes 1081352 | tf_op jit(solution)/shard_map/ppermute | solution.py:1189
  53.3 23.5 %collective-permute-start.6 = (f32[22,32,128]{2,1,0:T(8,128)S(1)}, f32[22,32,128]{2,1,0:T(8,128)S(1)}, u32[]{:S(2)}, u32[]{:S(2)}) collective-permute-start(f32[22,32,128]{2,1,0:T(8,128)S(1)} %get-tuple-element.79), channel_id=1, source_target_pairs={{0,4},{1,5},{2,6},{3,7},{4,0},{5,1},{6,2},{7,3},{24,28},{25,29},{2... | collective-permute-start | bytes 1081352 | tf_op jit(solution)/shard_map/ppermute | solution.py:1189
  58.0 18.8 %collective-permute-start.7 = (f32[22,32,128]{2,1,0:T(8,128)S(1)}, f32[22,32,128]{2,1,0:T(8,128)S(1)}, u32[]{:S(2)}, u32[]{:S(2)}) collective-permute-start(f32[22,32,128]{2,1,0:T(8,128)S(1)} %get-tuple-element.80), channel_id=1, source_target_pairs={{0,6},{1,7},{2,4},{3,5},{4,2},{5,3},{6,0},{7,1},{24,30},{25,31},{2... | collective-permute-start | bytes 1081352 | tf_op jit(solution)/shard_map/ppermute | solution.py:1189
  60.1 1.0 copy-start.11
  60.2 1.4 copy-start.12
  61.6 15.3 %copy-start = (f32[128,128]{1,0:T(8,128)S(1)}, f32[128,128]{1,0:T(8,128)}, u32[]{:S(2)}) copy-start(f32[128,128]{1,0:T(8,128)} %refs_23_.3) | copy-start | bytes 196612
  61.6 15.3 %copy-start.1 = (f32[2,256,128]{2,1,0:T(8,128)S(1)}, f32[2,256,128]{2,1,0:T(8,128)}, u32[]{:S(2)}) copy-start(f32[2,256,128]{2,1,0:T(8,128)} %constant.14.clone.refs_4_) | copy-start | bytes 786436
  61.6 15.3 %copy-start.4 = (s32[32]{0:T(128)S(1)}, s32[32]{0:T(128)}, u32[]{:S(2)}) copy-start(s32[32]{0:T(128)} %scal.15) | copy-start | bytes 388
  61.6 15.3 %copy-start.5 = (f32[128]{0:T(128)S(1)}, f32[128]{0:T(128)}, u32[]{:S(2)}) copy-start(f32[128]{0:T(128)} %param.15) | copy-start | bytes 1540
  76.9 0.7 copy-start.6
  80.4 29.3 %all-to-all-start.1 = ((f32[8,216,128]{2,1,0:T(8,128)}), f32[8,216,128]{2,1,0:T(8,128)S(1)}, u32[]{:S(2)}, u32[]{:S(2)}) async-start(f32[8,216,128]{2,1,0:T(8,128)} %get-tuple-element.88), calls=%async_computation.1 | async-start | bytes 1769472 | tf_op jit(solution)/shard_map/all_to_all | solution.py:1193
  85.3 24.3 %collective-permute-start.8 = (f32[16,32,128]{2,1,0:T(8,128)S(1)}, f32[16,32,128]{2,1,0:T(8,128)S(1)}, u32[]{:S(2)}, u32[]{:S(2)}) collective-permute-start(f32[16,32,128]{2,1,0:T(8,128)S(1)} %get-tuple-element.107), channel_id=1, source_target_pairs={{0,1},{1,0},{2,3},{3,2},{4,5},{5,4},{6,7},{7,6},{24,25},{25,24},{2... | collective-permute-start | bytes 786440 | tf_op jit(solution)/shard_map/ppermute | solution.py:1189
  109.7 28.1 %copy-start.9 = (f32[2,16,32,128]{3,2,1,0:T(8,128)}, f32[2,16,32,128]{3,2,1,0:T(8,128)S(1)}, u32[]{:S(2)}) copy-start(f32[2,16,32,128]{3,2,1,0:T(8,128)S(1)} %pad_maximum_fusion.refs_17_) | copy-start | bytes 1572868
  109.7 1.0 copy-start.7
  125.6 14.7 %all-to-all-start.2 = ((f32[8,16,384]{2,1,0:T(8,128)}), f32[8,16,384]{2,1,0:T(8,128)S(1)}, u32[]{:S(2)}, u32[]{:S(2)}) async-start(f32[8,16,384]{2,1,0:T(8,128)} %get-tuple-element.109), calls=%async_computation.2 | async-start | bytes 393216 | tf_op jit(solution)/shard_map/all_to_all | solution.py:1193
  130.1 35.6 %collective-permute-start.11 = (f32[2,16,32,128]{3,2,1,0:T(8,128)S(1)}, f32[2,16,32,128]{3,2,1,0:T(8,128)S(1)}, u32[]{:S(2)}, u32[]{:S(2)}) collective-permute-start(f32[2,16,32,128]{3,2,1,0:T(8,128)S(1)} %pad_maximum_fusion.refs_17_), channel_id=1, source_target_pairs={{0,6},{1,7},{2,4},{3,5},{4,2},{5,3},{6,0},{7,1},{24,30},{25,31},{2... | collective-permute-start | bytes 1572872 | tf_op jit(solution)/shard_map/ppermute | solution.py:1189
  135.9 29.8 %collective-permute-start.10 = (f32[2,16,32,128]{3,2,1,0:T(8,128)S(1)}, f32[2,16,32,128]{3,2,1,0:T(8,128)S(1)}, u32[]{:S(2)}, u32[]{:S(2)}) collective-permute-start(f32[2,16,32,128]{3,2,1,0:T(8,128)S(1)} %pad_maximum_fusion.refs_17_), channel_id=1, source_target_pairs={{0,4},{1,5},{2,6},{3,7},{4,0},{5,1},{6,2},{7,3},{24,28},{25,29},{2... | collective-permute-start | bytes 1572872 | tf_op jit(solution)/shard_map/ppermute | solution.py:1189
  137.8 27.9 %collective-permute-start.9 = (f32[2,16,32,128]{3,2,1,0:T(8,128)S(1)}, f32[2,16,32,128]{3,2,1,0:T(8,128)S(1)}, u32[]{:S(2)}, u32[]{:S(2)}) collective-permute-start(f32[2,16,32,128]{3,2,1,0:T(8,128)S(1)} %pad_maximum_fusion.refs_17_), channel_id=1, source_target_pairs={{0,2},{1,3},{2,0},{3,1},{4,6},{5,7},{6,4},{7,5},{24,26},{25,27},{2... | collective-permute-start | bytes 1572872 | tf_op jit(solution)/shard_map/ppermute | solution.py:1189
  140.3 0.7 copy-start.14
  159.7 13.8 %all-to-all-start.3 = ((f32[8,16,384]{2,1,0:T(8,128)}), f32[8,16,384]{2,1,0:T(8,128)S(1)}, u32[]{:S(2)}, u32[]{:S(2)}) async-start(f32[8,16,384]{2,1,0:T(8,128)} %get-tuple-element.116), calls=%async_computation.3 | async-start | bytes 393216 | tf_op jit(solution)/shard_map/all_to_all | solution.py:1193
  165.7 7.8 %copy-start.17 = (f32[2,16,32,128]{3,2,1,0:T(8,128)}, f32[2,16,32,128]{3,2,1,0:T(8,128)S(1)}, u32[]{:S(2)}) copy-start(f32[2,16,32,128]{3,2,1,0:T(8,128)S(1)} %collective-permute-done.11.refs_20_) | copy-start | bytes 1572868
  165.7 7.8 %copy-start.18 = (f32[2,16,32,128]{3,2,1,0:T(8,128)}, f32[2,16,32,128]{3,2,1,0:T(8,128)S(1)}, u32[]{:S(2)}) copy-start(f32[2,16,32,128]{3,2,1,0:T(8,128)S(1)} %collective-permute-done.10.refs_19_) | copy-start | bytes 1572868
  165.7 7.7 %copy-start.19 = (f32[2,16,32,128]{3,2,1,0:T(8,128)}, f32[2,16,32,128]{3,2,1,0:T(8,128)S(1)}, u32[]{:S(2)}) copy-start(f32[2,16,32,128]{3,2,1,0:T(8,128)S(1)} %collective-permute-done.9.refs_18_) | copy-start | bytes 1572868
  173.5 0.7 copy-start.13

commit v6 on v5

--- a/solution.py
+++ b/solution.py
@@ -232,7 +232,7 @@
 def free_kernel(blocks, parts, scal, *refs):
     scal = Place(scal)
     sums, refs = refs[:parts], refs[parts:]
-    rotate, courant, mix, edge, early, late, state, mask, xcat, vcat = refs
+    rotate, courant, mix, edge, cap_coef, early, late, state, mask, xcat, vcat = refs
     part = NK // blocks
     some = part // 2
     owner = lax.rem(scal[2], 2) * (blocks // 2) + scal[2] // 2
@@ -272,20 +272,21 @@
                 late[...] = state[1 : NPOLE + 1]
         for to in range(blocks):
             early[to, 0:part, :] = top
-            early[to, STEPS * part :, :] = edge[...]
-
-
-def free_steps(blocks, scal, sums, rotate, courant, mix, edge):
+            early[to, STEPS * part : STEPS * part + edge.shape[0], :] = edge[...]
+            early[to, STEPS * part + edge.shape[0] :, :] = cap_coef[...]
+
+
+def free_steps(blocks, scal, sums, rotate, courant, mix, edge, cap_coef):
     part = NK // blocks
     vmem = pl.BlockSpec(memory_space=pltpu.VMEM)
     shape = jax.ShapeDtypeStruct
     return pl.pallas_call(
         functools.partial(free_kernel, blocks, len(sums)),
         out_shape=[
-            shape((blocks, STEPS * part + edge.shape[0], 128), F32),
+            shape((blocks, STEPS * part + edge.shape[0] + cap_coef.shape[0], 128), F32),
             shape((NPOLE, part, 128), F32),
         ],
-        in_specs=[pl.BlockSpec(memory_space=pltpu.SMEM)] + [vmem] * (len(sums) + 4),
+        in_specs=[pl.BlockSpec(memory_space=pltpu.SMEM)] + [vmem] * (len(sums) + 5),
         out_specs=[vmem] * 2,
         scratch_shapes=[
             pltpu.VMEM((CAP + 2, part, 128), F32),
@@ -295,7 +296,7 @@
         ],
         compiler_params=pltpu.CompilerParams(vmem_limit_bytes=VMEM_LIMIT // 4),
         name="free_steps",
-    )(scal, *sums, rotate, courant, mix, edge)
+    )(scal, *sums, rotate, courant, mix, edge, cap_coef)
 
 
 def advance(
@@ -349,20 +350,24 @@
 
 def share_kernel(rows, count, blocks, sea, land, out):
     per = rows // blocks
-    for i in range(blocks):
-        piece = sea[:, i * count : (i + 1) * count]
-        for to in range(blocks):
-            out[to, i * per : (i + 1) * per, :] = piece
-    coef = jnp.where(land[...] == 1, sea_coef, land_coef).astype(F32)
+    coef = coefficients(land)
+    ends = (coef[:, 0:HALO], coef[:, count - HALO : count])
     for to in range(blocks):
-        out[to, rows:, :] = coef
+        for i in range(blocks):
+            out[to, i * per : (i + 1) * per, 0:count] = sea[:, i * count : (i + 1) * count]
+        for n, end in enumerate(ends):
+            out[to, :, count + HALO * n : count + HALO * (n + 1)] = end
+
+
+def coefficients(land):
+    return jnp.where(land[...] == 1, sea_coef, land_coef).astype(F32)
 
 
 def shares_of_sea(rows, count, blocks, sea, land):
     vmem = pl.BlockSpec(memory_space=pltpu.VMEM)
     return pl.pallas_call(
         functools.partial(share_kernel, rows, count, blocks),
-        out_shape=jax.ShapeDtypeStruct((blocks, 2 * rows, count), F32),
+        out_shape=jax.ShapeDtypeStruct((blocks, rows, count + 2 * HALO), F32),
         in_specs=[vmem, vmem],
         out_specs=vmem,
         compiler_params=pltpu.CompilerParams(vmem_limit_bytes=VMEM_LIMIT // 4),
@@ -370,11 +375,11 @@
     )(sea, land)
 
 
-def windows_kernel(rows, count, width, blocks, scal, got, air, west, east, *refs):
+def windows_kernel(rows, count, width, blocks, scal, got, land, air, west, east, *refs):
     scal = Place(scal)
-    own, ring_sea, ring_coef = refs[:3]
-    wide, sems = refs[-2:]
-    edges = list(zip(refs[3:-2], (rows - ROW0, 0)))
+    own, ring_sea, cap_coef = refs[:3]
+    wide, held, sems = refs[-3:]
+    edges = list(zip(refs[3:-3], (rows - ROW0, 0)))
     copies = []
     for n, (ref, first) in enumerate(edges):
         some = pl.ds(first, ROW0)
@@ -392,16 +397,22 @@
     for j in range(blocks):
         columns = slice(j * width + HALO, j * width + HALO + count)
         for i in range(blocks):
-            wide[0, per * i : per * (i + 1), columns] = got[i, per * j : per * (j + 1), :]
-        wide[1, :, columns] = got[j, rows:, :]
+            wide[per * i : per * (i + 1), columns] = got[i, per * j : per * (j + 1), 0:count]
     rest = width - HALO - count
     for j in range(blocks):
         before = ((j - 1) % blocks) * width + count
         after = ((j + 1) % blocks) * width + HALO
         end = j * width + HALO + count
-        wide[:, :, j * width : j * width + HALO] = wide[:, :, before : before + HALO]
-        wide[:, :, end : end + rest] = wide[:, :, after : after + rest]
-    own[...] = wide[:, :, pl.ds(pl.multiple_of(scal[2] * width, 128), width)]
+        wide[:, j * width : j * width + HALO] = wide[:, before : before + HALO]
+        wide[:, end : end + rest] = wide[:, after : after + rest]
+    block = scal[2]
+    own[0] = wide[:, pl.ds(pl.multiple_of(block * width, 128), width)]
+    before, after = lax.rem(block + blocks - 1, blocks), lax.rem(block + 1, blocks)
+    own[1, :, 0:HALO] = got[before, :, count + HALO : count + 2 * HALO]
+    own[1, :, HALO : HALO + count] = coefficients(land)
+    own[1, :, HALO + count : 2 * HALO + count] = got[after, :, count : count + HALO]
+    if rest > HALO:
+        own[1, :, 2 * HALO + count :] = jnp.zeros((rows, rest - HALO), F32)
     for ref, first in edges:
         base = count + 2 * HALO
         for n in range(2):
@@ -415,12 +426,15 @@
         @pl.loop(0, 24)
         def _(q):
             r = jnp.where(scal[0] == 1, rows - 1 - q, q)
-            ring_sea[pl.ds(q, 1), :] = wide[0, pl.ds(r, 1), :]
+            ring_sea[pl.ds(q, 1), :] = wide[pl.ds(r, 1), :]
 
         @pl.loop(0, NPOLE)
         def _(q):
             r = jnp.where(scal[0] == 1, rows - 1 - q, q)
-            ring_coef[pl.ds(q, 1), :] = wide[1, pl.ds(r, 1), :]
+            held[pl.ds(q, 1), :] = own[1, pl.ds(r, 1), :]
+
+        for o in range(width // 128):
+            cap_coef[NPOLE * o : NPOLE * (o + 1), :] = held[:, 128 * o : 128 * (o + 1)]
 
     for copy in copies:
         copy.wait()
@@ -431,7 +445,7 @@
     return round_up(inner, 8), round_up(inner, 8) + 8
 
 
-def windows(rows, count, width, blocks, fast, scal, got, air, west, east):
+def windows(rows, count, width, blocks, fast, scal, got, land, air, west, east):
     any_spec = pl.BlockSpec(memory_space=pl.ANY)
     edges = [jax.ShapeDtypeStruct((ROW0, edge_extent(count, width)[1], 128), F32)] * 2
     vmem = pl.BlockSpec(memory_space=pltpu.VMEM)
@@ -441,18 +455,19 @@
         out_shape=[
             shape((2, rows, width), F32),
             shape((24, blocks * width), F32),
-            shape((NPOLE, blocks * width), F32),
+            shape((NPOLE * (width // 128), 128), F32),
         ]
         + (edges if fast else []),
-        in_specs=[pl.BlockSpec(memory_space=pltpu.SMEM), vmem] + [any_spec] * 3,
+        in_specs=[pl.BlockSpec(memory_space=pltpu.SMEM), vmem, vmem] + [any_spec] * 3,
         out_specs=[vmem] * (5 if fast else 3),
         scratch_shapes=[
-            pltpu.VMEM((2, rows, blocks * width), F32),
+            pltpu.VMEM((rows, blocks * width), F32),
+            pltpu.VMEM((NPOLE, width), F32),
             pltpu.SemaphoreType.DMA((6,)),
         ],
         compiler_params=pltpu.CompilerParams(vmem_limit_bytes=VMEM_LIMIT),
         name="windows",
-    )(scal, got, air, west, east)
+    )(scal, got, land, air, west, east)
 
 
 def outside_kernel(rows, count, width, fast, steps, scal, *refs):
@@ -487,7 +502,7 @@
     def low_row(step):
         return jnp.where(polar == 1, NPOLE + step - 1, step - STEPS)
 
-    def row_range(body, step, *sizes):
+    def row_range(body, step, *sizes, meanwhile=lambda: None):
         hi = rows - 1 + STEPS - step
         ref, extent, sem = sizes
 
@@ -495,6 +510,7 @@
         def _(q):
             body(q).start()
 
+        meanwhile()
         for kind, count_rows in ((1, hi + 1 - NPOLE - step + 1), (0, hi + 1 + STEPS - step)):
             @pl.when(polar == kind)
             def _(count_rows=count_rows):
@@ -595,15 +611,14 @@
         ]
         for copy in small:
             copy.start()
-        begin()
-        for copy in small:
-            copy.wait()
         row_range(
             lambda q: pltpu.make_async_copy(
                 state.at[q + ROW0], buf_a.at[pl.ds(base_of(q), width)], sems.at[0]
             ),
-            steps[0] - 1, buf_a, width, sems.at[0],
+            steps[0] - 1, buf_a, width, sems.at[0], meanwhile=begin,
         )
+        for copy in small:
+            copy.wait()
 
     def with_flux(y, q):
         gain = air_gain * pltpu.roll(flux[...], 128 - (q + ROW0), 1)
@@ -766,7 +781,7 @@
     wedge_steps = [step + 1 for step in steps if step < STEPS]
     spec_in, refs = refs[:parts], refs[parts:]
     hists, refs = refs[: 4 * len(cap_hists(steps))], refs[4 * len(cap_hists(steps)) :]
-    names = ["free", "t_high", "t_low", "rotate", "coef", "sea", "sea_ring", "coef_ring"]
+    names = ["free", "t_high", "t_low", "rotate", "coef", "sea", "sea_ring"]
     if steps[0] > 1:
         names += ["gathered", "flux", "ring_flux", "wedge"]
     if last:
@@ -993,7 +1008,14 @@
                         loads["free"].at[i, pl.ds(STEPS * part + 8 * o, 8)],
                         gathered.at[i, pl.ds(8, 8), pl.ds(128 * o, 128)],
                     )
-        fetch("coef_ring", loads["coef_ring"], coef_ring)
+        for i in range(blocks):
+            for o in range(width // 128):
+                at = STEPS * (NK // blocks) + width // 16 + NPOLE * o
+                fetch(
+                    "coef_ring",
+                    loads["free"].at[i, pl.ds(at, NPOLE)],
+                    coef_ring.at[:, pl.ds(i * width + 128 * o, 128)],
+                )
         fetch("coef", loads["coef"], coef)
         fetch("sea", loads["sea"], sea)
         fetch("flux", loads["flux"] if steps[0] > 1 else hist(3, 1), flux)
@@ -1162,7 +1184,7 @@
             pltpu.VMEM((8, NK), F32),
             pltpu.VMEM((1, 128), F32),
             pltpu.VMEM((128, 128), F32),
-            pltpu.SemaphoreType.DMA((9 * blocks + 32,)),
+            pltpu.SemaphoreType.DMA((13 * blocks + 32,)),
             pltpu.SemaphoreType.DMA((CAP,)),
         ]
         + extra,
@@ -1215,14 +1237,16 @@
     mine = shares_of_sea(rows, count, blocks, sea_temp, land_sea)
     half = blocks // 2
     keep, send = start_spectra(blocks, scal, air_temp, jnp.asarray(forward))
-    mine, west, east, send = lax.optimization_barrier((mine, west, east, send))
+    mine, west, east = lax.optimization_barrier((mine, west, east))
     got = spread(mine)
 
     taken = between_caps(send, 1)
     half_sum = [keep[j] + taken[j] for j in range(half)]
 
-    outs = windows(rows, count, width, blocks, fast, scal, got, air_temp, west, east)
-    own_window, sea_ring, coef_ring = outs[:3]
+    outs = windows(
+        rows, count, width, blocks, fast, scal, got, land_sea, air_temp, west, east
+    )
+    own_window, sea_ring, cap_coef = outs[:3]
     if fast:
         last_rows, first_rows = outs[3:]
     else:
@@ -1254,7 +1278,8 @@
     state, early, sea, coef, gathered = outs[0], tuple(outs[1:5]), outs[5], outs[6], outs[7]
     parts, state = lax.optimization_barrier((parts, state))
     gathered, late_free = free_steps(
-        blocks, scal, (half_sum[0], *parts), rotate_owned, courant, vertical_mix, gathered
+        blocks, scal, (half_sum[0], *parts), rotate_owned, courant, vertical_mix, gathered,
+        cap_coef,
     )
     gathered, state = lax.optimization_barrier((gathered, state))
     late_pair = jnp.stack([late_free, between_caps(late_free, 1)])
@@ -1269,7 +1294,7 @@
     more, spec = (), ()
     for steps in ((1, 2), (3, 4), (5, 6)):
         hists = sum(((early, late)[h] for h in cap_hists(steps)), ())
-        big = hists + (free, t_high, t_low, rotate, coef, sea, sea_ring, coef_ring) + more
+        big = hists + (free, t_high, t_low, rotate, coef, sea, sea_ring) + more
         if steps[-1] == STEPS:
             big += tuple(late_free)
         outs = cap_steps(

time: 207 us -> 204 us (0.986)
  blocking collectives: 9.22 us -> 31.6 us
  waiting for transfers between devices: 19.7 us -> 7.76 us
  starting transfers between devices: 58.4 us -> 50.1 us
  local copies, waits for them, and re-layouts: 9.49 us -> 7.07 us
    all_to_all x0 -> x1, blocking collectives: none -> 22.4 us  [spread(): lax.all_to_all(copies, 'lon', split_axis=0, concat_axis=0, tiled=True)]
    all_to_all x4 -> x3, waiting for transfers between devices: 17.7 us -> 7.73 us  [spread(): lax.all_to_all(copies, 'lon', split_axis=0, concat_axis=0, tiled=True)]
    all_to_all x4 -> x3, starting transfers between devices: 21.5 us -> 15.3 us  [spread(): lax.all_to_all(copies, 'lon', split_axis=0, concat_axis=0, tiled=True)]
    unnamed x40, local copies, waits for them, and re-layouts: 6.95 us -> 4.54 us
    ppermute x8, starting transfers between devices: 28.2 us -> 26.1 us  [between_caps(): return lax.ppermute(x, ('lat', 'lon'), pairs)]
  transfers between devices with their start and end apart: 16 -> 15, of which waited for: 3 -> 1; matrix products, arithmetic and copies ran while one was open for 1% -> 0% of each run, Pallas kernels for 33% -> 33%
where the time goes in v6:
time: 204 us; the launch traced here: 203 us
  Pallas kernels  105 us (51%)
  starting transfers between devices  50.1 us (25%)
  blocking collectives  31.6 us (15%)
  waiting for transfers between devices  7.76 us (4%)
  local copies, waits for them, and re-layouts  7.07 us (3%)
    pallas_call x3, Pallas kernels, cap_steps(): pl.pallas_call(functools.partial(cap_kernel, rows, count, width, blocks,...  55 us
    pallas_call x2, Pallas kernels, outside_steps(): pl.pallas_call(functools.partial(outside_kernel, rows, count, width, fast...  34.7 us
    ppermute x8, starting transfers between devices, between_caps(): return lax.ppermute(x, ('lat', 'lon'), pairs)  26.1 us
    all_to_all x1, blocking collectives, spread(): lax.all_to_all(copies, 'lon', split_axis=0, concat_axis=0, tiled=True)  22.4 us
    all_to_all x3, starting transfers between devices, spread(): lax.all_to_all(copies, 'lon', split_axis=0, concat_axis=0, tiled=True)  15.3 us
    all_to_all x1, blocking collectives, local(): sea = lax.all_to_all(sea, 'lon', split_axis=0, concat_axis=1, tiled=True)  9.21 us
    ppermute x4, starting transfers between devices, shift(): return lax.ppermute(x, axis, pairs)  8.72 us
    all_to_all x3, waiting for transfers between devices, spread(): lax.all_to_all(copies, 'lon', split_axis=0, concat_axis=0, tiled=True)  7.73 us
  transfers between devices with their start and end apart: 15, of which 1 were waited for; matrix products, arithmetic and copies ran while one was open for 0% of the time, Pallas kernels for 33%

profile of v6, /device:TPU:0, one launch (start us, length us, event | category | flops | bytes accessed | tf_op | source)
XLA Modules:
  0.0 202.9 jit_solution(7527663350718660945)
XLA Ops:
  0.6 1.0 fusion.4
  1.6 6.1 %collective-permute-start.1 = (f32[32,8,128]{2,1,0:T(8,128)S(1)}, f32[32,8,128]{2,1,0:T(8,128)S(1)}, u32[]{:S(2)}, u32[]{:S(2)}) collective-permute-start(f32[32,8,128]{2,1,0:T(8,128)S(1)} %get-tuple-element.122), channel_id=1, source_target_pairs={{0,7},{1,0},{2,1},{3,2},{4,3},{5,4},{6,5},{7,6},{8,15},{9,8},{10,9... | collective-permute-start | bytes 393224 | tf_op jit(solution)/shard_map/ppermute | solution.py:1205
  7.7 0.0 collective-permute-start
  7.7 7.7 %start_spectra.1 = (f32[4,22,32,128]{3,2,1,0:T(8,128)}, f32[4,22,32,128]{3,2,1,0:T(8,128)}) custom-call(s32[32]{0:T(128)} %scal.15, f32[32,360,128]{2,1,0:T(8,128)} %refs_0_.1, bf16[8,256,1152]{2,1,0:T(8,128)(2,1)} %constant.17.clone.table), custom_call_target="tpu_custom_call" | custom-call | tf_op jit(solution)/shard_map/start_spectra/pallas_call | solution.py:212
  15.4 1.9 collective-permute-start.4
  17.3 0.0 copy-done.2
  17.3 0.0 copy-done.3
  17.3 0.3 shares_of_sea.1
  17.6 0.0 collective-permute-done.1.east.refs_2_
  17.6 0.0 copy-start.18
  17.6 0.0 collective-permute-done.west.refs_1_
  17.6 0.0 copy-start.19
  17.7 22.4 %all_to_all.39.got = f32[8,32,376]{2,1,0:T(8,128)} all-to-all(f32[8,32,376]{2,1,0:T(8,128)S(1)} %shares_of_sea.1), channel_id=1, replica_groups=mesh['lat'=4,'lon'=8] {'lon'}, dimensions={0} | all-to-all | bytes 770048 | tf_op jit(solution)/shard_map/all_to_all | solution.py:1215
  40.0 0.0 copy-done.18
  40.0 0.0 copy-done.19
  40.0 4.5 %windows.1 = (f32[2,32,384]{2,1,0:T(8,128)}, f32[24,3072]{1,0:T(8,128)}, f32[48,128]{1,0:T(8,128)}, f32[6,384,128]{2,1,0:T(8,128)}, f32[6,384,128]{2,1,0:T(8,128)}) custom-call(s32[32]{0:T(128)} %scal.15, f32[8,32,376]{2,1,0:T(8,128)} %all_to_all.39.got, s32[32,360]{1,0:T(8,128)} %land.3, f32[32,360,128]{2,1,0:T(8,128)} %refs_0_.1, ...), custom_call_target="tpu_custom_call" | custom-call | tf_op jit(solution)/shard_map/windows/pallas_call | solution.py:453
  44.5 1.4 collective-permute-start.2
  45.9 1.3 collective-permute-start.3
  47.2 0.0 collective-permute-done.4
  47.2 0.3 fusion
  47.5 2.0 collective-permute-start.5
  49.5 5.1 %collective-permute-start.6 = (f32[22,32,128]{2,1,0:T(8,128)S(1)}, f32[22,32,128]{2,1,0:T(8,128)S(1)}, u32[]{:S(2)}, u32[]{:S(2)}) collective-permute-start(f32[22,32,128]{2,1,0:T(8,128)S(1)} %get-tuple-element.77), channel_id=1, source_target_pairs={{0,4},{1,5},{2,6},{3,7},{4,0},{5,1},{6,2},{7,3},{24,28},{25,29},{2... | collective-permute-start | bytes 1081352 | tf_op jit(solution)/shard_map/ppermute | solution.py:1211
  54.6 3.0 %collective-permute-start.7 = (f32[22,32,128]{2,1,0:T(8,128)S(1)}, f32[22,32,128]{2,1,0:T(8,128)S(1)}, u32[]{:S(2)}, u32[]{:S(2)}) collective-permute-start(f32[22,32,128]{2,1,0:T(8,128)S(1)} %get-tuple-element.78), channel_id=1, source_target_pairs={{0,6},{1,7},{2,4},{3,5},{4,2},{5,3},{6,0},{7,1},{24,30},{25,31},{2... | collective-permute-start | bytes 1081352 | tf_op jit(solution)/shard_map/ppermute | solution.py:1211
  57.6 0.0 collective-permute-done.2.refs_3_
  57.6 0.0 copy-start.11
  57.6 0.0 collective-permute-done.3.refs_4_
  57.7 1.0 copy-done.11
  58.7 0.4 copy-done.12
  59.1 0.0 copy-start.6
  59.1 15.2 %outside_steps.2 = (f32[44,384,128]{2,1,0:T(8,128)}, f32[2,384,128]{2,1,0:T(8,128)}, f32[2,384,128]{2,1,0:T(8,128)}, f32[2,384,128]{2,1,0:T(8,128)}, f32[2,384,1...) custom-call(s32[32]{0:T(128)} %scal.15, f32[32,360,128]{2,1,0:T(8,128)} %refs_0_.1, ...), custom_call_target="tpu_custom_call" | custom-call | flops 1610612736 | bytes 15728640 | tf_op jit(solution)/shard_map/outside_steps/pallas_call | solution.py:741
  74.3 0.0 collective-permute-done.5.refs_1_
  74.3 0.0 collective-permute-done.6.refs_2_
  74.3 0.0 collective-permute-done.7.refs_3_
  74.4 0.7 copy-done.7
  75.1 2.9 %free_steps.1 = (f32[8,264,128]{2,1,0:T(8,128)}, f32[16,32,128]{2,1,0:T(8,128)S(1)}) custom-call(s32[32]{0:T(128)S(1)} %copy-done.4, f32[22,32,128]{2,1,0:T(8,128)S(1)} %get-tuple-element.75.refs_0_, f32[22,32,128]{2,1,0:T(8,128)S(1)} %collective-permute-done.5.refs_1_, f32[22,32,128]{2,1,0:T(8,128)S(1)} %collective-permute-done.6.refs_2_, ...), custom_call_target="tpu_custom_call" | custom-call | tf_op jit(solution)/shard_map/free_steps/pallas_call | solution.py:283
  78.0 4.7 %all-to-all-start.1 = ((f32[8,264,128]{2,1,0:T(8,128)}), f32[8,264,128]{2,1,0:T(8,128)S(1)}, u32[]{:S(2)}, u32[]{:S(2)}) async-start(f32[8,264,128]{2,1,0:T(8,128)} %get-tuple-element.87), calls=%async_computation.1 | async-start | bytes 2162688 | tf_op jit(solution)/shard_map/all_to_all | solution.py:1215
  82.8 3.9 %collective-permute-start.8 = (f32[16,32,128]{2,1,0:T(8,128)S(1)}, f32[16,32,128]{2,1,0:T(8,128)S(1)}, u32[]{:S(2)}, u32[]{:S(2)}) collective-permute-start(f32[16,32,128]{2,1,0:T(8,128)S(1)} %get-tuple-element.105), channel_id=1, source_target_pairs={{0,1},{1,0},{2,3},{3,2},{4,5},{5,4},{6,7},{7,6},{24,25},{25,24},{2... | collective-permute-start | bytes 786440 | tf_op jit(solution)/shard_map/ppermute | solution.py:1211
  86.7 19.5 %outside_steps.3 = (f32[32,360,128]{2,1,0:T(8,128)}, f32[4,384,128]{2,1,0:T(8,128)}, f32[4,384,128]{2,1,0:T(8,128)}, f32[4,384,128]{2,1,0:T(8,128)}, f32[4,384,128]{2,1,0:T(8,128)}) custom-call(s32[32]{0:T(128)} %scal.15, f32[44,384,128]{2,1,0:T(8,128)} %get-tuple-element.88.refs_0_, f32[2,384,128]{2,1,0:T(8,128)} %get-tuple-element.73.refs_1_.refs_2_.refs_3_, ...), custom_call_target="tpu_custom_call" | custom-call | flops 3221225472 | bytes 15728640 | tf_op jit(solution)/shard_map/outside_steps/pallas_call | solution.py:741
  106.2 0.0 collective-permute-done.8
  106.2 0.0 copy-start.9
  106.2 0.0 all-to-all-done.1.refs_8_.refs_9_.refs_5_
  106.2 1.1 copy-done.8
  107.3 15.2 %cap_steps.3 = (f32[22,256,128]{2,1,0:T(8,128)}, f32[2,384,128]{2,1,0:T(8,128)}, f32[384,128]{1,0:T(8,128)}, f32[384,128]{1,0:T(8,128)}, f32[24,3072]{1,0:T(8,12...) custom-call(s32[32]{0:T(128)} %scal.15, f32[2,384,128]{2,1,0:T(8,128)} %get-tuple-element.71.refs_0_.refs_1_, ...), custom_call_target="tpu_custom_call" | custom-call | flops 738197504 | bytes 20000000 | tf_op jit(solution)/shard_map/cap_steps/pallas_call | solution.py:1149
  122.5 4.6 %all-to-all-start.2 = ((f32[8,16,384]{2,1,0:T(8,128)}), f32[8,16,384]{2,1,0:T(8,128)S(1)}, u32[]{:S(2)}, u32[]{:S(2)}) async-start(f32[8,16,384]{2,1,0:T(8,128)} %get-tuple-element.107), calls=%async_computation.2 | async-start | bytes 393216 | tf_op jit(solution)/shard_map/all_to_all | solution.py:1215
  127.1 5.7 %collective-permute-start.11 = (f32[2,16,32,128]{3,2,1,0:T(8,128)S(1)}, f32[2,16,32,128]{3,2,1,0:T(8,128)S(1)}, u32[]{:S(2)}, u32[]{:S(2)}) collective-permute-start(f32[2,16,32,128]{3,2,1,0:T(8,128)S(1)} %pad_maximum_fusion.refs_16_), channel_id=1, source_target_pairs={{0,6},{1,7},{2,4},{3,5},{4,2},{5,3},{6,0},{7,1},{24,30},{25,31},{2... | collective-permute-start | bytes 1572872 | tf_op jit(solution)/shard_map/ppermute | solution.py:1211
  132.8 1.9 collective-permute-start.10
  134.7 2.5 %collective-permute-start.9 = (f32[2,16,32,128]{3,2,1,0:T(8,128)S(1)}, f32[2,16,32,128]{3,2,1,0:T(8,128)S(1)}, u32[]{:S(2)}, u32[]{:S(2)}) collective-permute-start(f32[2,16,32,128]{3,2,1,0:T(8,128)S(1)} %pad_maximum_fusion.refs_16_), channel_id=1, source_target_pairs={{0,2},{1,3},{2,0},{3,1},{4,6},{5,7},{6,4},{7,5},{24,26},{25,27},{2... | collective-permute-start | bytes 1572872 | tf_op jit(solution)/shard_map/ppermute | solution.py:1211
  137.2 0.0 all-to-all-done.2.refs_16_
  137.2 0.0 copy-start.14
  137.2 0.7 copy-done.14
  137.9 19.1 %cap_steps.4 = (f32[22,256,128]{2,1,0:T(8,128)}, f32[4,384,128]{2,1,0:T(8,128)}, f32[384,128]{1,0:T(8,128)}, f32[384,128]{1,0:T(8,128)}, f32[24,3072]{1,0:T(8,12...) custom-call(s32[32]{0:T(128)} %scal.15, f32[22,256,128]{2,1,0:T(8,128)} %get-tuple-element.102.refs_0_, ...), custom_call_target="tpu_custom_call" | custom-call | flops 738197504 | bytes 20000000 | tf_op jit(solution)/shard_map/cap_steps/pallas_call | solution.py:1149
  156.9 6.0 %all-to-all-start.3 = ((f32[8,16,384]{2,1,0:T(8,128)}), f32[8,16,384]{2,1,0:T(8,128)S(1)}, u32[]{:S(2)}, u32[]{:S(2)}) async-start(f32[8,16,384]{2,1,0:T(8,128)} %get-tuple-element.114), calls=%async_computation.3 | async-start | bytes 393216 | tf_op jit(solution)/shard_map/all_to_all | solution.py:1215
  162.9 0.0 collective-permute-done.11.refs_19_
  163.0 0.0 collective-permute-done.10.refs_18_
  163.0 0.0 collective-permute-done.9.refs_17_
  163.0 0.0 copy-start.17
  163.0 7.7 %all-to-all-done.3.refs_12_ = f32[8,16,384]{2,1,0:T(8,128)S(1)} async-done(((f32[8,16,384]{2,1,0:T(8,128)}), f32[8,16,384]{2,1,0:T(8,128)S(1)}, u32[]{:S(2)}, u32[]{:S(2)}) %all-to-all-start.3) | async-done | bytes 196640 | tf_op jit(solution)/shard_map/all_to_all | solution.py:1215
  170.7 0.0 copy-done.15
  170.7 0.0 copy-done.17
  170.7 0.7 copy-done.13
  171.4 20.8 %cap_steps.5 = (f32[32,360,128]{2,1,0:T(8,128)}, f32[32,360]{1,0:T(8,128)}) custom-call(s32[32]{0:T(128)} %scal.15, f32[22,256,128]{2,1,0:T(8,128)} %get-tuple-element.111.refs_0_, f32[4,384,128]{2,1,0:T(8,128)} %get-tuple-element.95.refs_4_.refs_5_.refs_1_, ...), custom_call_target="tpu_custom_call", output_to_operand_aliasing={{0}: (24, {})} | custom-call | flops 738197504 | bytes 20000000 | tf_op jit(solution)/shard_map/cap_steps/pallas_call | solution.py:1149
  192.2 0.8 all_to_all.30
  193.0 9.2 %all_to_all.40 = f32[8,4,360]{2,1,0:T(4,128)S(1)} all-to-all(f32[8,4,360]{2,1,0:T(4,128)S(1)} %all_to_all.30), channel_id=1, replica_groups=mesh['lat'=4,'lon'=8] {'lon'}, dimensions={0} | all-to-all | bytes 92160 | tf_op jit(solution)/shard_map/all_to_all | solution.py:1316
  202.2 0.7 all_to_all.33
  (23 shorter events, 0.1 us)
Async XLA Ops:
  1.6 16.0 %collective-permute-start.1 = (f32[32,8,128]{2,1,0:T(8,128)S(1)}, f32[32,8,128]{2,1,0:T(8,128)S(1)}, u32[]{:S(2)}, u32[]{:S(2)}) collective-permute-start(f32[32,8,128]{2,1,0:T(8,128)S(1)} %get-tuple-element.122), channel_id=1, source_target_pairs={{0,7},{1,0},{2,1},{3,2},{4,3},{5,4},{6,5},{7,6},{8,15},{9,8},{10,9... | collective-permute-start | bytes 393224 | tf_op jit(solution)/shard_map/ppermute | solution.py:1205
  7.7 9.6 %copy-start.2 = (s32[32,360]{1,0:T(8,128)S(1)}, s32[32,360]{1,0:T(8,128)}, u32[]{:S(2)}) copy-start(s32[32,360]{1,0:T(8,128)} %land.3) | copy-start | bytes 138244
  7.7 9.6 %copy-start.3 = (f32[4,2880]{1,0:T(4,128)S(1)}, f32[4,2880]{1,0:T(4,128)}, u32[]{:S(2)}) copy-start(f32[4,2880]{1,0:T(4,128)} %sea.1) | copy-start | bytes 138244
  7.7 10.0 %collective-permute-start = (f32[32,8,128]{2,1,0:T(8,128)S(1)}, f32[32,8,128]{2,1,0:T(8,128)S(1)}, u32[]{:S(2)}, u32[]{:S(2)}) collective-permute-start(f32[32,8,128]{2,1,0:T(8,128)S(1)} %get-tuple-element.123), channel_id=1, source_target_pairs={{0,1},{1,2},{2,3},{3,4},{4,5},{5,6},{6,7},{7,0},{8,9},{9,10},{10,1... | collective-permute-start | bytes 393224 | tf_op jit(solution)/shard_map/ppermute | solution.py:1205
  15.4 31.8 %collective-permute-start.4 = (f32[4,22,32,128]{3,2,1,0:T(8,128)}, f32[4,22,32,128]{3,2,1,0:T(8,128)S(1)}, u32[]{:S(2)}, u32[]{:S(2)}) collective-permute-start(f32[4,22,32,128]{3,2,1,0:T(8,128)} %get-tuple-element.68), channel_id=1, source_target_pairs={{0,1},{1,0},{2,3},{3,2},{4,5},{5,4},{6,7},{7,6},{24,25},{25,24},{2... | collective-permute-start | bytes 4325384 | tf_op jit(solution)/shard_map/ppermute | solution.py:1211
  17.6 22.4 %copy-start.18 = (f32[32,8,128]{2,1,0:T(8,128)}, f32[32,8,128]{2,1,0:T(8,128)S(1)}, u32[]{:S(2)}) copy-start(f32[32,8,128]{2,1,0:T(8,128)S(1)} %collective-permute-done.1.east.refs_2_) | copy-start | bytes 393220
  17.6 22.4 %copy-start.19 = (f32[32,8,128]{2,1,0:T(8,128)}, f32[32,8,128]{2,1,0:T(8,128)S(1)}, u32[]{:S(2)}) copy-start(f32[32,8,128]{2,1,0:T(8,128)S(1)} %collective-permute-done.west.refs_1_) | copy-start | bytes 393220
  40.0 7.2 %copy-start.10 = (f32[4,22,32,128]{3,2,1,0:T(8,128)S(1)}, f32[4,22,32,128]{3,2,1,0:T(8,128)}, u32[]{:S(2)}) copy-start(f32[4,22,32,128]{3,2,1,0:T(8,128)} %get-tuple-element.67) | copy-start | bytes 4325380
  44.5 13.1 %collective-permute-start.2 = (f32[6,384,128]{2,1,0:T(8,128)}, f32[6,384,128]{2,1,0:T(8,128)S(1)}, u32[]{:S(2)}, u32[]{:S(2)}) collective-permute-start(f32[6,384,128]{2,1,0:T(8,128)} %get-tuple-element.65), channel_id=1, source_target_pairs={{0,8},{8,16},{16,24},{1,9},{9,17},{17,25},{2,10},{10,18},{18,26},{... | collective-permute-start | bytes 3538952 | tf_op jit(solution)/shard_map/ppermute | solution.py:1205
  45.9 11.8 %collective-permute-start.3 = (f32[6,384,128]{2,1,0:T(8,128)}, f32[6,384,128]{2,1,0:T(8,128)S(1)}, u32[]{:S(2)}, u32[]{:S(2)}) collective-permute-start(f32[6,384,128]{2,1,0:T(8,128)} %get-tuple-element.66), channel_id=1, source_target_pairs={{8,0},{16,8},{24,16},{9,1},{17,9},{25,17},{10,2},{18,10},{26,18},{... | collective-permute-start | bytes 3538952 | tf_op jit(solution)/shard_map/ppermute | solution.py:1205
  47.5 26.8 %collective-permute-start.5 = (f32[22,32,128]{2,1,0:T(8,128)S(1)}, f32[22,32,128]{2,1,0:T(8,128)S(1)}, u32[]{:S(2)}, u32[]{:S(2)}) collective-permute-start(f32[22,32,128]{2,1,0:T(8,128)S(1)} %get-tuple-element.76), channel_id=1, source_target_pairs={{0,2},{1,3},{2,0},{3,1},{4,6},{5,7},{6,4},{7,5},{24,26},{25,27},{2... | collective-permute-start | bytes 1081352 | tf_op jit(solution)/shard_map/ppermute | solution.py:1211
  49.5 24.8 %collective-permute-start.6 = (f32[22,32,128]{2,1,0:T(8,128)S(1)}, f32[22,32,128]{2,1,0:T(8,128)S(1)}, u32[]{:S(2)}, u32[]{:S(2)}) collective-permute-start(f32[22,32,128]{2,1,0:T(8,128)S(1)} %get-tuple-element.77), channel_id=1, source_target_pairs={{0,4},{1,5},{2,6},{3,7},{4,0},{5,1},{6,2},{7,3},{24,28},{25,29},{2... | collective-permute-start | bytes 1081352 | tf_op jit(solution)/shard_map/ppermute | solution.py:1211
  54.6 19.7 %collective-permute-start.7 = (f32[22,32,128]{2,1,0:T(8,128)S(1)}, f32[22,32,128]{2,1,0:T(8,128)S(1)}, u32[]{:S(2)}, u32[]{:S(2)}) collective-permute-start(f32[22,32,128]{2,1,0:T(8,128)S(1)} %get-tuple-element.78), channel_id=1, source_target_pairs={{0,6},{1,7},{2,4},{3,5},{4,2},{5,3},{6,0},{7,1},{24,30},{25,31},{2... | collective-permute-start | bytes 1081352 | tf_op jit(solution)/shard_map/ppermute | solution.py:1211
  57.6 1.0 copy-start.11
  57.7 1.4 copy-start.12
  59.1 15.3 %copy-start = (f32[128,128]{1,0:T(8,128)S(1)}, f32[128,128]{1,0:T(8,128)}, u32[]{:S(2)}) copy-start(f32[128,128]{1,0:T(8,128)} %refs_22_.3) | copy-start | bytes 196612
  59.1 15.3 %copy-start.1 = (f32[2,256,128]{2,1,0:T(8,128)S(1)}, f32[2,256,128]{2,1,0:T(8,128)}, u32[]{:S(2)}) copy-start(f32[2,256,128]{2,1,0:T(8,128)} %constant.14.clone.refs_4_) | copy-start | bytes 786436
  59.1 15.3 %copy-start.4 = (s32[32]{0:T(128)S(1)}, s32[32]{0:T(128)}, u32[]{:S(2)}) copy-start(s32[32]{0:T(128)} %scal.15) | copy-start | bytes 388
  59.1 15.3 %copy-start.5 = (f32[48,128]{1,0:T(8,128)S(1)}, f32[48,128]{1,0:T(8,128)}, u32[]{:S(2)}) copy-start(f32[48,128]{1,0:T(8,128)} %get-tuple-element.84.refs_8_) | copy-start | bytes 73732
  59.1 15.3 %copy-start.6 = (f32[128]{0:T(128)S(1)}, f32[128]{0:T(128)}, u32[]{:S(2)}) copy-start(f32[128]{0:T(128)} %param.15) | copy-start | bytes 1540
  74.4 0.7 copy-start.7
  78.0 28.2 %all-to-all-start.1 = ((f32[8,264,128]{2,1,0:T(8,128)}), f32[8,264,128]{2,1,0:T(8,128)S(1)}, u32[]{:S(2)}, u32[]{:S(2)}) async-start(f32[8,264,128]{2,1,0:T(8,128)} %get-tuple-element.87), calls=%async_computation.1 | async-start | bytes 2162688 | tf_op jit(solution)/shard_map/all_to_all | solution.py:1215
  82.8 23.4 %collective-permute-start.8 = (f32[16,32,128]{2,1,0:T(8,128)S(1)}, f32[16,32,128]{2,1,0:T(8,128)S(1)}, u32[]{:S(2)}, u32[]{:S(2)}) collective-permute-start(f32[16,32,128]{2,1,0:T(8,128)S(1)} %get-tuple-element.105), channel_id=1, source_target_pairs={{0,1},{1,0},{2,3},{3,2},{4,5},{5,4},{6,7},{7,6},{24,25},{25,24},{2... | collective-permute-start | bytes 786440 | tf_op jit(solution)/shard_map/ppermute | solution.py:1211
  106.2 28.5 %copy-start.9 = (f32[2,16,32,128]{3,2,1,0:T(8,128)}, f32[2,16,32,128]{3,2,1,0:T(8,128)S(1)}, u32[]{:S(2)}) copy-start(f32[2,16,32,128]{3,2,1,0:T(8,128)S(1)} %pad_maximum_fusion.refs_16_) | copy-start | bytes 1572868
  106.2 1.1 copy-start.8
  122.5 14.7 %all-to-all-start.2 = ((f32[8,16,384]{2,1,0:T(8,128)}), f32[8,16,384]{2,1,0:T(8,128)S(1)}, u32[]{:S(2)}, u32[]{:S(2)}) async-start(f32[8,16,384]{2,1,0:T(8,128)} %get-tuple-element.107), calls=%async_computation.2 | async-start | bytes 393216 | tf_op jit(solution)/shard_map/all_to_all | solution.py:1215
  127.1 35.9 %collective-permute-start.11 = (f32[2,16,32,128]{3,2,1,0:T(8,128)S(1)}, f32[2,16,32,128]{3,2,1,0:T(8,128)S(1)}, u32[]{:S(2)}, u32[]{:S(2)}) collective-permute-start(f32[2,16,32,128]{3,2,1,0:T(8,128)S(1)} %pad_maximum_fusion.refs_16_), channel_id=1, source_target_pairs={{0,6},{1,7},{2,4},{3,5},{4,2},{5,3},{6,0},{7,1},{24,30},{25,31},{2... | collective-permute-start | bytes 1572872 | tf_op jit(solution)/shard_map/ppermute | solution.py:1211
  132.8 30.2 %collective-permute-start.10 = (f32[2,16,32,128]{3,2,1,0:T(8,128)S(1)}, f32[2,16,32,128]{3,2,1,0:T(8,128)S(1)}, u32[]{:S(2)}, u32[]{:S(2)}) collective-permute-start(f32[2,16,32,128]{3,2,1,0:T(8,128)S(1)} %pad_maximum_fusion.refs_16_), channel_id=1, source_target_pairs={{0,4},{1,5},{2,6},{3,7},{4,0},{5,1},{6,2},{7,3},{24,28},{25,29},{2... | collective-permute-start | bytes 1572872 | tf_op jit(solution)/shard_map/ppermute | solution.py:1211
  134.7 28.3 %collective-permute-start.9 = (f32[2,16,32,128]{3,2,1,0:T(8,128)S(1)}, f32[2,16,32,128]{3,2,1,0:T(8,128)S(1)}, u32[]{:S(2)}, u32[]{:S(2)}) collective-permute-start(f32[2,16,32,128]{3,2,1,0:T(8,128)S(1)} %pad_maximum_fusion.refs_16_), channel_id=1, source_target_pairs={{0,2},{1,3},{2,0},{3,1},{4,6},{5,7},{6,4},{7,5},{24,26},{25,27},{2... | collective-permute-start | bytes 1572872 | tf_op jit(solution)/shard_map/ppermute | solution.py:1211
  137.2 0.7 copy-start.14
  156.9 13.8 %all-to-all-start.3 = ((f32[8,16,384]{2,1,0:T(8,128)}), f32[8,16,384]{2,1,0:T(8,128)S(1)}, u32[]{:S(2)}, u32[]{:S(2)}) async-start(f32[8,16,384]{2,1,0:T(8,128)} %get-tuple-element.114), calls=%async_computation.3 | async-start | bytes 393216 | tf_op jit(solution)/shard_map/all_to_all | solution.py:1215
  162.9 7.8 %copy-start.15 = (f32[2,16,32,128]{3,2,1,0:T(8,128)}, f32[2,16,32,128]{3,2,1,0:T(8,128)S(1)}, u32[]{:S(2)}) copy-start(f32[2,16,32,128]{3,2,1,0:T(8,128)S(1)} %collective-permute-done.11.refs_19_) | copy-start | bytes 1572868
  163.0 7.8 %copy-start.16 = (f32[2,16,32,128]{3,2,1,0:T(8,128)}, f32[2,16,32,128]{3,2,1,0:T(8,128)S(1)}, u32[]{:S(2)}) copy-start(f32[2,16,32,128]{3,2,1,0:T(8,128)S(1)} %collective-permute-done.10.refs_18_) | copy-start | bytes 1572868
  163.0 7.7 %copy-start.17 = (f32[2,16,32,128]{3,2,1,0:T(8,128)}, f32[2,16,32,128]{3,2,1,0:T(8,128)S(1)}, u32[]{:S(2)}) copy-start(f32[2,16,32,128]{3,2,1,0:T(8,128)S(1)} %collective-permute-done.9.refs_17_) | copy-start | bytes 1572868
  170.7 0.7 copy-start.13

commit v7 on v6

--- a/solution.py
+++ b/solution.py
@@ -19,7 +19,7 @@
 ROW0 = STEPS
 WEDGE = STEPS - 1
 BEYOND = 5
-SPLIT = 2
+SPLIT = 3
 
 diffusion_rate = 0.1
 air_gain = 0.5

time: 204 us -> 203 us (level)
  transfers between devices with their start and end apart: 15 -> 15, of which waited for: 1 -> 1; matrix products, arithmetic and copies ran while one was open for 0% -> 0% of each run, Pallas kernels for 33% -> 32%
where the time goes in v7:
time: 203 us; the launch traced here: 202 us
  Pallas kernels  104 us (51%)
  starting transfers between devices  50.1 us (25%)
  blocking collectives  31.6 us (16%)
  waiting for transfers between devices  7.76 us (4%)
  local copies, waits for them, and re-layouts  7.03 us (3%)
    pallas_call x3, Pallas kernels, cap_steps(): pl.pallas_call(functools.partial(cap_kernel, rows, count, width, blocks,...  55 us
    pallas_call x2, Pallas kernels, outside_steps(): pl.pallas_call(functools.partial(outside_kernel, rows, count, width, fast...  33.9 us
    ppermute x8, starting transfers between devices, between_caps(): return lax.ppermute(x, ('lat', 'lon'), pairs)  26.1 us
    all_to_all x1, blocking collectives, spread(): lax.all_to_all(copies, 'lon', split_axis=0, concat_axis=0, tiled=True)  22.4 us
    all_to_all x3, starting transfers between devices, spread(): lax.all_to_all(copies, 'lon', split_axis=0, concat_axis=0, tiled=True)  15.3 us
    all_to_all x1, blocking collectives, local(): sea = lax.all_to_all(sea, 'lon', split_axis=0, concat_axis=1, tiled=True)  9.22 us
    ppermute x4, starting transfers between devices, shift(): return lax.ppermute(x, axis, pairs)  8.72 us
    all_to_all x3, waiting for transfers between devices, spread(): lax.all_to_all(copies, 'lon', split_axis=0, concat_axis=0, tiled=True)  7.73 us
  transfers between devices with their start and end apart: 15, of which 1 were waited for; matrix products, arithmetic and copies ran while one was open for 0% of the time, Pallas kernels for 32%

profile of v7, /device:TPU:0, one launch (start us, length us, event | category | flops | bytes accessed | tf_op | source)
XLA Modules:
  0.0 202.1 jit_solution(8012864090323290487)
XLA Ops:
  0.6 1.0 fusion.4
  1.6 6.1 %collective-permute-start.1 = (f32[32,8,128]{2,1,0:T(8,128)S(1)}, f32[32,8,128]{2,1,0:T(8,128)S(1)}, u32[]{:S(2)}, u32[]{:S(2)}) collective-permute-start(f32[32,8,128]{2,1,0:T(8,128)S(1)} %get-tuple-element.122), channel_id=1, source_target_pairs={{0,7},{1,0},{2,1},{3,2},{4,3},{5,4},{6,5},{7,6},{8,15},{9,8},{10,9... | collective-permute-start | bytes 393224 | tf_op jit(solution)/shard_map/ppermute | solution.py:1205
  7.7 0.0 collective-permute-start
  7.7 7.7 %start_spectra.1 = (f32[4,22,32,128]{3,2,1,0:T(8,128)}, f32[4,22,32,128]{3,2,1,0:T(8,128)}) custom-call(s32[32]{0:T(128)} %scal.15, f32[32,360,128]{2,1,0:T(8,128)} %refs_0_.1, bf16[8,256,1152]{2,1,0:T(8,128)(2,1)} %constant.17.clone.table), custom_call_target="tpu_custom_call" | custom-call | tf_op jit(solution)/shard_map/start_spectra/pallas_call | solution.py:212
  15.4 1.9 collective-permute-start.4
  17.3 0.0 copy-done.2
  17.3 0.0 copy-done.3
  17.3 0.3 shares_of_sea.1
  17.6 0.0 collective-permute-done.1.east.refs_2_
  17.6 0.0 copy-start.16
  17.6 0.0 collective-permute-done.west.refs_1_
  17.6 0.0 copy-start.17
  17.7 22.4 %all_to_all.39.got = f32[8,32,376]{2,1,0:T(8,128)} all-to-all(f32[8,32,376]{2,1,0:T(8,128)S(1)} %shares_of_sea.1), channel_id=1, replica_groups=mesh['lat'=4,'lon'=8] {'lon'}, dimensions={0} | all-to-all | bytes 770048 | tf_op jit(solution)/shard_map/all_to_all | solution.py:1215
  40.0 0.0 copy-done.16
  40.0 0.0 copy-done.17
  40.0 4.5 %windows.1 = (f32[2,32,384]{2,1,0:T(8,128)}, f32[24,3072]{1,0:T(8,128)}, f32[48,128]{1,0:T(8,128)}, f32[6,384,128]{2,1,0:T(8,128)}, f32[6,384,128]{2,1,0:T(8,128)}) custom-call(s32[32]{0:T(128)} %scal.15, f32[8,32,376]{2,1,0:T(8,128)} %all_to_all.39.got, s32[32,360]{1,0:T(8,128)} %land.3, f32[32,360,128]{2,1,0:T(8,128)} %refs_0_.1, ...), custom_call_target="tpu_custom_call" | custom-call | tf_op jit(solution)/shard_map/windows/pallas_call | solution.py:453
  44.5 1.4 collective-permute-start.2
  45.9 1.3 collective-permute-start.3
  47.2 0.0 collective-permute-done.4
  47.2 0.0 copy-done.10
  47.2 0.3 fusion
  47.5 2.0 %collective-permute-start.5 = (f32[22,32,128]{2,1,0:T(8,128)S(1)}, f32[22,32,128]{2,1,0:T(8,128)S(1)}, u32[]{:S(2)}, u32[]{:S(2)}) collective-permute-start(f32[22,32,128]{2,1,0:T(8,128)S(1)} %get-tuple-element.76), channel_id=1, source_target_pairs={{0,2},{1,3},{2,0},{3,1},{4,6},{5,7},{6,4},{7,5},{24,26},{25,27},{2... | collective-permute-start | bytes 1081352 | tf_op jit(solution)/shard_map/ppermute | solution.py:1211
  49.5 5.1 %collective-permute-start.6 = (f32[22,32,128]{2,1,0:T(8,128)S(1)}, f32[22,32,128]{2,1,0:T(8,128)S(1)}, u32[]{:S(2)}, u32[]{:S(2)}) collective-permute-start(f32[22,32,128]{2,1,0:T(8,128)S(1)} %get-tuple-element.77), channel_id=1, source_target_pairs={{0,4},{1,5},{2,6},{3,7},{4,0},{5,1},{6,2},{7,3},{24,28},{25,29},{2... | collective-permute-start | bytes 1081352 | tf_op jit(solution)/shard_map/ppermute | solution.py:1211
  54.6 3.0 %collective-permute-start.7 = (f32[22,32,128]{2,1,0:T(8,128)S(1)}, f32[22,32,128]{2,1,0:T(8,128)S(1)}, u32[]{:S(2)}, u32[]{:S(2)}) collective-permute-start(f32[22,32,128]{2,1,0:T(8,128)S(1)} %get-tuple-element.78), channel_id=1, source_target_pairs={{0,6},{1,7},{2,4},{3,5},{4,2},{5,3},{6,0},{7,1},{24,30},{25,31},{2... | collective-permute-start | bytes 1081352 | tf_op jit(solution)/shard_map/ppermute | solution.py:1211
  57.6 0.0 collective-permute-done.2.refs_3_
  57.6 0.0 copy-start.18
  57.6 0.0 collective-permute-done.3.refs_4_
  57.7 0.0 copy-start.19
  57.7 1.0 copy-done.18
  58.7 0.4 copy-done.19
  59.1 0.0 copy-start.6
  59.1 18.7 %outside_steps.2 = (f32[44,384,128]{2,1,0:T(8,128)}, f32[3,384,128]{2,1,0:T(8,128)}, f32[3,384,128]{2,1,0:T(8,128)}, f32[3,384,128]{2,1,0:T(8,128)}, f32[3,384,1...) custom-call(s32[32]{0:T(128)} %scal.15, f32[32,360,128]{2,1,0:T(8,128)} %refs_0_.1, ...), custom_call_target="tpu_custom_call" | custom-call | flops 2415919104 | bytes 15728640 | tf_op jit(solution)/shard_map/outside_steps/pallas_call | solution.py:741
  77.8 0.0 collective-permute-done.5.refs_1_
  77.8 0.0 collective-permute-done.6.refs_2_
  77.8 0.0 collective-permute-done.7.refs_3_
  77.8 0.0 copy-done
  77.9 0.0 copy-done.1
  77.9 0.7 copy-done.7
  78.6 2.9 %free_steps.1 = (f32[8,264,128]{2,1,0:T(8,128)}, f32[16,32,128]{2,1,0:T(8,128)S(1)}) custom-call(s32[32]{0:T(128)S(1)} %copy-done.4, f32[22,32,128]{2,1,0:T(8,128)S(1)} %get-tuple-element.75.refs_0_, f32[22,32,128]{2,1,0:T(8,128)S(1)} %collective-permute-done.5.refs_1_, f32[22,32,128]{2,1,0:T(8,128)S(1)} %collective-permute-done.6.refs_2_, ...), custom_call_target="tpu_custom_call" | custom-call | tf_op jit(solution)/shard_map/free_steps/pallas_call | solution.py:283
  81.5 4.7 %all-to-all-start.1 = ((f32[8,264,128]{2,1,0:T(8,128)}), f32[8,264,128]{2,1,0:T(8,128)S(1)}, u32[]{:S(2)}, u32[]{:S(2)}) async-start(f32[8,264,128]{2,1,0:T(8,128)} %get-tuple-element.87), calls=%async_computation.1 | async-start | bytes 2162688 | tf_op jit(solution)/shard_map/all_to_all | solution.py:1215
  86.2 3.9 %collective-permute-start.8 = (f32[16,32,128]{2,1,0:T(8,128)S(1)}, f32[16,32,128]{2,1,0:T(8,128)S(1)}, u32[]{:S(2)}, u32[]{:S(2)}) collective-permute-start(f32[16,32,128]{2,1,0:T(8,128)S(1)} %get-tuple-element.105), channel_id=1, source_target_pairs={{0,1},{1,0},{2,3},{3,2},{4,5},{5,4},{6,7},{7,6},{24,25},{25,24},{2... | collective-permute-start | bytes 786440 | tf_op jit(solution)/shard_map/ppermute | solution.py:1211
  90.1 15.2 %outside_steps.3 = (f32[32,360,128]{2,1,0:T(8,128)}, f32[3,384,128]{2,1,0:T(8,128)}, f32[3,384,128]{2,1,0:T(8,128)}, f32[3,384,128]{2,1,0:T(8,128)}, f32[3,384,128]{2,1,0:T(8,128)}) custom-call(s32[32]{0:T(128)} %scal.15, f32[44,384,128]{2,1,0:T(8,128)} %get-tuple-element.88.refs_0_, f32[3,384,128]{2,1,0:T(8,128)} %get-tuple-element.73.refs_1_.refs_2_.refs_3_, ...), custom_call_target="tpu_custom_call" | custom-call | flops 2415919104 | bytes 15728640 | tf_op jit(solution)/shard_map/outside_steps/pallas_call | solution.py:741
  105.4 0.0 collective-permute-done.8
  105.4 0.0 all-to-all-done.1.refs_4_.refs_9_.refs_5_
  105.4 1.0 copy-done.8
  106.5 15.2 %cap_steps.3 = (f32[22,256,128]{2,1,0:T(8,128)}, f32[2,384,128]{2,1,0:T(8,128)}, f32[384,128]{1,0:T(8,128)}, f32[384,128]{1,0:T(8,128)}, f32[24,3072]{1,0:T(8,12...) custom-call(s32[32]{0:T(128)} %scal.15, f32[3,384,128]{2,1,0:T(8,128)} %get-tuple-element.71.refs_0_.refs_1_, ...), custom_call_target="tpu_custom_call" | custom-call | flops 738197504 | bytes 20000000 | tf_op jit(solution)/shard_map/cap_steps/pallas_call | solution.py:1149
  121.7 4.6 %all-to-all-start.2 = ((f32[8,16,384]{2,1,0:T(8,128)}), f32[8,16,384]{2,1,0:T(8,128)S(1)}, u32[]{:S(2)}, u32[]{:S(2)}) async-start(f32[8,16,384]{2,1,0:T(8,128)} %get-tuple-element.107), calls=%async_computation.2 | async-start | bytes 393216 | tf_op jit(solution)/shard_map/all_to_all | solution.py:1215
  126.2 5.7 %collective-permute-start.11 = (f32[2,16,32,128]{3,2,1,0:T(8,128)S(1)}, f32[2,16,32,128]{3,2,1,0:T(8,128)S(1)}, u32[]{:S(2)}, u32[]{:S(2)}) collective-permute-start(f32[2,16,32,128]{3,2,1,0:T(8,128)S(1)} %pad_maximum_fusion.refs_16_), channel_id=1, source_target_pairs={{0,6},{1,7},{2,4},{3,5},{4,2},{5,3},{6,0},{7,1},{24,30},{25,31},{2... | collective-permute-start | bytes 1572872 | tf_op jit(solution)/shard_map/ppermute | solution.py:1211
  131.9 1.9 collective-permute-start.10
  133.9 2.5 %collective-permute-start.9 = (f32[2,16,32,128]{3,2,1,0:T(8,128)S(1)}, f32[2,16,32,128]{3,2,1,0:T(8,128)S(1)}, u32[]{:S(2)}, u32[]{:S(2)}) collective-permute-start(f32[2,16,32,128]{3,2,1,0:T(8,128)S(1)} %pad_maximum_fusion.refs_16_), channel_id=1, source_target_pairs={{0,2},{1,3},{2,0},{3,1},{4,6},{5,7},{6,4},{7,5},{24,26},{25,27},{2... | collective-permute-start | bytes 1572872 | tf_op jit(solution)/shard_map/ppermute | solution.py:1211
  136.3 0.0 all-to-all-done.2.refs_16_
  136.4 0.7 copy-done.12
  137.0 19.1 %cap_steps.4 = (f32[22,256,128]{2,1,0:T(8,128)}, f32[4,384,128]{2,1,0:T(8,128)}, f32[384,128]{1,0:T(8,128)}, f32[384,128]{1,0:T(8,128)}, f32[24,3072]{1,0:T(8,12...) custom-call(s32[32]{0:T(128)} %scal.15, f32[22,256,128]{2,1,0:T(8,128)} %get-tuple-element.98.refs_0_, ...), custom_call_target="tpu_custom_call" | custom-call | flops 738197504 | bytes 20000000 | tf_op jit(solution)/shard_map/cap_steps/pallas_call | solution.py:1149
  156.1 6.0 %all-to-all-start.3 = ((f32[8,16,384]{2,1,0:T(8,128)}), f32[8,16,384]{2,1,0:T(8,128)S(1)}, u32[]{:S(2)}, u32[]{:S(2)}) async-start(f32[8,16,384]{2,1,0:T(8,128)} %get-tuple-element.114), calls=%async_computation.3 | async-start | bytes 393216 | tf_op jit(solution)/shard_map/all_to_all | solution.py:1215
  162.1 0.0 collective-permute-done.11.refs_19_
  162.1 0.0 copy-start.13
  162.1 0.0 collective-permute-done.10.refs_18_
  162.1 0.0 collective-permute-done.9.refs_17_
  162.1 7.7 %all-to-all-done.3.refs_12_ = f32[8,16,384]{2,1,0:T(8,128)S(1)} async-done(((f32[8,16,384]{2,1,0:T(8,128)}), f32[8,16,384]{2,1,0:T(8,128)S(1)}, u32[]{:S(2)}, u32[]{:S(2)}) %all-to-all-start.3) | async-done | bytes 196640 | tf_op jit(solution)/shard_map/all_to_all | solution.py:1215
  169.9 0.7 copy-done.11
  170.5 20.8 %cap_steps.5 = (f32[32,360,128]{2,1,0:T(8,128)}, f32[32,360]{1,0:T(8,128)}) custom-call(s32[32]{0:T(128)} %scal.15, f32[22,256,128]{2,1,0:T(8,128)} %get-tuple-element.111.refs_0_, f32[3,384,128]{2,1,0:T(8,128)} %get-tuple-element.99.refs_5_.refs_1_, f32[3,384,128]{2,1,0:T(8,128)} %get-tuple-element.100.refs_6_.refs_2_, ...), custom_call_target="tpu_custom_call", output_to_operand_aliasing={{0}: (24, {})} | custom-call | flops 738197504 | bytes 20000000 | tf_op jit(solution)/shard_map/cap_steps/pallas_call | solution.py:1149
  191.3 0.8 all_to_all.30
  192.2 9.2 %all_to_all.40 = f32[8,4,360]{2,1,0:T(4,128)S(1)} all-to-all(f32[8,4,360]{2,1,0:T(4,128)S(1)} %all_to_all.30), channel_id=1, replica_groups=mesh['lat'=4,'lon'=8] {'lon'}, dimensions={0} | all-to-all | bytes 92160 | tf_op jit(solution)/shard_map/all_to_all | solution.py:1316
  201.4 0.7 all_to_all.33
  (23 shorter events, 0.1 us)
Async XLA Ops:
  1.6 16.0 %collective-permute-start.1 = (f32[32,8,128]{2,1,0:T(8,128)S(1)}, f32[32,8,128]{2,1,0:T(8,128)S(1)}, u32[]{:S(2)}, u32[]{:S(2)}) collective-permute-start(f32[32,8,128]{2,1,0:T(8,128)S(1)} %get-tuple-element.122), channel_id=1, source_target_pairs={{0,7},{1,0},{2,1},{3,2},{4,3},{5,4},{6,5},{7,6},{8,15},{9,8},{10,9... | collective-permute-start | bytes 393224 | tf_op jit(solution)/shard_map/ppermute | solution.py:1205
  7.7 9.6 %copy-start.2 = (s32[32,360]{1,0:T(8,128)S(1)}, s32[32,360]{1,0:T(8,128)}, u32[]{:S(2)}) copy-start(s32[32,360]{1,0:T(8,128)} %land.3) | copy-start | bytes 138244
  7.7 9.6 %copy-start.3 = (f32[4,2880]{1,0:T(4,128)S(1)}, f32[4,2880]{1,0:T(4,128)}, u32[]{:S(2)}) copy-start(f32[4,2880]{1,0:T(4,128)} %sea.1) | copy-start | bytes 138244
  7.7 10.0 %collective-permute-start = (f32[32,8,128]{2,1,0:T(8,128)S(1)}, f32[32,8,128]{2,1,0:T(8,128)S(1)}, u32[]{:S(2)}, u32[]{:S(2)}) collective-permute-start(f32[32,8,128]{2,1,0:T(8,128)S(1)} %get-tuple-element.123), channel_id=1, source_target_pairs={{0,1},{1,2},{2,3},{3,4},{4,5},{5,6},{6,7},{7,0},{8,9},{9,10},{10,1... | collective-permute-start | bytes 393224 | tf_op jit(solution)/shard_map/ppermute | solution.py:1205
  15.4 31.8 %collective-permute-start.4 = (f32[4,22,32,128]{3,2,1,0:T(8,128)}, f32[4,22,32,128]{3,2,1,0:T(8,128)S(1)}, u32[]{:S(2)}, u32[]{:S(2)}) collective-permute-start(f32[4,22,32,128]{3,2,1,0:T(8,128)} %get-tuple-element.68), channel_id=1, source_target_pairs={{0,1},{1,0},{2,3},{3,2},{4,5},{5,4},{6,7},{7,6},{24,25},{25,24},{2... | collective-permute-start | bytes 4325384 | tf_op jit(solution)/shard_map/ppermute | solution.py:1211
  17.6 22.4 %copy-start.16 = (f32[32,8,128]{2,1,0:T(8,128)}, f32[32,8,128]{2,1,0:T(8,128)S(1)}, u32[]{:S(2)}) copy-start(f32[32,8,128]{2,1,0:T(8,128)S(1)} %collective-permute-done.1.east.refs_2_) | copy-start | bytes 393220
  17.6 22.4 %copy-start.17 = (f32[32,8,128]{2,1,0:T(8,128)}, f32[32,8,128]{2,1,0:T(8,128)S(1)}, u32[]{:S(2)}) copy-start(f32[32,8,128]{2,1,0:T(8,128)S(1)} %collective-permute-done.west.refs_1_) | copy-start | bytes 393220
  40.0 7.2 %copy-start.10 = (f32[4,22,32,128]{3,2,1,0:T(8,128)S(1)}, f32[4,22,32,128]{3,2,1,0:T(8,128)}, u32[]{:S(2)}) copy-start(f32[4,22,32,128]{3,2,1,0:T(8,128)} %get-tuple-element.67) | copy-start | bytes 4325380
  44.5 13.1 %collective-permute-start.2 = (f32[6,384,128]{2,1,0:T(8,128)}, f32[6,384,128]{2,1,0:T(8,128)S(1)}, u32[]{:S(2)}, u32[]{:S(2)}) collective-permute-start(f32[6,384,128]{2,1,0:T(8,128)} %get-tuple-element.65), channel_id=1, source_target_pairs={{0,8},{8,16},{16,24},{1,9},{9,17},{17,25},{2,10},{10,18},{18,26},{... | collective-permute-start | bytes 3538952 | tf_op jit(solution)/shard_map/ppermute | solution.py:1205
  45.9 11.8 %collective-permute-start.3 = (f32[6,384,128]{2,1,0:T(8,128)}, f32[6,384,128]{2,1,0:T(8,128)S(1)}, u32[]{:S(2)}, u32[]{:S(2)}) collective-permute-start(f32[6,384,128]{2,1,0:T(8,128)} %get-tuple-element.66), channel_id=1, source_target_pairs={{8,0},{16,8},{24,16},{9,1},{17,9},{25,17},{10,2},{18,10},{26,18},{... | collective-permute-start | bytes 3538952 | tf_op jit(solution)/shard_map/ppermute | solution.py:1205
  47.5 30.3 %collective-permute-start.5 = (f32[22,32,128]{2,1,0:T(8,128)S(1)}, f32[22,32,128]{2,1,0:T(8,128)S(1)}, u32[]{:S(2)}, u32[]{:S(2)}) collective-permute-start(f32[22,32,128]{2,1,0:T(8,128)S(1)} %get-tuple-element.76), channel_id=1, source_target_pairs={{0,2},{1,3},{2,0},{3,1},{4,6},{5,7},{6,4},{7,5},{24,26},{25,27},{2... | collective-permute-start | bytes 1081352 | tf_op jit(solution)/shard_map/ppermute | solution.py:1211
  49.5 28.3 %collective-permute-start.6 = (f32[22,32,128]{2,1,0:T(8,128)S(1)}, f32[22,32,128]{2,1,0:T(8,128)S(1)}, u32[]{:S(2)}, u32[]{:S(2)}) collective-permute-start(f32[22,32,128]{2,1,0:T(8,128)S(1)} %get-tuple-element.77), channel_id=1, source_target_pairs={{0,4},{1,5},{2,6},{3,7},{4,0},{5,1},{6,2},{7,3},{24,28},{25,29},{2... | collective-permute-start | bytes 1081352 | tf_op jit(solution)/shard_map/ppermute | solution.py:1211
  54.6 23.2 %collective-permute-start.7 = (f32[22,32,128]{2,1,0:T(8,128)S(1)}, f32[22,32,128]{2,1,0:T(8,128)S(1)}, u32[]{:S(2)}, u32[]{:S(2)}) collective-permute-start(f32[22,32,128]{2,1,0:T(8,128)S(1)} %get-tuple-element.78), channel_id=1, source_target_pairs={{0,6},{1,7},{2,4},{3,5},{4,2},{5,3},{6,0},{7,1},{24,30},{25,31},{2... | collective-permute-start | bytes 1081352 | tf_op jit(solution)/shard_map/ppermute | solution.py:1211
  57.6 1.0 copy-start.18
  57.7 1.4 copy-start.19
  59.1 18.8 %copy-start = (f32[128,128]{1,0:T(8,128)S(1)}, f32[128,128]{1,0:T(8,128)}, u32[]{:S(2)}) copy-start(f32[128,128]{1,0:T(8,128)} %refs_22_.3) | copy-start | bytes 196612
  59.1 18.8 %copy-start.1 = (f32[2,256,128]{2,1,0:T(8,128)S(1)}, f32[2,256,128]{2,1,0:T(8,128)}, u32[]{:S(2)}) copy-start(f32[2,256,128]{2,1,0:T(8,128)} %constant.14.clone.refs_4_) | copy-start | bytes 786436
  59.1 18.8 %copy-start.4 = (s32[32]{0:T(128)S(1)}, s32[32]{0:T(128)}, u32[]{:S(2)}) copy-start(s32[32]{0:T(128)} %scal.15) | copy-start | bytes 388
  59.1 18.8 %copy-start.5 = (f32[48,128]{1,0:T(8,128)S(1)}, f32[48,128]{1,0:T(8,128)}, u32[]{:S(2)}) copy-start(f32[48,128]{1,0:T(8,128)} %get-tuple-element.84.refs_8_) | copy-start | bytes 73732
  59.1 18.8 %copy-start.6 = (f32[128]{0:T(128)S(1)}, f32[128]{0:T(128)}, u32[]{:S(2)}) copy-start(f32[128]{0:T(128)} %param.15) | copy-start | bytes 1540
  77.9 0.7 copy-start.7
  81.5 23.9 %all-to-all-start.1 = ((f32[8,264,128]{2,1,0:T(8,128)}), f32[8,264,128]{2,1,0:T(8,128)S(1)}, u32[]{:S(2)}, u32[]{:S(2)}) async-start(f32[8,264,128]{2,1,0:T(8,128)} %get-tuple-element.87), calls=%async_computation.1 | async-start | bytes 2162688 | tf_op jit(solution)/shard_map/all_to_all | solution.py:1215
  86.2 19.1 %collective-permute-start.8 = (f32[16,32,128]{2,1,0:T(8,128)S(1)}, f32[16,32,128]{2,1,0:T(8,128)S(1)}, u32[]{:S(2)}, u32[]{:S(2)}) collective-permute-start(f32[16,32,128]{2,1,0:T(8,128)S(1)} %get-tuple-element.105), channel_id=1, source_target_pairs={{0,1},{1,0},{2,3},{3,2},{4,5},{5,4},{6,7},{7,6},{24,25},{25,24},{2... | collective-permute-start | bytes 786440 | tf_op jit(solution)/shard_map/ppermute | solution.py:1211
  105.4 50.7 %copy-start.9 = (f32[2,16,32,128]{3,2,1,0:T(8,128)}, f32[2,16,32,128]{3,2,1,0:T(8,128)S(1)}, u32[]{:S(2)}) copy-start(f32[2,16,32,128]{3,2,1,0:T(8,128)S(1)} %pad_maximum_fusion.refs_16_) | copy-start | bytes 1572868
  105.4 1.0 copy-start.8
  121.7 14.7 %all-to-all-start.2 = ((f32[8,16,384]{2,1,0:T(8,128)}), f32[8,16,384]{2,1,0:T(8,128)S(1)}, u32[]{:S(2)}, u32[]{:S(2)}) async-start(f32[8,16,384]{2,1,0:T(8,128)} %get-tuple-element.107), calls=%async_computation.2 | async-start | bytes 393216 | tf_op jit(solution)/shard_map/all_to_all | solution.py:1215
  126.2 35.9 %collective-permute-start.11 = (f32[2,16,32,128]{3,2,1,0:T(8,128)S(1)}, f32[2,16,32,128]{3,2,1,0:T(8,128)S(1)}, u32[]{:S(2)}, u32[]{:S(2)}) collective-permute-start(f32[2,16,32,128]{3,2,1,0:T(8,128)S(1)} %pad_maximum_fusion.refs_16_), channel_id=1, source_target_pairs={{0,6},{1,7},{2,4},{3,5},{4,2},{5,3},{6,0},{7,1},{24,30},{25,31},{2... | collective-permute-start | bytes 1572872 | tf_op jit(solution)/shard_map/ppermute | solution.py:1211
  131.9 30.2 %collective-permute-start.10 = (f32[2,16,32,128]{3,2,1,0:T(8,128)S(1)}, f32[2,16,32,128]{3,2,1,0:T(8,128)S(1)}, u32[]{:S(2)}, u32[]{:S(2)}) collective-permute-start(f32[2,16,32,128]{3,2,1,0:T(8,128)S(1)} %pad_maximum_fusion.refs_16_), channel_id=1, source_target_pairs={{0,4},{1,5},{2,6},{3,7},{4,0},{5,1},{6,2},{7,3},{24,28},{25,29},{2... | collective-permute-start | bytes 1572872 | tf_op jit(solution)/shard_map/ppermute | solution.py:1211
  133.9 28.3 %collective-permute-start.9 = (f32[2,16,32,128]{3,2,1,0:T(8,128)S(1)}, f32[2,16,32,128]{3,2,1,0:T(8,128)S(1)}, u32[]{:S(2)}, u32[]{:S(2)}) collective-permute-start(f32[2,16,32,128]{3,2,1,0:T(8,128)S(1)} %pad_maximum_fusion.refs_16_), channel_id=1, source_target_pairs={{0,2},{1,3},{2,0},{3,1},{4,6},{5,7},{6,4},{7,5},{24,26},{25,27},{2... | collective-permute-start | bytes 1572872 | tf_op jit(solution)/shard_map/ppermute | solution.py:1211
  136.4 0.7 copy-start.12
  156.1 13.8 %all-to-all-start.3 = ((f32[8,16,384]{2,1,0:T(8,128)}), f32[8,16,384]{2,1,0:T(8,128)S(1)}, u32[]{:S(2)}, u32[]{:S(2)}) async-start(f32[8,16,384]{2,1,0:T(8,128)} %get-tuple-element.114), calls=%async_computation.3 | async-start | bytes 393216 | tf_op jit(solution)/shard_map/all_to_all | solution.py:1215
  162.1 7.8 %copy-start.13 = (f32[2,16,32,128]{3,2,1,0:T(8,128)}, f32[2,16,32,128]{3,2,1,0:T(8,128)S(1)}, u32[]{:S(2)}) copy-start(f32[2,16,32,128]{3,2,1,0:T(8,128)S(1)} %collective-permute-done.11.refs_19_) | copy-start | bytes 1572868
  162.1 7.8 %copy-start.14 = (f32[2,16,32,128]{3,2,1,0:T(8,128)}, f32[2,16,32,128]{3,2,1,0:T(8,128)S(1)}, u32[]{:S(2)}) copy-start(f32[2,16,32,128]{3,2,1,0:T(8,128)S(1)} %collective-permute-done.10.refs_18_) | copy-start | bytes 1572868
  162.1 7.7 %copy-start.15 = (f32[2,16,32,128]{3,2,1,0:T(8,128)}, f32[2,16,32,128]{3,2,1,0:T(8,128)S(1)}, u32[]{:S(2)}) copy-start(f32[2,16,32,128]{3,2,1,0:T(8,128)S(1)} %collective-permute-done.9.refs_17_) | copy-start | bytes 1572868
  169.9 0.7 copy-start.11
